TPU v7x, 32 devices: a whole 2x2x4 slice. The times are simulated.
32 devices in a mesh: dp: 8 (over y, x, core), mp: 4 (over z).
Axes of the slice: x: 2, y: 2, z: 4, core: 2. Of those that a mesh axis runs over, the one named last changes fastest.
Arguments:
- layer_input: bfloat16 [8, 1024, 2048], P(None, 'dp', 'mp'), may hold values from -6 to 6
- output_grad: bfloat16 [8, 1024, 2048], P('dp', None, 'mp'), may hold values from -6 to 6
- seq_lengths: int32 [8], replicated, may hold values from 1 to 1024, 4352 in all
- deal_order: int32 [8], replicated, may hold values from 0 to 7, each once
- bucket_index: int32 [2047], replicated, may hold values from 0 to 31
- query_weight: float32 [2048, 2048], P('dp', 'mp'), may hold values from -0.015625 to 0.015625
- key_weight: float32 [2048, 2048], P('dp', 'mp'), may hold values from -0.125 to 0.125
- value_weight: float32 [2048, 2048], P('dp', 'mp'), may hold values from -0.125 to 0.125
- out_weight: float32 [2048, 2048], P('mp', 'dp'), may hold values from -1 to 1
- gate_weight: float32 [2048, 5120], P('dp', 'mp'), may hold values from -0.125 to 0.125
- up_weight: float32 [2048, 5120], P('dp', 'mp'), may hold values from -0.125 to 0.125
- down_weight: float32 [5120, 2048], P('mp', 'dp'), may hold values from -0.078125 to 0.078125
- attn_gain: float32 [2048], P('dp'), may hold values from 0.5 to 1.5
- ffn_gain: float32 [2048], P('dp'), may hold values from 0.5 to 1.5
- bias_table: float32 [32, 32], P('dp', 'mp'), may hold values from -6 to 6
- query_moment: float32 [2048, 2048], P('dp', 'mp'), may hold values from -12 to 12
- key_moment: float32 [2048, 2048], P('dp', 'mp'), may hold values from -1.5 to 1.5
- value_moment: float32 [2048, 2048], P('dp', 'mp'), may hold values from -1.5 to 1.5
- out_moment: float32 [2048, 2048], P('mp', 'dp'), may hold values from -0.18 to 0.18
- gate_moment: float32 [2048, 5120], P('dp', 'mp'), may hold values from -0.6 to 0.6
- up_moment: float32 [2048, 5120], P('dp', 'mp'), may hold values from -0.6 to 0.6
- down_moment: float32 [5120, 2048], P('mp', 'dp'), may hold values from -0.9 to 0.9
- attn_gain_moment: float32 [2048], P('dp'), may hold values from -2.4 to 2.4
- ffn_gain_moment: float32 [2048], P('dp'), may hold values from -1.2 to 1.2
- table_moment: float32 [32, 32], P('dp', 'mp'), may hold values from -2.1 to 2.1
Outputs:
- layer_out: bfloat16 [8, 1024, 2048], P('dp', None, 'mp')
- input_grad: bfloat16 [8, 1024, 2048], P(None, 'dp', 'mp')
- grad_norm: float32 [], replicated
- next_query_moment: float32 [2048, 2048], P('dp', 'mp')
- next_key_moment: float32 [2048, 2048], P('dp', 'mp')
- next_value_moment: float32 [2048, 2048], P('dp', 'mp')
- next_out_moment: float32 [2048, 2048], P('mp', 'dp')
- next_gate_moment: float32 [2048, 5120], P('dp', 'mp')
- next_up_moment: float32 [2048, 5120], P('dp', 'mp')
- next_down_moment: float32 [5120, 2048], P('mp', 'dp')
- next_attn_gain_moment: float32 [2048], P('dp')
- next_ffn_gain_moment: float32 [2048], P('dp')
- next_table_moment: float32 [32, 32], P('dp', 'mp')
Inputs may be any that keep to these rules, and one draw needn't show every extreme that they name: `seq_lengths`: one sequence has exactly 1024 valid tokens. Every sequence is named once; index g of dp processes sequence deal_order[g]. `bucket_index`: entry r + 1023 is the bucket of key position minus query position r.
All inputs are finite; a program needn't handle non-finite values.
Results may differ from a plain program's by a relative error of at most 0.015.
Values may be sent and summed in bfloat16 or wider, within the bound.
No kernel may reach another device: no remote copies, remote signals or barrier semaphores. Data moves between devices by JAX's collectives and lax.ppermute only.
A program may use at most 320 MiB of HBM per device.

v0:
```python
import math

import jax
import jax.numpy as jnp
from jax import lax
from jax.sharding import PartitionSpec as P

D = 2048
H = 32
DH = 64
FF = 5120
NB = 32


EPS = 1e-06
NEG = -1e30


def norm_forward(row_data, gain_row):
    inv_rms = lax.rsqrt(jnp.mean(row_data * row_data, axis=-1, keepdims=True) + EPS)
    return ((row_data * inv_rms * gain_row).astype(jnp.bfloat16), inv_rms)


def norm_backward(grad_normed, row_data, inv_rms, gain_row):
    grad_gain = jnp.sum(grad_normed * (row_data * inv_rms), axis=0)
    weighted = grad_normed * gain_row
    row_inner = jnp.mean(weighted * row_data, axis=-1, keepdims=True)
    return (inv_rms * weighted - row_data * (inv_rms * inv_rms * inv_rms) * row_inner, grad_gain)


def skew_bias(rel_rows, start_row, block_rows, key_count):
    width = block_rows + key_count - 1
    segment = lax.dynamic_slice_in_dim(rel_rows, key_count - start_row - block_rows, width, 1)
    heads_dev = segment.shape[0]
    tiled = jnp.tile(segment, (1, block_rows))
    tiled = lax.slice_in_dim(
        tiled, block_rows - 1, block_rows - 1 + block_rows * (width - 1), axis=1
    )
    return tiled.reshape(heads_dev, block_rows, width - 1)[:, :, :key_count]


def unskew_grad(grad_block, block_rows, key_count):
    width = block_rows + key_count - 1
    heads_dev = grad_block.shape[0]
    padded = jnp.pad(grad_block, ((0, 0), (0, 0), (0, width - 1 - key_count)))
    flat = padded.reshape(heads_dev, block_rows * (width - 1))
    flat = jnp.pad(flat, ((0, 0), (block_rows - 1, 1)))
    return jnp.sum(flat.reshape(heads_dev, block_rows, width), axis=1)


def block_scores(query_block, start_row, key_rows, rel_rows, key_valid):
    block_rows = query_block.shape[0]
    key_count = key_rows.shape[0]
    bias_block = skew_bias(rel_rows, start_row, block_rows, key_count)
    scores = (
        jnp.einsum("qhd,khd->hqk", query_block, key_rows, preferred_element_type=jnp.float32)
        + bias_block
    )
    return jnp.where(key_valid[None, None, :], scores, NEG)


def attend_forward(queries, key_rows, values, rel_rows, key_valid, block_rows):
    seq_len, heads_dev, head_size = queries.shape
    count_blocks = seq_len // block_rows
    stacked = queries.reshape(count_blocks, block_rows, heads_dev, head_size)
    starts = jnp.arange(count_blocks, dtype=jnp.int32) * block_rows

    def one_block(block_item):
        query_block, start_row = block_item
        scores = block_scores(query_block, start_row, key_rows, rel_rows, key_valid)
        row_peak = jnp.max(scores, axis=-1, keepdims=True)
        exp_terms = jnp.exp(scores - row_peak)
        row_total = jnp.sum(exp_terms, axis=-1, keepdims=True)
        soft_low = (exp_terms / row_total).astype(jnp.bfloat16)
        mixed_rows = jnp.einsum(
            "hqk,khd->qhd", soft_low, values, preferred_element_type=jnp.float32
        )
        return (mixed_rows.astype(jnp.bfloat16), (row_peak + jnp.log(row_total))[..., 0])

    outputs, log_total = lax.map(one_block, (stacked, starts))
    return (outputs.reshape(seq_len, heads_dev * head_size), log_total)


def attend_backward(
    queries, key_rows, values, rel_rows, key_valid, log_total, grad_heads, block_rows
):
    seq_len, heads_dev, head_size = queries.shape
    key_count = key_rows.shape[0]
    width = block_rows + key_count - 1
    count_blocks = seq_len // block_rows
    query_blocks = queries.reshape(count_blocks, block_rows, heads_dev, head_size)
    grad_blocks = grad_heads.reshape(count_blocks, block_rows, heads_dev, head_size)
    starts = jnp.arange(count_blocks, dtype=jnp.int32) * block_rows
    initial = (
        jnp.zeros(key_rows.shape, jnp.float32),
        jnp.zeros(values.shape, jnp.float32),
        jnp.zeros(rel_rows.shape, jnp.float32),
    )

    def step_block(carry, block_item):
        key_acc, value_acc, rel_acc = carry
        query_block, grad_block, lse_block, start_row = block_item
        scores = block_scores(query_block, start_row, key_rows, rel_rows, key_valid)
        soft = jnp.exp(scores - lse_block[..., None])
        grad_soft = jnp.einsum(
            "qhd,khd->hqk", grad_block, values, preferred_element_type=jnp.float32
        )
        row_inner = jnp.sum(soft * grad_soft, axis=-1, keepdims=True)
        grad_scores = (soft * (grad_soft - row_inner)).astype(jnp.bfloat16)
        grad_query = jnp.einsum(
            "hqk,khd->qhd", grad_scores, key_rows, preferred_element_type=jnp.float32
        )
        key_acc = key_acc + jnp.einsum(
            "hqk,qhd->khd", grad_scores, query_block, preferred_element_type=jnp.float32
        )
        value_acc = value_acc + jnp.einsum(
            "hqk,qhd->khd",
            soft.astype(jnp.bfloat16),
            grad_block,
            preferred_element_type=jnp.float32,
        )
        segment_grad = unskew_grad(grad_scores.astype(jnp.float32), block_rows, key_count)
        offset = key_count - start_row - block_rows
        current = lax.dynamic_slice_in_dim(rel_acc, offset, width, 1)
        rel_acc = lax.dynamic_update_slice_in_dim(rel_acc, current + segment_grad, offset, 1)
        return ((key_acc, value_acc, rel_acc), grad_query.astype(jnp.bfloat16))

    finals, grad_query = lax.scan(
        step_block, initial, (query_blocks, grad_blocks, log_total, starts)
    )
    return (grad_query.reshape(seq_len, heads_dev * head_size), finals[0], finals[1], finals[2])


def update(moment, grad_owned, factor):
    return 0.5 * moment + 0.5 * (factor * grad_owned)


def shards(
    layer_input,
    output_grad,
    seq_lengths,
    deal_order,
    bucket_index,
    query_weight,
    key_weight,
    value_weight,
    out_weight,
    gate_weight,
    up_weight,
    down_weight,
    attn_gain,
    ffn_gain,
    bias_table,
    query_moment,
    key_moment,
    value_moment,
    out_moment,
    gate_moment,
    up_moment,
    down_moment,
    attn_gain_moment,
    ffn_gain_moment,
    table_moment,
):
    group_index = lax.axis_index("dp")
    member = lax.axis_index("mp")
    tensor_count = lax.axis_size("mp")
    picked = jnp.take(layer_input, deal_order, axis=0)
    dealt = lax.all_to_all(picked, "dp", split_axis=0, concat_axis=1, tiled=True)
    length = seq_lengths[deal_order[group_index]]
    x_rows, cot_rows = (
        lax.all_gather(dealt[0], "mp", axis=1, tiled=True),
        lax.all_gather(output_grad[0], "mp", axis=1, tiled=True),
    )
    seq_len = x_rows.shape[0]
    quarter = dealt.shape[2]
    low_query = query_weight.astype(jnp.bfloat16)
    low_key = key_weight.astype(jnp.bfloat16)
    low_value = value_weight.astype(jnp.bfloat16)
    low_out = out_weight.astype(jnp.bfloat16)
    low_gate = gate_weight.astype(jnp.bfloat16)
    low_up = up_weight.astype(jnp.bfloat16)
    low_down = down_weight.astype(jnp.bfloat16)
    low_attn_gain = attn_gain.astype(jnp.bfloat16)
    low_ffn_gain = ffn_gain.astype(jnp.bfloat16)
    low_table = bias_table.astype(jnp.bfloat16)
    (
        full_query,
        full_key,
        full_value,
        full_out,
        full_gate,
        full_up,
        full_down,
        full_attn_gain,
        full_ffn_gain,
        full_table,
    ) = (
        lax.all_gather(low_query, "dp", axis=0, tiled=True),
        lax.all_gather(low_key, "dp", axis=0, tiled=True),
        lax.all_gather(low_value, "dp", axis=0, tiled=True),
        lax.all_gather(low_out, "dp", axis=1, tiled=True),
        lax.all_gather(low_gate, "dp", axis=0, tiled=True),
        lax.all_gather(low_up, "dp", axis=0, tiled=True),
        lax.all_gather(low_down, "dp", axis=1, tiled=True),
        lax.all_gather(low_attn_gain, "dp", axis=0, tiled=True),
        lax.all_gather(low_ffn_gain, "dp", axis=0, tiled=True),
        lax.all_gather(low_table, "dp", axis=0, tiled=True),
    )
    bucket_hot = bucket_index[:, None] == lax.broadcasted_iota(
        jnp.int32, (bucket_index.shape[0], full_table.shape[0]), 1
    )
    rel_rows = jnp.dot(
        bucket_hot.astype(jnp.bfloat16), full_table, preferred_element_type=jnp.float32
    ).T
    first_gain = full_attn_gain.astype(jnp.float32)
    x_float = x_rows.astype(jnp.float32)
    h_first, inv_first = norm_forward(x_float, first_gain)
    heads_dev = full_query.shape[1] // DH

    def project(weight_cols):
        product = jnp.dot(h_first, weight_cols, preferred_element_type=jnp.float32)
        return product.astype(jnp.bfloat16).reshape(seq_len, heads_dev, DH)

    queries = project(full_query)
    key_rows = project(full_key)
    values = project(full_value)
    key_valid = lax.broadcasted_iota(jnp.int32, (seq_len,), 0) < length
    block_rows = min(512, seq_len)
    attended, log_total = attend_forward(queries, key_rows, values, rel_rows, key_valid, block_rows)
    attn_part = jnp.dot(attended, full_out, preferred_element_type=jnp.float32)
    attn_branch = lax.psum(attn_part, "mp")
    after_attn = x_float + attn_branch
    second_gain = full_ffn_gain.astype(jnp.float32)
    h_second, inv_second = norm_forward(after_attn, second_gain)
    gate_pre = jnp.dot(h_second, full_gate, preferred_element_type=jnp.float32)
    up_pre = jnp.dot(h_second, full_up, preferred_element_type=jnp.float32)
    mix_value, mix_back = jax.vjp(
        lambda gate_in, up_in: jax.nn.gelu(gate_in, approximate=True) * up_in, gate_pre, up_pre
    )
    hidden = mix_value.astype(jnp.bfloat16)
    ffn_part = jnp.dot(hidden, full_down, preferred_element_type=jnp.float32)
    ffn_branch = lax.psum(ffn_part.astype(jnp.bfloat16), "mp").astype(jnp.float32)
    result_rows = after_attn + ffn_branch
    layer_out = lax.dynamic_slice_in_dim(result_rows, member * quarter, quarter, 1).astype(
        jnp.bfloat16
    )[None]
    row_valid = (lax.broadcasted_iota(jnp.int32, (seq_len, 1), 0) < length).astype(jnp.float32)
    grad_y = cot_rows.astype(jnp.float32) * row_valid
    grad_y_low = grad_y.astype(jnp.bfloat16)
    grad_down = jnp.einsum("lf,ld->fd", hidden, grad_y_low, preferred_element_type=jnp.float32)
    grad_hidden = jnp.einsum("ld,fd->lf", grad_y_low, full_down, preferred_element_type=jnp.float32)
    grad_gate_pre, grad_up_pre = mix_back(grad_hidden)
    grad_gate_low = grad_gate_pre.astype(jnp.bfloat16)
    grad_up_low = grad_up_pre.astype(jnp.bfloat16)
    grad_gate = jnp.einsum("ld,lf->df", h_second, grad_gate_low, preferred_element_type=jnp.float32)
    grad_up = jnp.einsum("ld,lf->df", h_second, grad_up_low, preferred_element_type=jnp.float32)
    second_part = jnp.einsum(
        "lf,df->ld", grad_gate_low, full_gate, preferred_element_type=jnp.float32
    ) + jnp.einsum("lf,df->ld", grad_up_low, full_up, preferred_element_type=jnp.float32)
    grad_h_second = lax.psum(second_part, "mp")
    back_second, grad_ffn_gain = norm_backward(grad_h_second, after_attn, inv_second, second_gain)
    grad_after = grad_y + back_second
    grad_after_low = grad_after.astype(jnp.bfloat16)
    grad_out_w = jnp.einsum(
        "lc,ld->cd", attended, grad_after_low, preferred_element_type=jnp.float32
    )
    grad_heads = jnp.einsum(
        "ld,cd->lc", grad_after_low, full_out, preferred_element_type=jnp.float32
    )
    grad_heads = grad_heads.astype(jnp.bfloat16).reshape(seq_len, heads_dev, DH)
    grad_queries, key_acc, value_acc, rel_acc = attend_backward(
        queries, key_rows, values, rel_rows, key_valid, log_total, grad_heads, block_rows
    )
    grad_keys = key_acc.astype(jnp.bfloat16).reshape(seq_len, heads_dev * DH)
    grad_values = value_acc.astype(jnp.bfloat16).reshape(seq_len, heads_dev * DH)
    grad_query_w = jnp.einsum(
        "ld,lc->dc", h_first, grad_queries, preferred_element_type=jnp.float32
    )
    grad_key_w = jnp.einsum("ld,lc->dc", h_first, grad_keys, preferred_element_type=jnp.float32)
    grad_value_w = jnp.einsum("ld,lc->dc", h_first, grad_values, preferred_element_type=jnp.float32)
    grad_table = jnp.einsum(
        "rn,hr->nh", bucket_hot.astype(jnp.float32), rel_acc, precision=lax.Precision.HIGHEST
    )
    first_part = (
        jnp.einsum("lc,dc->ld", grad_queries, full_query, preferred_element_type=jnp.float32)
        + jnp.einsum("lc,dc->ld", grad_keys, full_key, preferred_element_type=jnp.float32)
        + jnp.einsum("lc,dc->ld", grad_values, full_value, preferred_element_type=jnp.float32)
    )
    grad_h_first = lax.psum(first_part, "mp")
    back_first, grad_attn_gain = norm_backward(grad_h_first, x_float, inv_first, first_gain)
    grad_input_rows = grad_after + back_first
    grad_mine = lax.dynamic_slice_in_dim(grad_input_rows, member * quarter, quarter, 1).astype(
        jnp.bfloat16
    )
    (
        owned_query,
        owned_key,
        owned_value,
        owned_out,
        owned_gate,
        owned_up,
        owned_down,
        owned_attn_gain,
        owned_ffn_gain,
        owned_table,
    ) = (
        lax.psum_scatter(
            grad_query_w.astype(jnp.bfloat16), "dp", scatter_dimension=0, tiled=True
        ).astype(jnp.float32),
        lax.psum_scatter(
            grad_key_w.astype(jnp.bfloat16), "dp", scatter_dimension=0, tiled=True
        ).astype(jnp.float32),
        lax.psum_scatter(
            grad_value_w.astype(jnp.bfloat16), "dp", scatter_dimension=0, tiled=True
        ).astype(jnp.float32),
        lax.psum_scatter(
            grad_out_w.astype(jnp.bfloat16), "dp", scatter_dimension=1, tiled=True
        ).astype(jnp.float32),
        lax.psum_scatter(
            grad_gate.astype(jnp.bfloat16), "dp", scatter_dimension=0, tiled=True
        ).astype(jnp.float32),
        lax.psum_scatter(
            grad_up.astype(jnp.bfloat16), "dp", scatter_dimension=0, tiled=True
        ).astype(jnp.float32),
        lax.psum_scatter(
            grad_down.astype(jnp.bfloat16), "dp", scatter_dimension=1, tiled=True
        ).astype(jnp.float32),
        lax.psum_scatter(
            grad_attn_gain.astype(jnp.bfloat16), "dp", scatter_dimension=0, tiled=True
        ).astype(jnp.float32),
        lax.psum_scatter(
            grad_ffn_gain.astype(jnp.bfloat16), "dp", scatter_dimension=0, tiled=True
        ).astype(jnp.float32),
        lax.psum_scatter(
            grad_table.astype(jnp.bfloat16), "dp", scatter_dimension=0, tiled=True
        ).astype(jnp.float32),
    )
    came_back = lax.all_to_all(grad_mine[None], "dp", split_axis=1, concat_axis=0, tiled=True)
    input_grad = jnp.zeros_like(came_back).at[deal_order].set(came_back)
    matrix_owned = (
        owned_query,
        owned_key,
        owned_value,
        owned_out,
        owned_gate,
        owned_up,
        owned_down,
        owned_table,
    )
    local_sq = jnp.zeros((), jnp.float32)
    for piece_grad in matrix_owned:
        local_sq = local_sq + jnp.sum(piece_grad * piece_grad)
    gain_sq = jnp.sum(owned_attn_gain * owned_attn_gain) + jnp.sum(owned_ffn_gain * owned_ffn_gain)
    local_sq = local_sq + gain_sq / tensor_count
    total_sq = lax.psum(local_sq, ("dp", "mp"))
    grad_norm = jnp.sqrt(total_sq)
    limit = math.sqrt(4 * D * H * DH + 3 * D * FF + 2 * D + NB * H)
    factor = jnp.minimum(1.0, limit / grad_norm)
    moment_query = update(query_moment, owned_query, factor)
    moment_key = update(key_moment, owned_key, factor)
    moment_value = update(value_moment, owned_value, factor)
    moment_out = update(out_moment, owned_out, factor)
    moment_gate = update(gate_moment, owned_gate, factor)
    moment_up = update(up_moment, owned_up, factor)
    moment_down = update(down_moment, owned_down, factor)
    moment_first_gain = update(attn_gain_moment, owned_attn_gain, factor)
    moment_second_gain = update(ffn_gain_moment, owned_ffn_gain, factor)
    moment_table = update(table_moment, owned_table, factor)
    return (
        layer_out,
        input_grad,
        grad_norm,
        moment_query,
        moment_key,
        moment_value,
        moment_out,
        moment_gate,
        moment_up,
        moment_down,
        moment_first_gain,
        moment_second_gain,
        moment_table,
    )


def solution(mesh):
    in_specs = (
        P(None, "dp", "mp"),
        P("dp", None, "mp"),
        P(),
        P(),
        P(),
        P("dp", "mp"),
        P("dp", "mp"),
        P("dp", "mp"),
        P("mp", "dp"),
        P("dp", "mp"),
        P("dp", "mp"),
        P("mp", "dp"),
        P("dp"),
        P("dp"),
        P("dp", "mp"),
        P("dp", "mp"),
        P("dp", "mp"),
        P("dp", "mp"),
        P("mp", "dp"),
        P("dp", "mp"),
        P("dp", "mp"),
        P("mp", "dp"),
        P("dp"),
        P("dp"),
        P("dp", "mp"),
    )
    out_specs = (
        P("dp", None, "mp"),
        P(None, "dp", "mp"),
        P(),
        P("dp", "mp"),
        P("dp", "mp"),
        P("dp", "mp"),
        P("mp", "dp"),
        P("dp", "mp"),
        P("dp", "mp"),
        P("mp", "dp"),
        P("dp"),
        P("dp"),
        P("dp", "mp"),
    )
    return jax.shard_map(shards, mesh=mesh, in_specs=in_specs, out_specs=out_specs, check_vma=False)
```

profile of v0, /device:TPU:0, one launch (start us, length us, event | category | flops | bytes accessed | tf_op | source)
XLA Modules:
  0.0 2787.6 jit_solution(4486777468460004474)
XLA Ops:
  9.6 20.6 all_to_all.21
  54.7 55.8 %all-gather.14.cloned.1.call-done = bf16[1024,2048]{1,0:T(8,128)(2,1)} async-done(((bf16[1024,512]{1,0:T(8,128)(2,1)}), bf16[1024,2048]{1,0:T(8,128)(2,1)}) %all-gather.14.cloned.1.call-update) | async-done | bytes 4194320 | tf_op jit(solution)/shard_map/all_gather | solution.py:172
  114.2 25.2 all-gather.16.cloned.1.call-done
  148.0 21.8 all-gather.18.cloned.1.call-done
  175.2 24.9 all-gather.20.cloned.1.call-done
  207.5 317.2 %while.38 = (s32[]{:T(128)}, bf16[2,512,8,64]{1,3,2,0:T(8,128)(2,1)}, f32[2,8,512]{2,1,0:T(8,128)}, bf16[2,512,8,64]{1,3,2,0:T(8,128)(2,1)}, bf16[1024,8,64]{0,2...) while((s32[]{:T(128)}, ...), condition=%wide.region_4.5_spmd.clone, body=%wide.region_1.0_spmd.clone.sunk | while | flops 1107555328 | bytes 359729344 | solution.py:80
  211.3 11.9 tile.38
  223.1 37.8 %reshape.270 = f32[6287360]{0:T(1024)} reshape(f32[8,512,1535]{2,1,0:T(8,128)} %tile.38) | data formatting | bytes 50298880 | tf_op jit(solution)/shard_map/while
  260.9 23.8 tile.39
  284.8 19.2 slice.58
  304.0 20.1 reshape.271
  324.1 24.2 reshape.272
  369.8 11.5 tile.38
  381.3 37.8 %reshape.270 = f32[6287360]{0:T(1024)} reshape(f32[8,512,1535]{2,1,0:T(8,128)} %tile.38) | data formatting | bytes 50298880 | tf_op jit(solution)/shard_map/while
  419.1 23.8 tile.39
  442.9 19.2 slice.58
  462.1 20.1 reshape.271
  482.2 24.2 reshape.272
  553.0 273.5 %all-reduce.11.cloned.1.call-done = f32[1024,2048]{1,0:T(8,128)} async-done(((f32[1024,2048]{1,0:T(8,128)}), f32[1024,2048]{1,0:T(8,128)}) %all-reduce.11.cloned.1.call-update) | async-done | bytes 8388624 | tf_op jit(solution)/shard_map/psum | solution.py:232
  838.3 30.8 %all-gather.26.cloned.1.call-done = bf16[2048,1280]{1,0:T(8,128)(2,1)} async-done(((bf16[256,1280]{1,0:T(8,128)(2,1)}), bf16[2048,1280]{1,0:T(8,128)(2,1)}) %all-gather.26.cloned.1.call-update) | async-done | bytes 5242896 | tf_op jit(solution)/shard_map/all_gather | solution.py:204
  869.1 10.7 fusion.97
  879.7 33.0 %all-gather.24.cloned.1.call-done = bf16[2048,1280]{1,0:T(8,128)(2,1)} async-done(((bf16[256,1280]{1,0:T(8,128)(2,1)}), bf16[2048,1280]{1,0:T(8,128)(2,1)}) %all-gather.24.cloned.1.call-update) | async-done | bytes 5242896 | tf_op jit(solution)/shard_map/all_gather | solution.py:203
  912.7 10.4 fusion.96
  923.1 72.0 %all-gather.30.cloned.1.call-done = bf16[1,1024,2048]{2,1,0:T(8,128)(2,1)} async-done(((bf16[1,1024,512]{2,1,0:T(8,128)(2,1)}), bf16[1,1024,2048]{2,1,0:T(8,128)(2,1)}) %all-gather.30.cloned.1.call-update) | async-done | bytes 4194320 | tf_op jit(solution)/shard_map/all_gather | solution.py:173
  995.0 42.3 %all-gather.28.cloned.1.call-done = bf16[1280,2048]{1,0:T(8,128)(2,1)} async-done(((bf16[1280,256]{1,0:T(8,128)(2,1)}), bf16[1280,2048]{1,0:T(8,128)(2,1)}) %all-gather.28.cloned.1.call-update) | async-done | bytes 5242896 | tf_op jit(solution)/shard_map/all_gather | solution.py:205
  1037.4 16.0 multiply_convert_fusion.3
  1061.2 11.8 convolution_add_fusion
  1073.0 10.0 convolution_convert_fusion.1
  1102.9 261.0 %all-reduce.15.cloned.1.call-done = f32[1024,2048]{1,0:T(8,128)} async-done(((f32[1024,2048]{1,0:T(8,128)}), f32[1024,2048]{1,0:T(8,128)}) %all-reduce.15.cloned.1.call-update) | async-done | bytes 8388624 | tf_op jit(solution)/shard_map/psum | solution.py:261
  1397.2 662.8 %while.39 = (s32[]{:T(128)}, f32[1024,8,64]{0,2,1:T(8,128)S(1)}, f32[1024,8,64]{0,2,1:T(8,128)}, f32[8,2047]{1,0:T(8,128)}, bf16[2,512,8,64]{1,3,2,0:T(8,128)(2,...) while((s32[]{:T(128)}, f32[1024,8,64]{0,2,1:T(8,128)S(1)}, ...), condition=%wide.region_13.14_spmd.clone, body=%wide.region_10.13_spmd.clone.sunk | while | flops 2737034240 | bytes 803260544 | solution.py:128
  1411.0 11.7 tile.40
  1422.8 38.5 %reshape.274 = f32[6287360]{0:T(1024)} reshape(f32[8,512,1535]{2,1,0:T(8,128)} %tile.40) | data formatting | bytes 50298880 | tf_op jit(solution)/shard_map/while
  1461.3 24.3 tile.41
  1485.6 20.1 slice.59
  1505.7 21.3 reshape.275
  1527.0 24.2 reshape.276
  1551.2 19.7 multiply_reduce_fusion.8
  1570.9 15.5 multiply_convert_fusion.12
  1607.5 21.8 reshape.277
  1629.3 14.4 reshape.278
  1643.7 14.6 pad_convert_fusion.2
  1658.3 18.1 reshape.279
  1676.4 39.1 %reshape.280 = f32[8,512,1535]{2,1,0:T(8,128)} reshape(f32[6287360]{0:T(1024)} %reshape.279) | data formatting | bytes 50298880 | tf_op jit(solution)/shard_map/while/body/eval_jaxpr/reshape | solution.py:48
  1740.1 11.5 tile.40
  1751.6 38.0 %reshape.274 = f32[6287360]{0:T(1024)} reshape(f32[8,512,1535]{2,1,0:T(8,128)} %tile.40) | data formatting | bytes 50298880 | tf_op jit(solution)/shard_map/while
  1789.6 23.8 tile.41
  1813.4 19.7 slice.59
  1833.1 20.1 reshape.275
  1853.2 24.2 reshape.276
  1877.3 19.6 multiply_reduce_fusion.8
  1896.9 15.2 multiply_convert_fusion.12
  1933.5 21.8 reshape.277
  1955.4 14.4 reshape.278
  1969.8 14.6 pad_convert_fusion.2
  1984.4 18.1 reshape.279
  2002.4 39.1 %reshape.280 = f32[8,512,1535]{2,1,0:T(8,128)} reshape(f32[6287360]{0:T(1024)} %reshape.279) | data formatting | bytes 50298880 | tf_op jit(solution)/shard_map/while/body/eval_jaxpr/reshape | solution.py:48
  2103.0 10.1 convolution_convert_fusion.4
  2130.4 22.7 reduce-scatter.8.cloned.1.call-done
  2156.1 41.7 %reduce-scatter.12.cloned.1.call-done = bf16[256,512]{1,0:T(8,128)(2,1)} async-done(((bf16[2048,512]{1,0:T(8,128)(2,1)}), bf16[256,512]{1,0:T(8,128)(2,1)}) %reduce-scatter.12.cloned.1.call-update) | async-done | bytes 262160 | tf_op jit(solution)/shard_map/reduce_scatter | solution.py:314
  2200.2 42.0 %reduce-scatter.14.cloned.1.call-done = bf16[512,256]{1,0:T(8,128)(2,1)} async-done(((bf16[512,2048]{1,0:T(8,128)(2,1)}), bf16[512,256]{1,0:T(8,128)(2,1)}) %reduce-scatter.14.cloned.1.call-update) | async-done | bytes 262160 | tf_op jit(solution)/shard_map/reduce_scatter | solution.py:317
  2246.6 289.2 %all-reduce.17.cloned.1.call-done = f32[1024,2048]{1,0:T(8,128)} async-done(((f32[1024,2048]{1,0:T(8,128)}), f32[1024,2048]{1,0:T(8,128)}) %all-reduce.17.cloned.1.call-update) | async-done | bytes 8388624 | tf_op jit(solution)/shard_map/psum | solution.py:290
  2543.9 25.6 all-reduce.5
  2572.7 119.4 %all-reduce.13.cloned.1.call-done = bf16[1024,2048]{1,0:T(8,128)(2,1)} async-done(((bf16[1024,2048]{1,0:T(8,128)(2,1)}), bf16[1024,2048]{1,0:T(8,128)(2,1)}) %all-reduce.13.cloned.1.call-update) | async-done | bytes 4194320 | tf_op jit(solution)/shard_map/psum | solution.py:243
  2695.3 39.4 %psum.39 = f32[]{:T(128)} all-reduce(f32[]{:T(128)S(6)} %add.313), channel_id=1, replica_groups=mesh['dp'=8,'mp'=4] {'dp','mp'}, use_global_device_ids=true, to_apply=%region_39.40 | all-reduce | flops 1 | bytes 8 | tf_op jit(solution)/shard_map/psum | solution.py:356
  (359 shorter events, 399.4 us)
Async XLA Ops:
  7.2 23.1 copy-start.42
  7.2 23.9 copy-start.43
  7.2 103.3 %all-gather.14.cloned.1.call-start = ((), (), s32[]{:S(2)}) async-start(), calls=%async_computation.9 | async-start | bytes 5242880 | tf_op jit(solution)/shard_map/all_gather | solution.py:172
  9.4 24.2 copy-start.64
  9.4 26.1 copy-start.62
  9.4 26.1 copy-start.53
  9.4 43.6 %copy-start.65 = (s32[8]{0:T(128)S(1)}, s32[8]{0:T(128)}, u32[]{:S(2)}) copy-start(s32[8]{0:T(128)} %param.31) | copy-start | bytes 100
  9.4 44.1 %copy-start.60 = (s32[2047]{0:T(1024)S(1)}, s32[2047]{0:T(1024)}, u32[]{:S(2)}) copy-start(s32[2047]{0:T(1024)} %param.33) | copy-start | bytes 24568
  9.6 22.3 copy-start.44
  9.6 23.1 copy-start.45
  30.2 109.2 %all-gather.16.cloned.1.call-start = ((), (), s32[]{:S(2)}) async-start(), calls=%async_computation.10 | async-start | bytes 2359296 | tf_op jit(solution)/shard_map/all_gather | solution.py:199
  31.0 138.8 %all-gather.18.cloned.1.call-start = ((), (), s32[]{:S(2)}) async-start(), calls=%async_computation.11 | async-start | bytes 2359296 | tf_op jit(solution)/shard_map/all_gather | solution.py:200
  31.9 168.2 %all-gather.20.cloned.1.call-start = ((), (), s32[]{:S(2)}) async-start(), calls=%async_computation.12 | async-start | bytes 2359296 | tf_op jit(solution)/shard_map/all_gather | solution.py:201
  32.7 494.6 %all-gather.22.cloned.1.call-start = ((), (), s32[]{:S(2)}) async-start(), calls=%async_computation.13 | async-start | bytes 2359296 | tf_op jit(solution)/shard_map/all_gather | solution.py:202
  33.5 793.0 %all-reduce.11.cloned.1.call-start = ((), (), s32[]{:S(2)}) async-start(), calls=%async_computation.14 | async-start | bytes 16777216 | tf_op jit(solution)/shard_map/psum | solution.py:232
  52.3 147.8 %copy-start.48 = (f32[8,1,256]{2,1,0:T(1,128)}, f32[8,1,256]{2,1,0:T(1,128)S(1)}, u32[]{:S(2)}) copy-start(f32[8,1,256]{2,1,0:T(1,128)S(1)} %convert_element_type.280) | copy-start | bytes 24580
  114.2 85.9 %copy-start.46 = (f32[1024]{0:T(1024)}, f32[1024]{0:T(1024)S(1)}, u32[]{:S(2)}) copy-start(f32[1024]{0:T(1024)S(1)} %get-tuple-element.674) | copy-start | bytes 12292
  535.5 333.6 %all-gather.26.cloned.1.call-start = ((), (), s32[]{:S(2)}) async-start(), calls=%async_computation.16 | async-start | bytes 5898240 | tf_op jit(solution)/shard_map/all_gather | solution.py:204
  537.7 375.0 %all-gather.24.cloned.1.call-start = ((), (), s32[]{:S(2)}) async-start(), calls=%async_computation.15 | async-start | bytes 5898240 | tf_op jit(solution)/shard_map/all_gather | solution.py:203
  540.0 455.1 %all-gather.30.cloned.1.call-start = ((), (), s32[]{:S(2)}) async-start(), calls=%async_computation.28 | async-start | bytes 5242880 | tf_op jit(solution)/shard_map/all_gather | solution.py:173
  540.7 496.7 %all-gather.28.cloned.1.call-start = ((), (), s32[]{:S(2)}) async-start(), calls=%async_computation.17 | async-start | bytes 5898240 | tf_op jit(solution)/shard_map/all_gather | solution.py:205
  543.3 820.6 %all-reduce.15.cloned.1.call-start = ((), (), s32[]{:S(2)}) async-start(), calls=%async_computation.19 | async-start | bytes 16777216 | tf_op jit(solution)/shard_map/psum | solution.py:261
  1037.4 16.0 copy-start.58
  1073.0 1048.6 %reduce-scatter.20.cloned.1.call-start = ((), (), s32[]{:S(2)}) async-start(), calls=%async_computation.27 | async-start | bytes 5898240 | tf_op jit(solution)/shard_map/reduce_scatter | solution.py:326
  1083.1 1040.6 %reduce-scatter.16.cloned.1.call-start = ((), (), s32[]{:S(2)}) async-start(), calls=%async_computation.25 | async-start | bytes 5898240 | tf_op jit(solution)/shard_map/reduce_scatter | solution.py:320
  1092.9 1032.8 %reduce-scatter.18.cloned.1.call-start = ((), (), s32[]{:S(2)}) async-start(), calls=%async_computation.26 | async-start | bytes 5898240 | tf_op jit(solution)/shard_map/reduce_scatter | solution.py:323
  1102.9 1025.9 %reduce-scatter.10.cloned.1.call-start = ((), (), s32[]{:S(2)}) async-start(), calls=%async_computation.22 | async-start | bytes 2359296 | tf_op jit(solution)/shard_map/reduce_scatter | solution.py:311
  1364.0 9.9 copy-start.19
  1397.2 664.0 %copy-start.47 = (f32[1024]{0:T(1024)S(1)}, f32[1024]{0:T(1024)}, u32[]{:S(2)}) copy-start(f32[1024]{0:T(1024)} %copy-done.46) | copy-start | bytes 12292
  1397.2 664.0 %copy-start.49 = (f32[8,1,256]{2,1,0:T(1,128)S(1)}, f32[8,1,256]{2,1,0:T(1,128)}, u32[]{:S(2)}) copy-start(f32[8,1,256]{2,1,0:T(1,128)} %copy-done.48) | copy-start | bytes 24580
  1397.3 13.7 copy-start.67
  1570.9 18.4 copy-start.2
  1570.9 19.0 copy-start.7
  1570.9 19.2 copy-start.10
  1715.5 9.5 copy-start.25
  1715.5 10.6 copy-start.68
  1726.3 13.7 copy-start.67
  1896.9 18.4 copy-start.2
  1896.9 19.0 copy-start.7
  1896.9 19.2 copy-start.10
  2041.5 9.5 copy-start.25
  2041.5 10.7 copy-start.68
  2067.6 85.5 %reduce-scatter.8.cloned.1.call-start = ((), (), s32[]{:S(2)}) async-start(), calls=%async_computation.21 | async-start | bytes 2359296 | tf_op jit(solution)/shard_map/reduce_scatter | solution.py:308
  2075.9 122.0 %reduce-scatter.12.cloned.1.call-start = ((), (), s32[]{:S(2)}) async-start(), calls=%async_computation.23 | async-start | bytes 2359296 | tf_op jit(solution)/shard_map/reduce_scatter | solution.py:314
  2082.9 159.4 %reduce-scatter.14.cloned.1.call-start = ((), (), s32[]{:S(2)}) async-start(), calls=%async_computation.24 | async-start | bytes 2359296 | tf_op jit(solution)/shard_map/reduce_scatter | solution.py:317
  2090.3 445.5 %all-reduce.17.cloned.1.call-start = ((), (), s32[]{:S(2)}) async-start(), calls=%async_computation.20 | async-start | bytes 16777216 | tf_op jit(solution)/shard_map/psum | solution.py:290
  2102.7 10.4 copy-start.66
  2102.7 589.4 %all-reduce.13.cloned.1.call-start = ((), (), s32[]{:S(2)}) async-start(), calls=%async_computation.18 | async-start | bytes 8388608 | tf_op jit(solution)/shard_map/psum | solution.py:243
  2115.0 12.7 copy-start.27
  2115.0 12.7 copy-start.61
  2246.5 297.4 %copy-start.51 = (bf16[2048]{0:T(1024)(128)(2,1)S(1)}, bf16[2048]{0:T(1024)(128)(2,1)}, u32[]{:S(2)}) copy-start(bf16[2048]{0:T(1024)(128)(2,1)} %get-tuple-element.612) | copy-start | bytes 12292
  2246.5 488.9 %copy-start.52 = (f32[4,8]{1,0:T(4,128)S(1)}, f32[4,8]{1,0:T(4,128)}, u32[]{:S(2)}) copy-start(f32[4,8]{1,0:T(4,128)} %param.53) | copy-start | bytes 388
  2246.5 489.5 %copy-start.56 = (f32[256]{0:T(256)S(1)}, f32[256]{0:T(256)}, u32[]{:S(2)}) copy-start(f32[256]{0:T(256)} %param.52) | copy-start | bytes 3076
  2246.6 490.1 %copy-start.50 = (f32[1024]{0:T(1024)S(1)}, f32[1024]{0:T(1024)}, u32[]{:S(2)}) copy-start(f32[1024]{0:T(1024)} %get-tuple-element.673) | copy-start | bytes 12292
  2740.1 15.1 copy-start.33
  2749.3 10.1 copy-start.36
  2749.3 11.9 copy-start.23
  2749.3 14.5 copy-start.21
  2750.9 19.7 all-to-all-start.1
  2755.2 9.9 copy-start.57
  2755.2 10.5 copy-start.34
  2755.2 10.5 copy-start.41
  2766.6 9.7 copy-start.55
  2766.6 12.6 copy-start.1
  (44 other events, 209.2 us)
Sparse Core Ops, SparseCore 0:
  30.3 80.1 all-gather.13
  113.0 26.4 all-gather.15
  141.9 27.9 all-gather.17
  172.2 27.8 all-gather.19
  202.4 28.1 all-gather.21
  535.6 290.8 all-reduce.10
  828.9 40.1 all-gather.25
  871.5 41.1 all-gather.23
  914.3 80.7 all-gather.29
  996.8 40.5 all-gather.27
  1073.1 290.8 all-reduce.14
  1367.2 55.5 reduce-scatter.19
  1426.6 56.5 reduce-scatter.15
  1486.4 56.5 reduce-scatter.17
  2067.8 40.9 reduce-scatter.9
  2111.9 41.1 reduce-scatter.7
  2156.6 41.2 reduce-scatter.11
  2201.0 41.1 reduce-scatter.13
  2244.9 290.8 all-reduce.16
  2538.1 153.9 all-reduce.12
where the time goes:
time: 2800 us; the launch traced here: 2790 us
  waiting for transfers between devices  1360 us (49%)
  local copies, waits for them, and re-layouts  813 us (29%)
  matrix products  271 us (10%)
  other arithmetic  186 us (7%)
  blocking collectives  111 us (4%)
    while x76, local copies, waits for them, and re-layouts  323 us
    psum x1, waiting for transfers between devices, shards(): grad_h_first = lax.psum(first_part, 'mp')  289 us
    psum x1, waiting for transfers between devices, shards(): attn_branch = lax.psum(attn_part, 'mp')  273 us
    psum x1, waiting for transfers between devices, shards(): grad_h_second = lax.psum(second_part, 'mp')  261 us
    another operation x8, local copies, waits for them, and re-layouts, skew_bias(): tiled = jnp.tile(segment, (1, block_rows))  142 us
    psum x1, waiting for transfers between devices, shards(): lax.psum(ffn_part.astype(jnp.bfloat16), 'mp').astype(jnp.float32)  119 us
    reshape x4, local copies, waits for them, and re-layouts, skew_bias(): return tiled.reshape(heads_dev, block_rows, width - 1)[:, :, :key_count]  96.7 us
    slice x4, local copies, waits for them, and re-layouts, skew_bias(): lax.slice_in_dim(tiled, block_rows - 1, block_rows - 1 + block_rows * (wi...  78.2 us
  transfers between devices with their start and end apart: 21, of which 16 were waited for; matrix products, arithmetic and copies ran while one was open for 42% of the time, Pallas kernels for 0%

commit v1 on v0

v1 whole, which is shorter than its diff:
```python
import functools
import math

import jax
import jax.numpy as jnp
from jax import lax
from jax.experimental import pallas as pl
from jax.experimental.pallas import tpu as pltpu
from jax.sharding import PartitionSpec as P

D = 2048
H = 32
DH = 64
FF = 5120
NB = 32


EPS = 1e-06
NEG = -1e30
LANES = 128
BLOCK_ROWS = 256

NN = (((1,), (0,)), ((), ()))
NT = (((1,), (1,)), ((), ()))
TN = (((0,), (0,)), ((), ()))


def dot(left, right, dims=NN):
    return lax.dot_general(left, right, dims, preferred_element_type=jnp.float32)


def pick_head(pair_rows, which):
    lane = lax.broadcasted_iota(jnp.int32, (1, LANES), 1)
    return jnp.where(lane // DH == which, pair_rows, jnp.zeros_like(pair_rows))


def forward_kernel(length, rel_ref, query_ref, key_ref, value_ref, out_ref, soft_ref, skew):
    block = pl.program_id(1)
    rows = query_ref.shape[0]
    key_count = key_ref.shape[0]
    width = rel_ref.shape[2]

    @pl.when(block == 0)
    def _():
        for which in range(2):
            spread = jnp.broadcast_to(rel_ref[0, which : which + 1, :], (LANES, width))
            skew[which] = pltpu.roll(spread, width - (LANES - 1), 1, stride=1, stride_axis=0)

    key_at = lax.broadcasted_iota(jnp.int32, (1, key_count), 1)
    key_mask = jnp.where(key_at < length[0], 0.0, NEG)
    keys = key_ref[...]
    values = value_ref[...]
    mixed = jnp.zeros((rows, LANES), jnp.float32)
    for which in range(2):
        products = dot(pick_head(query_ref[...], which), keys, NT)
        parts = []
        for part in range(rows // LANES):
            offset = pl.multiple_of(key_count - LANES * (part + 1) - rows * block, LANES)
            parts.append(
                products[LANES * part : LANES * (part + 1)] + skew[which, :, pl.ds(offset, key_count)]
            )
        scores = jnp.concatenate(parts, 0) + key_mask
        exp_terms = jnp.exp(scores - jnp.max(scores, axis=1, keepdims=True))
        total = jnp.sum(exp_terms, axis=1, keepdims=True)
        soft_low = (exp_terms * (1.0 / total)).astype(jnp.bfloat16)
        soft_ref[which] = soft_low
        mixed = mixed + dot(soft_low, pick_head(values, which))
    out_ref[...] = mixed.astype(jnp.bfloat16)


def attend_forward(qkv, rel_rows, length):
    seq_len = qkv.shape[0]
    columns = qkv.shape[1] // 3
    pairs = columns // LANES
    width = rel_rows.shape[1]
    rows = min(BLOCK_ROWS, seq_len)
    return pl.pallas_call(
        forward_kernel,
        grid_spec=pltpu.PrefetchScalarGridSpec(
            num_scalar_prefetch=1,
            grid=(pairs, seq_len // rows),
            in_specs=[
                pl.BlockSpec((1, 2, width), lambda pair, block, n: (pair, 0, 0)),
                pl.BlockSpec((rows, LANES), lambda pair, block, n: (block, pair)),
                pl.BlockSpec((seq_len, LANES), lambda pair, block, n: (0, pairs + pair)),
                pl.BlockSpec((seq_len, LANES), lambda pair, block, n: (0, 2 * pairs + pair)),
            ],
            out_specs=[
                pl.BlockSpec((rows, LANES), lambda pair, block, n: (block, pair)),
                pl.BlockSpec((2, rows, seq_len), lambda pair, block, n: (pair, block, 0)),
            ],
            scratch_shapes=[pltpu.VMEM((2, LANES, width), jnp.float32)],
        ),
        out_shape=[
            jax.ShapeDtypeStruct((seq_len, columns), jnp.bfloat16),
            jax.ShapeDtypeStruct((2 * pairs, seq_len, seq_len), jnp.bfloat16),
        ],
        compiler_params=pltpu.CompilerParams(vmem_limit_bytes=40 << 20),
        cost_estimate=pl.CostEstimate(
            flops=16 * seq_len * seq_len * columns,
            bytes_accessed=4 * pairs * seq_len * seq_len,
            transcendentals=2 * pairs * seq_len * seq_len,
        ),
        name="attend_forward",
    )(length.reshape(1), rel_rows.reshape(pairs, 2, width), qkv, qkv, qkv)


def backward_kernel(
    soft_ref,
    query_ref,
    grad_ref,
    out_ref,
    key_ref,
    value_ref,
    grad_qkv_ref,
    rel_ref,
    skew,
    key_acc,
    value_acc,
):
    pair = pl.program_id(0)
    block = pl.program_id(1)
    rows = query_ref.shape[0]
    key_count = key_ref.shape[0]
    columns = grad_qkv_ref.shape[1] // 3

    @pl.when(block == 0)
    def _():
        skew[...] = jnp.zeros_like(skew)
        key_acc[...] = jnp.zeros_like(key_acc)
        value_acc[...] = jnp.zeros_like(value_acc)

    keys = key_ref[...]
    values = value_ref[...]
    queries = query_ref[...]
    grads = grad_ref[...]
    inner = grads.astype(jnp.float32) * out_ref[...].astype(jnp.float32)
    grad_query = jnp.zeros((rows, LANES), jnp.float32)
    for which in range(2):
        grad_head = pick_head(grads, which)
        row_inner = jnp.sum(pick_head(inner, which), axis=1, keepdims=True)
        grad_soft = dot(grad_head, values, NT)
        soft_low = soft_ref[which]
        grad_scores = soft_low.astype(jnp.float32) * (grad_soft - row_inner)
        for part in range(rows // LANES):
            offset = pl.multiple_of(key_count - LANES * (part + 1) - rows * block, LANES)
            skew[which, :, pl.ds(offset, key_count)] += grad_scores[
                LANES * part : LANES * (part + 1)
            ]
        grad_low = grad_scores.astype(jnp.bfloat16)
        grad_query = grad_query + dot(grad_low, pick_head(keys, which))
        key_acc[...] += dot(pick_head(queries, which), grad_low, TN)
        value_acc[...] += dot(grad_head, soft_low, TN)
    own_rows = pl.ds(pl.multiple_of(block * rows, rows), rows)
    own_columns = pl.multiple_of(pair * LANES, LANES)
    grad_qkv_ref[own_rows, pl.ds(own_columns, LANES)] = grad_query.astype(jnp.bfloat16)

    @pl.when(block == pl.num_programs(1) - 1)
    def _():
        grad_qkv_ref[:, pl.ds(columns + own_columns, LANES)] = key_acc[...].T.astype(jnp.bfloat16)
        grad_qkv_ref[:, pl.ds(2 * columns + own_columns, LANES)] = value_acc[...].T.astype(
            jnp.bfloat16
        )
        down = lax.broadcasted_iota(jnp.int32, (LANES, LANES), 0)
        across = lax.broadcasted_iota(jnp.int32, (LANES, LANES), 1)
        flip = (down + across == LANES - 1).astype(jnp.float32)
        for which in range(2):
            turned = lax.dot_general(
                flip,
                skew[which],
                NN,
                precision=lax.Precision.HIGHEST,
                preferred_element_type=jnp.float32,
            )
            rel_ref[0, which : which + 1, :] = jnp.sum(
                pltpu.roll(turned, 0, 1, stride=1, stride_axis=0), axis=0, keepdims=True
            )


def attend_backward(soft_low, qkv, grad_heads, attended):
    seq_len, columns = attended.shape
    pairs = columns // LANES
    width = 2 * seq_len
    rows = min(BLOCK_ROWS, seq_len)
    row_block = pl.BlockSpec((rows, LANES), lambda pair, block: (block, pair))
    grad_qkv, rel_grad = pl.pallas_call(
        backward_kernel,
        grid=(pairs, seq_len // rows),
        in_specs=[
            pl.BlockSpec((2, rows, seq_len), lambda pair, block: (pair, block, 0)),
            row_block,
            row_block,
            row_block,
            pl.BlockSpec((seq_len, LANES), lambda pair, block: (0, pairs + pair)),
            pl.BlockSpec((seq_len, LANES), lambda pair, block: (0, 2 * pairs + pair)),
        ],
        out_specs=[
            pl.BlockSpec((seq_len, 3 * columns), lambda pair, block: (0, 0)),
            pl.BlockSpec((1, 2, width), lambda pair, block: (pair, 0, 0)),
        ],
        scratch_shapes=[
            pltpu.VMEM((2, LANES, width), jnp.float32),
            pltpu.VMEM((LANES, seq_len), jnp.float32),
            pltpu.VMEM((LANES, seq_len), jnp.float32),
        ],
        out_shape=[
            jax.ShapeDtypeStruct((seq_len, 3 * columns), jnp.bfloat16),
            jax.ShapeDtypeStruct((pairs, 2, width), jnp.float32),
        ],
        compiler_params=pltpu.CompilerParams(vmem_limit_bytes=40 << 20),
        cost_estimate=pl.CostEstimate(
            flops=40 * seq_len * seq_len * columns,
            bytes_accessed=4 * pairs * seq_len * seq_len,
            transcendentals=0,
        ),
        name="attend_backward",
    )(soft_low, qkv, grad_heads, attended, qkv, qkv)
    return grad_qkv, rel_grad.reshape(2 * pairs, width)


def around(block):
    count = lax.axis_size("mp")
    return lax.ppermute(block, "mp", [(i, (i + 1) % count) for i in range(count)])


def ring_gather(own):
    blocks = [own]
    for _ in range(lax.axis_size("mp") - 1):
        blocks.append(around(blocks[-1]))
    return blocks


def ring_scatter(part_of):
    running = part_of(1).astype(jnp.bfloat16)
    for step in range(2, lax.axis_size("mp")):
        running = (around(running).astype(jnp.float32) + part_of(step)).astype(jnp.bfloat16)
    return around(running).astype(jnp.float32) + part_of(0)


def update(moment, grad_owned, factor):
    return 0.5 * moment + (0.5 * factor) * grad_owned


def shards(
    layer_input,
    output_grad,
    seq_lengths,
    deal_order,
    bucket_index,
    query_weight,
    key_weight,
    value_weight,
    out_weight,
    gate_weight,
    up_weight,
    down_weight,
    attn_gain,
    ffn_gain,
    bias_table,
    query_moment,
    key_moment,
    value_moment,
    out_moment,
    gate_moment,
    up_moment,
    down_moment,
    attn_gain_moment,
    ffn_gain_moment,
    table_moment,
):
    low = jnp.bfloat16
    f32 = jnp.float32
    group_index = lax.axis_index("dp")
    member = lax.axis_index("mp")
    group_count = lax.axis_size("dp")
    tensor_count = lax.axis_size("mp")

    def back(step):
        return lax.rem(member - step + tensor_count, tensor_count)

    picked = jnp.take(layer_input, deal_order, axis=0)
    x_own = lax.all_to_all(picked, "dp", split_axis=0, concat_axis=1, tiled=True)[0]
    length = seq_lengths[deal_order[group_index]]
    seq_len, quarter = x_own.shape
    features = quarter * tensor_count
    part_rows = seq_len // tensor_count
    row_valid = lax.broadcasted_iota(jnp.int32, (seq_len, 1), 0) < length

    def row_part(array, step):
        return lax.dynamic_slice_in_dim(array, back(step) * part_rows, part_rows, 0)

    def column_part(array, step):
        return lax.dynamic_slice_in_dim(array, back(step) * quarter, quarter, 1)

    def set_rows(whole, part, step):
        return lax.dynamic_update_slice_in_dim(whole, part, back(step) * part_rows, 0)

    def whole_columns(parts):
        whole = jnp.zeros((seq_len, features), parts[0].dtype)
        for step, part in enumerate(parts):
            whole = lax.dynamic_update_slice_in_dim(whole, part, back(step) * quarter, 1)
        return whole

    small = jnp.concatenate([attn_gain, ffn_gain, bias_table.reshape(-1)]).astype(low)
    small = lax.all_gather(small, "dp", axis=0)
    gain_size = attn_gain.shape[0]
    first_gain = small[:, :gain_size].reshape(-1).astype(f32)
    second_gain = small[:, gain_size : 2 * gain_size].reshape(-1).astype(f32)
    full_table = small[:, 2 * gain_size :].reshape(NB, bias_table.shape[1])
    qkv_weight = jnp.concatenate([query_weight, key_weight, value_weight], axis=1).astype(low)
    qkv_weight = lax.all_gather(qkv_weight, "dp", axis=0, tiled=True)
    gate_up = jnp.concatenate([gate_weight, up_weight], axis=1).astype(low)
    out_down = jnp.concatenate([out_weight, down_weight], axis=0).astype(low)
    heads_columns = out_weight.shape[0]
    units = down_weight.shape[0]
    gate_up, out_down = lax.optimization_barrier((gate_up, out_down, qkv_weight))[:2]
    out_down = lax.all_gather(out_down, "dp", axis=1, tiled=True)
    gate_up = lax.optimization_barrier((gate_up, out_down))[0]
    gate_up = lax.all_gather(gate_up, "dp", axis=0, tiled=True)
    full_out = out_down[:heads_columns]
    full_down = out_down[heads_columns:]

    x_rows = whole_columns(ring_gather(x_own))
    grad_own = jnp.where(row_valid, output_grad[0], jnp.zeros((), low))
    grad_own, x_rows = lax.optimization_barrier((grad_own, x_rows))
    grad_y = whole_columns(ring_gather(grad_own))

    offsets = jnp.concatenate([bucket_index, jnp.full((1,), NB, jnp.int32)])
    bucket_hot = offsets[:, None] == lax.broadcasted_iota(jnp.int32, (2 * seq_len, NB), 1)
    rel_rows = dot(full_table, bucket_hot.astype(low), (((0,), (1,)), ((), ())))

    x_float = x_rows.astype(f32)
    inv_first = lax.rsqrt(jnp.mean(x_float * x_float, axis=-1, keepdims=True) + EPS)
    h_first = (x_float * inv_first * first_gain).astype(low)
    qkv = dot(h_first, qkv_weight).astype(low)
    attended, soft_low = attend_forward(qkv, rel_rows, length)
    attn_branch = ring_scatter(lambda step: dot(row_part(attended, step), full_out))

    after_attn = row_part(x_rows, 0).astype(f32) + attn_branch
    inv_second = lax.rsqrt(jnp.mean(after_attn * after_attn, axis=-1, keepdims=True) + EPS)
    h_second = (after_attn * inv_second * second_gain).astype(low)

    h_parts = ring_gather(h_second)
    hidden = jnp.zeros((seq_len, units), low)
    gate_up_grads = []
    for step, h_part in enumerate(h_parts):
        both = dot(h_part, gate_up)
        mixed, mix_back = jax.vjp(
            lambda gate_in, up_in: jax.nn.gelu(gate_in, approximate=True) * up_in,
            both[:, :units],
            both[:, units:],
        )
        hidden = set_rows(hidden, mixed.astype(low), step)
        grad_hidden = dot(row_part(grad_y, step), full_down, NT)
        gate_up_grads.append(jnp.concatenate(mix_back(grad_hidden), axis=1).astype(low))
    grad_h_second = ring_scatter(lambda step: dot(gate_up_grads[step], gate_up, NT))
    h_rotated = jnp.concatenate(h_parts, axis=0)
    grads_rotated = jnp.concatenate(gate_up_grads, axis=0)
    grad_gate_up = dot(h_rotated, grads_rotated, TN).astype(low)
    grad_down = dot(hidden, grad_y, TN).astype(low)
    owned_gate_up = lax.psum_scatter(grad_gate_up, "dp", scatter_dimension=0, tiled=True)
    owned_down = lax.psum_scatter(grad_down, "dp", scatter_dimension=1, tiled=True)

    grad_ffn_gain = jnp.sum(grad_h_second * (after_attn * inv_second), axis=0)
    weighted = grad_h_second * second_gain
    row_inner = jnp.mean(weighted * after_attn, axis=-1, keepdims=True)
    grad_after = (
        row_part(grad_y, 0).astype(f32)
        + inv_second * weighted
        - after_attn * (inv_second * inv_second * inv_second) * row_inner
    ).astype(low)
    after_parts = ring_gather(grad_after)
    grad_after = jnp.zeros((seq_len, features), low)
    grad_heads = jnp.zeros((seq_len, heads_columns), low)
    for step, part in enumerate(after_parts):
        grad_after = set_rows(grad_after, part, step)
        grad_heads = set_rows(grad_heads, dot(part, full_out, NT).astype(low), step)
    grad_out = dot(attended, grad_after, TN).astype(low)
    owned_out = lax.psum_scatter(grad_out, "dp", scatter_dimension=1, tiled=True)

    grad_qkv, rel_grad = attend_backward(soft_low, qkv, grad_heads, attended)
    grad_qkv_weight = dot(h_first, grad_qkv, TN).astype(low)
    owned_qkv = lax.psum_scatter(grad_qkv_weight, "dp", scatter_dimension=0, tiled=True)
    grad_table = lax.dot_general(
        bucket_hot.astype(f32),
        rel_grad,
        (((0,), (1,)), ((), ())),
        precision=lax.Precision.HIGHEST,
        preferred_element_type=f32,
    )
    grad_h_first = ring_scatter(
        lambda step: dot(
            grad_qkv,
            lax.dynamic_slice_in_dim(qkv_weight, back(step) * quarter, quarter, 0),
            NT,
        )
    )
    own_gain = lax.dynamic_slice_in_dim(first_gain, member * quarter, quarter, 0)
    x_own = x_own.astype(f32)
    grad_attn_gain = jnp.sum(grad_h_first * (x_own * inv_first), axis=0)
    weighted = grad_h_first * own_gain
    row_inner = lax.psum(jnp.sum(weighted * x_own, axis=-1), "mp")[:, None] / features
    grad_input = (
        column_part(grad_after, 0).astype(f32)
        + inv_first * weighted
        - x_own * (inv_first * inv_first * inv_first) * row_inner
    ).astype(low)
    came_back = lax.all_to_all(grad_input[None], "dp", split_axis=1, concat_axis=0, tiled=True)
    group_iota = lax.broadcasted_iota(jnp.int32, (group_count, group_count), 1)
    place = jnp.argmax(deal_order[None, :] == group_iota.T, axis=1)
    input_grad = jnp.take(came_back, place, axis=0)

    hidden, grad_after = lax.optimization_barrier((hidden, grad_after))

    def output_part(step):
        part = dot(hidden, column_part(full_down, step))
        mine = row_part(part, 0) + column_part(after_attn, step)
        return set_rows(part, mine, 0)

    layer_out = ring_scatter(output_part).astype(low)[None]

    local_sq = jnp.zeros((), f32)
    for piece in (owned_qkv, owned_out, owned_gate_up, owned_down):
        piece = piece.astype(f32)
        local_sq = local_sq + jnp.sum(piece * piece)
    heads_dev = bias_table.shape[1]
    first_wide = lax.dynamic_update_slice_in_dim(
        jnp.zeros((features,), f32), grad_attn_gain, member * quarter, 0
    )
    table_wide = lax.dynamic_update_slice_in_dim(
        jnp.zeros((NB, heads_dev * tensor_count), f32), grad_table, member * heads_dev, 1
    )
    sums = lax.psum(
        jnp.concatenate([first_wide, grad_ffn_gain, table_wide.reshape(-1), local_sq[None]]),
        ("dp", "mp"),
    )
    total_sq = sums[-1] + jnp.sum(sums[:-1] * sums[:-1])
    grad_norm = jnp.sqrt(total_sq)
    limit = math.sqrt(4 * D * H * DH + 3 * D * FF + 2 * D + NB * H)
    factor = jnp.minimum(1.0, limit / grad_norm)
    owned_first = lax.dynamic_slice_in_dim(sums, group_index * gain_size, gain_size, 0)
    owned_second = lax.dynamic_slice_in_dim(
        sums, features + group_index * gain_size, gain_size, 0
    )
    table_rows = bias_table.shape[0]
    owned_table = lax.dynamic_slice(
        sums[2 * features : -1].reshape(NB, heads_dev * tensor_count),
        (group_index * table_rows, member * heads_dev),
        (table_rows, heads_dev),
    )
    return (
        layer_out,
        input_grad,
        grad_norm,
        update(query_moment, owned_qkv[:, :heads_columns], factor),
        update(key_moment, owned_qkv[:, heads_columns : 2 * heads_columns], factor),
        update(value_moment, owned_qkv[:, 2 * heads_columns :], factor),
        update(out_moment, owned_out, factor),
        update(gate_moment, owned_gate_up[:, :units], factor),
        update(up_moment, owned_gate_up[:, units:], factor),
        update(down_moment, owned_down, factor),
        update(attn_gain_moment, owned_first, factor),
        update(ffn_gain_moment, owned_second, factor),
        update(table_moment, owned_table, factor),
    )


def solution(mesh):
    in_specs = (
        P(None, "dp", "mp"),
        P("dp", None, "mp"),
        P(),
        P(),
        P(),
        P("dp", "mp"),
        P("dp", "mp"),
        P("dp", "mp"),
        P("mp", "dp"),
        P("dp", "mp"),
        P("dp", "mp"),
        P("mp", "dp"),
        P("dp"),
        P("dp"),
        P("dp", "mp"),
        P("dp", "mp"),
        P("dp", "mp"),
        P("dp", "mp"),
        P("mp", "dp"),
        P("dp", "mp"),
        P("dp", "mp"),
        P("mp", "dp"),
        P("dp"),
        P("dp"),
        P("dp", "mp"),
    )
    out_specs = (
        P("dp", None, "mp"),
        P(None, "dp", "mp"),
        P(),
        P("dp", "mp"),
        P("dp", "mp"),
        P("dp", "mp"),
        P("mp", "dp"),
        P("dp", "mp"),
        P("dp", "mp"),
        P("mp", "dp"),
        P("dp"),
        P("dp"),
        P("dp", "mp"),
    )
    return jax.shard_map(shards, mesh=mesh, in_specs=in_specs, out_specs=out_specs, check_vma=False)
```

time: 2800 us -> 945 us (0.34)
  waiting for transfers between devices: 1360 us -> 519 us
  local copies, waits for them, and re-layouts: 813 us -> 39.9 us
  other arithmetic: 186 us -> 54 us
  matrix products: 271 us -> 150 us
  Pallas kernels: 0 us -> 60.2 us
  blocking collectives: 111 us -> 81.2 us
    psum x4 -> x0, waiting for transfers between devices: 943 us -> none  [the longest x1 289 us: shards(): grad_h_first = lax.psum(first_part, 'mp')]
    ppermute x0 -> x24, waiting for transfers between devices: none -> 413 us  [around(): lax.ppermute(block, 'mp', [(i, (i + 1) % count) for i in range(count)])]
    while x78 -> x0, local copies, waits for them, and re-layouts: 326 us -> none
    all_gather x9 -> x3, waiting for transfers between devices: 306 us -> 97.4 us  [the longest x1 53.7 us: shards(): out_down = lax.all_gather(out_down, 'dp', axis=1, tiled=True)]
    reshape x8 -> x4, local copies, waits for them, and re-layouts: 204 us -> 0.27 us  [the longest x1 0.08 us: shards(): full_table = small[:, 2 * gain_size:].reshape(NB, bias_table.shape[1])]
    another operation x12 -> x3, local copies, waits for them, and re-layouts: 150 us -> 3.54 us  [the longest x8 142 us: skew_bias(): tiled = jnp.tile(segment, (1, block_rows))]
    dot_general x37 -> x35, matrix products: 271 us -> 150 us  [the longest x34 150 us: dot(): lax.dot_general(left, right, dims, preferred_element_type=jnp.float32)]
    reduce_scatter x7 -> x4, waiting for transfers between devices: 106 us -> 0.01 us  [the longest x1 0.01 us: shards(): lax.psum_scatter(grad_down, 'dp', scatter_dimension=1, tiled=True)]
  transfers between devices with their start and end apart: 21 -> 32, of which waited for: 16 -> 25; matrix products, arithmetic and copies ran while one was open for 42% -> 23% of each run, Pallas kernels for 0% -> 6%
where the time goes in v1:
time: 945 us; the launch traced here: 936 us
  waiting for transfers between devices  519 us (55%)
  matrix products  150 us (16%)
  blocking collectives  81.2 us (9%)
  Pallas kernels  60.2 us (6%)
  other arithmetic  54 us (6%)
  local copies, waits for them, and re-layouts  39.9 us (4%)
  between operations  23.4 us (2%)
    ppermute x24, waiting for transfers between devices, around(): lax.ppermute(block, 'mp', [(i, (i + 1) % count) for i in range(count)])  413 us
    dot_general x34, matrix products, dot(): lax.dot_general(left, right, dims, preferred_element_type=jnp.float32)  150 us
    all_gather x1, waiting for transfers between devices, shards(): out_down = lax.all_gather(out_down, 'dp', axis=1, tiled=True)  53.7 us
    all_gather x1, waiting for transfers between devices, shards(): qkv_weight = lax.all_gather(qkv_weight, 'dp', axis=0, tiled=True)  43.7 us
    psum x1, blocking collectives, shards(): lax.psum(jnp.concatenate([first_wide, grad_ffn_gain, table_wide.reshape(-...  39.8 us
    pallas_call x1, Pallas kernels, attend_backward(): pl.pallas_call(backward_kernel, grid=(pairs, seq_len // rows), in_specs=[...  32.2 us
    pallas_call x1, Pallas kernels, attend_forward(): pl.pallas_call(forward_kernel, grid_spec=pltpu.PrefetchScalarGridSpec(num...  27.9 us
    all_to_all x1, blocking collectives, shards(): lax.all_to_all(picked, 'dp', split_axis=0, concat_axis=1, tiled=True)[0]  24 us
  transfers between devices with their start and end apart: 32, of which 25 were waited for; matrix products, arithmetic and copies ran while one was open for 23% of the time, Pallas kernels for 6%

profile of v1, /device:TPU:0, one launch (start us, length us, event | category | flops | bytes accessed | tf_op | source)
XLA Modules:
  0.0 935.8 jit_solution(17616409896906491050)
XLA Ops:
  16.3 43.7 %all-gather.5.cloned.1.call-done = bf16[2048,1536]{1,0:T(8,128)(2,1)} async-done(((bf16[256,1536]{1,0:T(8,128)(2,1)}), bf16[2048,1536]{1,0:T(8,128)(2,1)}) %all-gather.5.cloned.1.call-update) | async-done | bytes 6291472 | tf_op jit(solution)/shard_map/all_gather | solution.py:311
  60.1 53.7 %all-gather.7.cloned.1.call-done = bf16[1792,2048]{1,0:T(8,128)(2,1)} async-done(((bf16[1792,256]{1,0:T(8,128)(2,1)}), bf16[1792,2048]{1,0:T(8,128)(2,1)}) %all-gather.7.cloned.1.call-update) | async-done | bytes 7340048 | tf_op jit(solution)/shard_map/all_gather | solution.py:317
  115.9 24.0 %all_to_all.21 = bf16[8,128,512]{2,1,0:T(8,128)(2,1)S(1)} all-to-all(bf16[8,128,512]{2,1,0:T(8,128)(2,1)S(1)} %broadcast_select_fusion.1), channel_id=1, replica_groups=mesh['dp'=8,'mp'=4] {'dp'}, dimensions={0} | all-to-all | bytes 2097152 | tf_op jit(solution)/shard_map/all_to_all | solution.py:282
  141.4 23.1 %collective-permute-done = bf16[1024,512]{1,0:T(8,128)(2,1)S(1)} collective-permute-done((bf16[1024,512]{1,0:T(8,128)(2,1)S(1)}, bf16[1024,512]{1,0:T(8,128)(2,1)S(1)}, u32[]{:S(2)}, u32[]{:S(2)}) %collective-permute-start) | collective-permute-done | bytes 1048608 | tf_op jit(solution)/shard_map/ppermute | solution.py:223
  166.6 8.1 all-gather
  176.0 12.4 %collective-permute-done.1 = bf16[1024,512]{1,0:T(8,128)(2,1)} collective-permute-done((bf16[1024,512]{1,0:T(8,128)(2,1)S(1)}, bf16[1024,512]{1,0:T(8,128)(2,1)}, u32[]{:S(2)}, u32[]{:S(2)}) %collective-permute-start.1) | collective-permute-done | bytes 1048608 | tf_op jit(solution)/shard_map/ppermute | solution.py:223
  194.0 17.5 %collective-permute-done.2 = bf16[1024,512]{1,0:T(8,128)(2,1)} collective-permute-done((bf16[1024,512]{1,0:T(8,128)(2,1)}, bf16[1024,512]{1,0:T(8,128)(2,1)}, u32[]{:S(2)}, u32[]{:S(2)}) %collective-permute-start.2) | collective-permute-done | bytes 1048608 | tf_op jit(solution)/shard_map/ppermute | solution.py:223
  215.5 7.1 convolution_convert_fusion.3.query_ref.key_ref.value_ref
  222.6 27.9 %attend_forward.1 = (bf16[1024,512]{1,0:T(8,128)(2,1)S(1)}, bf16[8,1024,1024]{2,1,0:T(8,128)(2,1)}) custom-call(s32[1]{0:T(128)} %dynamic_slice.98.length, f32[4,2,2048]{2,1,0:T(2,128)S(1)} %fusion.140.rel_ref, bf16[1024,1536]{1,0:T(8,128)(2,1)S(1)} %convolution_convert_fusion.3.query_ref.key_ref.value_ref, ...), custom_call_target="tpu_custom_call" | custom-call | flops 8589934592 | bytes 16777216 | tf_op jit(solution)/shard_map/attend_forward/pallas_call | solution.py:77
  252.9 21.9 %collective-permute-done.3 = bf16[256,2048]{1,0:T(8,128)(2,1)} collective-permute-done((bf16[256,2048]{1,0:T(8,128)(2,1)S(1)}, bf16[256,2048]{1,0:T(8,128)(2,1)}, u32[]{:S(2)}, u32[]{:S(2)}) %collective-permute-start.3) | collective-permute-done | bytes 1048608 | tf_op jit(solution)/shard_map/ppermute | solution.py:223
  274.9 2.6 add_convert_fusion.8
  277.6 2.3 fusion.127
  279.9 25.6 %collective-permute-done.4 = bf16[256,2048]{1,0:T(8,128)(2,1)} collective-permute-done((bf16[256,2048]{1,0:T(8,128)(2,1)S(1)}, bf16[256,2048]{1,0:T(8,128)(2,1)}, u32[]{:S(2)}, u32[]{:S(2)}) %collective-permute-start.4) | collective-permute-done | bytes 1048608 | tf_op jit(solution)/shard_map/ppermute | solution.py:223
  307.1 20.8 %collective-permute-done.9 = bf16[1024,512]{1,0:T(8,128)(2,1)} collective-permute-done((bf16[1024,512]{1,0:T(8,128)(2,1)S(1)}, bf16[1024,512]{1,0:T(8,128)(2,1)}, u32[]{:S(2)}, u32[]{:S(2)}) %collective-permute-start.9) | collective-permute-done | bytes 1048608 | tf_op jit(solution)/shard_map/ppermute | solution.py:223
  328.5 2.3 fusion.125
  330.8 19.6 %collective-permute-done.5 = bf16[256,2048]{1,0:T(8,128)(2,1)} collective-permute-done((bf16[256,2048]{1,0:T(8,128)(2,1)S(1)}, bf16[256,2048]{1,0:T(8,128)(2,1)}, u32[]{:S(2)}, u32[]{:S(2)}) %collective-permute-start.5) | collective-permute-done | bytes 1048608 | tf_op jit(solution)/shard_map/ppermute | solution.py:223
  352.8 20.0 %collective-permute-done.10 = bf16[1024,512]{1,0:T(8,128)(2,1)S(1)} collective-permute-done((bf16[1024,512]{1,0:T(8,128)(2,1)}, bf16[1024,512]{1,0:T(8,128)(2,1)S(1)}, u32[]{:S(2)}, u32[]{:S(2)}) %collective-permute-start.10) | collective-permute-done | bytes 1048608 | tf_op jit(solution)/shard_map/ppermute | solution.py:223
  372.8 22.5 %collective-permute-done.6 = bf16[256,2048]{1,0:T(8,128)(2,1)S(1)} collective-permute-done((bf16[256,2048]{1,0:T(8,128)(2,1)S(1)}, bf16[256,2048]{1,0:T(8,128)(2,1)S(1)}, u32[]{:S(2)}, u32[]{:S(2)}) %collective-permute-start.6) | collective-permute-done | bytes 1048608 | tf_op jit(solution)/shard_map/ppermute | solution.py:223
  395.3 2.5 broadcast.103.clone.1
  402.3 15.5 %collective-permute-done.11 = bf16[1024,512]{1,0:T(8,128)(2,1)S(1)} collective-permute-done((bf16[1024,512]{1,0:T(8,128)(2,1)S(1)}, bf16[1024,512]{1,0:T(8,128)(2,1)S(1)}, u32[]{:S(2)}, u32[]{:S(2)}) %collective-permute-start.11) | collective-permute-done | bytes 1048608 | tf_op jit(solution)/shard_map/ppermute | solution.py:223
  418.9 16.6 %collective-permute-done.7 = bf16[256,2048]{1,0:T(8,128)(2,1)} collective-permute-done((bf16[256,2048]{1,0:T(8,128)(2,1)S(1)}, bf16[256,2048]{1,0:T(8,128)(2,1)}, u32[]{:S(2)}, u32[]{:S(2)}) %collective-permute-start.7) | collective-permute-done | bytes 1048608 | tf_op jit(solution)/shard_map/ppermute | solution.py:223
  435.4 6.0 fusion.172
  441.5 5.3 fusion.59
  446.9 3.9 convolution_convert_fusion.5
  451.0 2.9 fusion.171
  455.4 4.1 fusion.173
  461.0 2.6 collective-permute-done.8
  463.6 4.1 fusion.174
  471.2 9.6 %convolution_convert_fusion.1 = bf16[1280,2048]{1,0:T(8,128)(2,1)} fusion(bf16[1024,1280]{1,0:T(8,128)(2,1)S(1)} %fusion.118, bf16[1024,2048]{1,0:T(8,128)(2,1)} %constant_dynamic-update-slice_fusion.4), kind=kOutput, calls=%fused_computation.8 | convolution fusion | flops 5371330560 | bytes 12058624 | tf_op jit(solution)/shard_map/dot_general | solution.py:29
  481.1 6.5 fusion.66
  487.6 8.8 add_convert_fusion.6
  496.6 4.8 fusion.73
  501.4 6.6 fusion.83
  508.0 14.6 %collective-permute-done.13 = bf16[256,2048]{1,0:T(8,128)(2,1)S(1)} collective-permute-done((bf16[256,2048]{1,0:T(8,128)(2,1)S(1)}, bf16[256,2048]{1,0:T(8,128)(2,1)S(1)}, u32[]{:S(2)}, u32[]{:S(2)}) %collective-permute-start.13) | collective-permute-done | bytes 1048608 | tf_op jit(solution)/shard_map/ppermute | solution.py:223
  523.0 4.0 fusion.52
  527.1 14.3 %collective-permute-done.14 = bf16[256,2048]{1,0:T(8,128)(2,1)S(1)} collective-permute-done((bf16[256,2048]{1,0:T(8,128)(2,1)S(1)}, bf16[256,2048]{1,0:T(8,128)(2,1)S(1)}, u32[]{:S(2)}, u32[]{:S(2)}) %collective-permute-start.14) | collective-permute-done | bytes 1048608 | tf_op jit(solution)/shard_map/ppermute | solution.py:223
  541.4 6.0 multiply_reduce_fusion.1
  550.1 27.4 %collective-permute-done.15 = bf16[256,2048]{1,0:T(8,128)(2,1)S(1)} collective-permute-done((bf16[256,2048]{1,0:T(8,128)(2,1)S(1)}, bf16[256,2048]{1,0:T(8,128)(2,1)S(1)}, u32[]{:S(2)}, u32[]{:S(2)}) %collective-permute-start.15) | collective-permute-done | bytes 1048608 | tf_op jit(solution)/shard_map/ppermute | solution.py:223
  577.5 27.1 %collective-permute-done.16 = bf16[256,2048]{1,0:T(8,128)(2,1)S(1)} collective-permute-done((bf16[256,2048]{1,0:T(8,128)(2,1)S(1)}, bf16[256,2048]{1,0:T(8,128)(2,1)S(1)}, u32[]{:S(2)}, u32[]{:S(2)}) %collective-permute-start.16) | collective-permute-done | bytes 1048608 | tf_op jit(solution)/shard_map/ppermute | solution.py:223
  605.6 16.0 %collective-permute-done.17 = bf16[256,2048]{1,0:T(8,128)(2,1)S(1)} collective-permute-done((bf16[256,2048]{1,0:T(8,128)(2,1)S(1)}, bf16[256,2048]{1,0:T(8,128)(2,1)S(1)}, u32[]{:S(2)}, u32[]{:S(2)}) %collective-permute-start.17) | collective-permute-done | bytes 1048608 | tf_op jit(solution)/shard_map/ppermute | solution.py:223
  624.5 3.8 convolution_convert_fusion.4
  628.4 20.2 %convolution_convert_fusion = bf16[2048,2560]{1,0:T(8,128)(2,1)} fusion(bf16[256,1280]{1,0:T(8,128)(2,1)} %get-tuple-element.49, bf16[256,1280]{1,0:T(8,128)(2,1)} %copy-done.71, bf16[256,1280]{1,0:T(8,128)(2,1)} %copy-done.73, bf16[256,1280]{1,0:T(8,128)(2,1)} %copy-done.72, bf16[256,1280]{1,0:T(8,128)(2,1)} %copy-done.75, ...), kind=kOutput, calls=%fused_computation.2 | convolution fusion | flops 10801381376 | bytes 19922944 | tf_op jit(solution)/shard_map/dot_general | solution.py:29
  648.9 2.8 fusion.101
  651.7 2.4 fusion.102
  654.2 2.5 fusion.103
  656.7 2.5 fusion.104.grad_ref
  659.2 32.2 %attend_backward.1 = (bf16[1024,1536]{1,0:T(8,128)(2,1)S(1)}, f32[4,2,2048]{2,1,0:T(2,128)S(1)}) custom-call(bf16[8,1024,1024]{2,1,0:T(8,128)(2,1)} %get-tuple-element.32.soft_ref, bf16[1024,1536]{1,0:T(8,128)(2,1)S(1)} %copy-done.6, bf16[1024,512]{1,0:T(8,128)(2,1)S(1)} %fusion.104.grad_ref, bf16[1024,512]{1,0:T(8,128)(2,1)S(1)} %get-tuple-element.26.out_ref, ...), custom_call_target="tpu_custom_call" | custom-call | flops 21474836480 | bytes 16777216 | tf_op jit(solution)/shard_map/attend_backward/pallas_call | solution.py:186
  693.2 9.0 convolution_convert_fusion.2
  702.3 3.4 slice.101
  706.1 3.6 fusion.39
  717.0 20.9 %collective-permute-done.21 = bf16[1024,512]{1,0:T(8,128)(2,1)S(1)} collective-permute-done((bf16[1024,512]{1,0:T(8,128)(2,1)S(1)}, bf16[1024,512]{1,0:T(8,128)(2,1)S(1)}, u32[]{:S(2)}, u32[]{:S(2)}) %collective-permute-start.21) | collective-permute-done | bytes 1048608 | tf_op jit(solution)/shard_map/ppermute | solution.py:223
  739.8 20.6 %collective-permute-done.18 = bf16[1024,512]{1,0:T(8,128)(2,1)S(1)} collective-permute-done((bf16[1024,512]{1,0:T(8,128)(2,1)S(1)}, bf16[1024,512]{1,0:T(8,128)(2,1)S(1)}, u32[]{:S(2)}, u32[]{:S(2)}) %collective-permute-start.18) | collective-permute-done | bytes 1048608 | tf_op jit(solution)/shard_map/ppermute | solution.py:223
  762.6 20.2 %collective-permute-done.22 = bf16[1024,512]{1,0:T(8,128)(2,1)S(1)} collective-permute-done((bf16[1024,512]{1,0:T(8,128)(2,1)S(1)}, bf16[1024,512]{1,0:T(8,128)(2,1)S(1)}, u32[]{:S(2)}, u32[]{:S(2)}) %collective-permute-start.22) | collective-permute-done | bytes 1048608 | tf_op jit(solution)/shard_map/ppermute | solution.py:223
  784.2 21.3 %collective-permute-done.19 = bf16[1024,512]{1,0:T(8,128)(2,1)} collective-permute-done((bf16[1024,512]{1,0:T(8,128)(2,1)S(1)}, bf16[1024,512]{1,0:T(8,128)(2,1)}, u32[]{:S(2)}, u32[]{:S(2)}) %collective-permute-start.19) | collective-permute-done | bytes 1048608 | tf_op jit(solution)/shard_map/ppermute | solution.py:223
  805.5 2.7 add_convert_fusion.3
  808.2 12.8 %collective-permute-done.23 = bf16[1024,512]{1,0:T(8,128)(2,1)} collective-permute-done((bf16[1024,512]{1,0:T(8,128)(2,1)}, bf16[1024,512]{1,0:T(8,128)(2,1)}, u32[]{:S(2)}, u32[]{:S(2)}) %collective-permute-start.23) | collective-permute-done | bytes 1048608 | tf_op jit(solution)/shard_map/ppermute | solution.py:223
  820.9 3.9 fusion.30
  824.9 9.3 psum.14
  838.6 7.0 reduce.19
  847.3 4.0 all-to-all-start.1
  855.8 2.5 fusion.105
  858.4 8.2 all-to-all-done.1
  869.7 2.7 multiply_reduce_fusion
  877.2 39.8 %psum.15 = f32[5121]{0:T(1024)S(1)} all-reduce(f32[5121]{0:T(1024)S(1)} %pad_maximum_fusion.3), channel_id=1, replica_groups=mesh['dp'=8,'mp'=4] {'dp','mp'}, use_global_device_ids=true, to_apply=%region_16.18 | all-reduce | flops 5121 | bytes 40968 | tf_op jit(solution)/shard_map/psum | solution.py:433
  (327 shorter events, 89.6 us)
Async XLA Ops:
  7.2 107.8 %copy-start = (bf16[8,128,512]{2,1,0:T(8,128)(2,1)S(1)}, bf16[8,128,512]{2,1,0:T(8,128)(2,1)}, u32[]{:S(2)}) copy-start(bf16[8,128,512]{2,1,0:T(8,128)(2,1)} %param.27) | copy-start | bytes 3145732
  7.2 52.8 %all-gather.5.cloned.1.call-start = ((), (), s32[]{:S(2)}) async-start(), calls=%async_computation.6 | async-start | bytes 7077888 | tf_op jit(solution)/shard_map/all_gather | solution.py:311
  11.6 102.2 %all-gather.7.cloned.1.call-start = ((), (), s32[]{:S(2)}) async-start(), calls=%async_computation.7 | async-start | bytes 8257536 | tf_op jit(solution)/shard_map/all_gather | solution.py:317
  15.2 98.7 %copy-start.62 = (s32[8]{0:T(128)S(1)}, s32[8]{0:T(128)}, u32[]{:S(2)}) copy-start(s32[8]{0:T(128)} %param.30) | copy-start | bytes 100
  60.0 375.4 %all-gather.9.cloned.1.call-start = ((), (), s32[]{:S(2)}) async-start(), calls=%async_computation.8 | async-start | bytes 11796480 | tf_op jit(solution)/shard_map/all_gather | solution.py:319
  113.8 738.1 %reduce-scatter.11.cloned.1.call-start = ((), (), s32[]{:S(2)}) async-start(), calls=%async_computation.12 | async-start | bytes 5898240 | tf_op jit(solution)/shard_map/reduce_scatter | solution.py:362
  115.7 50.8 %copy-start.57 = (f32[4,8]{1,0:T(4,128)S(1)}, f32[4,8]{1,0:T(4,128)}, u32[]{:S(2)}) copy-start(f32[4,8]{1,0:T(4,128)} %param.41) | copy-start | bytes 388
  115.7 50.9 %copy-start.66 = (f32[256]{0:T(256)S(1)}, f32[256]{0:T(256)}, u32[]{:S(2)}) copy-start(f32[256]{0:T(256)} %param.40) | copy-start | bytes 3076
  115.7 50.9 %copy-start.67 = (f32[256]{0:T(256)S(1)}, f32[256]{0:T(256)}, u32[]{:S(2)}) copy-start(f32[256]{0:T(256)} %param.39) | copy-start | bytes 3076
  115.7 59.7 %copy-start.68 = (s32[8]{0:T(128)S(1)}, s32[8]{0:T(128)}, u32[]{:S(2)}) copy-start(s32[8]{0:T(128)} %param.29) | copy-start | bytes 100
  115.7 73.6 %copy-start.54 = (s32[2047]{0:T(1024)S(1)}, s32[2047]{0:T(1024)}, u32[]{:S(2)}) copy-start(s32[2047]{0:T(1024)} %param.31) | copy-start | bytes 24568
  139.9 51.6 %copy-start.9 = (bf16[8,128,512]{2,1,0:T(8,128)(2,1)}, bf16[8,128,512]{2,1,0:T(8,128)(2,1)S(1)}, u32[]{:S(2)}) copy-start(bf16[8,128,512]{2,1,0:T(8,128)(2,1)S(1)} %all_to_all.21) | copy-start | bytes 3145732
  139.9 24.6 %collective-permute-start = (bf16[1024,512]{1,0:T(8,128)(2,1)S(1)}, bf16[1024,512]{1,0:T(8,128)(2,1)S(1)}, u32[]{:S(2)}, u32[]{:S(2)}) collective-permute-start(bf16[1024,512]{1,0:T(8,128)(2,1)S(1)} %bitcast.73), channel_id=1, source_target_pairs={{0,1},{1,2},{2,3},{3,0},{4,5},{5,6},{6,7},{7,4},{8,9},{9,10},{10,1... | collective-permute-start | bytes 3145736 | tf_op jit(solution)/shard_map/ppermute | solution.py:223
  164.6 23.8 %collective-permute-start.1 = (bf16[1024,512]{1,0:T(8,128)(2,1)S(1)}, bf16[1024,512]{1,0:T(8,128)(2,1)}, u32[]{:S(2)}, u32[]{:S(2)}) collective-permute-start(bf16[1024,512]{1,0:T(8,128)(2,1)S(1)} %collective-permute-done), channel_id=1, source_target_pairs={{0,1},{1,2},{2,3},{3,0},{4,5},{5,6},{6,7},{7,4},{8,9},{9,10},{10,1... | collective-permute-start | bytes 3145736 | tf_op jit(solution)/shard_map/ppermute | solution.py:223
  188.4 23.1 %collective-permute-start.2 = (bf16[1024,512]{1,0:T(8,128)(2,1)}, bf16[1024,512]{1,0:T(8,128)(2,1)}, u32[]{:S(2)}, u32[]{:S(2)}) collective-permute-start(bf16[1024,512]{1,0:T(8,128)(2,1)} %collective-permute-done.1), channel_id=1, source_target_pairs={{0,1},{1,2},{2,3},{3,0},{4,5},{5,6},{6,7},{7,4},{8,9},{9,10},{10,1... | collective-permute-start | bytes 3145736 | tf_op jit(solution)/shard_map/ppermute | solution.py:223
  189.3 25.6 %copy-start.52 = (f32[1,2,8,128]{3,1,2,0:T(2,128)}, f32[1,2,8,128]{3,1,2,0:T(2,128)S(1)}, u32[]{:S(2)}) copy-start(f32[1,2,8,128]{3,1,2,0:T(2,128)S(1)} %copy.63) | copy-start | bytes 24580
  191.0 86.5 %copy-start.13 = (bf16[1024,512]{1,0:T(8,128)(2,1)}, bf16[1024,512]{1,0:T(8,128)(2,1)S(1)}, u32[]{:S(2)}) copy-start(bf16[1024,512]{1,0:T(8,128)(2,1)S(1)} %bitcast_select_fusion) | copy-start | bytes 3145732
  191.0 24.5 %slice-start.5 = ((s8[6291456]{0:T(1024)(128)(4,1)}), s8[4194304]{0:T(1024)(128)(4,1)S(1)}, s32[]{:S(2)}) async-start(s8[6291456]{0:T(1024)(128)(4,1)} %bitcast.90), calls=%async_computation.18 | async-start | bytes 8388608
  191.9 23.6 %slice-start.6 = ((s8[6291456]{0:T(1024)(128)(4,1)}), s8[2097152]{0:T(1024)(128)(4,1)S(1)}, s32[]{:S(2)}) async-start(s8[6291456]{0:T(1024)(128)(4,1)} %bitcast.90), calls=%async_computation.19 | async-start | bytes 4194304
  222.6 28.0 %copy-start.5 = (bf16[1024,1536]{1,0:T(8,128)(2,1)}, bf16[1024,1536]{1,0:T(8,128)(2,1)S(1)}, u32[]{:S(2)}) copy-start(bf16[1024,1536]{1,0:T(8,128)(2,1)S(1)} %convolution_convert_fusion.3.query_ref.key_ref.value_ref) | copy-start | bytes 9437188
  252.8 22.0 %collective-permute-start.3 = (bf16[256,2048]{1,0:T(8,128)(2,1)S(1)}, bf16[256,2048]{1,0:T(8,128)(2,1)}, u32[]{:S(2)}, u32[]{:S(2)}) collective-permute-start(bf16[256,2048]{1,0:T(8,128)(2,1)S(1)} %convolution_convert_fusion.6), channel_id=1, source_target_pairs={{0,1},{1,2},{2,3},{3,0},{4,5},{5,6},{6,7},{7,4},{8,9},{9,10},{10,1... | collective-permute-start | bytes 3145736 | tf_op jit(solution)/shard_map/ppermute | solution.py:223
  277.4 28.1 %collective-permute-start.4 = (bf16[256,2048]{1,0:T(8,128)(2,1)S(1)}, bf16[256,2048]{1,0:T(8,128)(2,1)}, u32[]{:S(2)}, u32[]{:S(2)}) collective-permute-start(bf16[256,2048]{1,0:T(8,128)(2,1)S(1)} %add_convert_fusion.8), channel_id=1, source_target_pairs={{0,1},{1,2},{2,3},{3,0},{4,5},{5,6},{6,7},{7,4},{8,9},{9,10},{10,1... | collective-permute-start | bytes 3145736 | tf_op jit(solution)/shard_map/ppermute | solution.py:223
  277.5 50.4 %collective-permute-start.9 = (bf16[1024,512]{1,0:T(8,128)(2,1)S(1)}, bf16[1024,512]{1,0:T(8,128)(2,1)}, u32[]{:S(2)}, u32[]{:S(2)}) collective-permute-start(bf16[1024,512]{1,0:T(8,128)(2,1)S(1)} %bitcast_select_fusion), channel_id=1, source_target_pairs={{0,1},{1,2},{2,3},{3,0},{4,5},{5,6},{6,7},{7,4},{8,9},{9,10},{10,1... | collective-permute-start | bytes 3145736 | tf_op jit(solution)/shard_map/ppermute | solution.py:223
  307.0 43.4 %collective-permute-start.5 = (bf16[256,2048]{1,0:T(8,128)(2,1)S(1)}, bf16[256,2048]{1,0:T(8,128)(2,1)}, u32[]{:S(2)}, u32[]{:S(2)}) collective-permute-start(bf16[256,2048]{1,0:T(8,128)(2,1)S(1)} %add_convert_fusion.7), channel_id=1, source_target_pairs={{0,1},{1,2},{2,3},{3,0},{4,5},{5,6},{6,7},{7,4},{8,9},{9,10},{10,1... | collective-permute-start | bytes 3145736 | tf_op jit(solution)/shard_map/ppermute | solution.py:223
  328.0 44.8 %collective-permute-start.10 = (bf16[1024,512]{1,0:T(8,128)(2,1)}, bf16[1024,512]{1,0:T(8,128)(2,1)S(1)}, u32[]{:S(2)}, u32[]{:S(2)}) collective-permute-start(bf16[1024,512]{1,0:T(8,128)(2,1)} %collective-permute-done.9), channel_id=1, source_target_pairs={{0,1},{1,2},{2,3},{3,0},{4,5},{5,6},{6,7},{7,4},{8,9},{9,10},{10,1... | collective-permute-start | bytes 3145736 | tf_op jit(solution)/shard_map/ppermute | solution.py:223
  352.8 45.0 %copy-start.14 = (bf16[1024,512]{1,0:T(8,128)(2,1)S(1)}, bf16[1024,512]{1,0:T(8,128)(2,1)}, u32[]{:S(2)}) copy-start(bf16[1024,512]{1,0:T(8,128)(2,1)} %copy-done.13) | copy-start | bytes 3145732
  352.8 42.5 %collective-permute-start.6 = (bf16[256,2048]{1,0:T(8,128)(2,1)S(1)}, bf16[256,2048]{1,0:T(8,128)(2,1)S(1)}, u32[]{:S(2)}, u32[]{:S(2)}) collective-permute-start(bf16[256,2048]{1,0:T(8,128)(2,1)S(1)} %multiply_convert_fusion), channel_id=1, source_target_pairs={{0,1},{1,2},{2,3},{3,0},{4,5},{5,6},{6,7},{7,4},{8,9},{9,10},{10,1... | collective-permute-start | bytes 3145736 | tf_op jit(solution)/shard_map/ppermute | solution.py:223
  372.8 44.9 %collective-permute-start.11 = (bf16[1024,512]{1,0:T(8,128)(2,1)S(1)}, bf16[1024,512]{1,0:T(8,128)(2,1)S(1)}, u32[]{:S(2)}, u32[]{:S(2)}) collective-permute-start(bf16[1024,512]{1,0:T(8,128)(2,1)S(1)} %collective-permute-done.10), channel_id=1, source_target_pairs={{0,1},{1,2},{2,3},{3,0},{4,5},{5,6},{6,7},{7,4},{8,9},{9,10},{10,1... | collective-permute-start | bytes 3145736 | tf_op jit(solution)/shard_map/ppermute | solution.py:223
  395.3 40.2 %collective-permute-start.7 = (bf16[256,2048]{1,0:T(8,128)(2,1)S(1)}, bf16[256,2048]{1,0:T(8,128)(2,1)}, u32[]{:S(2)}, u32[]{:S(2)}) collective-permute-start(bf16[256,2048]{1,0:T(8,128)(2,1)S(1)} %collective-permute-done.6), channel_id=1, source_target_pairs={{0,1},{1,2},{2,3},{3,0},{4,5},{5,6},{6,7},{7,4},{8,9},{9,10},{10,1... | collective-permute-start | bytes 3145736 | tf_op jit(solution)/shard_map/ppermute | solution.py:223
  435.4 28.2 %collective-permute-start.8 = (bf16[256,2048]{1,0:T(8,128)(2,1)}, bf16[256,2048]{1,0:T(8,128)(2,1)}, u32[]{:S(2)}, u32[]{:S(2)}) collective-permute-start(bf16[256,2048]{1,0:T(8,128)(2,1)} %collective-permute-done.7), channel_id=1, source_target_pairs={{0,1},{1,2},{2,3},{3,0},{4,5},{5,6},{6,7},{7,4},{8,9},{9,10},{10,1... | collective-permute-start | bytes 3145736 | tf_op jit(solution)/shard_map/ppermute | solution.py:223
  450.8 36.8 %collective-permute-start.12 = (bf16[256,2048]{1,0:T(8,128)(2,1)}, bf16[256,2048]{1,0:T(8,128)(2,1)}, u32[]{:S(2)}, u32[]{:S(2)}) collective-permute-start(bf16[256,2048]{1,0:T(8,128)(2,1)} %convolution_convert_fusion.5), channel_id=1, source_target_pairs={{0,1},{1,2},{2,3},{3,0},{4,5},{5,6},{6,7},{7,4},{8,9},{9,10},{10,1... | collective-permute-start | bytes 3145736 | tf_op jit(solution)/shard_map/ppermute | solution.py:223
  480.9 373.3 %reduce-scatter.7.cloned.1.call-start = ((), (), s32[]{:S(2)}) async-start(), calls=%async_computation.10 | async-start | bytes 2359296 | tf_op jit(solution)/shard_map/reduce_scatter | solution.py:379
  496.5 26.1 %collective-permute-start.13 = (bf16[256,2048]{1,0:T(8,128)(2,1)S(1)}, bf16[256,2048]{1,0:T(8,128)(2,1)S(1)}, u32[]{:S(2)}, u32[]{:S(2)}) collective-permute-start(bf16[256,2048]{1,0:T(8,128)(2,1)S(1)} %add_convert_fusion.6), channel_id=1, source_target_pairs={{0,1},{1,2},{2,3},{3,0},{4,5},{5,6},{6,7},{7,4},{8,9},{9,10},{10,1... | collective-permute-start | bytes 3145736 | tf_op jit(solution)/shard_map/ppermute | solution.py:223
  523.0 18.5 %collective-permute-start.14 = (bf16[256,2048]{1,0:T(8,128)(2,1)S(1)}, bf16[256,2048]{1,0:T(8,128)(2,1)S(1)}, u32[]{:S(2)}, u32[]{:S(2)}) collective-permute-start(bf16[256,2048]{1,0:T(8,128)(2,1)S(1)} %add_convert_fusion.5), channel_id=1, source_target_pairs={{0,1},{1,2},{2,3},{3,0},{4,5},{5,6},{6,7},{7,4},{8,9},{9,10},{10,1... | collective-permute-start | bytes 3145736 | tf_op jit(solution)/shard_map/ppermute | solution.py:223
  550.0 55.2 %copy-start.34 = (bf16[256,2048]{1,0:T(8,128)(2,1)}, bf16[256,2048]{1,0:T(8,128)(2,1)S(1)}, u32[]{:S(2)}) copy-start(bf16[256,2048]{1,0:T(8,128)(2,1)S(1)} %get-tuple-element.41) | copy-start | bytes 3145732
  550.0 27.5 %collective-permute-start.15 = (bf16[256,2048]{1,0:T(8,128)(2,1)S(1)}, bf16[256,2048]{1,0:T(8,128)(2,1)S(1)}, u32[]{:S(2)}, u32[]{:S(2)}) collective-permute-start(bf16[256,2048]{1,0:T(8,128)(2,1)S(1)} %get-tuple-element.41), channel_id=1, source_target_pairs={{0,1},{1,2},{2,3},{3,0},{4,5},{5,6},{6,7},{7,4},{8,9},{9,10},{10,1... | collective-permute-start | bytes 3145736 | tf_op jit(solution)/shard_map/ppermute | solution.py:223
  577.5 27.7 %copy-start.35 = (bf16[256,2048]{1,0:T(8,128)(2,1)}, bf16[256,2048]{1,0:T(8,128)(2,1)S(1)}, u32[]{:S(2)}) copy-start(bf16[256,2048]{1,0:T(8,128)(2,1)S(1)} %collective-permute-done.15) | copy-start | bytes 3145732
  577.5 27.1 %collective-permute-start.16 = (bf16[256,2048]{1,0:T(8,128)(2,1)S(1)}, bf16[256,2048]{1,0:T(8,128)(2,1)S(1)}, u32[]{:S(2)}, u32[]{:S(2)}) collective-permute-start(bf16[256,2048]{1,0:T(8,128)(2,1)S(1)} %collective-permute-done.15), channel_id=1, source_target_pairs={{0,1},{1,2},{2,3},{3,0},{4,5},{5,6},{6,7},{7,4},{8,9},{9,10},{10,1... | collective-permute-start | bytes 3145736 | tf_op jit(solution)/shard_map/ppermute | solution.py:223
  604.6 17.0 %collective-permute-start.17 = (bf16[256,2048]{1,0:T(8,128)(2,1)S(1)}, bf16[256,2048]{1,0:T(8,128)(2,1)S(1)}, u32[]{:S(2)}, u32[]{:S(2)}) collective-permute-start(bf16[256,2048]{1,0:T(8,128)(2,1)S(1)} %collective-permute-done.16), channel_id=1, source_target_pairs={{0,1},{1,2},{2,3},{3,0},{4,5},{5,6},{6,7},{7,4},{8,9},{9,10},{10,1... | collective-permute-start | bytes 3145736 | tf_op jit(solution)/shard_map/ppermute | solution.py:223
  628.4 241.4 %reduce-scatter.9.cloned.1.call-start = ((), (), s32[]{:S(2)}) async-start(), calls=%async_computation.11 | async-start | bytes 11796480 | tf_op jit(solution)/shard_map/reduce_scatter | solution.py:361
  648.6 223.8 %reduce-scatter.5.cloned.1.call-start = ((), (), s32[]{:S(2)}) async-start(), calls=%async_computation.9 | async-start | bytes 7077888 | tf_op jit(solution)/shard_map/reduce_scatter | solution.py:383
  659.2 34.0 %copy-start.8 = (bf16[1024,2048]{1,0:T(8,128)(2,1)S(1)}, bf16[1024,2048]{1,0:T(8,128)(2,1)}, u32[]{:S(2)}) copy-start(bf16[1024,2048]{1,0:T(8,128)(2,1)} %copy-done.7) | copy-start | bytes 12582916
  659.2 34.0 %copy-start.51 = (f32[1024]{0:T(1024)S(1)}, f32[1024]{0:T(1024)}, u32[]{:S(2)}) copy-start(f32[1024]{0:T(1024)} %copy-done.50) | copy-start | bytes 12292
  659.2 34.0 %copy-start.53 = (f32[1,2,8,128]{3,1,2,0:T(2,128)S(1)}, f32[1,2,8,128]{3,1,2,0:T(2,128)}, u32[]{:S(2)}) copy-start(f32[1,2,8,128]{3,1,2,0:T(2,128)} %copy-done.52) | copy-start | bytes 24580
  709.7 28.2 %collective-permute-start.21 = (bf16[1024,512]{1,0:T(8,128)(2,1)S(1)}, bf16[1024,512]{1,0:T(8,128)(2,1)S(1)}, u32[]{:S(2)}, u32[]{:S(2)}) collective-permute-start(bf16[1024,512]{1,0:T(8,128)(2,1)S(1)} %fusion.39), channel_id=1, source_target_pairs={{0,1},{1,2},{2,3},{3,0},{4,5},{5,6},{6,7},{7,4},{8,9},{9,10},{10,1... | collective-permute-start | bytes 3145736 | tf_op jit(solution)/shard_map/ppermute | solution.py:223
  713.0 24.8 %slice-start.7 = ((s8[6291456]{0:T(1024)(128)(4,1)}), s8[4194304]{0:T(1024)(128)(4,1)S(1)}, s32[]{:S(2)}) async-start(s8[6291456]{0:T(1024)(128)(4,1)} %bitcast.92), calls=%async_computation.20 | async-start | bytes 8388608
  714.6 23.3 %slice-start.8 = ((s8[6291456]{0:T(1024)(128)(4,1)}), s8[2097152]{0:T(1024)(128)(4,1)S(1)}, s32[]{:S(2)}) async-start(s8[6291456]{0:T(1024)(128)(4,1)} %bitcast.92), calls=%async_computation.21 | async-start | bytes 4194304
  716.8 22.9 %copy-start.15 = (f32[1024,512]{1,0:T(8,128)}, f32[1024,512]{1,0:T(8,128)S(1)}, u32[]{:S(2)}) copy-start(f32[1024,512]{1,0:T(8,128)S(1)} %get-tuple-element.54) | copy-start | bytes 6291460
  716.8 22.9 %copy-start.17 = (f32[1024,512]{1,0:T(8,128)}, f32[1024,512]{1,0:T(8,128)S(1)}, u32[]{:S(2)}) copy-start(f32[1024,512]{1,0:T(8,128)S(1)} %get-tuple-element.55) | copy-start | bytes 6291460
  716.9 43.4 %collective-permute-start.18 = (bf16[1024,512]{1,0:T(8,128)(2,1)S(1)}, bf16[1024,512]{1,0:T(8,128)(2,1)S(1)}, u32[]{:S(2)}, u32[]{:S(2)}) collective-permute-start(bf16[1024,512]{1,0:T(8,128)(2,1)S(1)} %convert_element_type.234), channel_id=1, source_target_pairs={{0,1},{1,2},{2,3},{3,0},{4,5},{5,6},{6,7},{7,4},{8,9},{9,10},{10,1... | collective-permute-start | bytes 3145736 | tf_op jit(solution)/shard_map/ppermute | solution.py:223
  739.7 43.1 %collective-permute-start.22 = (bf16[1024,512]{1,0:T(8,128)(2,1)S(1)}, bf16[1024,512]{1,0:T(8,128)(2,1)S(1)}, u32[]{:S(2)}, u32[]{:S(2)}) collective-permute-start(bf16[1024,512]{1,0:T(8,128)(2,1)S(1)} %add_convert_fusion.1), channel_id=1, source_target_pairs={{0,1},{1,2},{2,3},{3,0},{4,5},{5,6},{6,7},{7,4},{8,9},{9,10},{10,1... | collective-permute-start | bytes 3145736 | tf_op jit(solution)/shard_map/ppermute | solution.py:223
  760.7 44.8 %collective-permute-start.19 = (bf16[1024,512]{1,0:T(8,128)(2,1)S(1)}, bf16[1024,512]{1,0:T(8,128)(2,1)}, u32[]{:S(2)}, u32[]{:S(2)}) collective-permute-start(bf16[1024,512]{1,0:T(8,128)(2,1)S(1)} %add_convert_fusion.4), channel_id=1, source_target_pairs={{0,1},{1,2},{2,3},{3,0},{4,5},{5,6},{6,7},{7,4},{8,9},{9,10},{10,1... | collective-permute-start | bytes 3145736 | tf_op jit(solution)/shard_map/ppermute | solution.py:223
  762.6 42.9 %copy-start.18 = (f32[1024,512]{1,0:T(8,128)S(1)}, f32[1024,512]{1,0:T(8,128)}, u32[]{:S(2)}) copy-start(f32[1024,512]{1,0:T(8,128)} %copy-done.17) | copy-start | bytes 6291460
  784.1 36.8 %collective-permute-start.23 = (bf16[1024,512]{1,0:T(8,128)(2,1)}, bf16[1024,512]{1,0:T(8,128)(2,1)}, u32[]{:S(2)}, u32[]{:S(2)}) collective-permute-start(bf16[1024,512]{1,0:T(8,128)(2,1)} %add_convert_fusion), channel_id=1, source_target_pairs={{0,1},{1,2},{2,3},{3,0},{4,5},{5,6},{6,7},{7,4},{8,9},{9,10},{10,1... | collective-permute-start | bytes 3145736 | tf_op jit(solution)/shard_map/ppermute | solution.py:223
  808.2 26.1 %copy-start.49 = (f32[1024]{0:T(1024)S(1)}, f32[1024]{0:T(1024)}, u32[]{:S(2)}) copy-start(f32[1024]{0:T(1024)} %get-tuple-element.65) | copy-start | bytes 12292
  808.2 47.7 %collective-permute-start.20 = (bf16[1024,512]{1,0:T(8,128)(2,1)}, bf16[1024,512]{1,0:T(8,128)(2,1)}, u32[]{:S(2)}, u32[]{:S(2)}) collective-permute-start(bf16[1024,512]{1,0:T(8,128)(2,1)} %add_convert_fusion.3), channel_id=1, source_target_pairs={{0,1},{1,2},{2,3},{3,0},{4,5},{5,6},{6,7},{7,4},{8,9},{9,10},{10,1... | collective-permute-start | bytes 3145736 | tf_op jit(solution)/shard_map/ppermute | solution.py:223
  847.3 19.3 %all-to-all-start.1 = ((bf16[8,2,32768]{2,1,0:T(2,128)(2,1)}), bf16[8,2,32768]{2,1,0:T(2,128)(2,1)S(1)}, u32[]{:S(2)}, u32[]{:S(2)}) async-start(bf16[8,2,32768]{2,1,0:T(2,128)(2,1)} %reshape.188), calls=%async_computation.1 | async-start | bytes 2097152 | tf_op jit(solution)/shard_map/all_to_all | solution.py:408
  868.5 51.0 %copy-start.59 = (f32[4,8]{1,0:T(4,128)S(1)}, f32[4,8]{1,0:T(4,128)}, u32[]{:S(2)}) copy-start(f32[4,8]{1,0:T(4,128)} %param.51) | copy-start | bytes 388
  868.6 51.7 %copy-start.60 = (f32[256]{0:T(256)S(1)}, f32[256]{0:T(256)}, u32[]{:S(2)}) copy-start(f32[256]{0:T(256)} %param.50) | copy-start | bytes 3076
  868.6 51.7 %copy-start.61 = (f32[256]{0:T(256)S(1)}, f32[256]{0:T(256)}, u32[]{:S(2)}) copy-start(f32[256]{0:T(256)} %param.49) | copy-start | bytes 3076
  868.6 52.3 %copy-start.41 = (bf16[512,256]{1,0:T(8,128)(2,1)S(1)}, bf16[512,256]{1,0:T(8,128)(2,1)}, u32[]{:S(2)}) copy-start(bf16[512,256]{1,0:T(8,128)(2,1)} %reduce-scatter.7.cloned.1.call-done) | copy-start | bytes 786436
  868.6 52.3 %copy-start.44 = (f32[512,256]{1,0:T(8,128)S(1)}, f32[512,256]{1,0:T(8,128)}, u32[]{:S(2)}) copy-start(f32[512,256]{1,0:T(8,128)} %param.45) | copy-start | bytes 1572868
  869.7 52.1 %copy-start.27 = (bf16[1280,256]{1,0:T(8,128)(2,1)S(1)}, bf16[1280,256]{1,0:T(8,128)(2,1)}, u32[]{:S(2)}) copy-start(bf16[1280,256]{1,0:T(8,128)(2,1)} %reduce-scatter.11.cloned.1.call-done) | copy-start | bytes 1966084
  869.7 52.1 %copy-start.28 = (f32[1280,256]{1,0:T(8,128)S(1)}, f32[1280,256]{1,0:T(8,128)}, u32[]{:S(2)}) copy-start(f32[1280,256]{1,0:T(8,128)} %param.48) | copy-start | bytes 3932164
  (53 other events, 309.6 us)
Sparse Core Ops, SparseCore 0:
  11.7 48.2 all-gather.4
  62.5 51.2 all-gather.6
  116.3 68.5 all-gather.8
  481.0 54.5 reduce-scatter.10
  628.5 37.4 reduce-scatter.6
  669.4 81.5 reduce-scatter.8
  754.4 61.6 reduce-scatter.4

commit v2 on v1

--- a/solution.py
+++ b/solution.py
@@ -68,26 +68,35 @@
     out_ref[...] = mixed.astype(jnp.bfloat16)
 
 
-def attend_forward(qkv, rel_rows, length):
+def attend_forward(qkv, rel_rows, length, first, last, so_far=None):
     seq_len = qkv.shape[0]
     columns = qkv.shape[1] // 3
     pairs = columns // LANES
     width = rel_rows.shape[1]
     rows = min(BLOCK_ROWS, seq_len)
+    kernel = forward_kernel
+    operands = [length.reshape(1), rel_rows.reshape(pairs, 2, width), qkv, qkv, qkv]
+    in_specs = [
+        pl.BlockSpec((1, 2, width), lambda pair, block, n: (first + pair, 0, 0)),
+        pl.BlockSpec((rows, LANES), lambda pair, block, n: (block, first + pair)),
+        pl.BlockSpec((seq_len, LANES), lambda pair, block, n: (0, pairs + first + pair)),
+        pl.BlockSpec((seq_len, LANES), lambda pair, block, n: (0, 2 * pairs + first + pair)),
+    ]
+    aliases = {}
+    if so_far is not None:
+        kernel = second_forward_kernel
+        operands += so_far
+        in_specs += [pl.BlockSpec(memory_space=pl.ANY)] * 2
+        aliases = {5: 0, 6: 1}
     return pl.pallas_call(
-        forward_kernel,
+        kernel,
         grid_spec=pltpu.PrefetchScalarGridSpec(
             num_scalar_prefetch=1,
-            grid=(pairs, seq_len // rows),
-            in_specs=[
-                pl.BlockSpec((1, 2, width), lambda pair, block, n: (pair, 0, 0)),
-                pl.BlockSpec((rows, LANES), lambda pair, block, n: (block, pair)),
-                pl.BlockSpec((seq_len, LANES), lambda pair, block, n: (0, pairs + pair)),
-                pl.BlockSpec((seq_len, LANES), lambda pair, block, n: (0, 2 * pairs + pair)),
-            ],
+            grid=(last - first, seq_len // rows),
+            in_specs=in_specs,
             out_specs=[
-                pl.BlockSpec((rows, LANES), lambda pair, block, n: (block, pair)),
-                pl.BlockSpec((2, rows, seq_len), lambda pair, block, n: (pair, block, 0)),
+                pl.BlockSpec((rows, LANES), lambda pair, block, n: (block, first + pair)),
+                pl.BlockSpec((2, rows, seq_len), lambda pair, block, n: (first + pair, block, 0)),
             ],
             scratch_shapes=[pltpu.VMEM((2, LANES, width), jnp.float32)],
         ),
@@ -95,30 +104,35 @@
             jax.ShapeDtypeStruct((seq_len, columns), jnp.bfloat16),
             jax.ShapeDtypeStruct((2 * pairs, seq_len, seq_len), jnp.bfloat16),
         ],
+        input_output_aliases=aliases,
         compiler_params=pltpu.CompilerParams(vmem_limit_bytes=40 << 20),
         cost_estimate=pl.CostEstimate(
-            flops=16 * seq_len * seq_len * columns,
-            bytes_accessed=4 * pairs * seq_len * seq_len,
-            transcendentals=2 * pairs * seq_len * seq_len,
+            flops=16 * seq_len * seq_len * columns * (last - first) // pairs,
+            bytes_accessed=4 * (last - first) * seq_len * seq_len,
+            transcendentals=2 * (last - first) * seq_len * seq_len,
         ),
         name="attend_forward",
-    )(length.reshape(1), rel_rows.reshape(pairs, 2, width), qkv, qkv, qkv)
+    )(*operands)
+
+
+def second_forward_kernel(
+    length, rel_ref, query_ref, key_ref, value_ref, _, __, out_ref, soft_ref, skew
+):
+    forward_kernel(length, rel_ref, query_ref, key_ref, value_ref, out_ref, soft_ref, skew)
 
 
 def backward_kernel(
+    first,
     soft_ref,
     query_ref,
     grad_ref,
     out_ref,
     key_ref,
     value_ref,
-    grad_qkv_ref,
-    rel_ref,
-    skew,
-    key_acc,
-    value_acc,
+    *rest,
 ):
-    pair = pl.program_id(0)
+    grad_qkv_ref, rel_ref, skew, key_acc, value_acc = rest[-5:]
+    pair = first + pl.program_id(0)
     block = pl.program_id(1)
     rows = query_ref.shape[0]
     key_count = key_ref.shape[0]
@@ -129,6 +143,12 @@
         skew[...] = jnp.zeros_like(skew)
         key_acc[...] = jnp.zeros_like(key_acc)
         value_acc[...] = jnp.zeros_like(value_acc)
+
+    if len(rest) > 5:
+
+        @pl.when((block == 0) & (pair == first))
+        def _():
+            grad_qkv_ref[...] = rest[0][...]
 
     keys = key_ref[...]
     values = value_ref[...]
@@ -177,27 +197,26 @@
             )
 
 
-def attend_backward(soft_low, qkv, grad_heads, attended):
+def attend_backward(soft_low, qkv, grad_heads, attended, first, last, so_far=()):
     seq_len, columns = attended.shape
     pairs = columns // LANES
     width = 2 * seq_len
     rows = min(BLOCK_ROWS, seq_len)
-    row_block = pl.BlockSpec((rows, LANES), lambda pair, block: (block, pair))
+    row_block = pl.BlockSpec((rows, LANES), lambda pair, block: (block, first + pair))
+    whole = pl.BlockSpec((seq_len, 3 * columns), lambda pair, block: (0, 0))
     grad_qkv, rel_grad = pl.pallas_call(
-        backward_kernel,
-        grid=(pairs, seq_len // rows),
+        functools.partial(backward_kernel, first),
+        grid=(last - first, seq_len // rows),
         in_specs=[
-            pl.BlockSpec((2, rows, seq_len), lambda pair, block: (pair, block, 0)),
+            pl.BlockSpec((2, rows, seq_len), lambda pair, block: (first + pair, block, 0)),
             row_block,
             row_block,
             row_block,
-            pl.BlockSpec((seq_len, LANES), lambda pair, block: (0, pairs + pair)),
-            pl.BlockSpec((seq_len, LANES), lambda pair, block: (0, 2 * pairs + pair)),
-        ],
-        out_specs=[
-            pl.BlockSpec((seq_len, 3 * columns), lambda pair, block: (0, 0)),
-            pl.BlockSpec((1, 2, width), lambda pair, block: (pair, 0, 0)),
-        ],
+            pl.BlockSpec((seq_len, LANES), lambda pair, block: (0, pairs + first + pair)),
+            pl.BlockSpec((seq_len, LANES), lambda pair, block: (0, 2 * pairs + first + pair)),
+        ]
+        + [whole] * len(so_far),
+        out_specs=[whole, pl.BlockSpec((1, 2, width), lambda pair, block: (pair, 0, 0))],
         scratch_shapes=[
             pltpu.VMEM((2, LANES, width), jnp.float32),
             pltpu.VMEM((LANES, seq_len), jnp.float32),
@@ -205,22 +224,26 @@
         ],
         out_shape=[
             jax.ShapeDtypeStruct((seq_len, 3 * columns), jnp.bfloat16),
-            jax.ShapeDtypeStruct((pairs, 2, width), jnp.float32),
+            jax.ShapeDtypeStruct((last - first, 2, width), jnp.float32),
         ],
-        compiler_params=pltpu.CompilerParams(vmem_limit_bytes=40 << 20),
+        compiler_params=pltpu.CompilerParams(vmem_limit_bytes=48 << 20),
         cost_estimate=pl.CostEstimate(
-            flops=40 * seq_len * seq_len * columns,
-            bytes_accessed=4 * pairs * seq_len * seq_len,
+            flops=40 * seq_len * seq_len * columns * (last - first) // pairs,
+            bytes_accessed=4 * (last - first) * seq_len * seq_len,
             transcendentals=0,
         ),
         name="attend_backward",
-    )(soft_low, qkv, grad_heads, attended, qkv, qkv)
-    return grad_qkv, rel_grad.reshape(2 * pairs, width)
+    )(soft_low, qkv, grad_heads, attended, qkv, qkv, *so_far)
+    return grad_qkv, rel_grad.reshape(2 * (last - first), width)
 
 
 def around(block):
     count = lax.axis_size("mp")
     return lax.ppermute(block, "mp", [(i, (i + 1) % count) for i in range(count)])
+
+
+def together(*values):
+    return lax.optimization_barrier(values)
 
 
 def ring_gather(own):
@@ -230,11 +253,27 @@
     return blocks
 
 
+def add_low(received, term):
+    return (received.astype(jnp.float32) + term).astype(jnp.bfloat16)
+
+
 def ring_scatter(part_of):
+    count = lax.axis_size("mp")
     running = part_of(1).astype(jnp.bfloat16)
-    for step in range(2, lax.axis_size("mp")):
-        running = (around(running).astype(jnp.float32) + part_of(step)).astype(jnp.bfloat16)
-    return around(running).astype(jnp.float32) + part_of(0)
+    for step in range(2, count):
+        received, term = together(around(running), part_of(step))
+        running = add_low(received, term)
+    received, term = together(around(running), part_of(0))
+    return received.astype(jnp.float32) + term
+
+
+def total_over(value, axis):
+    count = lax.axis_size(axis)
+    apart = 1
+    while apart < count:
+        value = value + lax.ppermute(value, axis, [(i, i ^ apart) for i in range(count)])
+        apart *= 2
+    return value
 
 
 def update(moment, grad_owned, factor):
@@ -278,8 +317,11 @@
     def back(step):
         return lax.rem(member - step + tensor_count, tensor_count)
 
+    qkv_weight = jnp.concatenate([query_weight, key_weight, value_weight], axis=1).astype(low)
     picked = jnp.take(layer_input, deal_order, axis=0)
-    x_own = lax.all_to_all(picked, "dp", split_axis=0, concat_axis=1, tiled=True)[0]
+    picked, qkv_weight = lax.optimization_barrier((picked, qkv_weight))
+    dealt = lax.all_to_all(picked, "dp", split_axis=0, concat_axis=0, tiled=True)
+    x_own = dealt.reshape(-1, dealt.shape[2])
     length = seq_lengths[deal_order[group_index]]
     seq_len, quarter = x_own.shape
     features = quarter * tensor_count
@@ -307,23 +349,26 @@
     first_gain = small[:, :gain_size].reshape(-1).astype(f32)
     second_gain = small[:, gain_size : 2 * gain_size].reshape(-1).astype(f32)
     full_table = small[:, 2 * gain_size :].reshape(NB, bias_table.shape[1])
-    qkv_weight = jnp.concatenate([query_weight, key_weight, value_weight], axis=1).astype(low)
     qkv_weight = lax.all_gather(qkv_weight, "dp", axis=0, tiled=True)
     gate_up = jnp.concatenate([gate_weight, up_weight], axis=1).astype(low)
     out_down = jnp.concatenate([out_weight, down_weight], axis=0).astype(low)
     heads_columns = out_weight.shape[0]
     units = down_weight.shape[0]
-    gate_up, out_down = lax.optimization_barrier((gate_up, out_down, qkv_weight))[:2]
+    out_down, x_own = together(out_down, x_own)
     out_down = lax.all_gather(out_down, "dp", axis=1, tiled=True)
-    gate_up = lax.optimization_barrier((gate_up, out_down))[0]
+
+    def down_columns(step):
+        return lax.dynamic_slice(
+            out_down, (heads_columns, back(step) * quarter), (units, quarter)
+        )
+
+    x_parts = ring_gather(x_own)
+    gate_up, x_parts[1] = together(gate_up, x_parts[1])
     gate_up = lax.all_gather(gate_up, "dp", axis=0, tiled=True)
-    full_out = out_down[:heads_columns]
-    full_down = out_down[heads_columns:]
-
-    x_rows = whole_columns(ring_gather(x_own))
     grad_own = jnp.where(row_valid, output_grad[0], jnp.zeros((), low))
-    grad_own, x_rows = lax.optimization_barrier((grad_own, x_rows))
-    grad_y = whole_columns(ring_gather(grad_own))
+    grad_own, x_parts[-1] = together(grad_own, x_parts[-1])
+    x_rows = whole_columns(x_parts)
+    grad_parts = [grad_own, around(grad_own)]
 
     offsets = jnp.concatenate([bucket_index, jnp.full((1,), NB, jnp.int32)])
     bucket_hot = offsets[:, None] == lax.broadcasted_iota(jnp.int32, (2 * seq_len, NB), 1)
@@ -333,33 +378,68 @@
     inv_first = lax.rsqrt(jnp.mean(x_float * x_float, axis=-1, keepdims=True) + EPS)
     h_first = (x_float * inv_first * first_gain).astype(low)
     qkv = dot(h_first, qkv_weight).astype(low)
-    attended, soft_low = attend_forward(qkv, rel_rows, length)
-    attn_branch = ring_scatter(lambda step: dot(row_part(attended, step), full_out))
+    pairs = heads_columns // LANES
+    half = pairs // 2
+    so_far = attend_forward(qkv, rel_rows, length, 0, half)
+    rel_rows, grad_parts[1], *so_far = lax.optimization_barrier((rel_rows, grad_parts[1], *so_far))
+    grad_parts.append(around(grad_parts[1]))
+    attended, soft_low = attend_forward(qkv, rel_rows, length, half, pairs, so_far)
+    attended, grad_parts[2] = together(attended, grad_parts[2])
+    grad_parts.append(around(grad_parts[2]))
+    attn_branch = ring_scatter(
+        lambda step: dot(row_part(attended, step), out_down[:heads_columns])
+    )
+    attn_branch, *grad_parts = together(attn_branch, *grad_parts)
+    grad_y = whole_columns(grad_parts)
 
     after_attn = row_part(x_rows, 0).astype(f32) + attn_branch
     inv_second = lax.rsqrt(jnp.mean(after_attn * after_attn, axis=-1, keepdims=True) + EPS)
     h_second = (after_attn * inv_second * second_gain).astype(low)
 
-    h_parts = ring_gather(h_second)
+    h_parts = [h_second]
     hidden = jnp.zeros((seq_len, units), low)
     gate_up_grads = []
-    for step, h_part in enumerate(h_parts):
-        both = dot(h_part, gate_up)
+    terms = {}
+
+    def normed_part(step):
+        return dot(gate_up_grads[step], gate_up, NT)
+
+    for step in range(tensor_count):
+        if step == 1:
+            h_parts[1], gate_up_grads[0] = together(h_parts[1], gate_up_grads[0])
+        elif step == 2:
+            h_parts[2], gate_up_grads[1], terms[0] = together(
+                h_parts[2], gate_up_grads[1], normed_part(0)
+            )
+        elif step == 3:
+            h_parts[3], gate_up_grads[2], terms[1] = together(
+                h_parts[3], gate_up_grads[2], normed_part(1).astype(low)
+            )
+            running = around(terms[1])
+        if step < tensor_count - 1:
+            h_parts.append(around(h_parts[step]))
+        both = dot(h_parts[step], gate_up)
         mixed, mix_back = jax.vjp(
             lambda gate_in, up_in: jax.nn.gelu(gate_in, approximate=True) * up_in,
             both[:, :units],
             both[:, units:],
         )
         hidden = set_rows(hidden, mixed.astype(low), step)
-        grad_hidden = dot(row_part(grad_y, step), full_down, NT)
+        grad_hidden = dot(row_part(grad_y, step), out_down[heads_columns:], NT)
         gate_up_grads.append(jnp.concatenate(mix_back(grad_hidden), axis=1).astype(low))
-    grad_h_second = ring_scatter(lambda step: dot(gate_up_grads[step], gate_up, NT))
+
+    received, terms[2], gate_up_grads[3] = together(running, normed_part(2), gate_up_grads[3])
+    running = around(add_low(received, terms[2]))
     h_rotated = jnp.concatenate(h_parts, axis=0)
     grads_rotated = jnp.concatenate(gate_up_grads, axis=0)
     grad_gate_up = dot(h_rotated, grads_rotated, TN).astype(low)
+    received, terms[3], grad_gate_up = together(running, normed_part(3), grad_gate_up)
+    owned_gate_up = lax.psum_scatter(grad_gate_up, "dp", scatter_dimension=0, tiled=True)
+    running = around(add_low(received, terms[3]))
     grad_down = dot(hidden, grad_y, TN).astype(low)
-    owned_gate_up = lax.psum_scatter(grad_gate_up, "dp", scatter_dimension=0, tiled=True)
+    received, terms[0], grad_down, hidden = together(running, terms[0], grad_down, hidden)
     owned_down = lax.psum_scatter(grad_down, "dp", scatter_dimension=1, tiled=True)
+    grad_h_second = received.astype(f32) + terms[0]
 
     grad_ffn_gain = jnp.sum(grad_h_second * (after_attn * inv_second), axis=0)
     weighted = grad_h_second * second_gain
@@ -369,18 +449,68 @@
         + inv_second * weighted
         - after_attn * (inv_second * inv_second * inv_second) * row_inner
     ).astype(low)
-    after_parts = ring_gather(grad_after)
+
+    def output_part(step):
+        part = dot(hidden, down_columns(step))
+        mine = row_part(part, 0) + column_part(after_attn, step)
+        return set_rows(part, mine, 0)
+
+    after_parts = [grad_after]
+    after_parts.append(around(after_parts[0]))
+    output_terms = [output_part(step) for step in range(tensor_count)]
+    after_parts[1], output_terms[1], output_terms[2] = together(
+        after_parts[1], output_terms[1], output_terms[2]
+    )
+    after_parts.append(around(after_parts[1]))
+    after_parts[2], output_terms[3], output_terms[0] = together(
+        after_parts[2], output_terms[3], output_terms[0]
+    )
+    after_parts.append(around(after_parts[2]))
     grad_after = jnp.zeros((seq_len, features), low)
     grad_heads = jnp.zeros((seq_len, heads_columns), low)
-    for step, part in enumerate(after_parts):
+    for step in range(tensor_count):
+        if step == tensor_count - 1:
+            grad_after, grad_heads, after_parts[step] = together(
+                grad_after, grad_heads, after_parts[step]
+            )
+        part = after_parts[step]
         grad_after = set_rows(grad_after, part, step)
-        grad_heads = set_rows(grad_heads, dot(part, full_out, NT).astype(low), step)
+        grad_heads = set_rows(grad_heads, dot(part, out_down[:heads_columns], NT).astype(low), step)
+    output_first = output_terms[1].astype(low)
+    output_first, grad_after, grad_heads = together(output_first, grad_after, grad_heads)
+    output_sum = around(output_first)
     grad_out = dot(attended, grad_after, TN).astype(low)
+    grad_out, grad_heads = together(grad_out, grad_heads)
     owned_out = lax.psum_scatter(grad_out, "dp", scatter_dimension=1, tiled=True)
 
-    grad_qkv, rel_grad = attend_backward(soft_low, qkv, grad_heads, attended)
+    def square_sum(piece):
+        return jnp.sum(jnp.square(piece.astype(f32)))
+
+    first_grads, first_rel = attend_backward(soft_low, qkv, grad_heads, attended, 0, half)
+    output_sum, first_grads, early_sq = together(
+        output_sum, first_grads, square_sum(owned_gate_up)
+    )
+    output_sum = around(add_low(output_sum, output_terms[2]))
+    grad_qkv, second_rel = attend_backward(
+        soft_low, qkv, grad_heads, attended, half, pairs, (first_grads,)
+    )
+    rel_grad = jnp.concatenate([first_rel, second_rel], axis=0)
+    grad_qkv, output_sum, down_sq = together(grad_qkv, output_sum, square_sum(owned_down))
+
+    def first_part(step):
+        weight = lax.dynamic_slice_in_dim(qkv_weight, back(step) * quarter, quarter, 0)
+        return dot(grad_qkv, weight, NT)
+
+    running, grad_qkv = together(first_part(1).astype(low), grad_qkv)
+    running = around(running)
     grad_qkv_weight = dot(h_first, grad_qkv, TN).astype(low)
     owned_qkv = lax.psum_scatter(grad_qkv_weight, "dp", scatter_dimension=0, tiled=True)
+    received, term, grad_qkv_weight = together(running, first_part(2), grad_qkv_weight)
+    running = around(add_low(received, term))
+    inner = jnp.sum(grad_qkv.astype(f32) * qkv.astype(f32), axis=-1)
+    inner = total_over(inner.reshape(-1, LANES), "mp").reshape(-1, 1) / features
+    received, term = together(running, first_part(3))
+    running = around(add_low(received, term))
     grad_table = lax.dot_general(
         bucket_hot.astype(f32),
         rel_grad,
@@ -388,41 +518,30 @@
         precision=lax.Precision.HIGHEST,
         preferred_element_type=f32,
     )
-    grad_h_first = ring_scatter(
-        lambda step: dot(
-            grad_qkv,
-            lax.dynamic_slice_in_dim(qkv_weight, back(step) * quarter, quarter, 0),
-            NT,
-        )
-    )
+    early_sq = early_sq + down_sq + square_sum(owned_out)
+    received, term, grad_table, early_sq, inner = together(
+        running, first_part(0), grad_table, early_sq, inner
+    )
+    received, term, output_sum = together(received, term, output_sum)
+    for step in range(3, tensor_count):
+        output_sum = around(add_low(output_sum, output_terms[step]))
+    grad_h_first = received.astype(f32) + term
     own_gain = lax.dynamic_slice_in_dim(first_gain, member * quarter, quarter, 0)
     x_own = x_own.astype(f32)
     grad_attn_gain = jnp.sum(grad_h_first * (x_own * inv_first), axis=0)
-    weighted = grad_h_first * own_gain
-    row_inner = lax.psum(jnp.sum(weighted * x_own, axis=-1), "mp")[:, None] / features
     grad_input = (
         column_part(grad_after, 0).astype(f32)
-        + inv_first * weighted
-        - x_own * (inv_first * inv_first * inv_first) * row_inner
+        + inv_first * (grad_h_first * own_gain)
+        - x_own * (inv_first * inv_first) * inner
     ).astype(low)
-    came_back = lax.all_to_all(grad_input[None], "dp", split_axis=1, concat_axis=0, tiled=True)
-    group_iota = lax.broadcasted_iota(jnp.int32, (group_count, group_count), 1)
-    place = jnp.argmax(deal_order[None, :] == group_iota.T, axis=1)
+    came_back = lax.all_to_all(
+        grad_input.reshape(group_count, -1, quarter), "dp", split_axis=0, concat_axis=0, tiled=True
+    )
+    group_iota = lax.broadcasted_iota(jnp.int32, (group_count, group_count), 0)
+    place = jnp.argmax(deal_order[None, :] == group_iota, axis=1)
     input_grad = jnp.take(came_back, place, axis=0)
 
-    hidden, grad_after = lax.optimization_barrier((hidden, grad_after))
-
-    def output_part(step):
-        part = dot(hidden, column_part(full_down, step))
-        mine = row_part(part, 0) + column_part(after_attn, step)
-        return set_rows(part, mine, 0)
-
-    layer_out = ring_scatter(output_part).astype(low)[None]
-
-    local_sq = jnp.zeros((), f32)
-    for piece in (owned_qkv, owned_out, owned_gate_up, owned_down):
-        piece = piece.astype(f32)
-        local_sq = local_sq + jnp.sum(piece * piece)
+    local_sq = early_sq + square_sum(owned_qkv)
     heads_dev = bias_table.shape[1]
     first_wide = lax.dynamic_update_slice_in_dim(
         jnp.zeros((features,), f32), grad_attn_gain, member * quarter, 0
@@ -430,11 +549,14 @@
     table_wide = lax.dynamic_update_slice_in_dim(
         jnp.zeros((NB, heads_dev * tensor_count), f32), grad_table, member * heads_dev, 1
     )
-    sums = lax.psum(
-        jnp.concatenate([first_wide, grad_ffn_gain, table_wide.reshape(-1), local_sq[None]]),
-        ("dp", "mp"),
-    )
-    total_sq = sums[-1] + jnp.sum(sums[:-1] * sums[:-1])
+    sums = jnp.concatenate([first_wide, grad_ffn_gain, table_wide.reshape(-1)])
+    small_count = sums.shape[0]
+    sums = jnp.concatenate([sums, jnp.broadcast_to(local_sq, (LANES,))])
+    sums = total_over(sums.reshape(-1, LANES), "dp")
+    sums, output_sum = together(sums, output_sum)
+    layer_out = (output_sum.astype(f32) + output_terms[0]).astype(low)[None]
+    sums = total_over(sums, "mp").reshape(-1)
+    total_sq = sums[small_count] + jnp.sum(sums[:small_count] * sums[:small_count])
     grad_norm = jnp.sqrt(total_sq)
     limit = math.sqrt(4 * D * H * DH + 3 * D * FF + 2 * D + NB * H)
     factor = jnp.minimum(1.0, limit / grad_norm)
@@ -444,7 +566,7 @@
     )
     table_rows = bias_table.shape[0]
     owned_table = lax.dynamic_slice(
-        sums[2 * features : -1].reshape(NB, heads_dev * tensor_count),
+        sums[2 * features : small_count].reshape(NB, heads_dev * tensor_count),
         (group_index * table_rows, member * heads_dev),
         (table_rows, heads_dev),
     )

time: 945 us -> 711 us (0.75)
  waiting for transfers between devices: 519 us -> 303 us
  blocking collectives: 81.2 us -> 8.24 us
  starting transfers between devices: 8.13 us -> 30.2 us
  other arithmetic: 54 us -> 67.5 us
  matrix products: 150 us -> 163 us
    ppermute x24, waiting for transfers between devices: 413 us -> 257 us  [around(): lax.ppermute(block, 'mp', [(i, (i + 1) % count) for i in range(count)])]
    all_gather x1, waiting for transfers between devices: 53.7 us -> 0.01 us  [shards(): out_down = lax.all_gather(out_down, 'dp', axis=1, tiled=True)]
    psum x2 -> x0, blocking collectives: 49.1 us -> none  [the longest x1 39.8 us: shards(): lax.psum(jnp.concatenate([first_wide, grad_ffn_gain, table_wide.reshape(-...]
    all_gather x1, waiting for transfers between devices: 43.7 us -> 0.01 us  [shards(): qkv_weight = lax.all_gather(qkv_weight, 'dp', axis=0, tiled=True)]
    ppermute x0 -> x7, waiting for transfers between devices: none -> 24.5 us  [total_over(): lax.ppermute(value, axis, [(i, i ^ apart) for i in range(count)])]
    all_to_all x1 -> x0, blocking collectives: 24 us -> none  [shards(): lax.all_to_all(picked, 'dp', split_axis=0, concat_axis=1, tiled=True)[0]]
    convert_element_type x6 -> x10, other arithmetic: 6.39 us -> 20 us  [the longest x8 16.6 us: add_low(): return (received.astype(jnp.float32) + term).astype(jnp.bfloat16)]
    all_to_all x1 -> x2, waiting for transfers between devices: 8.21 us -> 21.2 us  [the longest x1 21.2 us: shards(): lax.all_to_all(picked, 'dp', split_axis=0, concat_axis=0, tiled=True)]
  transfers between devices with their start and end apart: 32 -> 40, of which waited for: 25 -> 27; matrix products, arithmetic and copies ran while one was open for 23% -> 33% of each run, Pallas kernels for 6% -> 9%
where the time goes in v2:
time: 711 us; the launch traced here: 700 us
  waiting for transfers between devices  303 us (43%)
  matrix products  163 us (23%)
  other arithmetic  67.5 us (9%)
  Pallas kernels  64.1 us (9%)
  local copies, waits for them, and re-layouts  41.3 us (6%)
  starting transfers between devices  30.2 us (4%)
  between operations  23.1 us (3%)
  blocking collectives  8.24 us (1%)
    ppermute x24, waiting for transfers between devices, around(): lax.ppermute(block, 'mp', [(i, (i + 1) % count) for i in range(count)])  257 us
    dot_general x34, matrix products, dot(): lax.dot_general(left, right, dims, preferred_element_type=jnp.float32)  162 us
    pallas_call x2, Pallas kernels, attend_backward(): pl.pallas_call(functools.partial(backward_kernel, first), grid=(last - fi...  34.4 us
    pallas_call x2, Pallas kernels, attend_forward(): pl.pallas_call(kernel, grid_spec=pltpu.PrefetchScalarGridSpec(num_scalar_...  29.7 us
    ppermute x7, waiting for transfers between devices, total_over(): lax.ppermute(value, axis, [(i, i ^ apart) for i in range(count)])  24.5 us
    all_to_all x1, waiting for transfers between devices, shards(): lax.all_to_all(picked, 'dp', split_axis=0, concat_axis=0, tiled=True)  21.2 us
    unnamed x155, local copies, waits for them, and re-layouts  20.6 us
    convert_element_type x8, other arithmetic, add_low(): return (received.astype(jnp.float32) + term).astype(jnp.bfloat16)  16.6 us
  transfers between devices with their start and end apart: 40, of which 27 were waited for; matrix products, arithmetic and copies ran while one was open for 33% of the time, Pallas kernels for 9%

profile of v2, /device:TPU:0, one launch (start us, length us, event | category | flops | bytes accessed | tf_op | source)
XLA Modules:
  0.0 700.1 jit_solution(5563405711557779066)
XLA Ops:
  14.7 5.3 all-to-all-start
  21.2 21.2 %all-to-all-done = bf16[8,128,512]{2,1,0:T(8,128)(2,1)S(1)} async-done(((bf16[8,128,512]{2,1,0:T(8,128)(2,1)}), bf16[8,128,512]{2,1,0:T(8,128)(2,1)S(1)}, u32[]{:S(2)}, u32[]{:S(2)}) %all-to-all-start) | async-done | bytes 1048608 | tf_op jit(solution)/shard_map/all_to_all | solution.py:323
  45.6 20.3 %collective-permute-done = bf16[1024,512]{1,0:T(8,128)(2,1)S(1)} collective-permute-done((bf16[1024,512]{1,0:T(8,128)(2,1)S(1)}, bf16[1024,512]{1,0:T(8,128)(2,1)S(1)}, u32[]{:S(2)}, u32[]{:S(2)}) %collective-permute-start) | collective-permute-done | bytes 1048608 | tf_op jit(solution)/shard_map/ppermute | solution.py:242
  66.8 8.2 %all-gather = bf16[8,1,544]{2,1,0:T(2,128)(2,1)S(1)} all-gather(bf16[1,1,544]{2,1,0:T(2,128)(2,1)S(1)} %maximum_bitcast_fusion.1), channel_id=1, replica_groups=mesh['dp'=8,'mp'=4] {'dp'}, dimensions={0}, use_global_device_ids=true | all-gather | bytes 9792 | tf_op jit(solution)/shard_map/all_gather | solution.py:347
  75.0 14.1 %collective-permute-done.1 = bf16[1024,512]{1,0:T(8,128)(2,1)} collective-permute-done((bf16[1024,512]{1,0:T(8,128)(2,1)S(1)}, bf16[1024,512]{1,0:T(8,128)(2,1)}, u32[]{:S(2)}, u32[]{:S(2)}) %collective-permute-start.1) | collective-permute-done | bytes 1048608 | tf_op jit(solution)/shard_map/ppermute | solution.py:242
  99.3 13.2 %collective-permute-done.2 = bf16[1024,512]{1,0:T(8,128)(2,1)} collective-permute-done((bf16[1024,512]{1,0:T(8,128)(2,1)}, bf16[1024,512]{1,0:T(8,128)(2,1)}, u32[]{:S(2)}, u32[]{:S(2)}) %collective-permute-start.2) | collective-permute-done | bytes 1048608 | tf_op jit(solution)/shard_map/ppermute | solution.py:242
  118.0 10.5 %convolution_convert_fusion.3.query_ref.key_ref.value_ref = bf16[1024,1536]{1,0:T(8,128)(2,1)S(1)} fusion(bf16[2048,1536]{1,0:T(8,128)(2,1)} %all-gather.5.cloned.1.call-done, bf16[1024,2048]{1,0:T(8,128)(2,1)} %copy-done.12, f32[2048]{0:T(1024)S(1)} %bitcast.84, f32[1024]{0:T(1024)S(1)} %get-tuple-element.220), kind=kOutput, calls=%fused_computation.25 | convolution fusion | flops 6452412416 | bytes 13643776 | tf_op jit(solution)/shard_map/dot_general | solution.py:29
  128.6 14.8 %attend_forward.2 = (bf16[1024,512]{1,0:T(8,128)(2,1)S(1)}, bf16[8,1024,1024]{2,1,0:T(8,128)(2,1)}) custom-call(s32[1]{0:T(128)} %dynamic_slice.98.length, f32[4,2,2048]{2,1,0:T(2,128)S(1)} %reshape.188.rel_ref, bf16[1024,1536]{1,0:T(8,128)(2,1)S(1)} %convolution_convert_fusion.3.query_ref.key_ref.value_ref, ...), custom_call_target="tpu_custom_call" | custom-call | flops 4294967296 | bytes 8388608 | tf_op jit(solution)/shard_map/attend_forward/pallas_call | solution.py:91
  144.4 2.9 collective-permute-start.4
  148.6 14.8 %attend_forward.3 = (bf16[1024,512]{1,0:T(8,128)(2,1)S(1)}, bf16[8,1024,1024]{2,1,0:T(8,128)(2,1)}) custom-call(s32[1]{0:T(128)} %dynamic_slice.98.length, f32[4,2,2048]{2,1,0:T(2,128)S(1)} %reshape.189.rel_ref, bf16[1024,1536]{1,0:T(8,128)(2,1)S(1)} %convolution_convert_fusion.3.query_ref.key_ref.value_ref, ...), custom_call_target="tpu_custom_call", output_to_operand_aliasing={{0}: (5, {}), {1}: (6, {})} | custom-call | flops 4294967296 | bytes 8388608 | tf_op jit(solution)/shard_map/attend_forward/pallas_call | solution.py:91
  164.9 2.5 convolution_convert_fusion.6
  171.4 19.5 %collective-permute-done.5 = bf16[256,2048]{1,0:T(8,128)(2,1)S(1)} collective-permute-done((bf16[256,2048]{1,0:T(8,128)(2,1)S(1)}, bf16[256,2048]{1,0:T(8,128)(2,1)S(1)}, u32[]{:S(2)}, u32[]{:S(2)}) %collective-permute-start.5) | collective-permute-done | bytes 1048608 | tf_op jit(solution)/shard_map/ppermute | solution.py:242
  193.6 19.4 %collective-permute-done.6 = bf16[256,2048]{1,0:T(8,128)(2,1)} collective-permute-done((bf16[256,2048]{1,0:T(8,128)(2,1)S(1)}, bf16[256,2048]{1,0:T(8,128)(2,1)}, u32[]{:S(2)}, u32[]{:S(2)}) %collective-permute-start.6) | collective-permute-done | bytes 1048608 | tf_op jit(solution)/shard_map/ppermute | solution.py:242
  218.1 23.8 %collective-permute-done.7 = bf16[256,2048]{1,0:T(8,128)(2,1)S(1)} collective-permute-done((bf16[256,2048]{1,0:T(8,128)(2,1)S(1)}, bf16[256,2048]{1,0:T(8,128)(2,1)S(1)}, u32[]{:S(2)}, u32[]{:S(2)}) %collective-permute-start.7) | collective-permute-done | bytes 1048608 | tf_op jit(solution)/shard_map/ppermute | solution.py:242
  242.3 15.1 %collective-permute-done.8 = bf16[1024,512]{1,0:T(8,128)(2,1)} collective-permute-done((bf16[1024,512]{1,0:T(8,128)(2,1)}, bf16[1024,512]{1,0:T(8,128)(2,1)}, u32[]{:S(2)}, u32[]{:S(2)}) %collective-permute-start.8) | collective-permute-done | bytes 1048608 | tf_op jit(solution)/shard_map/ppermute | solution.py:242
  260.3 2.5 broadcast.112.clone.1
  269.7 2.3 constant_dynamic-update-slice_fusion.4
  272.0 5.9 fusion.139
  278.0 6.2 fusion.49
  285.6 6.6 fusion.140
  292.2 4.8 fusion.56
  297.2 8.7 %fusion.141 = f32[256,2048]{1,0:T(8,128)} fusion(bf16[256,2560]{1,0:T(8,128)(2,1)S(1)} %pad_maximum_fusion.1, bf16[2048,2560]{1,0:T(8,128)(2,1)} %all-gather.9.cloned.1.call-done), kind=kOutput, calls=%fused_computation.256 | convolution fusion | flops 2684354560 | bytes 13893632 | tf_op jit(solution)/shard_map/dot_general | solution.py:29
  308.2 6.0 fusion.142
  314.2 4.8 fusion.63
  319.1 8.3 %convolution_convert_fusion.5 = bf16[256,2048]{1,0:T(8,128)(2,1)} fusion(bf16[256,2560]{1,0:T(8,128)(2,1)S(1)} %pad_maximum_fusion.2, bf16[2048,2560]{1,0:T(8,128)(2,1)} %all-gather.9.cloned.1.call-done), kind=kOutput, calls=%fused_computation.38 | convolution fusion | flops 2684878848 | bytes 12845056 | tf_op jit(solution)/shard_map/dot_general | solution.py:29
  327.5 4.8 collective-permute-done.11
  332.5 5.9 fusion.144
  338.5 4.8 fusion.70
  344.5 5.6 fusion.143
  350.1 6.8 collective-permute-done.12
  358.2 16.6 %convolution_convert_fusion = bf16[2048,2560]{1,0:T(8,128)(2,1)} fusion(bf16[256,2560]{1,0:T(8,128)(2,1)} %pad_maximum_fusion.4, bf16[256,2560]{1,0:T(8,128)(2,1)} %copy-done.38, bf16[256,2560]{1,0:T(8,128)(2,1)} %copy-done.37, bf16[256,2560]{1,0:T(8,128)(2,1)S(1)} %pad_maximum_fusion.1, bf16[256,2048]{1,0:T(8,128)(2,1)} %collective-permute-done.11, ...), kind=kOutput, calls=%fused_computation.2 | convolution fusion | flops 10780409856 | bytes 19922944 | tf_op jit(solution)/shard_map/dot_general | solution.py:29
  374.8 8.7 %fusion.145 = f32[256,2048]{1,0:T(8,128)} fusion(bf16[256,2560]{1,0:T(8,128)(2,1)} %pad_maximum_fusion.4, bf16[2048,2560]{1,0:T(8,128)(2,1)} %all-gather.9.cloned.1.call-done), kind=kOutput, calls=%fused_computation.260 | convolution fusion | flops 2684354560 | bytes 13893632 | tf_op jit(solution)/shard_map/dot_general | solution.py:29
  393.9 3.5 add_convert_fusion.5
  399.5 9.8 %convolution_convert_fusion.2 = bf16[1280,2048]{1,0:T(8,128)(2,1)} fusion(bf16[1024,1280]{1,0:T(8,128)(2,1)S(1)} %fusion.95, bf16[1024,2048]{1,0:T(8,128)(2,1)} %constant_dynamic-update-slice_fusion.4), kind=kOutput, calls=%fused_computation.9 | convolution fusion | flops 5371330560 | bytes 12058624 | tf_op jit(solution)/shard_map/dot_general | solution.py:29
  409.3 16.3 %collective-permute-done.14 = bf16[256,2048]{1,0:T(8,128)(2,1)} collective-permute-done((bf16[256,2048]{1,0:T(8,128)(2,1)}, bf16[256,2048]{1,0:T(8,128)(2,1)}, u32[]{:S(2)}, u32[]{:S(2)}) %collective-permute-start.14) | collective-permute-done | bytes 1048608 | tf_op jit(solution)/shard_map/ppermute | solution.py:242
  425.7 2.5 multiply_reduce_fusion.2
  429.8 2.5 constant_dynamic-update-slice_fusion.3
  432.4 3.1 fusion.71
  440.7 15.0 %collective-permute-done.15 = bf16[256,2048]{1,0:T(8,128)(2,1)S(1)} collective-permute-done((bf16[256,2048]{1,0:T(8,128)(2,1)S(1)}, bf16[256,2048]{1,0:T(8,128)(2,1)S(1)}, u32[]{:S(2)}, u32[]{:S(2)}) %collective-permute-start.15) | collective-permute-done | bytes 1048608 | tf_op jit(solution)/shard_map/ppermute | solution.py:242
  456.9 21.4 %collective-permute-done.16 = bf16[256,2048]{1,0:T(8,128)(2,1)S(1)} collective-permute-done((bf16[256,2048]{1,0:T(8,128)(2,1)S(1)}, bf16[256,2048]{1,0:T(8,128)(2,1)S(1)}, u32[]{:S(2)}, u32[]{:S(2)}) %collective-permute-start.16) | collective-permute-done | bytes 1048608 | tf_op jit(solution)/shard_map/ppermute | solution.py:242
  480.0 17.7 %collective-permute-done.17 = bf16[256,2048]{1,0:T(8,128)(2,1)S(1)} collective-permute-done((bf16[256,2048]{1,0:T(8,128)(2,1)S(1)}, bf16[256,2048]{1,0:T(8,128)(2,1)S(1)}, u32[]{:S(2)}, u32[]{:S(2)}) %collective-permute-start.17) | collective-permute-done | bytes 1048608 | tf_op jit(solution)/shard_map/ppermute | solution.py:242
  499.8 3.8 convolution_convert_fusion.4
  503.6 16.5 %attend_backward.2 = (bf16[1024,1536]{1,0:T(8,128)(2,1)S(1)}, f32[2,2,2048]{2,1,0:T(2,128)S(1)}) custom-call(bf16[8,1024,1024]{2,1,0:T(8,128)(2,1)} %get-tuple-element.113.soft_ref, bf16[1024,1536]{1,0:T(8,128)(2,1)} %copy-done.2, bf16[1024,512]{1,0:T(8,128)(2,1)S(1)} %fusion.84.grad_ref, bf16[1024,512]{1,0:T(8,128)(2,1)S(1)} %copy-done.7, ...), custom_call_target="tpu_custom_call" | custom-call | flops 10737418240 | bytes 8388608 | tf_op jit(solution)/shard_map/attend_backward/pallas_call | solution.py:207
  521.8 2.6 multiply_reduce_fusion.1
  524.7 3.2 add_convert_fusion.4
  530.2 17.9 %attend_backward.3 = (bf16[1024,1536]{1,0:T(8,128)(2,1)S(1)}, f32[2,2,2048]{2,1,0:T(2,128)S(1)}) custom-call(bf16[8,1024,1024]{2,1,0:T(8,128)(2,1)} %get-tuple-element.113.soft_ref, bf16[1024,1536]{1,0:T(8,128)(2,1)} %copy-done.2, bf16[1024,512]{1,0:T(8,128)(2,1)S(1)} %fusion.84.grad_ref, bf16[1024,512]{1,0:T(8,128)(2,1)S(1)} %copy-done.7, ...), custom_call_target="tpu_custom_call" | custom-call | flops 10737418240 | bytes 8388608 | tf_op jit(solution)/shard_map/attend_backward/pallas_call | solution.py:207
  548.1 5.6 fusion.38
  553.8 9.0 %convolution_convert_fusion.1 = bf16[2048,1536]{1,0:T(8,128)(2,1)} fusion(bf16[1024,1536]{1,0:T(8,128)(2,1)S(1)} %get-tuple-element.166, bf16[1024,2048]{1,0:T(8,128)(2,1)S(1)} %copy-done.13, f32[2048]{0:T(1024)S(1)} %bitcast.85, f32[1024]{0:T(1024)S(1)} %copy-done.56), kind=kOutput, calls=%fused_computation.8 | convolution fusion | flops 6453985280 | bytes 13643776 | tf_op jit(solution)/shard_map/dot_general | solution.py:29
  564.8 3.2 fusion.34
  568.0 18.2 %collective-permute-done.20 = bf16[1024,512]{1,0:T(8,128)(2,1)S(1)} collective-permute-done((bf16[1024,512]{1,0:T(8,128)(2,1)}, bf16[1024,512]{1,0:T(8,128)(2,1)S(1)}, u32[]{:S(2)}, u32[]{:S(2)}) %collective-permute-start.20) | collective-permute-done | bytes 1048608 | tf_op jit(solution)/shard_map/ppermute | solution.py:242
  590.3 2.9 multiply_reduce_fusion
  594.4 3.2 fusion.32
  597.7 12.7 %collective-permute-done.21 = bf16[1024,512]{1,0:T(8,128)(2,1)} collective-permute-done((bf16[1024,512]{1,0:T(8,128)(2,1)}, bf16[1024,512]{1,0:T(8,128)(2,1)}, u32[]{:S(2)}, u32[]{:S(2)}) %collective-permute-start.21) | collective-permute-done | bytes 1048608 | tf_op jit(solution)/shard_map/ppermute | solution.py:242
  610.4 2.6 add_convert_fusion.2
  614.6 3.2 fusion.30
  619.8 10.9 %collective-permute-done.24 = f32[8,128]{1,0:T(8,128)S(1)} collective-permute-done((f32[8,128]{1,0:T(8,128)S(1)}, f32[8,128]{1,0:T(8,128)S(1)}, u32[]{:S(2)}, u32[]{:S(2)}) %collective-permute-start.24) | collective-permute-done | bytes 4128 | tf_op jit(solution)/shard_map/ppermute | solution.py:274
  630.7 3.8 collective-permute-done.22
  634.5 3.2 fusion.29
  637.7 3.7 all-to-all-start.1
  641.8 2.9 add_convert_fusion.1
  651.6 4.8 collective-permute-done.26
  660.3 11.9 %collective-permute-done.28 = bf16[1024,512]{1,0:T(8,128)(2,1)S(1)} collective-permute-done((bf16[1024,512]{1,0:T(8,128)(2,1)}, bf16[1024,512]{1,0:T(8,128)(2,1)S(1)}, u32[]{:S(2)}, u32[]{:S(2)}) %collective-permute-start.28) | collective-permute-done | bytes 1048608 | tf_op jit(solution)/shard_map/ppermute | solution.py:242
  673.3 2.7 collective-permute-done.29
  677.5 3.4 collective-permute-done.30
  (336 shorter events, 118.1 us)
Async XLA Ops:
  7.2 110.8 %all-gather.5.cloned.1.call-start = ((), (), s32[]{:S(2)}) async-start(), calls=%async_computation.6 | async-start | bytes 7077888 | tf_op jit(solution)/shard_map/all_gather | solution.py:352
  14.7 27.7 %all-to-all-start = ((bf16[8,128,512]{2,1,0:T(8,128)(2,1)}), bf16[8,128,512]{2,1,0:T(8,128)(2,1)S(1)}, u32[]{:S(2)}, u32[]{:S(2)}) async-start(bf16[8,128,512]{2,1,0:T(8,128)(2,1)} %broadcast_select_fusion.1), calls=%async_computation | async-start | bytes 2097152 | tf_op jit(solution)/shard_map/all_to_all | solution.py:323
  20.0 144.9 %all-gather.7.cloned.1.call-start = ((), (), s32[]{:S(2)}) async-start(), calls=%async_computation.7 | async-start | bytes 8257536 | tf_op jit(solution)/shard_map/all_gather | solution.py:358
  20.2 24.0 %copy-start.40 = (f32[256,1280]{1,0:T(8,128)S(1)}, f32[256,1280]{1,0:T(8,128)}, u32[]{:S(2)}) copy-start(f32[256,1280]{1,0:T(8,128)} %param.36) | copy-start | bytes 3932164
  42.4 53.7 %copy-start.14 = (bf16[8,128,512]{2,1,0:T(8,128)(2,1)}, bf16[8,128,512]{2,1,0:T(8,128)(2,1)S(1)}, u32[]{:S(2)}) copy-start(bf16[8,128,512]{2,1,0:T(8,128)(2,1)S(1)} %all-to-all-done) | copy-start | bytes 3145732
  42.4 229.6 %all-gather.9.cloned.1.call-start = ((), (), s32[]{:S(2)}) async-start(), calls=%async_computation.8 | async-start | bytes 11796480 | tf_op jit(solution)/shard_map/all_gather | solution.py:367
  42.5 23.4 %collective-permute-start = (bf16[1024,512]{1,0:T(8,128)(2,1)S(1)}, bf16[1024,512]{1,0:T(8,128)(2,1)S(1)}, u32[]{:S(2)}, u32[]{:S(2)}) collective-permute-start(bf16[1024,512]{1,0:T(8,128)(2,1)S(1)} %bitcast.68), channel_id=1, source_target_pairs={{0,1},{1,2},{2,3},{3,0},{4,5},{5,6},{6,7},{7,4},{8,9},{9,10},{10,1... | collective-permute-start | bytes 3145736 | tf_op jit(solution)/shard_map/ppermute | solution.py:242
  44.4 22.2 %copy-start.67 = (f32[256]{0:T(256)S(1)}, f32[256]{0:T(256)}, u32[]{:S(2)}) copy-start(f32[256]{0:T(256)} %param.39) | copy-start | bytes 3076
  44.4 22.2 %copy-start.68 = (f32[256]{0:T(256)S(1)}, f32[256]{0:T(256)}, u32[]{:S(2)}) copy-start(f32[256]{0:T(256)} %param.40) | copy-start | bytes 3076
  44.4 22.3 %copy-start.62 = (f32[4,8]{1,0:T(4,128)S(1)}, f32[4,8]{1,0:T(4,128)}, u32[]{:S(2)}) copy-start(f32[4,8]{1,0:T(4,128)} %param.41) | copy-start | bytes 388
  44.4 45.3 %copy-start.59 = (s32[2047]{0:T(1024)S(1)}, s32[2047]{0:T(1024)}, u32[]{:S(2)}) copy-start(s32[2047]{0:T(1024)} %param.31) | copy-start | bytes 24568
  44.4 45.3 %copy-start.70 = (s32[8]{0:T(128)S(1)}, s32[8]{0:T(128)}, u32[]{:S(2)}) copy-start(s32[8]{0:T(128)} %param.30) | copy-start | bytes 100
  44.4 48.8 %copy-start.69 = (s32[8]{0:T(128)S(1)}, s32[8]{0:T(128)}, u32[]{:S(2)}) copy-start(s32[8]{0:T(128)} %param.29) | copy-start | bytes 100
  44.5 50.0 %copy-start.47 = (bf16[1,1024,512]{2,1,0:T(8,128)(2,1)S(1)}, bf16[1,1024,512]{2,1,0:T(8,128)(2,1)}, u32[]{:S(2)}) copy-start(bf16[1,1024,512]{2,1,0:T(8,128)(2,1)} %param.28) | copy-start | bytes 3145732
  65.9 25.8 %copy-start.44 = (bf16[1024,512]{1,0:T(8,128)(2,1)}, bf16[1024,512]{1,0:T(8,128)(2,1)S(1)}, u32[]{:S(2)}) copy-start(bf16[1024,512]{1,0:T(8,128)(2,1)S(1)} %collective-permute-done) | copy-start | bytes 3145732
  65.9 455.9 %reduce-scatter.5.cloned.1.call-start = ((), (), s32[]{:S(2)}) async-start(), calls=%async_computation.9 | async-start | bytes 11796480 | tf_op jit(solution)/shard_map/reduce_scatter | solution.py:437
  66.0 23.2 %collective-permute-start.1 = (bf16[1024,512]{1,0:T(8,128)(2,1)S(1)}, bf16[1024,512]{1,0:T(8,128)(2,1)}, u32[]{:S(2)}, u32[]{:S(2)}) collective-permute-start(bf16[1024,512]{1,0:T(8,128)(2,1)S(1)} %collective-permute-done), channel_id=1, source_target_pairs={{0,1},{1,2},{2,3},{3,0},{4,5},{5,6},{6,7},{7,4},{8,9},{9,10},{10,1... | collective-permute-start | bytes 3145736 | tf_op jit(solution)/shard_map/ppermute | solution.py:242
  89.2 23.3 %collective-permute-start.2 = (bf16[1024,512]{1,0:T(8,128)(2,1)}, bf16[1024,512]{1,0:T(8,128)(2,1)}, u32[]{:S(2)}, u32[]{:S(2)}) collective-permute-start(bf16[1024,512]{1,0:T(8,128)(2,1)} %collective-permute-done.1), channel_id=1, source_target_pairs={{0,1},{1,2},{2,3},{3,0},{4,5},{5,6},{6,7},{7,4},{8,9},{9,10},{10,1... | collective-permute-start | bytes 3145736 | tf_op jit(solution)/shard_map/ppermute | solution.py:242
  91.8 26.2 %copy-start.57 = (f32[1,2,8,128]{3,1,2,0:T(2,128)}, f32[1,2,8,128]{3,1,2,0:T(2,128)S(1)}, u32[]{:S(2)}) copy-start(f32[1,2,8,128]{3,1,2,0:T(2,128)S(1)} %copy.44) | copy-start | bytes 24580
  112.5 31.9 %collective-permute-start.3 = (bf16[1024,512]{1,0:T(8,128)(2,1)}, bf16[1024,512]{1,0:T(8,128)(2,1)}, u32[]{:S(2)}, u32[]{:S(2)}) collective-permute-start(bf16[1024,512]{1,0:T(8,128)(2,1)} %bitcast_select_fusion), channel_id=1, source_target_pairs={{0,1},{1,2},{2,3},{3,0},{4,5},{5,6},{6,7},{7,4},{8,9},{9,10},{10,1... | collective-permute-start | bytes 3145736 | tf_op jit(solution)/shard_map/ppermute | solution.py:242
  128.6 18.8 %copy-start.2 = (bf16[1024,1536]{1,0:T(8,128)(2,1)}, bf16[1024,1536]{1,0:T(8,128)(2,1)S(1)}, u32[]{:S(2)}) copy-start(bf16[1024,1536]{1,0:T(8,128)(2,1)S(1)} %convolution_convert_fusion.3.query_ref.key_ref.value_ref) | copy-start | bytes 9437188
  144.4 20.5 %collective-permute-start.4 = (bf16[1024,512]{1,0:T(8,128)(2,1)}, bf16[1024,512]{1,0:T(8,128)(2,1)}, u32[]{:S(2)}, u32[]{:S(2)}) collective-permute-start(bf16[1024,512]{1,0:T(8,128)(2,1)} %collective-permute-done.3), channel_id=1, source_target_pairs={{0,1},{1,2},{2,3},{3,0},{4,5},{5,6},{6,7},{7,4},{8,9},{9,10},{10,1... | collective-permute-start | bytes 3145736 | tf_op jit(solution)/shard_map/ppermute | solution.py:242
  167.4 23.5 %collective-permute-start.5 = (bf16[256,2048]{1,0:T(8,128)(2,1)S(1)}, bf16[256,2048]{1,0:T(8,128)(2,1)S(1)}, u32[]{:S(2)}, u32[]{:S(2)}) collective-permute-start(bf16[256,2048]{1,0:T(8,128)(2,1)S(1)} %convolution_convert_fusion.6), channel_id=1, source_target_pairs={{0,1},{1,2},{2,3},{3,0},{4,5},{5,6},{6,7},{7,4},{8,9},{9,10},{10,1... | collective-permute-start | bytes 3145736 | tf_op jit(solution)/shard_map/ppermute | solution.py:242
  191.2 21.8 %collective-permute-start.6 = (bf16[256,2048]{1,0:T(8,128)(2,1)S(1)}, bf16[256,2048]{1,0:T(8,128)(2,1)}, u32[]{:S(2)}, u32[]{:S(2)}) collective-permute-start(bf16[256,2048]{1,0:T(8,128)(2,1)S(1)} %add_convert_fusion.8), channel_id=1, source_target_pairs={{0,1},{1,2},{2,3},{3,0},{4,5},{5,6},{6,7},{7,4},{8,9},{9,10},{10,1... | collective-permute-start | bytes 3145736 | tf_op jit(solution)/shard_map/ppermute | solution.py:242
  214.5 27.4 %collective-permute-start.7 = (bf16[256,2048]{1,0:T(8,128)(2,1)S(1)}, bf16[256,2048]{1,0:T(8,128)(2,1)S(1)}, u32[]{:S(2)}, u32[]{:S(2)}) collective-permute-start(bf16[256,2048]{1,0:T(8,128)(2,1)S(1)} %add_convert_fusion.7), channel_id=1, source_target_pairs={{0,1},{1,2},{2,3},{3,0},{4,5},{5,6},{6,7},{7,4},{8,9},{9,10},{10,1... | collective-permute-start | bytes 3145736 | tf_op jit(solution)/shard_map/ppermute | solution.py:242
  214.6 42.8 %collective-permute-start.8 = (bf16[1024,512]{1,0:T(8,128)(2,1)}, bf16[1024,512]{1,0:T(8,128)(2,1)}, u32[]{:S(2)}, u32[]{:S(2)}) collective-permute-start(bf16[1024,512]{1,0:T(8,128)(2,1)} %collective-permute-done.4), channel_id=1, source_target_pairs={{0,1},{1,2},{2,3},{3,0},{4,5},{5,6},{6,7},{7,4},{8,9},{9,10},{10,1... | collective-permute-start | bytes 3145736 | tf_op jit(solution)/shard_map/ppermute | solution.py:242
  260.3 24.0 %collective-permute-start.9 = (bf16[256,2048]{1,0:T(8,128)(2,1)}, bf16[256,2048]{1,0:T(8,128)(2,1)}, u32[]{:S(2)}, u32[]{:S(2)}) collective-permute-start(bf16[256,2048]{1,0:T(8,128)(2,1)} %multiply_convert_fusion), channel_id=1, source_target_pairs={{0,1},{1,2},{2,3},{3,0},{4,5},{5,6},{6,7},{7,4},{8,9},{9,10},{10,1... | collective-permute-start | bytes 3145736 | tf_op jit(solution)/shard_map/ppermute | solution.py:242
  284.3 23.9 %collective-permute-start.10 = (bf16[256,2048]{1,0:T(8,128)(2,1)}, bf16[256,2048]{1,0:T(8,128)(2,1)S(1)}, u32[]{:S(2)}, u32[]{:S(2)}) collective-permute-start(bf16[256,2048]{1,0:T(8,128)(2,1)} %collective-permute-done.9), channel_id=1, source_target_pairs={{0,1},{1,2},{2,3},{3,0},{4,5},{5,6},{6,7},{7,4},{8,9},{9,10},{10,1... | collective-permute-start | bytes 3145736 | tf_op jit(solution)/shard_map/ppermute | solution.py:242
  297.1 22.0 %copy-start.37 = (bf16[256,2560]{1,0:T(8,128)(2,1)}, bf16[256,2560]{1,0:T(8,128)(2,1)S(1)}, u32[]{:S(2)}) copy-start(bf16[256,2560]{1,0:T(8,128)(2,1)S(1)} %pad_maximum_fusion.2) | copy-start | bytes 3932164
  308.2 24.2 %collective-permute-start.11 = (bf16[256,2048]{1,0:T(8,128)(2,1)S(1)}, bf16[256,2048]{1,0:T(8,128)(2,1)}, u32[]{:S(2)}, u32[]{:S(2)}) collective-permute-start(bf16[256,2048]{1,0:T(8,128)(2,1)S(1)} %collective-permute-done.10), channel_id=1, source_target_pairs={{0,1},{1,2},{2,3},{3,0},{4,5},{5,6},{6,7},{7,4},{8,9},{9,10},{10,1... | collective-permute-start | bytes 3145736 | tf_op jit(solution)/shard_map/ppermute | solution.py:242
  319.1 25.3 %copy-start.38 = (bf16[256,2560]{1,0:T(8,128)(2,1)}, bf16[256,2560]{1,0:T(8,128)(2,1)S(1)}, u32[]{:S(2)}) copy-start(bf16[256,2560]{1,0:T(8,128)(2,1)S(1)} %pad_maximum_fusion.3) | copy-start | bytes 3932164
  332.3 24.5 %collective-permute-start.12 = (bf16[256,2048]{1,0:T(8,128)(2,1)}, bf16[256,2048]{1,0:T(8,128)(2,1)S(1)}, u32[]{:S(2)}, u32[]{:S(2)}) collective-permute-start(bf16[256,2048]{1,0:T(8,128)(2,1)} %convolution_convert_fusion.5), channel_id=1, source_target_pairs={{0,1},{1,2},{2,3},{3,0},{4,5},{5,6},{6,7},{7,4},{8,9},{9,10},{10,1... | collective-permute-start | bytes 3145736 | tf_op jit(solution)/shard_map/ppermute | solution.py:242
  358.2 25.3 %collective-permute-start.13 = (bf16[256,2048]{1,0:T(8,128)(2,1)}, bf16[256,2048]{1,0:T(8,128)(2,1)}, u32[]{:S(2)}, u32[]{:S(2)}) collective-permute-start(bf16[256,2048]{1,0:T(8,128)(2,1)} %add_convert_fusion.6), channel_id=1, source_target_pairs={{0,1},{1,2},{2,3},{3,0},{4,5},{5,6},{6,7},{7,4},{8,9},{9,10},{10,1... | collective-permute-start | bytes 3145736 | tf_op jit(solution)/shard_map/ppermute | solution.py:242
  383.5 144.6 %reduce-scatter.7.cloned.1.call-start = ((), (), s32[]{:S(2)}) async-start(), calls=%async_computation.10 | async-start | bytes 5898240 | tf_op jit(solution)/shard_map/reduce_scatter | solution.py:441
  397.4 28.2 %collective-permute-start.14 = (bf16[256,2048]{1,0:T(8,128)(2,1)}, bf16[256,2048]{1,0:T(8,128)(2,1)}, u32[]{:S(2)}, u32[]{:S(2)}) collective-permute-start(bf16[256,2048]{1,0:T(8,128)(2,1)} %add_convert_fusion.5), channel_id=1, source_target_pairs={{0,1},{1,2},{2,3},{3,0},{4,5},{5,6},{6,7},{7,4},{8,9},{9,10},{10,1... | collective-permute-start | bytes 3145736 | tf_op jit(solution)/shard_map/ppermute | solution.py:242
  425.6 162.9 %reduce-scatter.9.cloned.1.call-start = ((), (), s32[]{:S(2)}) async-start(), calls=%async_computation.11 | async-start | bytes 2359296 | tf_op jit(solution)/shard_map/reduce_scatter | solution.py:484
  432.3 23.4 %collective-permute-start.15 = (bf16[256,2048]{1,0:T(8,128)(2,1)S(1)}, bf16[256,2048]{1,0:T(8,128)(2,1)S(1)}, u32[]{:S(2)}, u32[]{:S(2)}) collective-permute-start(bf16[256,2048]{1,0:T(8,128)(2,1)S(1)} %get-tuple-element.193), channel_id=1, source_target_pairs={{0,1},{1,2},{2,3},{3,0},{4,5},{5,6},{6,7},{7,4},{8,9},{9,10},{10,1... | collective-permute-start | bytes 3145736 | tf_op jit(solution)/shard_map/ppermute | solution.py:242
  440.7 16.0 %copy-start.19 = (f32[1024,512]{1,0:T(8,128)}, f32[1024,512]{1,0:T(8,128)S(1)}, u32[]{:S(2)}) copy-start(f32[1024,512]{1,0:T(8,128)S(1)} %get-tuple-element.186) | copy-start | bytes 6291460
  440.7 16.0 %copy-start.21 = (f32[1024,512]{1,0:T(8,128)}, f32[1024,512]{1,0:T(8,128)S(1)}, u32[]{:S(2)}) copy-start(f32[1024,512]{1,0:T(8,128)S(1)} %get-tuple-element.184) | copy-start | bytes 6291460
  440.7 38.4 %copy-start.22 = (f32[1024,512]{1,0:T(8,128)}, f32[1024,512]{1,0:T(8,128)S(1)}, u32[]{:S(2)}) copy-start(f32[1024,512]{1,0:T(8,128)S(1)} %get-tuple-element.162) | copy-start | bytes 6291460
  455.7 22.5 %collective-permute-start.16 = (bf16[256,2048]{1,0:T(8,128)(2,1)S(1)}, bf16[256,2048]{1,0:T(8,128)(2,1)S(1)}, u32[]{:S(2)}, u32[]{:S(2)}) collective-permute-start(bf16[256,2048]{1,0:T(8,128)(2,1)S(1)} %collective-permute-done.15), channel_id=1, source_target_pairs={{0,1},{1,2},{2,3},{3,0},{4,5},{5,6},{6,7},{7,4},{8,9},{9,10},{10,1... | collective-permute-start | bytes 3145736 | tf_op jit(solution)/shard_map/ppermute | solution.py:242
  478.2 19.4 %collective-permute-start.17 = (bf16[256,2048]{1,0:T(8,128)(2,1)S(1)}, bf16[256,2048]{1,0:T(8,128)(2,1)S(1)}, u32[]{:S(2)}, u32[]{:S(2)}) collective-permute-start(bf16[256,2048]{1,0:T(8,128)(2,1)S(1)} %collective-permute-done.16), channel_id=1, source_target_pairs={{0,1},{1,2},{2,3},{3,0},{4,5},{5,6},{6,7},{7,4},{8,9},{9,10},{10,1... | collective-permute-start | bytes 3145736 | tf_op jit(solution)/shard_map/ppermute | solution.py:242
  498.6 26.2 %collective-permute-start.18 = (bf16[1024,512]{1,0:T(8,128)(2,1)S(1)}, bf16[1024,512]{1,0:T(8,128)(2,1)}, u32[]{:S(2)}, u32[]{:S(2)}) collective-permute-start(bf16[1024,512]{1,0:T(8,128)(2,1)S(1)} %convert_element_type.242), channel_id=1, source_target_pairs={{0,1},{1,2},{2,3},{3,0},{4,5},{5,6},{6,7},{7,4},{8,9},{9,10},{10,1... | collective-permute-start | bytes 3145736 | tf_op jit(solution)/shard_map/ppermute | solution.py:242
  503.6 142.0 %reduce-scatter.11.cloned.1.call-start = ((), (), s32[]{:S(2)}) async-start(), calls=%async_computation.12 | async-start | bytes 7077888 | tf_op jit(solution)/shard_map/reduce_scatter | solution.py:507
  527.9 20.2 %collective-permute-start.19 = (bf16[1024,512]{1,0:T(8,128)(2,1)}, bf16[1024,512]{1,0:T(8,128)(2,1)S(1)}, u32[]{:S(2)}, u32[]{:S(2)}) collective-permute-start(bf16[1024,512]{1,0:T(8,128)(2,1)} %add_convert_fusion.4), channel_id=1, source_target_pairs={{0,1},{1,2},{2,3},{3,0},{4,5},{5,6},{6,7},{7,4},{8,9},{9,10},{10,1... | collective-permute-start | bytes 3145736 | tf_op jit(solution)/shard_map/ppermute | solution.py:242
  562.8 23.4 %collective-permute-start.20 = (bf16[1024,512]{1,0:T(8,128)(2,1)}, bf16[1024,512]{1,0:T(8,128)(2,1)S(1)}, u32[]{:S(2)}, u32[]{:S(2)}) collective-permute-start(bf16[1024,512]{1,0:T(8,128)(2,1)} %fusion.38), channel_id=1, source_target_pairs={{0,1},{1,2},{2,3},{3,0},{4,5},{5,6},{6,7},{7,4},{8,9},{9,10},{10,1... | collective-permute-start | bytes 3145736 | tf_op jit(solution)/shard_map/ppermute | solution.py:242
  568.0 19.8 %copy-start.71 = (s32[8]{0:T(128)S(1)}, s32[8]{0:T(128)}, u32[]{:S(2)}) copy-start(s32[8]{0:T(128)} %param.30) | copy-start | bytes 100
  568.0 22.3 %copy-start.3 = (bf16[1024,1536]{1,0:T(8,128)(2,1)S(1)}, bf16[1024,1536]{1,0:T(8,128)(2,1)}, u32[]{:S(2)}) copy-start(bf16[1024,1536]{1,0:T(8,128)(2,1)} %copy-done.2) | copy-start | bytes 9437188
  587.5 22.8 %collective-permute-start.21 = (bf16[1024,512]{1,0:T(8,128)(2,1)}, bf16[1024,512]{1,0:T(8,128)(2,1)}, u32[]{:S(2)}, u32[]{:S(2)}) collective-permute-start(bf16[1024,512]{1,0:T(8,128)(2,1)} %add_convert_fusion.3), channel_id=1, source_target_pairs={{0,1},{1,2},{2,3},{3,0},{4,5},{5,6},{6,7},{7,4},{8,9},{9,10},{10,1... | collective-permute-start | bytes 3145736 | tf_op jit(solution)/shard_map/ppermute | solution.py:242
  593.2 20.3 %collective-permute-start.23 = (f32[8,128]{1,0:T(8,128)S(1)}, f32[8,128]{1,0:T(8,128)S(1)}, u32[]{:S(2)}, u32[]{:S(2)}) collective-permute-start(f32[8,128]{1,0:T(8,128)S(1)} %bitcast.82), channel_id=1, source_target_pairs={{0,1},{1,0},{2,3},{3,2},{4,5},{5,4},{6,7},{7,6},{8,9},{9,8},{10,11... | collective-permute-start | bytes 12296 | tf_op jit(solution)/shard_map/ppermute | solution.py:274
  597.6 15.3 %copy-start.61 = (s32[2048]{0:T(1024)S(1)}, s32[2048]{0:T(1024)}, u32[]{:S(2)}) copy-start(s32[2048]{0:T(1024)} %copy-done.60) | copy-start | bytes 24580
  612.9 21.6 %collective-permute-start.22 = (bf16[1024,512]{1,0:T(8,128)(2,1)}, bf16[1024,512]{1,0:T(8,128)(2,1)}, u32[]{:S(2)}, u32[]{:S(2)}) collective-permute-start(bf16[1024,512]{1,0:T(8,128)(2,1)} %add_convert_fusion.2), channel_id=1, source_target_pairs={{0,1},{1,2},{2,3},{3,0},{4,5},{5,6},{6,7},{7,4},{8,9},{9,10},{10,1... | collective-permute-start | bytes 3145736 | tf_op jit(solution)/shard_map/ppermute | solution.py:242
  613.5 21.0 %copy-start.15 = (bf16[8,128,512]{2,1,0:T(8,128)(2,1)S(1)}, bf16[8,128,512]{2,1,0:T(8,128)(2,1)}, u32[]{:S(2)}) copy-start(bf16[8,128,512]{2,1,0:T(8,128)(2,1)} %copy-done.14) | copy-start | bytes 3145732
  613.5 21.0 %copy-start.54 = (f32[1024]{0:T(1024)S(1)}, f32[1024]{0:T(1024)}, u32[]{:S(2)}) copy-start(f32[1024]{0:T(1024)} %get-tuple-element.219) | copy-start | bytes 12292
  613.5 17.2 %collective-permute-start.24 = (f32[8,128]{1,0:T(8,128)S(1)}, f32[8,128]{1,0:T(8,128)S(1)}, u32[]{:S(2)}, u32[]{:S(2)}) collective-permute-start(f32[8,128]{1,0:T(8,128)S(1)} %bitcast_add_fusion), channel_id=1, source_target_pairs={{0,2},{1,3},{2,0},{3,1},{4,6},{5,7},{6,4},{7,5},{8,10},{9,11},{10,... | collective-permute-start | bytes 12296 | tf_op jit(solution)/shard_map/ppermute | solution.py:274
  637.7 20.2 %all-to-all-start.1 = ((bf16[8,128,512]{2,1,0:T(8,128)(2,1)}), bf16[8,128,512]{2,1,0:T(8,128)(2,1)S(1)}, u32[]{:S(2)}, u32[]{:S(2)}) async-start(bf16[8,128,512]{2,1,0:T(8,128)(2,1)} %bitcast.10), calls=%async_computation.5 | async-start | bytes 2097152 | tf_op jit(solution)/shard_map/all_to_all | solution.py:537
  644.7 27.5 %collective-permute-start.28 = (bf16[1024,512]{1,0:T(8,128)(2,1)}, bf16[1024,512]{1,0:T(8,128)(2,1)S(1)}, u32[]{:S(2)}, u32[]{:S(2)}) collective-permute-start(bf16[1024,512]{1,0:T(8,128)(2,1)} %add_convert_fusion.1), channel_id=1, source_target_pairs={{0,1},{1,2},{2,3},{3,0},{4,5},{5,6},{6,7},{7,4},{8,9},{9,10},{10,1... | collective-permute-start | bytes 3145736 | tf_op jit(solution)/shard_map/ppermute | solution.py:242
  648.4 1.3 collective-permute-start.25
  649.6 6.7 collective-permute-start.26
  656.4 3.9 collective-permute-start.27
  658.6 17.6 %copy-start.20 = (f32[1024,512]{1,0:T(8,128)S(1)}, f32[1024,512]{1,0:T(8,128)}, u32[]{:S(2)}) copy-start(f32[1024,512]{1,0:T(8,128)} %copy-done.19) | copy-start | bytes 6291460
  672.2 3.8 collective-permute-start.29
  676.1 10.8 %copy-start.34 = (bf16[1280,256]{1,0:T(8,128)(2,1)S(1)}, bf16[1280,256]{1,0:T(8,128)(2,1)}, u32[]{:S(2)}) copy-start(bf16[1280,256]{1,0:T(8,128)(2,1)} %reduce-scatter.7.cloned.1.call-done) | copy-start | bytes 1966084
  676.1 4.8 collective-permute-start.30
  (52 other events, 223.9 us)
Sparse Core Ops, SparseCore 0:
  14.8 54.7 all-gather.4
  72.1 51.3 all-gather.6
  125.9 63.2 all-gather.8
  383.6 81.1 reduce-scatter.4
  468.1 56.5 reduce-scatter.6
  528.1 41.2 reduce-scatter.8
  572.8 61.7 reduce-scatter.10

commit v3 on v2

--- a/solution.py
+++ b/solution.py
@@ -317,16 +317,23 @@
     def back(step):
         return lax.rem(member - step + tensor_count, tensor_count)
 
-    qkv_weight = jnp.concatenate([query_weight, key_weight, value_weight], axis=1).astype(low)
     picked = jnp.take(layer_input, deal_order, axis=0)
-    picked, qkv_weight = lax.optimization_barrier((picked, qkv_weight))
     dealt = lax.all_to_all(picked, "dp", split_axis=0, concat_axis=0, tiled=True)
     x_own = dealt.reshape(-1, dealt.shape[2])
     length = seq_lengths[deal_order[group_index]]
     seq_len, quarter = x_own.shape
     features = quarter * tensor_count
     part_rows = seq_len // tensor_count
+
+    small = jnp.concatenate([attn_gain, ffn_gain, bias_table.reshape(-1)]).astype(low)
+    x_own, grad_next, small = together(
+        x_own, around(output_grad[0]), lax.all_gather(small, "dp", axis=0)
+    )
+    grad_parts = [output_grad[0], grad_next]
     row_valid = lax.broadcasted_iota(jnp.int32, (seq_len, 1), 0) < length
+
+    def valid_rows(part):
+        return jnp.where(row_valid, part, jnp.zeros((), low))
 
     def row_part(array, step):
         return lax.dynamic_slice_in_dim(array, back(step) * part_rows, part_rows, 0)
@@ -337,38 +344,40 @@
     def set_rows(whole, part, step):
         return lax.dynamic_update_slice_in_dim(whole, part, back(step) * part_rows, 0)
 
-    def whole_columns(parts):
-        whole = jnp.zeros((seq_len, features), parts[0].dtype)
+    def set_columns(whole, part, step):
+        return lax.dynamic_update_slice_in_dim(whole, part, back(step) * quarter, 1)
+
+    def whole_columns(parts, start):
+        whole = jnp.broadcast_to(start[:1, :1], (seq_len, features))
         for step, part in enumerate(parts):
-            whole = lax.dynamic_update_slice_in_dim(whole, part, back(step) * quarter, 1)
+            whole = set_columns(whole, part, step)
         return whole
 
-    small = jnp.concatenate([attn_gain, ffn_gain, bias_table.reshape(-1)]).astype(low)
-    small = lax.all_gather(small, "dp", axis=0)
     gain_size = attn_gain.shape[0]
     first_gain = small[:, :gain_size].reshape(-1).astype(f32)
     second_gain = small[:, gain_size : 2 * gain_size].reshape(-1).astype(f32)
     full_table = small[:, 2 * gain_size :].reshape(NB, bias_table.shape[1])
+    qkv_weight = jnp.concatenate([query_weight, key_weight, value_weight], axis=1).astype(low)
+    qkv_weight, x_own = together(qkv_weight, x_own)
     qkv_weight = lax.all_gather(qkv_weight, "dp", axis=0, tiled=True)
     gate_up = jnp.concatenate([gate_weight, up_weight], axis=1).astype(low)
     out_down = jnp.concatenate([out_weight, down_weight], axis=0).astype(low)
     heads_columns = out_weight.shape[0]
     units = down_weight.shape[0]
-    out_down, x_own = together(out_down, x_own)
+    x_parts = ring_gather(x_own)
+    out_down, x_parts[1] = together(out_down, x_parts[1])
     out_down = lax.all_gather(out_down, "dp", axis=1, tiled=True)
+    gate_up, x_parts[2] = together(gate_up, x_parts[2])
+    gate_up = lax.all_gather(gate_up, "dp", axis=0, tiled=True)
 
     def down_columns(step):
         return lax.dynamic_slice(
             out_down, (heads_columns, back(step) * quarter), (units, quarter)
         )
 
-    x_parts = ring_gather(x_own)
-    gate_up, x_parts[1] = together(gate_up, x_parts[1])
-    gate_up = lax.all_gather(gate_up, "dp", axis=0, tiled=True)
-    grad_own = jnp.where(row_valid, output_grad[0], jnp.zeros((), low))
-    grad_own, x_parts[-1] = together(grad_own, x_parts[-1])
-    x_rows = whole_columns(x_parts)
-    grad_parts = [grad_own, around(grad_own)]
+    grad_parts[1], x_parts[-1] = together(grad_parts[1], x_parts[-1])
+    x_rows = whole_columns(x_parts, x_own)
+    grad_parts.append(around(grad_parts[1]))
 
     offsets = jnp.concatenate([bucket_index, jnp.full((1,), NB, jnp.int32)])
     bucket_hot = offsets[:, None] == lax.broadcasted_iota(jnp.int32, (2 * seq_len, NB), 1)
@@ -379,41 +388,51 @@
     h_first = (x_float * inv_first * first_gain).astype(low)
     qkv = dot(h_first, qkv_weight).astype(low)
     pairs = heads_columns // LANES
-    half = pairs // 2
-    so_far = attend_forward(qkv, rel_rows, length, 0, half)
-    rel_rows, grad_parts[1], *so_far = lax.optimization_barrier((rel_rows, grad_parts[1], *so_far))
-    grad_parts.append(around(grad_parts[1]))
-    attended, soft_low = attend_forward(qkv, rel_rows, length, half, pairs, so_far)
-    attended, grad_parts[2] = together(attended, grad_parts[2])
+    so_far = attend_forward(qkv, rel_rows, length, 0, 1)
+    rel_rows, grad_parts[2], *so_far = together(rel_rows, grad_parts[2], *so_far)
     grad_parts.append(around(grad_parts[2]))
-    attn_branch = ring_scatter(
-        lambda step: dot(row_part(attended, step), out_down[:heads_columns])
-    )
-    attn_branch, *grad_parts = together(attn_branch, *grad_parts)
-    grad_y = whole_columns(grad_parts)
+    attended, soft_low = attend_forward(qkv, rel_rows, length, 1, pairs, so_far)
+    attended, grad_parts[3] = together(attended, grad_parts[3])
+
+    def attended_part(step):
+        return dot(row_part(attended, step), out_down[:heads_columns])
+
+    running = around(attended_part(1).astype(low))
+    grad_y = whole_columns([valid_rows(part) for part in grad_parts[:-1]], attended)
+    received, term, grad_y = together(running, attended_part(2), grad_y)
+    running = around(add_low(received, term))
+    grad_y = set_columns(grad_y, valid_rows(grad_parts[-1]), tensor_count - 1)
+    received, term, last_term, grad_y = together(
+        running, attended_part(3), attended_part(0), grad_y
+    )
+    running = around(add_low(received, term))
+    attn_branch = running.astype(f32) + last_term
 
     after_attn = row_part(x_rows, 0).astype(f32) + attn_branch
     inv_second = lax.rsqrt(jnp.mean(after_attn * after_attn, axis=-1, keepdims=True) + EPS)
     h_second = (after_attn * inv_second * second_gain).astype(low)
 
     h_parts = [h_second]
-    hidden = jnp.zeros((seq_len, units), low)
+    hidden = jnp.broadcast_to(h_second[:1, :1], (seq_len, units))
     gate_up_grads = []
     terms = {}
 
+    def square_sum(piece):
+        return jnp.sum(jnp.square(piece.astype(f32)))
+
     def normed_part(step):
         return dot(gate_up_grads[step], gate_up, NT)
 
     for step in range(tensor_count):
         if step == 1:
-            h_parts[1], gate_up_grads[0] = together(h_parts[1], gate_up_grads[0])
+            h_parts[1], gate_up_grads[0], hidden = together(h_parts[1], gate_up_grads[0], hidden)
         elif step == 2:
-            h_parts[2], gate_up_grads[1], terms[0] = together(
-                h_parts[2], gate_up_grads[1], normed_part(0)
+            h_parts[2], gate_up_grads[1], hidden, terms[0] = together(
+                h_parts[2], gate_up_grads[1], hidden, normed_part(0)
             )
         elif step == 3:
-            h_parts[3], gate_up_grads[2], terms[1] = together(
-                h_parts[3], gate_up_grads[2], normed_part(1).astype(low)
+            h_parts[3], gate_up_grads[2], hidden, terms[1] = together(
+                h_parts[3], gate_up_grads[2], hidden, normed_part(1).astype(low)
             )
             running = around(terms[1])
         if step < tensor_count - 1:
@@ -428,12 +447,14 @@
         grad_hidden = dot(row_part(grad_y, step), out_down[heads_columns:], NT)
         gate_up_grads.append(jnp.concatenate(mix_back(grad_hidden), axis=1).astype(low))
 
-    received, terms[2], gate_up_grads[3] = together(running, normed_part(2), gate_up_grads[3])
+    received, terms[2], terms[3], gate_up_grads[3], hidden = together(
+        running, normed_part(2), normed_part(3), gate_up_grads[3], hidden
+    )
     running = around(add_low(received, terms[2]))
     h_rotated = jnp.concatenate(h_parts, axis=0)
     grads_rotated = jnp.concatenate(gate_up_grads, axis=0)
     grad_gate_up = dot(h_rotated, grads_rotated, TN).astype(low)
-    received, terms[3], grad_gate_up = together(running, normed_part(3), grad_gate_up)
+    received, grad_gate_up = together(running, grad_gate_up)
     owned_gate_up = lax.psum_scatter(grad_gate_up, "dp", scatter_dimension=0, tiled=True)
     running = around(add_low(received, terms[3]))
     grad_down = dot(hidden, grad_y, TN).astype(low)
@@ -466,7 +487,7 @@
         after_parts[2], output_terms[3], output_terms[0]
     )
     after_parts.append(around(after_parts[2]))
-    grad_after = jnp.zeros((seq_len, features), low)
+    grad_after = grad_y
     grad_heads = jnp.zeros((seq_len, heads_columns), low)
     for step in range(tensor_count):
         if step == tensor_count - 1:
@@ -479,23 +500,20 @@
     output_first = output_terms[1].astype(low)
     output_first, grad_after, grad_heads = together(output_first, grad_after, grad_heads)
     output_sum = around(output_first)
+
+    half = pairs // 2
+    first_grads, first_rel = attend_backward(soft_low, qkv, grad_heads, attended, 0, half)
+    output_sum, first_grads, owned_gate_up = together(output_sum, first_grads, owned_gate_up)
+    output_sum = around(add_low(output_sum, output_terms[2]))
     grad_out = dot(attended, grad_after, TN).astype(low)
-    grad_out, grad_heads = together(grad_out, grad_heads)
+    first_grads, grad_out = together(first_grads, grad_out)
     owned_out = lax.psum_scatter(grad_out, "dp", scatter_dimension=1, tiled=True)
-
-    def square_sum(piece):
-        return jnp.sum(jnp.square(piece.astype(f32)))
-
-    first_grads, first_rel = attend_backward(soft_low, qkv, grad_heads, attended, 0, half)
-    output_sum, first_grads, early_sq = together(
-        output_sum, first_grads, square_sum(owned_gate_up)
-    )
-    output_sum = around(add_low(output_sum, output_terms[2]))
     grad_qkv, second_rel = attend_backward(
         soft_low, qkv, grad_heads, attended, half, pairs, (first_grads,)
     )
     rel_grad = jnp.concatenate([first_rel, second_rel], axis=0)
-    grad_qkv, output_sum, down_sq = together(grad_qkv, output_sum, square_sum(owned_down))
+    grad_qkv, output_sum, owned_down = together(grad_qkv, output_sum, owned_down)
+    output_sent = add_low(output_sum, output_terms[3])
 
     def first_part(step):
         weight = lax.dynamic_slice_in_dim(qkv_weight, back(step) * quarter, quarter, 0)
@@ -504,12 +522,12 @@
     running, grad_qkv = together(first_part(1).astype(low), grad_qkv)
     running = around(running)
     grad_qkv_weight = dot(h_first, grad_qkv, TN).astype(low)
+    received, term, grad_qkv_weight = together(running, first_part(2), grad_qkv_weight)
     owned_qkv = lax.psum_scatter(grad_qkv_weight, "dp", scatter_dimension=0, tiled=True)
-    received, term, grad_qkv_weight = together(running, first_part(2), grad_qkv_weight)
     running = around(add_low(received, term))
     inner = jnp.sum(grad_qkv.astype(f32) * qkv.astype(f32), axis=-1)
     inner = total_over(inner.reshape(-1, LANES), "mp").reshape(-1, 1) / features
-    received, term = together(running, first_part(3))
+    received, term, owned_out = together(running, first_part(3), owned_out)
     running = around(add_low(received, term))
     grad_table = lax.dot_general(
         bucket_hot.astype(f32),
@@ -518,13 +536,11 @@
         precision=lax.Precision.HIGHEST,
         preferred_element_type=f32,
     )
-    early_sq = early_sq + down_sq + square_sum(owned_out)
-    received, term, grad_table, early_sq, inner = together(
-        running, first_part(0), grad_table, early_sq, inner
-    )
-    received, term, output_sum = together(received, term, output_sum)
-    for step in range(3, tensor_count):
-        output_sum = around(add_low(output_sum, output_terms[step]))
+    early_sq = square_sum(owned_gate_up) + square_sum(owned_down) + square_sum(owned_out)
+    received, term, grad_table, early_sq, inner, output_sent = together(
+        running, first_part(0), grad_table, early_sq, inner, output_sent
+    )
+    output_sum = around(output_sent)
     grad_h_first = received.astype(f32) + term
     own_gain = lax.dynamic_slice_in_dim(first_gain, member * quarter, quarter, 0)
     x_own = x_own.astype(f32)

time: 711 us -> 687 us (0.966)
  local copies, waits for them, and re-layouts: 41.3 us -> 26.2 us
  waiting for transfers between devices: 303 us -> 288 us
  blocking collectives: 8.24 us -> 18.3 us
    all_to_all x1, waiting for transfers between devices: 21.2 us -> 0.01 us  [shards(): lax.all_to_all(picked, 'dp', split_axis=0, concat_axis=0, tiled=True)]
    unnamed x155 -> x135, local copies, waits for them, and re-layouts: 20.6 us -> 8.4 us
    dynamic_update_slice x8 -> x4, local copies, waits for them, and re-layouts: 12.7 us -> 1.87 us  [set_columns(): return lax.dynamic_update_slice_in_dim(whole, part, back(step) * quarter, 1)]
    all_gather x1, blocking collectives: 8.24 us -> 18.3 us  [shards(): lax.all_gather(small, 'dp', axis=0)]
    ppermute x24, waiting for transfers between devices: 257 us -> 267 us  [around(): lax.ppermute(block, 'mp', [(i, (i + 1) % count) for i in range(count)])]
    dynamic_update_slice x0 -> x4, other arithmetic: none -> 9.07 us  [set_columns(): return lax.dynamic_update_slice_in_dim(whole, part, back(step) * quarter, 1)]
  transfers between devices with their start and end apart: 40 -> 40, of which waited for: 27 -> 28; matrix products, arithmetic and copies ran while one was open for 33% -> 36% of each run, Pallas kernels for 9% -> 9%
where the time goes in v3:
time: 687 us; the launch traced here: 677 us
  waiting for transfers between devices  288 us (42%)
  matrix products  166 us (24%)
  other arithmetic  68.7 us (10%)
  Pallas kernels  64.2 us (9%)
  local copies, waits for them, and re-layouts  26.2 us (4%)
  starting transfers between devices  23.1 us (3%)
  between operations  22.8 us (3%)
  blocking collectives  18.3 us (3%)
    ppermute x24, waiting for transfers between devices, around(): lax.ppermute(block, 'mp', [(i, (i + 1) % count) for i in range(count)])  267 us
    dot_general x34, matrix products, dot(): lax.dot_general(left, right, dims, preferred_element_type=jnp.float32)  165 us
    pallas_call x2, Pallas kernels, attend_backward(): pl.pallas_call(functools.partial(backward_kernel, first), grid=(last - fi...  34.7 us
    pallas_call x2, Pallas kernels, attend_forward(): pl.pallas_call(kernel, grid_spec=pltpu.PrefetchScalarGridSpec(num_scalar_...  29.5 us
    ppermute x7, waiting for transfers between devices, total_over(): lax.ppermute(value, axis, [(i, i ^ apart) for i in range(count)])  21 us
    all_gather x1, blocking collectives, shards(): lax.all_gather(small, 'dp', axis=0)  18.3 us
    convert_element_type x8, other arithmetic, add_low(): return (received.astype(jnp.float32) + term).astype(jnp.bfloat16)  15.8 us
  transfers between devices with their start and end apart: 40, of which 28 were waited for; matrix products, arithmetic and copies ran while one was open for 36% of the time, Pallas kernels for 9%

profile of v3, /device:TPU:0, one launch (start us, length us, event | category | flops | bytes accessed | tf_op | source)
XLA Modules:
  0.0 677.2 jit_solution(5416159378237507589)
XLA Ops:
  7.2 3.1 collective-permute-start
  13.4 3.7 all-to-all-start
  17.4 18.3 %all-gather = bf16[8,1,544]{2,1,0:T(2,128)(2,1)S(1)} all-gather(bf16[1,1,544]{2,1,0:T(2,128)(2,1)S(1)} %maximum_bitcast_fusion.1), channel_id=1, replica_groups=mesh['dp'=8,'mp'=4] {'dp'}, dimensions={0}, use_global_device_ids=true | all-gather | bytes 9792 | tf_op jit(solution)/shard_map/all_gather | solution.py:330
  41.8 23.5 %collective-permute-done.1 = bf16[1024,512]{1,0:T(8,128)(2,1)S(1)} collective-permute-done((bf16[1024,512]{1,0:T(8,128)(2,1)S(1)}, bf16[1024,512]{1,0:T(8,128)(2,1)S(1)}, u32[]{:S(2)}, u32[]{:S(2)}) %collective-permute-start.1) | collective-permute-done | bytes 1048608 | tf_op jit(solution)/shard_map/ppermute | solution.py:242
  68.2 23.6 %collective-permute-done.2 = bf16[1024,512]{1,0:T(8,128)(2,1)} collective-permute-done((bf16[1024,512]{1,0:T(8,128)(2,1)S(1)}, bf16[1024,512]{1,0:T(8,128)(2,1)}, u32[]{:S(2)}, u32[]{:S(2)}) %collective-permute-start.2) | collective-permute-done | bytes 1048608 | tf_op jit(solution)/shard_map/ppermute | solution.py:242
  100.7 17.0 %collective-permute-done.3 = bf16[1024,512]{1,0:T(8,128)(2,1)S(1)} collective-permute-done((bf16[1024,512]{1,0:T(8,128)(2,1)}, bf16[1024,512]{1,0:T(8,128)(2,1)S(1)}, u32[]{:S(2)}, u32[]{:S(2)}) %collective-permute-start.3) | collective-permute-done | bytes 1048608 | tf_op jit(solution)/shard_map/ppermute | solution.py:242
  121.3 10.7 %convolution_convert_fusion.3.query_ref.key_ref.value_ref = bf16[1024,1536]{1,0:T(8,128)(2,1)S(1)} fusion(bf16[2048,1536]{1,0:T(8,128)(2,1)} %all-gather.5.cloned.1.call-done, bf16[1024,2048]{1,0:T(8,128)(2,1)} %copy-done.7, f32[2048]{0:T(1024)S(1)} %bitcast.88, f32[1024]{0:T(1024)S(1)} %get-tuple-element.224), kind=kOutput, calls=%fused_computation.25 | convolution fusion | flops 6452412416 | bytes 13643776 | tf_op jit(solution)/shard_map/dot_general | solution.py:29
  132.0 8.2 %attend_forward.2 = (bf16[1024,512]{1,0:T(8,128)(2,1)}, bf16[8,1024,1024]{2,1,0:T(8,128)(2,1)}) custom-call(s32[1]{0:T(128)} %dynamic_slice.98.length, f32[4,2,2048]{2,1,0:T(2,128)S(1)} %reshape.188.rel_ref, bf16[1024,1536]{1,0:T(8,128)(2,1)S(1)} %convolution_convert_fusion.3.query_ref.key_ref.value_ref, ...), custom_call_target="tpu_custom_call" | custom-call | flops 2147483648 | bytes 4194304 | tf_op jit(solution)/shard_map/attend_forward/pallas_call | solution.py:91
  143.3 21.3 %attend_forward.3 = (bf16[1024,512]{1,0:T(8,128)(2,1)}, bf16[8,1024,1024]{2,1,0:T(8,128)(2,1)}) custom-call(s32[1]{0:T(128)} %dynamic_slice.98.length, f32[4,2,2048]{2,1,0:T(2,128)S(1)} %reshape.189.rel_ref, bf16[1024,1536]{1,0:T(8,128)(2,1)S(1)} %convolution_convert_fusion.3.query_ref.key_ref.value_ref, ...), custom_call_target="tpu_custom_call", output_to_operand_aliasing={{0}: (5, {}), {1}: (6, {})} | custom-call | flops 6442450944 | bytes 12582912 | tf_op jit(solution)/shard_map/attend_forward/pallas_call | solution.py:91
  170.4 3.3 broadcast_in_dim.80
  175.0 2.5 select_dynamic-update-slice_fusion.2
  177.6 2.6 select_dynamic-update-slice_fusion.1
  182.6 10.8 %collective-permute-done.6 = bf16[256,2048]{1,0:T(8,128)(2,1)S(1)} collective-permute-done((bf16[256,2048]{1,0:T(8,128)(2,1)S(1)}, bf16[256,2048]{1,0:T(8,128)(2,1)S(1)}, u32[]{:S(2)}, u32[]{:S(2)}) %collective-permute-start.6) | collective-permute-done | bytes 1048608 | tf_op jit(solution)/shard_map/ppermute | solution.py:242
  198.6 2.6 select_dynamic-update-slice_fusion
  201.2 15.4 %collective-permute-done.7 = bf16[256,2048]{1,0:T(8,128)(2,1)S(1)} collective-permute-done((bf16[256,2048]{1,0:T(8,128)(2,1)S(1)}, bf16[256,2048]{1,0:T(8,128)(2,1)S(1)}, u32[]{:S(2)}, u32[]{:S(2)}) %collective-permute-start.7) | collective-permute-done | bytes 1048608 | tf_op jit(solution)/shard_map/ppermute | solution.py:242
  217.1 21.0 %collective-permute-done.8 = bf16[256,2048]{1,0:T(8,128)(2,1)S(1)} collective-permute-done((bf16[256,2048]{1,0:T(8,128)(2,1)S(1)}, bf16[256,2048]{1,0:T(8,128)(2,1)S(1)}, u32[]{:S(2)}, u32[]{:S(2)}) %collective-permute-start.8) | collective-permute-done | bytes 1048608 | tf_op jit(solution)/shard_map/ppermute | solution.py:242
  240.6 5.6 fusion.140
  246.2 5.2 fusion.49
  252.9 10.4 %collective-permute-done.9 = bf16[256,2048]{1,0:T(8,128)(2,1)} collective-permute-done((bf16[256,2048]{1,0:T(8,128)(2,1)S(1)}, bf16[256,2048]{1,0:T(8,128)(2,1)}, u32[]{:S(2)}, u32[]{:S(2)}) %collective-permute-start.9) | collective-permute-done | bytes 1048608 | tf_op jit(solution)/shard_map/ppermute | solution.py:242
  263.7 5.9 fusion.141
  270.2 4.0 fusion.56
  274.3 8.3 %fusion.142 = f32[256,2048]{1,0:T(8,128)} fusion(bf16[256,2560]{1,0:T(8,128)(2,1)S(1)} %pad_maximum_fusion.1, bf16[2048,2560]{1,0:T(8,128)(2,1)} %all-gather.9.cloned.1.call-done), kind=kOutput, calls=%fused_computation.255 | convolution fusion | flops 2684354560 | bytes 13893632 | tf_op jit(solution)/shard_map/dot_general | solution.py:29
  282.6 4.5 collective-permute-done.10
  287.1 5.9 fusion.143
  293.5 4.0 fusion.63
  297.6 8.3 %convolution_convert_fusion.5 = bf16[256,2048]{1,0:T(8,128)(2,1)} fusion(bf16[256,2560]{1,0:T(8,128)(2,1)S(1)} %pad_maximum_fusion.2, bf16[2048,2560]{1,0:T(8,128)(2,1)} %all-gather.9.cloned.1.call-done), kind=kOutput, calls=%fused_computation.38 | convolution fusion | flops 2684878848 | bytes 12845056 | tf_op jit(solution)/shard_map/dot_general | solution.py:29
  305.9 4.3 collective-permute-done.11
  310.4 5.9 fusion.145
  316.8 5.6 fusion.70
  322.4 8.5 %fusion.139 = f32[256,2048]{1,0:T(8,128)} fusion(bf16[2048,2560]{1,0:T(8,128)(2,1)} %all-gather.9.cloned.1.call-done, bf16[256,1280]{1,0:T(8,128)(2,1)} %get-tuple-element.203, bf16[256,1280]{1,0:T(8,128)(2,1)S(1)} %get-tuple-element.202), kind=kOutput, calls=%fused_computation.252 | convolution fusion | flops 2686976000 | bytes 13893632 | tf_op jit(solution)/shard_map/dot_general | solution.py:29
  332.0 5.6 fusion.144
  339.5 16.5 %convolution_convert_fusion = bf16[2048,2560]{1,0:T(8,128)(2,1)} fusion(bf16[256,2560]{1,0:T(8,128)(2,1)} %pad_maximum_fusion.4, bf16[256,2560]{1,0:T(8,128)(2,1)} %copy-done.26, bf16[256,2560]{1,0:T(8,128)(2,1)S(1)} %pad_maximum_fusion.2, bf16[256,2560]{1,0:T(8,128)(2,1)S(1)} %pad_maximum_fusion.1, bf16[256,2048]{1,0:T(8,128)(2,1)} %collective-permute-done.11, ...), kind=kOutput, calls=%fused_computation.2 | convolution fusion | flops 10780409856 | bytes 19922944 | tf_op jit(solution)/shard_map/dot_general | solution.py:29
  356.0 5.6 collective-permute-done.13
  361.7 3.3 add_convert_fusion.5
  365.0 10.4 %convolution_convert_fusion.2 = bf16[1280,2048]{1,0:T(8,128)(2,1)} fusion(bf16[1024,1280]{1,0:T(8,128)(2,1)S(1)} %copy-done.21, bf16[1024,2048]{1,0:T(8,128)(2,1)} %select_dynamic-update-slice_fusion), kind=kOutput, calls=%fused_computation.9 | convolution fusion | flops 5371330560 | bytes 12058624 | tf_op jit(solution)/shard_map/dot_general | solution.py:29
  375.4 11.1 %collective-permute-done.14 = bf16[256,2048]{1,0:T(8,128)(2,1)S(1)} collective-permute-done((bf16[256,2048]{1,0:T(8,128)(2,1)}, bf16[256,2048]{1,0:T(8,128)(2,1)S(1)}, u32[]{:S(2)}, u32[]{:S(2)}) %collective-permute-start.14) | collective-permute-done | bytes 1048608 | tf_op jit(solution)/shard_map/ppermute | solution.py:242
  386.5 2.8 multiply_reduce_fusion.2
  391.9 3.0 fusion.71
  400.2 19.5 %collective-permute-done.15 = bf16[256,2048]{1,0:T(8,128)(2,1)S(1)} collective-permute-done((bf16[256,2048]{1,0:T(8,128)(2,1)S(1)}, bf16[256,2048]{1,0:T(8,128)(2,1)S(1)}, u32[]{:S(2)}, u32[]{:S(2)}) %collective-permute-start.15) | collective-permute-done | bytes 1048608 | tf_op jit(solution)/shard_map/ppermute | solution.py:242
  421.8 24.9 %collective-permute-done.16 = bf16[256,2048]{1,0:T(8,128)(2,1)S(1)} collective-permute-done((bf16[256,2048]{1,0:T(8,128)(2,1)S(1)}, bf16[256,2048]{1,0:T(8,128)(2,1)S(1)}, u32[]{:S(2)}, u32[]{:S(2)}) %collective-permute-start.16) | collective-permute-done | bytes 1048608 | tf_op jit(solution)/shard_map/ppermute | solution.py:242
  450.4 23.9 %collective-permute-done.17 = bf16[256,2048]{1,0:T(8,128)(2,1)S(1)} collective-permute-done((bf16[256,2048]{1,0:T(8,128)(2,1)S(1)}, bf16[256,2048]{1,0:T(8,128)(2,1)S(1)}, u32[]{:S(2)}, u32[]{:S(2)}) %collective-permute-start.17) | collective-permute-done | bytes 1048608 | tf_op jit(solution)/shard_map/ppermute | solution.py:242
  476.2 16.8 %attend_backward.2 = (bf16[1024,1536]{1,0:T(8,128)(2,1)S(1)}, f32[2,2,2048]{2,1,0:T(2,128)S(1)}) custom-call(bf16[8,1024,1024]{2,1,0:T(8,128)(2,1)} %get-tuple-element.119.soft_ref, bf16[1024,1536]{1,0:T(8,128)(2,1)} %copy-done.2, bf16[1024,512]{1,0:T(8,128)(2,1)S(1)} %fusion.84.grad_ref, bf16[1024,512]{1,0:T(8,128)(2,1)} %get-tuple-element.122.out_ref, ...), custom_call_target="tpu_custom_call" | custom-call | flops 10737418240 | bytes 8388608 | tf_op jit(solution)/shard_map/attend_backward/pallas_call | solution.py:207
  494.8 8.4 %collective-permute-done.18 = bf16[1024,512]{1,0:T(8,128)(2,1)S(1)} collective-permute-done((bf16[1024,512]{1,0:T(8,128)(2,1)S(1)}, bf16[1024,512]{1,0:T(8,128)(2,1)S(1)}, u32[]{:S(2)}, u32[]{:S(2)}) %collective-permute-start.18) | collective-permute-done | bytes 1048608 | tf_op jit(solution)/shard_map/ppermute | solution.py:242
  505.0 6.2 convolution_convert_fusion.4
  512.5 17.9 %attend_backward.3 = (bf16[1024,1536]{1,0:T(8,128)(2,1)S(1)}, f32[2,2,2048]{2,1,0:T(2,128)S(1)}) custom-call(bf16[8,1024,1024]{2,1,0:T(8,128)(2,1)} %get-tuple-element.119.soft_ref, bf16[1024,1536]{1,0:T(8,128)(2,1)} %copy-done.2, bf16[1024,512]{1,0:T(8,128)(2,1)S(1)} %copy-done.5, bf16[1024,512]{1,0:T(8,128)(2,1)} %get-tuple-element.122.out_ref, ...), custom_call_target="tpu_custom_call" | custom-call | flops 10737418240 | bytes 8388608 | tf_op jit(solution)/shard_map/attend_backward/pallas_call | solution.py:207
  532.0 4.4 fusion.38
  536.6 9.1 %convolution_convert_fusion.1 = bf16[2048,1536]{1,0:T(8,128)(2,1)} fusion(bf16[1024,1536]{1,0:T(8,128)(2,1)S(1)} %get-tuple-element.172, bf16[1024,2048]{1,0:T(8,128)(2,1)S(1)} %copy-done.8, f32[2048]{0:T(1024)S(1)} %bitcast.89, f32[1024]{0:T(1024)S(1)} %copy-done.47), kind=kOutput, calls=%fused_computation.8 | convolution fusion | flops 6453985280 | bytes 13643776 | tf_op jit(solution)/shard_map/dot_general | solution.py:29
  545.7 4.7 fusion.34
  550.4 11.4 %collective-permute-done.20 = bf16[1024,512]{1,0:T(8,128)(2,1)} collective-permute-done((bf16[1024,512]{1,0:T(8,128)(2,1)}, bf16[1024,512]{1,0:T(8,128)(2,1)}, u32[]{:S(2)}, u32[]{:S(2)}) %collective-permute-start.20) | collective-permute-done | bytes 1048608 | tf_op jit(solution)/shard_map/ppermute | solution.py:242
  562.6 2.6 multiply_reduce_fusion.1
  565.8 3.4 add_convert_fusion.3
  571.9 4.8 fusion.32
  576.7 4.6 fusion.30
  581.3 13.7 %collective-permute-done.21 = bf16[1024,512]{1,0:T(8,128)(2,1)} collective-permute-done((bf16[1024,512]{1,0:T(8,128)(2,1)}, bf16[1024,512]{1,0:T(8,128)(2,1)}, u32[]{:S(2)}, u32[]{:S(2)}) %collective-permute-start.21) | collective-permute-done | bytes 1048608 | tf_op jit(solution)/shard_map/ppermute | solution.py:242
  595.0 3.2 add_convert_fusion.2
  598.3 2.7 add_convert_fusion.1
  603.2 7.7 %collective-permute-done.24 = f32[8,128]{1,0:T(8,128)S(1)} collective-permute-done((f32[8,128]{1,0:T(8,128)S(1)}, f32[8,128]{1,0:T(8,128)S(1)}, u32[]{:S(2)}, u32[]{:S(2)}) %collective-permute-start.24) | collective-permute-done | bytes 4128 | tf_op jit(solution)/shard_map/ppermute | solution.py:274
  612.3 2.9 collective-permute-done.22
  615.2 3.6 fusion.29
  618.8 3.7 all-to-all-start.1
  631.3 6.1 collective-permute-done.26
  641.4 9.1 %collective-permute-done.28 = bf16[1024,512]{1,0:T(8,128)(2,1)} collective-permute-done((bf16[1024,512]{1,0:T(8,128)(2,1)S(1)}, bf16[1024,512]{1,0:T(8,128)(2,1)}, u32[]{:S(2)}, u32[]{:S(2)}) %collective-permute-start.28) | collective-permute-done | bytes 1048608 | tf_op jit(solution)/shard_map/ppermute | solution.py:242
  651.9 2.5 collective-permute-done.29
  654.5 2.7 fusion.85
  (317 shorter events, 101.3 us)
Async XLA Ops:
  7.2 30.7 %collective-permute-start = (bf16[1024,512]{1,0:T(8,128)(2,1)}, bf16[1024,512]{1,0:T(8,128)(2,1)}, u32[]{:S(2)}, u32[]{:S(2)}) collective-permute-start(bf16[1024,512]{1,0:T(8,128)(2,1)} %bitcast.78), channel_id=1, source_target_pairs={{0,1},{1,2},{2,3},{3,0},{4,5},{5,6},{6,7},{7,4},{8,9},{9,10},{10,1... | collective-permute-start | bytes 3145736 | tf_op jit(solution)/shard_map/ppermute | solution.py:242
  12.3 23.4 %copy-start.43 = (f32[256,512]{1,0:T(8,128)S(1)}, f32[256,512]{1,0:T(8,128)}, u32[]{:S(2)}) copy-start(f32[256,512]{1,0:T(8,128)} %param.32) | copy-start | bytes 1572868
  12.3 23.5 %copy-start.44 = (f32[256,512]{1,0:T(8,128)S(1)}, f32[256,512]{1,0:T(8,128)}, u32[]{:S(2)}) copy-start(f32[256,512]{1,0:T(8,128)} %param.33) | copy-start | bytes 1572868
  13.4 24.5 %all-to-all-start = ((bf16[8,128,512]{2,1,0:T(8,128)(2,1)}), bf16[8,128,512]{2,1,0:T(8,128)(2,1)S(1)}, u32[]{:S(2)}, u32[]{:S(2)}) async-start(bf16[8,128,512]{2,1,0:T(8,128)(2,1)} %broadcast_select_fusion.1), calls=%async_computation | async-start | bytes 2097152 | tf_op jit(solution)/shard_map/all_to_all | solution.py:321
  17.1 104.2 %all-gather.5.cloned.1.call-start = ((), (), s32[]{:S(2)}) async-start(), calls=%async_computation.6 | async-start | bytes 7077888 | tf_op jit(solution)/shard_map/all_gather | solution.py:362
  37.9 59.9 %copy-start.9 = (bf16[8,128,512]{2,1,0:T(8,128)(2,1)}, bf16[8,128,512]{2,1,0:T(8,128)(2,1)S(1)}, u32[]{:S(2)}) copy-start(bf16[8,128,512]{2,1,0:T(8,128)(2,1)S(1)} %all-to-all-done) | copy-start | bytes 3145732
  38.0 129.8 %all-gather.7.cloned.1.call-start = ((), (), s32[]{:S(2)}) async-start(), calls=%async_computation.7 | async-start | bytes 8257536 | tf_op jit(solution)/shard_map/all_gather | solution.py:369
  38.0 27.2 %collective-permute-start.1 = (bf16[1024,512]{1,0:T(8,128)(2,1)S(1)}, bf16[1024,512]{1,0:T(8,128)(2,1)S(1)}, u32[]{:S(2)}, u32[]{:S(2)}) collective-permute-start(bf16[1024,512]{1,0:T(8,128)(2,1)S(1)} %bitcast.70), channel_id=1, source_target_pairs={{0,1},{1,2},{2,3},{3,0},{4,5},{5,6},{6,7},{7,4},{8,9},{9,10},{10,1... | collective-permute-start | bytes 3145736 | tf_op jit(solution)/shard_map/ppermute | solution.py:242
  40.8 24.6 %copy-start.28 = (f32[256,1280]{1,0:T(8,128)S(1)}, f32[256,1280]{1,0:T(8,128)}, u32[]{:S(2)}) copy-start(f32[256,1280]{1,0:T(8,128)} %param.36) | copy-start | bytes 3932164
  65.3 175.3 %all-gather.9.cloned.1.call-start = ((), (), s32[]{:S(2)}) async-start(), calls=%async_computation.8 | async-start | bytes 11796480 | tf_op jit(solution)/shard_map/all_gather | solution.py:371
  65.3 26.5 %collective-permute-start.2 = (bf16[1024,512]{1,0:T(8,128)(2,1)S(1)}, bf16[1024,512]{1,0:T(8,128)(2,1)}, u32[]{:S(2)}, u32[]{:S(2)}) collective-permute-start(bf16[1024,512]{1,0:T(8,128)(2,1)S(1)} %collective-permute-done.1), channel_id=1, source_target_pairs={{0,1},{1,2},{2,3},{3,0},{4,5},{5,6},{6,7},{7,4},{8,9},{9,10},{10,1... | collective-permute-start | bytes 3145736 | tf_op jit(solution)/shard_map/ppermute | solution.py:242
  67.1 25.0 %copy-start.60 = (s32[8]{0:T(128)S(1)}, s32[8]{0:T(128)}, u32[]{:S(2)}) copy-start(s32[8]{0:T(128)} %param.30) | copy-start | bytes 100
  67.1 27.6 %copy-start.59 = (s32[8]{0:T(128)S(1)}, s32[8]{0:T(128)}, u32[]{:S(2)}) copy-start(s32[8]{0:T(128)} %param.29) | copy-start | bytes 100
  67.1 28.1 %copy-start.50 = (s32[2047]{0:T(1024)S(1)}, s32[2047]{0:T(1024)}, u32[]{:S(2)}) copy-start(s32[2047]{0:T(1024)} %param.31) | copy-start | bytes 24568
  91.9 411.3 %reduce-scatter.5.cloned.1.call-start = ((), (), s32[]{:S(2)}) async-start(), calls=%async_computation.9 | async-start | bytes 11796480 | tf_op jit(solution)/shard_map/reduce_scatter | solution.py:458
  92.0 25.7 %collective-permute-start.3 = (bf16[1024,512]{1,0:T(8,128)(2,1)}, bf16[1024,512]{1,0:T(8,128)(2,1)S(1)}, u32[]{:S(2)}, u32[]{:S(2)}) collective-permute-start(bf16[1024,512]{1,0:T(8,128)(2,1)} %collective-permute-done.2), channel_id=1, source_target_pairs={{0,1},{1,2},{2,3},{3,0},{4,5},{5,6},{6,7},{7,4},{8,9},{9,10},{10,1... | collective-permute-start | bytes 3145736 | tf_op jit(solution)/shard_map/ppermute | solution.py:242
  95.9 25.4 %copy-start.48 = (f32[1,2,8,128]{3,1,2,0:T(2,128)}, f32[1,2,8,128]{3,1,2,0:T(2,128)S(1)}, u32[]{:S(2)}) copy-start(f32[1,2,8,128]{3,1,2,0:T(2,128)S(1)} %copy.44) | copy-start | bytes 24580
  117.7 24.9 %collective-permute-start.4 = (bf16[1024,512]{1,0:T(8,128)(2,1)}, bf16[1024,512]{1,0:T(8,128)(2,1)}, u32[]{:S(2)}, u32[]{:S(2)}) collective-permute-start(bf16[1024,512]{1,0:T(8,128)(2,1)} %collective-permute-done), channel_id=1, source_target_pairs={{0,1},{1,2},{2,3},{3,0},{4,5},{5,6},{6,7},{7,4},{8,9},{9,10},{10,1... | collective-permute-start | bytes 3145736 | tf_op jit(solution)/shard_map/ppermute | solution.py:242
  132.0 11.2 %copy-start.2 = (bf16[1024,1536]{1,0:T(8,128)(2,1)}, bf16[1024,1536]{1,0:T(8,128)(2,1)S(1)}, u32[]{:S(2)}) copy-start(bf16[1024,1536]{1,0:T(8,128)(2,1)S(1)} %convolution_convert_fusion.3.query_ref.key_ref.value_ref) | copy-start | bytes 9437188
  142.6 23.9 %collective-permute-start.5 = (bf16[1024,512]{1,0:T(8,128)(2,1)}, bf16[1024,512]{1,0:T(8,128)(2,1)}, u32[]{:S(2)}, u32[]{:S(2)}) collective-permute-start(bf16[1024,512]{1,0:T(8,128)(2,1)} %collective-permute-done.4), channel_id=1, source_target_pairs={{0,1},{1,2},{2,3},{3,0},{4,5},{5,6},{6,7},{7,4},{8,9},{9,10},{10,1... | collective-permute-start | bytes 3145736 | tf_op jit(solution)/shard_map/ppermute | solution.py:242
  170.1 23.2 %collective-permute-start.6 = (bf16[256,2048]{1,0:T(8,128)(2,1)S(1)}, bf16[256,2048]{1,0:T(8,128)(2,1)S(1)}, u32[]{:S(2)}, u32[]{:S(2)}) collective-permute-start(bf16[256,2048]{1,0:T(8,128)(2,1)S(1)} %convolution_convert_fusion.6), channel_id=1, source_target_pairs={{0,1},{1,2},{2,3},{3,0},{4,5},{5,6},{6,7},{7,4},{8,9},{9,10},{10,1... | collective-permute-start | bytes 3145736 | tf_op jit(solution)/shard_map/ppermute | solution.py:242
  193.7 23.0 %collective-permute-start.7 = (bf16[256,2048]{1,0:T(8,128)(2,1)S(1)}, bf16[256,2048]{1,0:T(8,128)(2,1)S(1)}, u32[]{:S(2)}, u32[]{:S(2)}) collective-permute-start(bf16[256,2048]{1,0:T(8,128)(2,1)S(1)} %add_convert_fusion.8), channel_id=1, source_target_pairs={{0,1},{1,2},{2,3},{3,0},{4,5},{5,6},{6,7},{7,4},{8,9},{9,10},{10,1... | collective-permute-start | bytes 3145736 | tf_op jit(solution)/shard_map/ppermute | solution.py:242
  217.0 21.1 %collective-permute-start.8 = (bf16[256,2048]{1,0:T(8,128)(2,1)S(1)}, bf16[256,2048]{1,0:T(8,128)(2,1)S(1)}, u32[]{:S(2)}, u32[]{:S(2)}) collective-permute-start(bf16[256,2048]{1,0:T(8,128)(2,1)S(1)} %add_convert_fusion.7), channel_id=1, source_target_pairs={{0,1},{1,2},{2,3},{3,0},{4,5},{5,6},{6,7},{7,4},{8,9},{9,10},{10,1... | collective-permute-start | bytes 3145736 | tf_op jit(solution)/shard_map/ppermute | solution.py:242
  240.6 22.7 %collective-permute-start.9 = (bf16[256,2048]{1,0:T(8,128)(2,1)S(1)}, bf16[256,2048]{1,0:T(8,128)(2,1)}, u32[]{:S(2)}, u32[]{:S(2)}) collective-permute-start(bf16[256,2048]{1,0:T(8,128)(2,1)S(1)} %multiply_convert_fusion), channel_id=1, source_target_pairs={{0,1},{1,2},{2,3},{3,0},{4,5},{5,6},{6,7},{7,4},{8,9},{9,10},{10,1... | collective-permute-start | bytes 3145736 | tf_op jit(solution)/shard_map/ppermute | solution.py:242
  252.4 17.7 %slice-start = ((s8[7340032]{0:T(1024)(128)(4,1)}), s8[4194304]{0:T(1024)(128)(4,1)S(1)}, s32[]{:S(2)}) async-start(s8[7340032]{0:T(1024)(128)(4,1)} %bitcast.74), calls=%async_computation.13 | async-start | bytes 8388608
  252.9 17.3 %slice-start.1 = ((s8[7340032]{0:T(1024)(128)(4,1)}), s8[3145728]{0:T(1024)(128)(4,1)S(1)}, s32[]{:S(2)}) async-start(s8[7340032]{0:T(1024)(128)(4,1)} %bitcast.74), calls=%async_computation.14 | async-start | bytes 6291456
  263.3 23.7 %collective-permute-start.10 = (bf16[256,2048]{1,0:T(8,128)(2,1)}, bf16[256,2048]{1,0:T(8,128)(2,1)}, u32[]{:S(2)}, u32[]{:S(2)}) collective-permute-start(bf16[256,2048]{1,0:T(8,128)(2,1)} %collective-permute-done.9), channel_id=1, source_target_pairs={{0,1},{1,2},{2,3},{3,0},{4,5},{5,6},{6,7},{7,4},{8,9},{9,10},{10,1... | collective-permute-start | bytes 3145736 | tf_op jit(solution)/shard_map/ppermute | solution.py:242
  287.1 23.2 %collective-permute-start.11 = (bf16[256,2048]{1,0:T(8,128)(2,1)}, bf16[256,2048]{1,0:T(8,128)(2,1)}, u32[]{:S(2)}, u32[]{:S(2)}) collective-permute-start(bf16[256,2048]{1,0:T(8,128)(2,1)} %collective-permute-done.10), channel_id=1, source_target_pairs={{0,1},{1,2},{2,3},{3,0},{4,5},{5,6},{6,7},{7,4},{8,9},{9,10},{10,1... | collective-permute-start | bytes 3145736 | tf_op jit(solution)/shard_map/ppermute | solution.py:242
  297.6 34.4 %copy-start.26 = (bf16[256,2560]{1,0:T(8,128)(2,1)}, bf16[256,2560]{1,0:T(8,128)(2,1)S(1)}, u32[]{:S(2)}) copy-start(bf16[256,2560]{1,0:T(8,128)(2,1)S(1)} %pad_maximum_fusion.3) | copy-start | bytes 3932164
  310.2 27.4 %collective-permute-start.12 = (bf16[256,2048]{1,0:T(8,128)(2,1)}, bf16[256,2048]{1,0:T(8,128)(2,1)S(1)}, u32[]{:S(2)}, u32[]{:S(2)}) collective-permute-start(bf16[256,2048]{1,0:T(8,128)(2,1)} %convolution_convert_fusion.5), channel_id=1, source_target_pairs={{0,1},{1,2},{2,3},{3,0},{4,5},{5,6},{6,7},{7,4},{8,9},{9,10},{10,1... | collective-permute-start | bytes 3145736 | tf_op jit(solution)/shard_map/ppermute | solution.py:242
  338.9 22.7 %collective-permute-start.13 = (bf16[256,2048]{1,0:T(8,128)(2,1)}, bf16[256,2048]{1,0:T(8,128)(2,1)}, u32[]{:S(2)}, u32[]{:S(2)}) collective-permute-start(bf16[256,2048]{1,0:T(8,128)(2,1)} %add_convert_fusion.6), channel_id=1, source_target_pairs={{0,1},{1,2},{2,3},{3,0},{4,5},{5,6},{6,7},{7,4},{8,9},{9,10},{10,1... | collective-permute-start | bytes 3145736 | tf_op jit(solution)/shard_map/ppermute | solution.py:242
  361.7 168.8 %reduce-scatter.7.cloned.1.call-start = ((), (), s32[]{:S(2)}) async-start(), calls=%async_computation.10 | async-start | bytes 5898240 | tf_op jit(solution)/shard_map/reduce_scatter | solution.py:462
  365.0 21.5 %collective-permute-start.14 = (bf16[256,2048]{1,0:T(8,128)(2,1)}, bf16[256,2048]{1,0:T(8,128)(2,1)S(1)}, u32[]{:S(2)}, u32[]{:S(2)}) collective-permute-start(bf16[256,2048]{1,0:T(8,128)(2,1)} %add_convert_fusion.5), channel_id=1, source_target_pairs={{0,1},{1,2},{2,3},{3,0},{4,5},{5,6},{6,7},{7,4},{8,9},{9,10},{10,1... | collective-permute-start | bytes 3145736 | tf_op jit(solution)/shard_map/ppermute | solution.py:242
  386.5 194.8 %reduce-scatter.9.cloned.1.call-start = ((), (), s32[]{:S(2)}) async-start(), calls=%async_computation.11 | async-start | bytes 2359296 | tf_op jit(solution)/shard_map/reduce_scatter | solution.py:510
  391.6 28.1 %collective-permute-start.15 = (bf16[256,2048]{1,0:T(8,128)(2,1)S(1)}, bf16[256,2048]{1,0:T(8,128)(2,1)S(1)}, u32[]{:S(2)}, u32[]{:S(2)}) collective-permute-start(bf16[256,2048]{1,0:T(8,128)(2,1)S(1)} %subtract_convert_fusion), channel_id=1, source_target_pairs={{0,1},{1,2},{2,3},{3,0},{4,5},{5,6},{6,7},{7,4},{8,9},{9,10},{10,1... | collective-permute-start | bytes 3145736 | tf_op jit(solution)/shard_map/ppermute | solution.py:242
  400.1 21.5 %copy-start.13 = (f32[1024,512]{1,0:T(8,128)}, f32[1024,512]{1,0:T(8,128)S(1)}, u32[]{:S(2)}) copy-start(f32[1024,512]{1,0:T(8,128)S(1)} %get-tuple-element.192) | copy-start | bytes 6291460
  400.1 21.5 %copy-start.15 = (f32[1024,512]{1,0:T(8,128)}, f32[1024,512]{1,0:T(8,128)S(1)}, u32[]{:S(2)}) copy-start(f32[1024,512]{1,0:T(8,128)S(1)} %get-tuple-element.184) | copy-start | bytes 6291460
  400.2 21.5 %copy-start.17 = (f32[1024,512]{1,0:T(8,128)}, f32[1024,512]{1,0:T(8,128)S(1)}, u32[]{:S(2)}) copy-start(f32[1024,512]{1,0:T(8,128)S(1)} %get-tuple-element.168) | copy-start | bytes 6291460
  419.7 27.0 %collective-permute-start.16 = (bf16[256,2048]{1,0:T(8,128)(2,1)S(1)}, bf16[256,2048]{1,0:T(8,128)(2,1)S(1)}, u32[]{:S(2)}, u32[]{:S(2)}) collective-permute-start(bf16[256,2048]{1,0:T(8,128)(2,1)S(1)} %collective-permute-done.15), channel_id=1, source_target_pairs={{0,1},{1,2},{2,3},{3,0},{4,5},{5,6},{6,7},{7,4},{8,9},{9,10},{10,1... | collective-permute-start | bytes 3145736 | tf_op jit(solution)/shard_map/ppermute | solution.py:242
  446.7 27.6 %collective-permute-start.17 = (bf16[256,2048]{1,0:T(8,128)(2,1)S(1)}, bf16[256,2048]{1,0:T(8,128)(2,1)S(1)}, u32[]{:S(2)}, u32[]{:S(2)}) collective-permute-start(bf16[256,2048]{1,0:T(8,128)(2,1)S(1)} %collective-permute-done.16), channel_id=1, source_target_pairs={{0,1},{1,2},{2,3},{3,0},{4,5},{5,6},{6,7},{7,4},{8,9},{9,10},{10,1... | collective-permute-start | bytes 3145736 | tf_op jit(solution)/shard_map/ppermute | solution.py:242
  476.1 16.9 %copy-start.4 = (bf16[1024,512]{1,0:T(8,128)(2,1)}, bf16[1024,512]{1,0:T(8,128)(2,1)S(1)}, u32[]{:S(2)}) copy-start(bf16[1024,512]{1,0:T(8,128)(2,1)S(1)} %fusion.84.grad_ref) | copy-start | bytes 3145732
  476.1 27.1 %collective-permute-start.18 = (bf16[1024,512]{1,0:T(8,128)(2,1)S(1)}, bf16[1024,512]{1,0:T(8,128)(2,1)S(1)}, u32[]{:S(2)}, u32[]{:S(2)}) collective-permute-start(bf16[1024,512]{1,0:T(8,128)(2,1)S(1)} %convert_element_type.242), channel_id=1, source_target_pairs={{0,1},{1,2},{2,3},{3,0},{4,5},{5,6},{6,7},{7,4},{8,9},{9,10},{10,1... | collective-permute-start | bytes 3145736 | tf_op jit(solution)/shard_map/ppermute | solution.py:242
  476.2 27.0 %copy-start.18 = (f32[1024,512]{1,0:T(8,128)S(1)}, f32[1024,512]{1,0:T(8,128)}, u32[]{:S(2)}) copy-start(f32[1024,512]{1,0:T(8,128)} %copy-done.17) | copy-start | bytes 6291460
  504.6 27.4 %collective-permute-start.19 = (bf16[1024,512]{1,0:T(8,128)(2,1)}, bf16[1024,512]{1,0:T(8,128)(2,1)}, u32[]{:S(2)}, u32[]{:S(2)}) collective-permute-start(bf16[1024,512]{1,0:T(8,128)(2,1)} %add_convert_fusion.4), channel_id=1, source_target_pairs={{0,1},{1,2},{2,3},{3,0},{4,5},{5,6},{6,7},{7,4},{8,9},{9,10},{10,1... | collective-permute-start | bytes 3145736 | tf_op jit(solution)/shard_map/ppermute | solution.py:242
  511.3 114.1 %reduce-scatter.11.cloned.1.call-start = ((), (), s32[]{:S(2)}) async-start(), calls=%async_computation.12 | async-start | bytes 7077888 | tf_op jit(solution)/shard_map/reduce_scatter | solution.py:526
  536.4 25.4 %collective-permute-start.20 = (bf16[1024,512]{1,0:T(8,128)(2,1)}, bf16[1024,512]{1,0:T(8,128)(2,1)}, u32[]{:S(2)}, u32[]{:S(2)}) collective-permute-start(bf16[1024,512]{1,0:T(8,128)(2,1)} %fusion.38), channel_id=1, source_target_pairs={{0,1},{1,2},{2,3},{3,0},{4,5},{5,6},{6,7},{7,4},{8,9},{9,10},{10,1... | collective-permute-start | bytes 3145736 | tf_op jit(solution)/shard_map/ppermute | solution.py:242
  550.4 11.4 %copy-start.61 = (s32[8]{0:T(128)S(1)}, s32[8]{0:T(128)}, u32[]{:S(2)}) copy-start(s32[8]{0:T(128)} %param.30) | copy-start | bytes 100
  550.4 14.8 %copy-start.52 = (s32[2048]{0:T(1024)S(1)}, s32[2048]{0:T(1024)}, u32[]{:S(2)}) copy-start(s32[2048]{0:T(1024)} %copy-done.51) | copy-start | bytes 24580
  569.2 25.8 %collective-permute-start.21 = (bf16[1024,512]{1,0:T(8,128)(2,1)}, bf16[1024,512]{1,0:T(8,128)(2,1)}, u32[]{:S(2)}, u32[]{:S(2)}) collective-permute-start(bf16[1024,512]{1,0:T(8,128)(2,1)} %add_convert_fusion.3), channel_id=1, source_target_pairs={{0,1},{1,2},{2,3},{3,0},{4,5},{5,6},{6,7},{7,4},{8,9},{9,10},{10,1... | collective-permute-start | bytes 3145736 | tf_op jit(solution)/shard_map/ppermute | solution.py:242
  570.1 30.9 %collective-permute-start.23 = (f32[8,128]{1,0:T(8,128)S(1)}, f32[8,128]{1,0:T(8,128)S(1)}, u32[]{:S(2)}, u32[]{:S(2)}) collective-permute-start(f32[8,128]{1,0:T(8,128)S(1)} %bitcast.86), channel_id=1, source_target_pairs={{0,1},{1,0},{2,3},{3,2},{4,5},{5,4},{6,7},{7,6},{8,9},{9,8},{10,11... | collective-permute-start | bytes 12296 | tf_op jit(solution)/shard_map/ppermute | solution.py:274
  581.3 17.0 %copy-start.16 = (f32[1024,512]{1,0:T(8,128)S(1)}, f32[1024,512]{1,0:T(8,128)}, u32[]{:S(2)}) copy-start(f32[1024,512]{1,0:T(8,128)} %copy-done.15) | copy-start | bytes 6291460
  598.2 12.7 %copy-start.34 = (bf16[512,256]{1,0:T(8,128)(2,1)S(1)}, bf16[512,256]{1,0:T(8,128)(2,1)}, u32[]{:S(2)}) copy-start(bf16[512,256]{1,0:T(8,128)(2,1)} %reduce-scatter.9.cloned.1.call-done) | copy-start | bytes 786436
  598.2 17.0 %copy-start.10 = (bf16[8,128,512]{2,1,0:T(8,128)(2,1)S(1)}, bf16[8,128,512]{2,1,0:T(8,128)(2,1)}, u32[]{:S(2)}) copy-start(bf16[8,128,512]{2,1,0:T(8,128)(2,1)} %copy-done.9) | copy-start | bytes 3145732
  598.2 17.0 %copy-start.45 = (f32[1024]{0:T(1024)S(1)}, f32[1024]{0:T(1024)}, u32[]{:S(2)}) copy-start(f32[1024]{0:T(1024)} %get-tuple-element.223) | copy-start | bytes 12292
  598.2 17.0 %collective-permute-start.22 = (bf16[1024,512]{1,0:T(8,128)(2,1)}, bf16[1024,512]{1,0:T(8,128)(2,1)}, u32[]{:S(2)}, u32[]{:S(2)}) collective-permute-start(bf16[1024,512]{1,0:T(8,128)(2,1)} %add_convert_fusion.2), channel_id=1, source_target_pairs={{0,1},{1,2},{2,3},{3,0},{4,5},{5,6},{6,7},{7,4},{8,9},{9,10},{10,1... | collective-permute-start | bytes 3145736 | tf_op jit(solution)/shard_map/ppermute | solution.py:242
  601.0 9.9 %collective-permute-start.24 = (f32[8,128]{1,0:T(8,128)S(1)}, f32[8,128]{1,0:T(8,128)S(1)}, u32[]{:S(2)}, u32[]{:S(2)}) collective-permute-start(f32[8,128]{1,0:T(8,128)S(1)} %bitcast_add_fusion), channel_id=1, source_target_pairs={{0,2},{1,3},{2,0},{3,1},{4,6},{5,7},{6,4},{7,5},{8,10},{9,11},{10,... | collective-permute-start | bytes 12296 | tf_op jit(solution)/shard_map/ppermute | solution.py:274
  618.8 20.2 %all-to-all-start.1 = ((bf16[8,128,512]{2,1,0:T(8,128)(2,1)}), bf16[8,128,512]{2,1,0:T(8,128)(2,1)S(1)}, u32[]{:S(2)}, u32[]{:S(2)}) async-start(bf16[8,128,512]{2,1,0:T(8,128)(2,1)} %bitcast.13), calls=%async_computation.5 | async-start | bytes 2097152 | tf_op jit(solution)/shard_map/all_to_all | solution.py:553
  622.9 27.6 %collective-permute-start.28 = (bf16[1024,512]{1,0:T(8,128)(2,1)S(1)}, bf16[1024,512]{1,0:T(8,128)(2,1)}, u32[]{:S(2)}, u32[]{:S(2)}) collective-permute-start(bf16[1024,512]{1,0:T(8,128)(2,1)S(1)} %copy-done.37), channel_id=1, source_target_pairs={{0,1},{1,2},{2,3},{3,0},{4,5},{5,6},{6,7},{7,4},{8,9},{9,10},{10,1... | collective-permute-start | bytes 3145736 | tf_op jit(solution)/shard_map/ppermute | solution.py:242
  628.1 1.3 collective-permute-start.25
  629.4 8.1 %collective-permute-start.26 = (f32[41,128]{1,0:T(8,128)S(1)}, f32[41,128]{1,0:T(8,128)S(1)}, u32[]{:S(2)}, u32[]{:S(2)}) collective-permute-start(f32[41,128]{1,0:T(8,128)S(1)} %fusion.138), channel_id=1, source_target_pairs={{0,8},{4,12},{8,0},{12,4},{16,24},{20,28},{24,16},{28,20},{1,9},{5... | collective-permute-start | bytes 62984 | tf_op jit(solution)/shard_map/ppermute | solution.py:274
  637.5 3.9 collective-permute-start.27
  639.7 14.8 %copy-start.14 = (f32[1024,512]{1,0:T(8,128)S(1)}, f32[1024,512]{1,0:T(8,128)}, u32[]{:S(2)}) copy-start(f32[1024,512]{1,0:T(8,128)} %copy-done.13) | copy-start | bytes 6291460
  650.5 3.8 collective-permute-start.29
  654.4 4.8 collective-permute-start.30
  (42 other events, 165.3 us)
Sparse Core Ops, SparseCore 0:
  38.1 43.8 all-gather.4
  84.5 51.2 all-gather.6
  138.3 63.2 all-gather.8
  361.8 80.0 reduce-scatter.4
  445.1 56.5 reduce-scatter.6
  511.4 40.7 reduce-scatter.8
  561.9 60.6 reduce-scatter.10

commit v4 on v3

--- a/solution.py
+++ b/solution.py
@@ -424,19 +424,20 @@
         return dot(gate_up_grads[step], gate_up, NT)
 
     for step in range(tensor_count):
-        if step == 1:
-            h_parts[1], gate_up_grads[0], hidden = together(h_parts[1], gate_up_grads[0], hidden)
-        elif step == 2:
-            h_parts[2], gate_up_grads[1], hidden, terms[0] = together(
-                h_parts[2], gate_up_grads[1], hidden, normed_part(0)
+        if step > 0:
+            last = step - 1
+            term = normed_part(last)
+            h_parts[step], gate_up_grads[last], hidden, terms[last] = together(
+                h_parts[step],
+                gate_up_grads[last],
+                hidden,
+                term.astype(low) if last == 1 else term,
             )
-        elif step == 3:
-            h_parts[3], gate_up_grads[2], hidden, terms[1] = together(
-                h_parts[3], gate_up_grads[2], hidden, normed_part(1).astype(low)
-            )
-            running = around(terms[1])
         if step < tensor_count - 1:
             h_parts.append(around(h_parts[step]))
+        else:
+            terms[1], h_parts[step] = together(terms[1], h_parts[step])
+            running = around(terms[1])
         both = dot(h_parts[step], gate_up)
         mixed, mix_back = jax.vjp(
             lambda gate_in, up_in: jax.nn.gelu(gate_in, approximate=True) * up_in,
@@ -448,7 +449,7 @@
         gate_up_grads.append(jnp.concatenate(mix_back(grad_hidden), axis=1).astype(low))
 
     received, terms[2], terms[3], gate_up_grads[3], hidden = together(
-        running, normed_part(2), normed_part(3), gate_up_grads[3], hidden
+        running, terms[2], normed_part(3), gate_up_grads[3], hidden
     )
     running = around(add_low(received, terms[2]))
     h_rotated = jnp.concatenate(h_parts, axis=0)
@@ -459,7 +460,6 @@
     running = around(add_low(received, terms[3]))
     grad_down = dot(hidden, grad_y, TN).astype(low)
     received, terms[0], grad_down, hidden = together(running, terms[0], grad_down, hidden)
-    owned_down = lax.psum_scatter(grad_down, "dp", scatter_dimension=1, tiled=True)
     grad_h_second = received.astype(f32) + terms[0]
 
     grad_ffn_gain = jnp.sum(grad_h_second * (after_attn * inv_second), axis=0)
@@ -501,18 +501,19 @@
     output_first, grad_after, grad_heads = together(output_first, grad_after, grad_heads)
     output_sum = around(output_first)
 
+    grad_out = dot(attended, grad_after, TN).astype(low)
+    grad_heads, grad_out = together(grad_heads, grad_out)
+    grad_out_down = jnp.concatenate([grad_out, grad_down], axis=0)
+    owned_out_down = lax.psum_scatter(grad_out_down, "dp", scatter_dimension=1, tiled=True)
     half = pairs // 2
     first_grads, first_rel = attend_backward(soft_low, qkv, grad_heads, attended, 0, half)
     output_sum, first_grads, owned_gate_up = together(output_sum, first_grads, owned_gate_up)
     output_sum = around(add_low(output_sum, output_terms[2]))
-    grad_out = dot(attended, grad_after, TN).astype(low)
-    first_grads, grad_out = together(first_grads, grad_out)
-    owned_out = lax.psum_scatter(grad_out, "dp", scatter_dimension=1, tiled=True)
     grad_qkv, second_rel = attend_backward(
         soft_low, qkv, grad_heads, attended, half, pairs, (first_grads,)
     )
     rel_grad = jnp.concatenate([first_rel, second_rel], axis=0)
-    grad_qkv, output_sum, owned_down = together(grad_qkv, output_sum, owned_down)
+    grad_qkv, output_sum = together(grad_qkv, output_sum)
     output_sent = add_low(output_sum, output_terms[3])
 
     def first_part(step):
@@ -527,7 +528,7 @@
     running = around(add_low(received, term))
     inner = jnp.sum(grad_qkv.astype(f32) * qkv.astype(f32), axis=-1)
     inner = total_over(inner.reshape(-1, LANES), "mp").reshape(-1, 1) / features
-    received, term, owned_out = together(running, first_part(3), owned_out)
+    received, term, owned_out_down = together(running, first_part(3), owned_out_down)
     running = around(add_low(received, term))
     grad_table = lax.dot_general(
         bucket_hot.astype(f32),
@@ -536,7 +537,7 @@
         precision=lax.Precision.HIGHEST,
         preferred_element_type=f32,
     )
-    early_sq = square_sum(owned_gate_up) + square_sum(owned_down) + square_sum(owned_out)
+    early_sq = square_sum(owned_gate_up) + square_sum(owned_out_down)
     received, term, grad_table, early_sq, inner, output_sent = together(
         running, first_part(0), grad_table, early_sq, inner, output_sent
     )
@@ -593,10 +594,10 @@
         update(query_moment, owned_qkv[:, :heads_columns], factor),
         update(key_moment, owned_qkv[:, heads_columns : 2 * heads_columns], factor),
         update(value_moment, owned_qkv[:, 2 * heads_columns :], factor),
-        update(out_moment, owned_out, factor),
+        update(out_moment, owned_out_down[:heads_columns], factor),
         update(gate_moment, owned_gate_up[:, :units], factor),
         update(up_moment, owned_gate_up[:, units:], factor),
-        update(down_moment, owned_down, factor),
+        update(down_moment, owned_out_down[heads_columns:], factor),
         update(attn_gain_moment, owned_first, factor),
         update(ffn_gain_moment, owned_second, factor),
         update(table_moment, owned_table, factor),

time: 687 us -> 653 us (0.951)
  waiting for transfers between devices: 288 us -> 249 us
    ppermute x24, waiting for transfers between devices: 267 us -> 232 us  [around(): lax.ppermute(block, 'mp', [(i, (i + 1) % count) for i in range(count)])]
  transfers between devices with their start and end apart: 40 -> 39, of which waited for: 28 -> 28; matrix products, arithmetic and copies ran while one was open for 36% -> 38% of each run, Pallas kernels for 9% -> 10%
where the time goes in v4:
time: 653 us; the launch traced here: 644 us
  waiting for transfers between devices  249 us (38%)
  matrix products  164 us (25%)
  other arithmetic  73.7 us (11%)
  Pallas kernels  64.5 us (10%)
  local copies, waits for them, and re-layouts  27.7 us (4%)
  starting transfers between devices  24.2 us (4%)
  between operations  22.4 us (3%)
  blocking collectives  18.3 us (3%)
    ppermute x24, waiting for transfers between devices, around(): lax.ppermute(block, 'mp', [(i, (i + 1) % count) for i in range(count)])  232 us
    dot_general x34, matrix products, dot(): lax.dot_general(left, right, dims, preferred_element_type=jnp.float32)  164 us
    pallas_call x2, Pallas kernels, attend_backward(): pl.pallas_call(functools.partial(backward_kernel, first), grid=(last - fi...  34.9 us
    pallas_call x2, Pallas kernels, attend_forward(): pl.pallas_call(kernel, grid_spec=pltpu.PrefetchScalarGridSpec(num_scalar_...  29.5 us
    all_gather x1, blocking collectives, shards(): lax.all_gather(small, 'dp', axis=0)  18.3 us
    ppermute x7, waiting for transfers between devices, total_over(): lax.ppermute(value, axis, [(i, i ^ apart) for i in range(count)])  17.1 us
    convert_element_type x8, other arithmetic, add_low(): return (received.astype(jnp.float32) + term).astype(jnp.bfloat16)  13.9 us
  transfers between devices with their start and end apart: 39, of which 28 were waited for; matrix products, arithmetic and copies ran while one was open for 38% of the time, Pallas kernels for 10%

profile of v4, /device:TPU:0, one launch (start us, length us, event | category | flops | bytes accessed | tf_op | source)
XLA Modules:
  0.0 644.2 jit_solution(10710325909170047767)
XLA Ops:
  7.2 3.1 collective-permute-start
  13.4 3.7 all-to-all-start
  17.4 18.3 %all-gather = bf16[8,1,544]{2,1,0:T(2,128)(2,1)S(1)} all-gather(bf16[1,1,544]{2,1,0:T(2,128)(2,1)S(1)} %maximum_bitcast_fusion.1), channel_id=1, replica_groups=mesh['dp'=8,'mp'=4] {'dp'}, dimensions={0}, use_global_device_ids=true | all-gather | bytes 9792 | tf_op jit(solution)/shard_map/all_gather | solution.py:330
  41.8 23.5 %collective-permute-done.1 = bf16[1024,512]{1,0:T(8,128)(2,1)S(1)} collective-permute-done((bf16[1024,512]{1,0:T(8,128)(2,1)S(1)}, bf16[1024,512]{1,0:T(8,128)(2,1)S(1)}, u32[]{:S(2)}, u32[]{:S(2)}) %collective-permute-start.1) | collective-permute-done | bytes 1048608 | tf_op jit(solution)/shard_map/ppermute | solution.py:242
  68.2 23.6 %collective-permute-done.2 = bf16[1024,512]{1,0:T(8,128)(2,1)} collective-permute-done((bf16[1024,512]{1,0:T(8,128)(2,1)S(1)}, bf16[1024,512]{1,0:T(8,128)(2,1)}, u32[]{:S(2)}, u32[]{:S(2)}) %collective-permute-start.2) | collective-permute-done | bytes 1048608 | tf_op jit(solution)/shard_map/ppermute | solution.py:242
  100.7 17.0 %collective-permute-done.3 = bf16[1024,512]{1,0:T(8,128)(2,1)S(1)} collective-permute-done((bf16[1024,512]{1,0:T(8,128)(2,1)}, bf16[1024,512]{1,0:T(8,128)(2,1)S(1)}, u32[]{:S(2)}, u32[]{:S(2)}) %collective-permute-start.3) | collective-permute-done | bytes 1048608 | tf_op jit(solution)/shard_map/ppermute | solution.py:242
  121.3 10.7 %convolution_convert_fusion.3.query_ref.key_ref.value_ref = bf16[1024,1536]{1,0:T(8,128)(2,1)S(1)} fusion(bf16[2048,1536]{1,0:T(8,128)(2,1)} %all-gather.5.cloned.1.call-done, bf16[1024,2048]{1,0:T(8,128)(2,1)} %copy-done.7, f32[2048]{0:T(1024)S(1)} %bitcast.85, f32[1024]{0:T(1024)S(1)} %get-tuple-element.228), kind=kOutput, calls=%fused_computation.26 | convolution fusion | flops 6452412416 | bytes 13643776 | tf_op jit(solution)/shard_map/dot_general | solution.py:29
  132.0 8.2 %attend_forward.2 = (bf16[1024,512]{1,0:T(8,128)(2,1)}, bf16[8,1024,1024]{2,1,0:T(8,128)(2,1)}) custom-call(s32[1]{0:T(128)} %dynamic_slice.98.length, f32[4,2,2048]{2,1,0:T(2,128)S(1)} %reshape.188.rel_ref, bf16[1024,1536]{1,0:T(8,128)(2,1)S(1)} %convolution_convert_fusion.3.query_ref.key_ref.value_ref, ...), custom_call_target="tpu_custom_call" | custom-call | flops 2147483648 | bytes 4194304 | tf_op jit(solution)/shard_map/attend_forward/pallas_call | solution.py:91
  143.3 21.4 %attend_forward.3 = (bf16[1024,512]{1,0:T(8,128)(2,1)}, bf16[8,1024,1024]{2,1,0:T(8,128)(2,1)}) custom-call(s32[1]{0:T(128)} %dynamic_slice.98.length, f32[4,2,2048]{2,1,0:T(2,128)S(1)} %reshape.189.rel_ref, bf16[1024,1536]{1,0:T(8,128)(2,1)S(1)} %convolution_convert_fusion.3.query_ref.key_ref.value_ref, ...), custom_call_target="tpu_custom_call", output_to_operand_aliasing={{0}: (5, {}), {1}: (6, {})} | custom-call | flops 6442450944 | bytes 12582912 | tf_op jit(solution)/shard_map/attend_forward/pallas_call | solution.py:91
  167.7 2.4 convolution_convert_fusion.6
  170.7 3.3 broadcast_in_dim.80
  175.3 2.6 select_dynamic-update-slice_fusion.2
  177.8 2.6 select_dynamic-update-slice_fusion.1
  180.4 2.4 fusion.104
  182.8 10.8 %collective-permute-done.6 = bf16[256,2048]{1,0:T(8,128)(2,1)S(1)} collective-permute-done((bf16[256,2048]{1,0:T(8,128)(2,1)S(1)}, bf16[256,2048]{1,0:T(8,128)(2,1)S(1)}, u32[]{:S(2)}, u32[]{:S(2)}) %collective-permute-start.6) | collective-permute-done | bytes 1048608 | tf_op jit(solution)/shard_map/ppermute | solution.py:242
  194.0 2.4 fusion.100
  196.4 2.5 fusion.102
  198.9 2.6 select_dynamic-update-slice_fusion
  201.5 15.4 %collective-permute-done.7 = bf16[256,2048]{1,0:T(8,128)(2,1)S(1)} collective-permute-done((bf16[256,2048]{1,0:T(8,128)(2,1)S(1)}, bf16[256,2048]{1,0:T(8,128)(2,1)S(1)}, u32[]{:S(2)}, u32[]{:S(2)}) %collective-permute-start.7) | collective-permute-done | bytes 1048608 | tf_op jit(solution)/shard_map/ppermute | solution.py:242
  217.3 21.0 %collective-permute-done.8 = bf16[256,2048]{1,0:T(8,128)(2,1)S(1)} collective-permute-done((bf16[256,2048]{1,0:T(8,128)(2,1)S(1)}, bf16[256,2048]{1,0:T(8,128)(2,1)S(1)}, u32[]{:S(2)}, u32[]{:S(2)}) %collective-permute-start.8) | collective-permute-done | bytes 1048608 | tf_op jit(solution)/shard_map/ppermute | solution.py:242
  242.5 5.9 fusion.138
  249.7 5.2 fusion.47
  255.0 8.4 %fusion.137 = f32[256,2048]{1,0:T(8,128)} fusion(bf16[2048,2560]{1,0:T(8,128)(2,1)} %all-gather.9.cloned.1.call-done, bf16[256,1280]{1,0:T(8,128)(2,1)S(1)} %get-tuple-element.213, bf16[256,1280]{1,0:T(8,128)(2,1)S(1)} %get-tuple-element.212), kind=kOutput, calls=%fused_computation.250 | convolution fusion | flops 2686976000 | bytes 13893632 | tf_op jit(solution)/shard_map/dot_general | solution.py:29
  264.3 5.9 fusion.139
  270.8 4.0 fusion.54
  276.0 7.8 %convolution_convert_fusion.5 = bf16[256,2048]{1,0:T(8,128)(2,1)} fusion(bf16[2048,2560]{1,0:T(8,128)(2,1)} %all-gather.9.cloned.1.call-done, bf16[256,1280]{1,0:T(8,128)(2,1)S(1)} %get-tuple-element.211, bf16[256,1280]{1,0:T(8,128)(2,1)S(1)} %get-tuple-element.210), kind=kOutput, calls=%fused_computation.39 | convolution fusion | flops 2687500288 | bytes 12845056 | tf_op jit(solution)/shard_map/dot_general | solution.py:29
  283.8 3.8 collective-permute-done.10
  287.6 5.9 fusion.140
  294.0 4.0 fusion.61
  300.0 5.8 fusion.136
  305.9 4.9 collective-permute-done.11
  310.9 5.9 fusion.141
  317.4 4.8 fusion.68
  324.4 8.7 %fusion.135 = f32[256,2048]{1,0:T(8,128)} fusion(bf16[2048,2560]{1,0:T(8,128)(2,1)} %all-gather.9.cloned.1.call-done, bf16[256,1280]{1,0:T(8,128)(2,1)} %copy-done.36, bf16[256,1280]{1,0:T(8,128)(2,1)} %copy-done.35), kind=kOutput, calls=%fused_computation.248 | convolution fusion | flops 2686976000 | bytes 13893632 | tf_op jit(solution)/shard_map/dot_general | solution.py:29
  334.7 16.7 %convolution_convert_fusion = bf16[2048,2560]{1,0:T(8,128)(2,1)} fusion(bf16[256,2560]{1,0:T(8,128)(2,1)} %pad_maximum_fusion.5, bf16[256,2560]{1,0:T(8,128)(2,1)} %pad_maximum_fusion.4, bf16[256,2560]{1,0:T(8,128)(2,1)} %pad_maximum_fusion.3, bf16[256,2560]{1,0:T(8,128)(2,1)S(1)} %pad_maximum_fusion.2, bf16[256,2048]{1,0:T(8,128)(2,1)} %collective-permute-done.11, ...), kind=kOutput, calls=%fused_computation.2 | convolution fusion | flops 10780409856 | bytes 19922944 | tf_op jit(solution)/shard_map/dot_general | solution.py:29
  351.4 3.6 collective-permute-done.13
  357.9 11.4 %convolution_convert_fusion.2 = bf16[1280,2048]{1,0:T(8,128)(2,1)} fusion(bf16[1024,1280]{1,0:T(8,128)(2,1)} %copy-done.22, bf16[1024,2048]{1,0:T(8,128)(2,1)} %select_dynamic-update-slice_fusion), kind=kOutput, calls=%fused_computation.9 | convolution fusion | flops 5371330560 | bytes 12058624 | tf_op jit(solution)/shard_map/dot_general | solution.py:29
  369.3 8.9 %collective-permute-done.14 = bf16[256,2048]{1,0:T(8,128)(2,1)S(1)} collective-permute-done((bf16[256,2048]{1,0:T(8,128)(2,1)S(1)}, bf16[256,2048]{1,0:T(8,128)(2,1)S(1)}, u32[]{:S(2)}, u32[]{:S(2)}) %collective-permute-start.14) | collective-permute-done | bytes 1048608 | tf_op jit(solution)/shard_map/ppermute | solution.py:242
  378.9 2.4 subtract_convert_fusion
  388.6 16.8 %collective-permute-done.15 = bf16[256,2048]{1,0:T(8,128)(2,1)S(1)} collective-permute-done((bf16[256,2048]{1,0:T(8,128)(2,1)S(1)}, bf16[256,2048]{1,0:T(8,128)(2,1)S(1)}, u32[]{:S(2)}, u32[]{:S(2)}) %collective-permute-start.15) | collective-permute-done | bytes 1048608 | tf_op jit(solution)/shard_map/ppermute | solution.py:242
  408.4 21.9 %collective-permute-done.16 = bf16[256,2048]{1,0:T(8,128)(2,1)S(1)} collective-permute-done((bf16[256,2048]{1,0:T(8,128)(2,1)S(1)}, bf16[256,2048]{1,0:T(8,128)(2,1)S(1)}, u32[]{:S(2)}, u32[]{:S(2)}) %collective-permute-start.16) | collective-permute-done | bytes 1048608 | tf_op jit(solution)/shard_map/ppermute | solution.py:242
  434.2 12.8 %collective-permute-done.17 = bf16[256,2048]{1,0:T(8,128)(2,1)S(1)} collective-permute-done((bf16[256,2048]{1,0:T(8,128)(2,1)S(1)}, bf16[256,2048]{1,0:T(8,128)(2,1)S(1)}, u32[]{:S(2)}, u32[]{:S(2)}) %collective-permute-start.17) | collective-permute-done | bytes 1048608 | tf_op jit(solution)/shard_map/ppermute | solution.py:242
  448.9 5.3 convolution_convert_fusion.4
  454.2 6.8 %pad_maximum_fusion = bf16[1792,2048]{1,0:T(8,128)(2,1)} fusion(bf16[1280,2048]{1,0:T(8,128)(2,1)} %convolution_convert_fusion.2, bf16[512,2048]{1,0:T(8,128)(2,1)S(1)} %convolution_convert_fusion.4), kind=kLoop, calls=%fused_computation.10 | loop fusion | flops 14680064 | bytes 14680064 | tf_op jit(solution)/shard_map/concatenate | solution.py:506
  461.1 17.1 %attend_backward.2 = (bf16[1024,1536]{1,0:T(8,128)(2,1)S(1)}, f32[2,2,2048]{2,1,0:T(2,128)S(1)}) custom-call(bf16[8,1024,1024]{2,1,0:T(8,128)(2,1)} %get-tuple-element.121.soft_ref, bf16[1024,1536]{1,0:T(8,128)(2,1)} %copy-done.2, bf16[1024,512]{1,0:T(8,128)(2,1)S(1)} %fusion.82.grad_ref, bf16[1024,512]{1,0:T(8,128)(2,1)} %get-tuple-element.124.out_ref, ...), custom_call_target="tpu_custom_call" | custom-call | flops 10737418240 | bytes 8388608 | tf_op jit(solution)/shard_map/attend_backward/pallas_call | solution.py:207
  479.9 4.0 collective-permute-done.18
  485.8 17.9 %attend_backward.3 = (bf16[1024,1536]{1,0:T(8,128)(2,1)S(1)}, f32[2,2,2048]{2,1,0:T(2,128)S(1)}) custom-call(bf16[8,1024,1024]{2,1,0:T(8,128)(2,1)} %get-tuple-element.121.soft_ref, bf16[1024,1536]{1,0:T(8,128)(2,1)} %copy-done.2, bf16[1024,512]{1,0:T(8,128)(2,1)S(1)} %copy-done.5, bf16[1024,512]{1,0:T(8,128)(2,1)} %get-tuple-element.124.out_ref, ...), custom_call_target="tpu_custom_call" | custom-call | flops 10737418240 | bytes 8388608 | tf_op jit(solution)/shard_map/attend_backward/pallas_call | solution.py:207
  503.7 2.8 collective-permute-done.19
  506.5 4.6 fusion.38
  511.1 9.1 %convolution_convert_fusion.1 = bf16[2048,1536]{1,0:T(8,128)(2,1)} fusion(bf16[1024,1536]{1,0:T(8,128)(2,1)S(1)} %get-tuple-element.176, bf16[1024,2048]{1,0:T(8,128)(2,1)S(1)} %copy-done.8, f32[2048]{0:T(1024)S(1)} %bitcast.86, f32[1024]{0:T(1024)S(1)} %copy-done.46), kind=kOutput, calls=%fused_computation.8 | convolution fusion | flops 6453985280 | bytes 13643776 | tf_op jit(solution)/shard_map/dot_general | solution.py:29
  520.3 4.6 fusion.34
  524.8 7.8 %collective-permute-done.20 = bf16[1024,512]{1,0:T(8,128)(2,1)} collective-permute-done((bf16[1024,512]{1,0:T(8,128)(2,1)}, bf16[1024,512]{1,0:T(8,128)(2,1)}, u32[]{:S(2)}, u32[]{:S(2)}) %collective-permute-start.20) | collective-permute-done | bytes 1048608 | tf_op jit(solution)/shard_map/ppermute | solution.py:242
  534.1 3.6 add_convert_fusion.3
  540.1 4.8 fusion.32
  544.9 17.2 %collective-permute-done.21 = bf16[1024,512]{1,0:T(8,128)(2,1)} collective-permute-done((bf16[1024,512]{1,0:T(8,128)(2,1)}, bf16[1024,512]{1,0:T(8,128)(2,1)}, u32[]{:S(2)}, u32[]{:S(2)}) %collective-permute-start.21) | collective-permute-done | bytes 1048608 | tf_op jit(solution)/shard_map/ppermute | solution.py:242
  562.1 3.2 add_convert_fusion.2
  565.3 4.7 fusion.30
  571.5 6.5 %collective-permute-done.24 = f32[8,128]{1,0:T(8,128)S(1)} collective-permute-done((f32[8,128]{1,0:T(8,128)S(1)}, f32[8,128]{1,0:T(8,128)S(1)}, u32[]{:S(2)}, u32[]{:S(2)}) %collective-permute-start.24) | collective-permute-done | bytes 4128 | tf_op jit(solution)/shard_map/ppermute | solution.py:274
  582.2 3.5 fusion.29
  585.8 3.6 all-to-all-start.1
  589.7 3.1 collective-permute-start.28
  599.0 5.3 collective-permute-done.26
  608.2 9.1 %collective-permute-done.28 = bf16[1024,512]{1,0:T(8,128)(2,1)} collective-permute-done((bf16[1024,512]{1,0:T(8,128)(2,1)}, bf16[1024,512]{1,0:T(8,128)(2,1)}, u32[]{:S(2)}, u32[]{:S(2)}) %collective-permute-start.28) | collective-permute-done | bytes 1048608 | tf_op jit(solution)/shard_map/ppermute | solution.py:242
  622.2 2.6 fusion.83
  (312 shorter events, 101.8 us)
Async XLA Ops:
  7.2 30.7 %collective-permute-start = (bf16[1024,512]{1,0:T(8,128)(2,1)}, bf16[1024,512]{1,0:T(8,128)(2,1)}, u32[]{:S(2)}, u32[]{:S(2)}) collective-permute-start(bf16[1024,512]{1,0:T(8,128)(2,1)} %bitcast.75), channel_id=1, source_target_pairs={{0,1},{1,2},{2,3},{3,0},{4,5},{5,6},{6,7},{7,4},{8,9},{9,10},{10,1... | collective-permute-start | bytes 3145736 | tf_op jit(solution)/shard_map/ppermute | solution.py:242
  12.3 23.4 %copy-start.42 = (f32[256,512]{1,0:T(8,128)S(1)}, f32[256,512]{1,0:T(8,128)}, u32[]{:S(2)}) copy-start(f32[256,512]{1,0:T(8,128)} %param.32) | copy-start | bytes 1572868
  12.3 23.5 %copy-start.43 = (f32[256,512]{1,0:T(8,128)S(1)}, f32[256,512]{1,0:T(8,128)}, u32[]{:S(2)}) copy-start(f32[256,512]{1,0:T(8,128)} %param.33) | copy-start | bytes 1572868
  13.4 24.5 %all-to-all-start = ((bf16[8,128,512]{2,1,0:T(8,128)(2,1)}), bf16[8,128,512]{2,1,0:T(8,128)(2,1)S(1)}, u32[]{:S(2)}, u32[]{:S(2)}) async-start(bf16[8,128,512]{2,1,0:T(8,128)(2,1)} %broadcast_select_fusion.1), calls=%async_computation | async-start | bytes 2097152 | tf_op jit(solution)/shard_map/all_to_all | solution.py:321
  17.1 104.2 %all-gather.5.cloned.1.call-start = ((), (), s32[]{:S(2)}) async-start(), calls=%async_computation.5 | async-start | bytes 7077888 | tf_op jit(solution)/shard_map/all_gather | solution.py:362
  37.9 59.9 %copy-start.9 = (bf16[8,128,512]{2,1,0:T(8,128)(2,1)}, bf16[8,128,512]{2,1,0:T(8,128)(2,1)S(1)}, u32[]{:S(2)}) copy-start(bf16[8,128,512]{2,1,0:T(8,128)(2,1)S(1)} %all-to-all-done) | copy-start | bytes 3145732
  38.0 129.8 %all-gather.7.cloned.1.call-start = ((), (), s32[]{:S(2)}) async-start(), calls=%async_computation.6 | async-start | bytes 8257536 | tf_op jit(solution)/shard_map/all_gather | solution.py:369
  38.0 27.2 %collective-permute-start.1 = (bf16[1024,512]{1,0:T(8,128)(2,1)S(1)}, bf16[1024,512]{1,0:T(8,128)(2,1)S(1)}, u32[]{:S(2)}, u32[]{:S(2)}) collective-permute-start(bf16[1024,512]{1,0:T(8,128)(2,1)S(1)} %bitcast.67), channel_id=1, source_target_pairs={{0,1},{1,2},{2,3},{3,0},{4,5},{5,6},{6,7},{7,4},{8,9},{9,10},{10,1... | collective-permute-start | bytes 3145736 | tf_op jit(solution)/shard_map/ppermute | solution.py:242
  40.8 24.6 %copy-start.26 = (f32[256,1280]{1,0:T(8,128)S(1)}, f32[256,1280]{1,0:T(8,128)}, u32[]{:S(2)}) copy-start(f32[256,1280]{1,0:T(8,128)} %param.36) | copy-start | bytes 3932164
  65.3 177.2 %all-gather.9.cloned.1.call-start = ((), (), s32[]{:S(2)}) async-start(), calls=%async_computation.7 | async-start | bytes 11796480 | tf_op jit(solution)/shard_map/all_gather | solution.py:371
  65.3 26.5 %collective-permute-start.2 = (bf16[1024,512]{1,0:T(8,128)(2,1)S(1)}, bf16[1024,512]{1,0:T(8,128)(2,1)}, u32[]{:S(2)}, u32[]{:S(2)}) collective-permute-start(bf16[1024,512]{1,0:T(8,128)(2,1)S(1)} %collective-permute-done.1), channel_id=1, source_target_pairs={{0,1},{1,2},{2,3},{3,0},{4,5},{5,6},{6,7},{7,4},{8,9},{9,10},{10,1... | collective-permute-start | bytes 3145736 | tf_op jit(solution)/shard_map/ppermute | solution.py:242
  67.1 25.0 %copy-start.59 = (s32[8]{0:T(128)S(1)}, s32[8]{0:T(128)}, u32[]{:S(2)}) copy-start(s32[8]{0:T(128)} %param.30) | copy-start | bytes 100
  67.1 27.6 %copy-start.58 = (s32[8]{0:T(128)S(1)}, s32[8]{0:T(128)}, u32[]{:S(2)}) copy-start(s32[8]{0:T(128)} %param.29) | copy-start | bytes 100
  67.1 28.1 %copy-start.49 = (s32[2047]{0:T(1024)S(1)}, s32[2047]{0:T(1024)}, u32[]{:S(2)}) copy-start(s32[2047]{0:T(1024)} %param.31) | copy-start | bytes 24568
  91.9 392.0 %reduce-scatter.4.cloned.1.call-start = ((), (), s32[]{:S(2)}) async-start(), calls=%async_computation.8 | async-start | bytes 11796480 | tf_op jit(solution)/shard_map/reduce_scatter | solution.py:459
  92.0 25.7 %collective-permute-start.3 = (bf16[1024,512]{1,0:T(8,128)(2,1)}, bf16[1024,512]{1,0:T(8,128)(2,1)S(1)}, u32[]{:S(2)}, u32[]{:S(2)}) collective-permute-start(bf16[1024,512]{1,0:T(8,128)(2,1)} %collective-permute-done.2), channel_id=1, source_target_pairs={{0,1},{1,2},{2,3},{3,0},{4,5},{5,6},{6,7},{7,4},{8,9},{9,10},{10,1... | collective-permute-start | bytes 3145736 | tf_op jit(solution)/shard_map/ppermute | solution.py:242
  95.9 25.4 %copy-start.47 = (f32[1,2,8,128]{3,1,2,0:T(2,128)}, f32[1,2,8,128]{3,1,2,0:T(2,128)S(1)}, u32[]{:S(2)}) copy-start(f32[1,2,8,128]{3,1,2,0:T(2,128)S(1)} %copy.44) | copy-start | bytes 24580
  117.7 24.9 %collective-permute-start.4 = (bf16[1024,512]{1,0:T(8,128)(2,1)}, bf16[1024,512]{1,0:T(8,128)(2,1)}, u32[]{:S(2)}, u32[]{:S(2)}) collective-permute-start(bf16[1024,512]{1,0:T(8,128)(2,1)} %collective-permute-done), channel_id=1, source_target_pairs={{0,1},{1,2},{2,3},{3,0},{4,5},{5,6},{6,7},{7,4},{8,9},{9,10},{10,1... | collective-permute-start | bytes 3145736 | tf_op jit(solution)/shard_map/ppermute | solution.py:242
  121.3 10.7 %copy-start.45 = (f32[1024]{0:T(1024)}, f32[1024]{0:T(1024)S(1)}, u32[]{:S(2)}) copy-start(f32[1024]{0:T(1024)S(1)} %get-tuple-element.228) | copy-start | bytes 12292
  132.0 11.2 %copy-start.2 = (bf16[1024,1536]{1,0:T(8,128)(2,1)}, bf16[1024,1536]{1,0:T(8,128)(2,1)S(1)}, u32[]{:S(2)}) copy-start(bf16[1024,1536]{1,0:T(8,128)(2,1)S(1)} %convolution_convert_fusion.3.query_ref.key_ref.value_ref) | copy-start | bytes 9437188
  142.6 23.9 %collective-permute-start.5 = (bf16[1024,512]{1,0:T(8,128)(2,1)}, bf16[1024,512]{1,0:T(8,128)(2,1)}, u32[]{:S(2)}, u32[]{:S(2)}) collective-permute-start(bf16[1024,512]{1,0:T(8,128)(2,1)} %collective-permute-done.4), channel_id=1, source_target_pairs={{0,1},{1,2},{2,3},{3,0},{4,5},{5,6},{6,7},{7,4},{8,9},{9,10},{10,1... | collective-permute-start | bytes 3145736 | tf_op jit(solution)/shard_map/ppermute | solution.py:242
  170.1 23.5 %collective-permute-start.6 = (bf16[256,2048]{1,0:T(8,128)(2,1)S(1)}, bf16[256,2048]{1,0:T(8,128)(2,1)S(1)}, u32[]{:S(2)}, u32[]{:S(2)}) collective-permute-start(bf16[256,2048]{1,0:T(8,128)(2,1)S(1)} %convolution_convert_fusion.6), channel_id=1, source_target_pairs={{0,1},{1,2},{2,3},{3,0},{4,5},{5,6},{6,7},{7,4},{8,9},{9,10},{10,1... | collective-permute-start | bytes 3145736 | tf_op jit(solution)/shard_map/ppermute | solution.py:242
  193.9 23.0 %collective-permute-start.7 = (bf16[256,2048]{1,0:T(8,128)(2,1)S(1)}, bf16[256,2048]{1,0:T(8,128)(2,1)S(1)}, u32[]{:S(2)}, u32[]{:S(2)}) collective-permute-start(bf16[256,2048]{1,0:T(8,128)(2,1)S(1)} %add_convert_fusion.8), channel_id=1, source_target_pairs={{0,1},{1,2},{2,3},{3,0},{4,5},{5,6},{6,7},{7,4},{8,9},{9,10},{10,1... | collective-permute-start | bytes 3145736 | tf_op jit(solution)/shard_map/ppermute | solution.py:242
  217.2 21.1 %collective-permute-start.8 = (bf16[256,2048]{1,0:T(8,128)(2,1)S(1)}, bf16[256,2048]{1,0:T(8,128)(2,1)S(1)}, u32[]{:S(2)}, u32[]{:S(2)}) collective-permute-start(bf16[256,2048]{1,0:T(8,128)(2,1)S(1)} %add_convert_fusion.7), channel_id=1, source_target_pairs={{0,1},{1,2},{2,3},{3,0},{4,5},{5,6},{6,7},{7,4},{8,9},{9,10},{10,1... | collective-permute-start | bytes 3145736 | tf_op jit(solution)/shard_map/ppermute | solution.py:242
  242.5 21.7 %collective-permute-start.9 = (bf16[256,2048]{1,0:T(8,128)(2,1)}, bf16[256,2048]{1,0:T(8,128)(2,1)}, u32[]{:S(2)}, u32[]{:S(2)}) collective-permute-start(bf16[256,2048]{1,0:T(8,128)(2,1)} %multiply_convert_fusion), channel_id=1, source_target_pairs={{0,1},{1,2},{2,3},{3,0},{4,5},{5,6},{6,7},{7,4},{8,9},{9,10},{10,1... | collective-permute-start | bytes 3145736 | tf_op jit(solution)/shard_map/ppermute | solution.py:242
  255.0 15.7 %slice-start = ((s8[7340032]{0:T(1024)(128)(4,1)}), s8[4194304]{0:T(1024)(128)(4,1)S(1)}, s32[]{:S(2)}) async-start(s8[7340032]{0:T(1024)(128)(4,1)} %bitcast.71), calls=%async_computation.11 | async-start | bytes 8388608
  264.1 23.5 %collective-permute-start.10 = (bf16[256,2048]{1,0:T(8,128)(2,1)}, bf16[256,2048]{1,0:T(8,128)(2,1)}, u32[]{:S(2)}, u32[]{:S(2)}) collective-permute-start(bf16[256,2048]{1,0:T(8,128)(2,1)} %collective-permute-done.9), channel_id=1, source_target_pairs={{0,1},{1,2},{2,3},{3,0},{4,5},{5,6},{6,7},{7,4},{8,9},{9,10},{10,1... | collective-permute-start | bytes 3145736 | tf_op jit(solution)/shard_map/ppermute | solution.py:242
  287.6 23.1 %collective-permute-start.11 = (bf16[256,2048]{1,0:T(8,128)(2,1)}, bf16[256,2048]{1,0:T(8,128)(2,1)}, u32[]{:S(2)}, u32[]{:S(2)}) collective-permute-start(bf16[256,2048]{1,0:T(8,128)(2,1)} %collective-permute-done.10), channel_id=1, source_target_pairs={{0,1},{1,2},{2,3},{3,0},{4,5},{5,6},{6,7},{7,4},{8,9},{9,10},{10,1... | collective-permute-start | bytes 3145736 | tf_op jit(solution)/shard_map/ppermute | solution.py:242
  310.7 22.3 %collective-permute-start.12 = (bf16[256,2048]{1,0:T(8,128)(2,1)}, bf16[256,2048]{1,0:T(8,128)(2,1)S(1)}, u32[]{:S(2)}, u32[]{:S(2)}) collective-permute-start(bf16[256,2048]{1,0:T(8,128)(2,1)} %convolution_convert_fusion.5), channel_id=1, source_target_pairs={{0,1},{1,2},{2,3},{3,0},{4,5},{5,6},{6,7},{7,4},{8,9},{9,10},{10,1... | collective-permute-start | bytes 3145736 | tf_op jit(solution)/shard_map/ppermute | solution.py:242
  334.4 20.7 %collective-permute-start.13 = (bf16[256,2048]{1,0:T(8,128)(2,1)}, bf16[256,2048]{1,0:T(8,128)(2,1)}, u32[]{:S(2)}, u32[]{:S(2)}) collective-permute-start(bf16[256,2048]{1,0:T(8,128)(2,1)} %add_convert_fusion.6), channel_id=1, source_target_pairs={{0,1},{1,2},{2,3},{3,0},{4,5},{5,6},{6,7},{7,4},{8,9},{9,10},{10,1... | collective-permute-start | bytes 3145736 | tf_op jit(solution)/shard_map/ppermute | solution.py:242
  355.1 189.8 %reduce-scatter.6.cloned.1.call-start = ((), (), s32[]{:S(2)}) async-start(), calls=%async_computation.9 | async-start | bytes 8257536 | tf_op jit(solution)/shard_map/reduce_scatter | solution.py:507
  355.1 26.3 %slice-start.2 = ((s8[7340032]{0:T(1024)(128)(4,1)}), s8[4194304]{0:T(1024)(128)(4,1)S(1)}, s32[]{:S(2)}) async-start(s8[7340032]{0:T(1024)(128)(4,1)} %bitcast.73), calls=%async_computation.13 | async-start | bytes 8388608
  357.4 20.8 %copy-start.11 = (f32[256,2048]{1,0:T(8,128)S(1)}, f32[256,2048]{1,0:T(8,128)}, u32[]{:S(2)}) copy-start(f32[256,2048]{1,0:T(8,128)} %fusion.137) | copy-start | bytes 6291460
  357.4 24.0 %slice-start.3 = ((s8[7340032]{0:T(1024)(128)(4,1)}), s8[3145728]{0:T(1024)(128)(4,1)S(1)}, s32[]{:S(2)}) async-start(s8[7340032]{0:T(1024)(128)(4,1)} %bitcast.73), calls=%async_computation.14 | async-start | bytes 6291456
  357.5 20.8 %collective-permute-start.14 = (bf16[256,2048]{1,0:T(8,128)(2,1)S(1)}, bf16[256,2048]{1,0:T(8,128)(2,1)S(1)}, u32[]{:S(2)}, u32[]{:S(2)}) collective-permute-start(bf16[256,2048]{1,0:T(8,128)(2,1)S(1)} %add_convert_fusion.5), channel_id=1, source_target_pairs={{0,1},{1,2},{2,3},{3,0},{4,5},{5,6},{6,7},{7,4},{8,9},{9,10},{10,1... | collective-permute-start | bytes 3145736 | tf_op jit(solution)/shard_map/ppermute | solution.py:242
  381.3 24.0 %collective-permute-start.15 = (bf16[256,2048]{1,0:T(8,128)(2,1)S(1)}, bf16[256,2048]{1,0:T(8,128)(2,1)S(1)}, u32[]{:S(2)}, u32[]{:S(2)}) collective-permute-start(bf16[256,2048]{1,0:T(8,128)(2,1)S(1)} %subtract_convert_fusion), channel_id=1, source_target_pairs={{0,1},{1,2},{2,3},{3,0},{4,5},{5,6},{6,7},{7,4},{8,9},{9,10},{10,1... | collective-permute-start | bytes 3145736 | tf_op jit(solution)/shard_map/ppermute | solution.py:242
  388.5 18.7 %copy-start.15 = (f32[1024,512]{1,0:T(8,128)}, f32[1024,512]{1,0:T(8,128)S(1)}, u32[]{:S(2)}) copy-start(f32[1024,512]{1,0:T(8,128)S(1)} %get-tuple-element.196) | copy-start | bytes 6291460
  388.5 18.7 %copy-start.17 = (f32[1024,512]{1,0:T(8,128)}, f32[1024,512]{1,0:T(8,128)S(1)}, u32[]{:S(2)}) copy-start(f32[1024,512]{1,0:T(8,128)S(1)} %get-tuple-element.188) | copy-start | bytes 6291460
  388.5 18.7 %copy-start.19 = (f32[1024,512]{1,0:T(8,128)}, f32[1024,512]{1,0:T(8,128)S(1)}, u32[]{:S(2)}) copy-start(f32[1024,512]{1,0:T(8,128)S(1)} %get-tuple-element.173) | copy-start | bytes 6291460
  405.4 24.9 %collective-permute-start.16 = (bf16[256,2048]{1,0:T(8,128)(2,1)S(1)}, bf16[256,2048]{1,0:T(8,128)(2,1)S(1)}, u32[]{:S(2)}, u32[]{:S(2)}) collective-permute-start(bf16[256,2048]{1,0:T(8,128)(2,1)S(1)} %collective-permute-done.15), channel_id=1, source_target_pairs={{0,1},{1,2},{2,3},{3,0},{4,5},{5,6},{6,7},{7,4},{8,9},{9,10},{10,1... | collective-permute-start | bytes 3145736 | tf_op jit(solution)/shard_map/ppermute | solution.py:242
  430.3 16.7 %collective-permute-start.17 = (bf16[256,2048]{1,0:T(8,128)(2,1)S(1)}, bf16[256,2048]{1,0:T(8,128)(2,1)S(1)}, u32[]{:S(2)}, u32[]{:S(2)}) collective-permute-start(bf16[256,2048]{1,0:T(8,128)(2,1)S(1)} %collective-permute-done.16), channel_id=1, source_target_pairs={{0,1},{1,2},{2,3},{3,0},{4,5},{5,6},{6,7},{7,4},{8,9},{9,10},{10,1... | collective-permute-start | bytes 3145736 | tf_op jit(solution)/shard_map/ppermute | solution.py:242
  448.9 12.2 %copy-start.4 = (bf16[1024,512]{1,0:T(8,128)(2,1)}, bf16[1024,512]{1,0:T(8,128)(2,1)S(1)}, u32[]{:S(2)}) copy-start(bf16[1024,512]{1,0:T(8,128)(2,1)S(1)} %fusion.82.grad_ref) | copy-start | bytes 3145732
  461.0 132.0 %reduce-scatter.8.cloned.1.call-start = ((), (), s32[]{:S(2)}) async-start(), calls=%async_computation.10 | async-start | bytes 7077888 | tf_op jit(solution)/shard_map/reduce_scatter | solution.py:527
  461.0 22.8 %collective-permute-start.18 = (bf16[1024,512]{1,0:T(8,128)(2,1)}, bf16[1024,512]{1,0:T(8,128)(2,1)}, u32[]{:S(2)}, u32[]{:S(2)}) collective-permute-start(bf16[1024,512]{1,0:T(8,128)(2,1)} %convert_element_type.243), channel_id=1, source_target_pairs={{0,1},{1,2},{2,3},{3,0},{4,5},{5,6},{6,7},{7,4},{8,9},{9,10},{10,1... | collective-permute-start | bytes 3145736 | tf_op jit(solution)/shard_map/ppermute | solution.py:242
  461.1 22.8 %copy-start.20 = (f32[1024,512]{1,0:T(8,128)S(1)}, f32[1024,512]{1,0:T(8,128)}, u32[]{:S(2)}) copy-start(f32[1024,512]{1,0:T(8,128)} %copy-done.19) | copy-start | bytes 6291460
  485.6 20.9 %collective-permute-start.19 = (bf16[1024,512]{1,0:T(8,128)(2,1)S(1)}, bf16[1024,512]{1,0:T(8,128)(2,1)S(1)}, u32[]{:S(2)}, u32[]{:S(2)}) collective-permute-start(bf16[1024,512]{1,0:T(8,128)(2,1)S(1)} %add_convert_fusion.4), channel_id=1, source_target_pairs={{0,1},{1,2},{2,3},{3,0},{4,5},{5,6},{6,7},{7,4},{8,9},{9,10},{10,1... | collective-permute-start | bytes 3145736 | tf_op jit(solution)/shard_map/ppermute | solution.py:242
  511.1 21.6 %collective-permute-start.20 = (bf16[1024,512]{1,0:T(8,128)(2,1)}, bf16[1024,512]{1,0:T(8,128)(2,1)}, u32[]{:S(2)}, u32[]{:S(2)}) collective-permute-start(bf16[1024,512]{1,0:T(8,128)(2,1)} %fusion.38), channel_id=1, source_target_pairs={{0,1},{1,2},{2,3},{3,0},{4,5},{5,6},{6,7},{7,4},{8,9},{9,10},{10,1... | collective-permute-start | bytes 3145736 | tf_op jit(solution)/shard_map/ppermute | solution.py:242
  524.8 8.6 %copy-start.51 = (s32[2048]{0:T(1024)S(1)}, s32[2048]{0:T(1024)}, u32[]{:S(2)}) copy-start(s32[2048]{0:T(1024)} %copy-done.50) | copy-start | bytes 24580
  537.6 24.5 %collective-permute-start.21 = (bf16[1024,512]{1,0:T(8,128)(2,1)}, bf16[1024,512]{1,0:T(8,128)(2,1)}, u32[]{:S(2)}, u32[]{:S(2)}) collective-permute-start(bf16[1024,512]{1,0:T(8,128)(2,1)} %add_convert_fusion.3), channel_id=1, source_target_pairs={{0,1},{1,2},{2,3},{3,0},{4,5},{5,6},{6,7},{7,4},{8,9},{9,10},{10,1... | collective-permute-start | bytes 3145736 | tf_op jit(solution)/shard_map/ppermute | solution.py:242
  540.1 29.9 %collective-permute-start.23 = (f32[8,128]{1,0:T(8,128)S(1)}, f32[8,128]{1,0:T(8,128)S(1)}, u32[]{:S(2)}, u32[]{:S(2)}) collective-permute-start(f32[8,128]{1,0:T(8,128)S(1)} %bitcast.83), channel_id=1, source_target_pairs={{0,1},{1,0},{2,3},{3,2},{4,5},{5,4},{6,7},{7,6},{8,9},{9,8},{10,11... | collective-permute-start | bytes 12296 | tf_op jit(solution)/shard_map/ppermute | solution.py:274
  565.3 17.0 %collective-permute-start.22 = (bf16[1024,512]{1,0:T(8,128)(2,1)}, bf16[1024,512]{1,0:T(8,128)(2,1)}, u32[]{:S(2)}, u32[]{:S(2)}) collective-permute-start(bf16[1024,512]{1,0:T(8,128)(2,1)} %add_convert_fusion.2), channel_id=1, source_target_pairs={{0,1},{1,2},{2,3},{3,0},{4,5},{5,6},{6,7},{7,4},{8,9},{9,10},{10,1... | collective-permute-start | bytes 3145736 | tf_op jit(solution)/shard_map/ppermute | solution.py:242
  570.0 7.9 %copy-start.14 = (bf16[1792,256]{1,0:T(8,128)(2,1)S(1)}, bf16[1792,256]{1,0:T(8,128)(2,1)}, u32[]{:S(2)}) copy-start(bf16[1792,256]{1,0:T(8,128)(2,1)} %reduce-scatter.6.cloned.1.call-done) | copy-start | bytes 2752516
  570.0 12.2 %copy-start.10 = (bf16[8,128,512]{2,1,0:T(8,128)(2,1)S(1)}, bf16[8,128,512]{2,1,0:T(8,128)(2,1)}, u32[]{:S(2)}) copy-start(bf16[8,128,512]{2,1,0:T(8,128)(2,1)} %copy-done.9) | copy-start | bytes 3145732
  570.0 12.2 %copy-start.44 = (f32[1024]{0:T(1024)S(1)}, f32[1024]{0:T(1024)}, u32[]{:S(2)}) copy-start(f32[1024]{0:T(1024)} %get-tuple-element.227) | copy-start | bytes 12292
  570.0 7.9 %collective-permute-start.24 = (f32[8,128]{1,0:T(8,128)S(1)}, f32[8,128]{1,0:T(8,128)S(1)}, u32[]{:S(2)}, u32[]{:S(2)}) collective-permute-start(f32[8,128]{1,0:T(8,128)S(1)} %bitcast_add_fusion), channel_id=1, source_target_pairs={{0,2},{1,3},{2,0},{3,1},{4,6},{5,7},{6,4},{7,5},{8,10},{9,11},{10,... | collective-permute-start | bytes 12296 | tf_op jit(solution)/shard_map/ppermute | solution.py:274
  585.8 20.1 %all-to-all-start.1 = ((bf16[8,128,512]{2,1,0:T(8,128)(2,1)}), bf16[8,128,512]{2,1,0:T(8,128)(2,1)S(1)}, u32[]{:S(2)}, u32[]{:S(2)}) async-start(bf16[8,128,512]{2,1,0:T(8,128)(2,1)} %bitcast.13), calls=%async_computation.4 | async-start | bytes 2097152 | tf_op jit(solution)/shard_map/all_to_all | solution.py:554
  589.7 27.6 %collective-permute-start.28 = (bf16[1024,512]{1,0:T(8,128)(2,1)}, bf16[1024,512]{1,0:T(8,128)(2,1)}, u32[]{:S(2)}, u32[]{:S(2)}) collective-permute-start(bf16[1024,512]{1,0:T(8,128)(2,1)} %add_convert_fusion.1), channel_id=1, source_target_pairs={{0,1},{1,2},{2,3},{3,0},{4,5},{5,6},{6,7},{7,4},{8,9},{9,10},{10,1... | collective-permute-start | bytes 3145736 | tf_op jit(solution)/shard_map/ppermute | solution.py:242
  595.8 1.3 collective-permute-start.25
  597.1 7.2 %collective-permute-start.26 = (f32[41,128]{1,0:T(8,128)S(1)}, f32[41,128]{1,0:T(8,128)S(1)}, u32[]{:S(2)}, u32[]{:S(2)}) collective-permute-start(f32[41,128]{1,0:T(8,128)S(1)} %fusion.134), channel_id=1, source_target_pairs={{0,8},{4,12},{8,0},{12,4},{16,24},{20,28},{24,16},{28,20},{1,9},{5... | collective-permute-start | bytes 62984 | tf_op jit(solution)/shard_map/ppermute | solution.py:274
  604.3 3.9 collective-permute-start.27
  606.5 15.7 %copy-start.16 = (f32[1024,512]{1,0:T(8,128)S(1)}, f32[1024,512]{1,0:T(8,128)}, u32[]{:S(2)}) copy-start(f32[1024,512]{1,0:T(8,128)} %copy-done.15) | copy-start | bytes 6291460
  617.3 3.8 collective-permute-start.29
  621.1 8.3 %copy-start.24 = (f32[1280,256]{1,0:T(8,128)S(1)}, f32[1280,256]{1,0:T(8,128)}, u32[]{:S(2)}) copy-start(f32[1280,256]{1,0:T(8,128)} %param.48) | copy-start | bytes 3932164
  621.2 4.8 collective-permute-start.30
  (40 other events, 140.3 us)
Sparse Core Ops, SparseCore 0:
  38.1 43.8 all-gather.4
  84.5 51.2 all-gather.6
  138.3 63.2 all-gather.8
  355.2 79.4 reduce-scatter.3
  461.1 62.8 reduce-scatter.5
  532.8 58.1 reduce-scatter.7

commit v5 on v4

--- a/solution.py
+++ b/solution.py
@@ -538,10 +538,11 @@
         preferred_element_type=f32,
     )
     early_sq = square_sum(owned_gate_up) + square_sum(owned_out_down)
-    received, term, grad_table, early_sq, inner, output_sent = together(
-        running, first_part(0), grad_table, early_sq, inner, output_sent
-    )
+    term, output_sent = together(first_part(0), output_sent)
     output_sum = around(output_sent)
+    received, term, grad_table, early_sq, inner = together(
+        running, term, grad_table, early_sq, inner
+    )
     grad_h_first = received.astype(f32) + term
     own_gain = lax.dynamic_slice_in_dim(first_gain, member * quarter, quarter, 0)
     x_own = x_own.astype(f32)
@@ -551,13 +552,6 @@
         + inv_first * (grad_h_first * own_gain)
         - x_own * (inv_first * inv_first) * inner
     ).astype(low)
-    came_back = lax.all_to_all(
-        grad_input.reshape(group_count, -1, quarter), "dp", split_axis=0, concat_axis=0, tiled=True
-    )
-    group_iota = lax.broadcasted_iota(jnp.int32, (group_count, group_count), 0)
-    place = jnp.argmax(deal_order[None, :] == group_iota, axis=1)
-    input_grad = jnp.take(came_back, place, axis=0)
-
     local_sq = early_sq + square_sum(owned_qkv)
     heads_dev = bias_table.shape[1]
     first_wide = lax.dynamic_update_slice_in_dim(
@@ -569,8 +563,16 @@
     sums = jnp.concatenate([first_wide, grad_ffn_gain, table_wide.reshape(-1)])
     small_count = sums.shape[0]
     sums = jnp.concatenate([sums, jnp.broadcast_to(local_sq, (LANES,))])
-    sums = total_over(sums.reshape(-1, LANES), "dp")
     sums, output_sum = together(sums, output_sum)
+    sums = jnp.sum(lax.all_gather(sums.reshape(-1, LANES), "dp", axis=0), axis=0)
+    sums, grad_input = together(sums, grad_input)
+    came_back = lax.all_to_all(
+        grad_input.reshape(group_count, -1, quarter), "dp", split_axis=0, concat_axis=0, tiled=True
+    )
+    group_iota = lax.broadcasted_iota(jnp.int32, (group_count, group_count), 0)
+    place = jnp.argmax(deal_order[None, :] == group_iota, axis=1)
+    input_grad = jnp.take(came_back, place, axis=0)
+
     layer_out = (output_sum.astype(f32) + output_terms[0]).astype(low)[None]
     sums = total_over(sums, "mp").reshape(-1)
     total_sq = sums[small_count] + jnp.sum(sums[:small_count] * sums[:small_count])

time: 653 us -> 646 us (0.989)
  waiting for transfers between devices: 249 us -> 237 us
  blocking collectives: 18.3 us -> 26.1 us
    all_gather x0 -> x1, blocking collectives: none -> 7.78 us  [shards(): lax.all_gather(sums.reshape(-1, LANES), 'dp', axis=0)]
    ppermute x7 -> x4, waiting for transfers between devices: 17.1 us -> 10.4 us  [total_over(): lax.ppermute(value, axis, [(i, i ^ apart) for i in range(count)])]
  transfers between devices with their start and end apart: 39 -> 36, of which waited for: 28 -> 25; matrix products, arithmetic and copies ran while one was open for 38% -> 40% of each run, Pallas kernels for 10% -> 10%
where the time goes in v5:
time: 646 us; the launch traced here: 637 us
  waiting for transfers between devices  237 us (37%)
  matrix products  165 us (26%)
  other arithmetic  75.7 us (12%)
  Pallas kernels  64.5 us (10%)
  local copies, waits for them, and re-layouts  27.3 us (4%)
  blocking collectives  26.1 us (4%)
  between operations  22.4 us (3%)
  starting transfers between devices  19.5 us (3%)
    ppermute x24, waiting for transfers between devices, around(): lax.ppermute(block, 'mp', [(i, (i + 1) % count) for i in range(count)])  227 us
    dot_general x34, matrix products, dot(): lax.dot_general(left, right, dims, preferred_element_type=jnp.float32)  164 us
    pallas_call x2, Pallas kernels, attend_backward(): pl.pallas_call(functools.partial(backward_kernel, first), grid=(last - fi...  35 us
    pallas_call x2, Pallas kernels, attend_forward(): pl.pallas_call(kernel, grid_spec=pltpu.PrefetchScalarGridSpec(num_scalar_...  29.5 us
    all_gather x1, blocking collectives, shards(): lax.all_gather(small, 'dp', axis=0)  18.3 us
    convert_element_type x8, other arithmetic, add_low(): return (received.astype(jnp.float32) + term).astype(jnp.bfloat16)  13.9 us
  transfers between devices with their start and end apart: 36, of which 25 were waited for; matrix products, arithmetic and copies ran while one was open for 40% of the time, Pallas kernels for 10%

profile of v5, /device:TPU:0, one launch (start us, length us, event | category | flops | bytes accessed | tf_op | source)
XLA Modules:
  0.0 637.1 jit_solution(9538106057626351085)
XLA Ops:
  7.2 3.1 collective-permute-start
  13.4 3.7 all-to-all-start
  17.4 18.3 %all-gather = bf16[8,1,544]{2,1,0:T(2,128)(2,1)S(1)} all-gather(bf16[1,1,544]{2,1,0:T(2,128)(2,1)S(1)} %maximum_bitcast_fusion), channel_id=1, replica_groups=mesh['dp'=8,'mp'=4] {'dp'}, dimensions={0}, use_global_device_ids=true | all-gather | bytes 9792 | tf_op jit(solution)/shard_map/all_gather | solution.py:330
  41.8 23.5 %collective-permute-done.1 = bf16[1024,512]{1,0:T(8,128)(2,1)S(1)} collective-permute-done((bf16[1024,512]{1,0:T(8,128)(2,1)S(1)}, bf16[1024,512]{1,0:T(8,128)(2,1)S(1)}, u32[]{:S(2)}, u32[]{:S(2)}) %collective-permute-start.1) | collective-permute-done | bytes 1048608 | tf_op jit(solution)/shard_map/ppermute | solution.py:242
  68.2 23.6 %collective-permute-done.2 = bf16[1024,512]{1,0:T(8,128)(2,1)} collective-permute-done((bf16[1024,512]{1,0:T(8,128)(2,1)S(1)}, bf16[1024,512]{1,0:T(8,128)(2,1)}, u32[]{:S(2)}, u32[]{:S(2)}) %collective-permute-start.2) | collective-permute-done | bytes 1048608 | tf_op jit(solution)/shard_map/ppermute | solution.py:242
  100.7 17.0 %collective-permute-done.3 = bf16[1024,512]{1,0:T(8,128)(2,1)S(1)} collective-permute-done((bf16[1024,512]{1,0:T(8,128)(2,1)}, bf16[1024,512]{1,0:T(8,128)(2,1)S(1)}, u32[]{:S(2)}, u32[]{:S(2)}) %collective-permute-start.3) | collective-permute-done | bytes 1048608 | tf_op jit(solution)/shard_map/ppermute | solution.py:242
  121.3 10.7 %convolution_convert_fusion.3.query_ref.key_ref.value_ref = bf16[1024,1536]{1,0:T(8,128)(2,1)S(1)} fusion(bf16[2048,1536]{1,0:T(8,128)(2,1)} %all-gather.5.cloned.1.call-done, bf16[1024,2048]{1,0:T(8,128)(2,1)} %copy-done.7, f32[2048]{0:T(1024)S(1)} %bitcast.81, f32[1024]{0:T(1024)S(1)} %get-tuple-element.234), kind=kOutput, calls=%fused_computation.26 | convolution fusion | flops 6452412416 | bytes 13643776 | tf_op jit(solution)/shard_map/dot_general | solution.py:29
  132.0 8.2 %attend_forward.2 = (bf16[1024,512]{1,0:T(8,128)(2,1)}, bf16[8,1024,1024]{2,1,0:T(8,128)(2,1)}) custom-call(s32[1]{0:T(128)} %dynamic_slice.98.length, f32[4,2,2048]{2,1,0:T(2,128)S(1)} %reshape.185.rel_ref, bf16[1024,1536]{1,0:T(8,128)(2,1)S(1)} %convolution_convert_fusion.3.query_ref.key_ref.value_ref, ...), custom_call_target="tpu_custom_call" | custom-call | flops 2147483648 | bytes 4194304 | tf_op jit(solution)/shard_map/attend_forward/pallas_call | solution.py:91
  143.3 21.4 %attend_forward.3 = (bf16[1024,512]{1,0:T(8,128)(2,1)}, bf16[8,1024,1024]{2,1,0:T(8,128)(2,1)}) custom-call(s32[1]{0:T(128)} %dynamic_slice.98.length, f32[4,2,2048]{2,1,0:T(2,128)S(1)} %reshape.186.rel_ref, bf16[1024,1536]{1,0:T(8,128)(2,1)S(1)} %convolution_convert_fusion.3.query_ref.key_ref.value_ref, ...), custom_call_target="tpu_custom_call", output_to_operand_aliasing={{0}: (5, {}), {1}: (6, {})} | custom-call | flops 6442450944 | bytes 12582912 | tf_op jit(solution)/shard_map/attend_forward/pallas_call | solution.py:91
  167.7 2.4 convolution_convert_fusion.6
  170.7 3.3 broadcast_in_dim.80
  175.3 2.7 select_dynamic-update-slice_fusion.2
  178.0 2.6 select_dynamic-update-slice_fusion.1
  183.0 10.6 %collective-permute-done.6 = bf16[256,2048]{1,0:T(8,128)(2,1)S(1)} collective-permute-done((bf16[256,2048]{1,0:T(8,128)(2,1)S(1)}, bf16[256,2048]{1,0:T(8,128)(2,1)S(1)}, u32[]{:S(2)}, u32[]{:S(2)}) %collective-permute-start.6) | collective-permute-done | bytes 1048608 | tf_op jit(solution)/shard_map/ppermute | solution.py:242
  194.0 2.4 fusion.100
  196.4 2.5 fusion.102
  198.9 2.5 select_dynamic-update-slice_fusion
  201.4 15.5 %collective-permute-done.7 = bf16[256,2048]{1,0:T(8,128)(2,1)S(1)} collective-permute-done((bf16[256,2048]{1,0:T(8,128)(2,1)S(1)}, bf16[256,2048]{1,0:T(8,128)(2,1)S(1)}, u32[]{:S(2)}, u32[]{:S(2)}) %collective-permute-start.7) | collective-permute-done | bytes 1048608 | tf_op jit(solution)/shard_map/ppermute | solution.py:242
  217.3 21.0 %collective-permute-done.8 = bf16[256,2048]{1,0:T(8,128)(2,1)S(1)} collective-permute-done((bf16[256,2048]{1,0:T(8,128)(2,1)S(1)}, bf16[256,2048]{1,0:T(8,128)(2,1)S(1)}, u32[]{:S(2)}, u32[]{:S(2)}) %collective-permute-start.8) | collective-permute-done | bytes 1048608 | tf_op jit(solution)/shard_map/ppermute | solution.py:242
  242.5 5.9 fusion.137
  249.7 5.2 fusion.47
  255.0 8.4 %fusion.136 = f32[256,2048]{1,0:T(8,128)} fusion(bf16[2048,2560]{1,0:T(8,128)(2,1)} %all-gather.9.cloned.1.call-done, bf16[256,1280]{1,0:T(8,128)(2,1)S(1)} %get-tuple-element.219, bf16[256,1280]{1,0:T(8,128)(2,1)S(1)} %get-tuple-element.218), kind=kOutput, calls=%fused_computation.249 | convolution fusion | flops 2686976000 | bytes 13893632 | tf_op jit(solution)/shard_map/dot_general | solution.py:29
  264.3 6.0 fusion.138
  270.8 4.0 fusion.54
  276.0 7.8 %convolution_convert_fusion.5 = bf16[256,2048]{1,0:T(8,128)(2,1)} fusion(bf16[2048,2560]{1,0:T(8,128)(2,1)} %all-gather.9.cloned.1.call-done, bf16[256,1280]{1,0:T(8,128)(2,1)S(1)} %get-tuple-element.217, bf16[256,1280]{1,0:T(8,128)(2,1)S(1)} %get-tuple-element.216), kind=kOutput, calls=%fused_computation.39 | convolution fusion | flops 2687500288 | bytes 12845056 | tf_op jit(solution)/shard_map/dot_general | solution.py:29
  283.8 3.8 collective-permute-done.10
  287.6 5.9 fusion.139
  294.0 4.0 fusion.61
  300.0 5.8 fusion.135
  305.9 4.9 collective-permute-done.11
  310.9 5.9 fusion.140
  317.3 4.8 fusion.68
  324.4 8.7 %fusion.134 = f32[256,2048]{1,0:T(8,128)} fusion(bf16[2048,2560]{1,0:T(8,128)(2,1)} %all-gather.9.cloned.1.call-done, bf16[256,1280]{1,0:T(8,128)(2,1)} %copy-done.35, bf16[256,1280]{1,0:T(8,128)(2,1)} %copy-done.34), kind=kOutput, calls=%fused_computation.247 | convolution fusion | flops 2686976000 | bytes 13893632 | tf_op jit(solution)/shard_map/dot_general | solution.py:29
  334.8 16.7 %convolution_convert_fusion = bf16[2048,2560]{1,0:T(8,128)(2,1)} fusion(bf16[256,2560]{1,0:T(8,128)(2,1)} %pad_maximum_fusion.5, bf16[256,2560]{1,0:T(8,128)(2,1)} %pad_maximum_fusion.4, bf16[256,2560]{1,0:T(8,128)(2,1)} %pad_maximum_fusion.3, bf16[256,2560]{1,0:T(8,128)(2,1)S(1)} %pad_maximum_fusion.2, bf16[256,2048]{1,0:T(8,128)(2,1)} %collective-permute-done.11, ...), kind=kOutput, calls=%fused_computation.2 | convolution fusion | flops 10780409856 | bytes 19922944 | tf_op jit(solution)/shard_map/dot_general | solution.py:29
  351.5 3.6 collective-permute-done.13
  357.9 11.4 %convolution_convert_fusion.2 = bf16[1280,2048]{1,0:T(8,128)(2,1)} fusion(bf16[1024,1280]{1,0:T(8,128)(2,1)} %copy-done.21, bf16[1024,2048]{1,0:T(8,128)(2,1)} %select_dynamic-update-slice_fusion), kind=kOutput, calls=%fused_computation.9 | convolution fusion | flops 5371330560 | bytes 12058624 | tf_op jit(solution)/shard_map/dot_general | solution.py:29
  369.4 8.9 %collective-permute-done.14 = bf16[256,2048]{1,0:T(8,128)(2,1)S(1)} collective-permute-done((bf16[256,2048]{1,0:T(8,128)(2,1)S(1)}, bf16[256,2048]{1,0:T(8,128)(2,1)S(1)}, u32[]{:S(2)}, u32[]{:S(2)}) %collective-permute-start.14) | collective-permute-done | bytes 1048608 | tf_op jit(solution)/shard_map/ppermute | solution.py:242
  378.9 2.4 subtract_convert_fusion
  388.6 16.8 %collective-permute-done.15 = bf16[256,2048]{1,0:T(8,128)(2,1)S(1)} collective-permute-done((bf16[256,2048]{1,0:T(8,128)(2,1)S(1)}, bf16[256,2048]{1,0:T(8,128)(2,1)S(1)}, u32[]{:S(2)}, u32[]{:S(2)}) %collective-permute-start.15) | collective-permute-done | bytes 1048608 | tf_op jit(solution)/shard_map/ppermute | solution.py:242
  408.4 21.9 %collective-permute-done.16 = bf16[256,2048]{1,0:T(8,128)(2,1)S(1)} collective-permute-done((bf16[256,2048]{1,0:T(8,128)(2,1)S(1)}, bf16[256,2048]{1,0:T(8,128)(2,1)S(1)}, u32[]{:S(2)}, u32[]{:S(2)}) %collective-permute-start.16) | collective-permute-done | bytes 1048608 | tf_op jit(solution)/shard_map/ppermute | solution.py:242
  434.3 12.8 %collective-permute-done.17 = bf16[256,2048]{1,0:T(8,128)(2,1)S(1)} collective-permute-done((bf16[256,2048]{1,0:T(8,128)(2,1)S(1)}, bf16[256,2048]{1,0:T(8,128)(2,1)S(1)}, u32[]{:S(2)}, u32[]{:S(2)}) %collective-permute-start.17) | collective-permute-done | bytes 1048608 | tf_op jit(solution)/shard_map/ppermute | solution.py:242
  448.9 5.3 convolution_convert_fusion.4
  454.2 6.8 %pad_maximum_fusion = bf16[1792,2048]{1,0:T(8,128)(2,1)} fusion(bf16[1280,2048]{1,0:T(8,128)(2,1)} %convolution_convert_fusion.2, bf16[512,2048]{1,0:T(8,128)(2,1)S(1)} %convolution_convert_fusion.4), kind=kLoop, calls=%fused_computation.10 | loop fusion | flops 14680064 | bytes 14680064 | tf_op jit(solution)/shard_map/concatenate | solution.py:506
  461.2 17.1 %attend_backward.2 = (bf16[1024,1536]{1,0:T(8,128)(2,1)S(1)}, f32[2,2,2048]{2,1,0:T(2,128)S(1)}) custom-call(bf16[8,1024,1024]{2,1,0:T(8,128)(2,1)} %get-tuple-element.124.soft_ref, bf16[1024,1536]{1,0:T(8,128)(2,1)} %copy-done.2, bf16[1024,512]{1,0:T(8,128)(2,1)S(1)} %fusion.82.grad_ref, bf16[1024,512]{1,0:T(8,128)(2,1)} %get-tuple-element.127.out_ref, ...), custom_call_target="tpu_custom_call" | custom-call | flops 10737418240 | bytes 8388608 | tf_op jit(solution)/shard_map/attend_backward/pallas_call | solution.py:207
  479.9 4.0 collective-permute-done.18
  485.9 17.9 %attend_backward.3 = (bf16[1024,1536]{1,0:T(8,128)(2,1)S(1)}, f32[2,2,2048]{2,1,0:T(2,128)S(1)}) custom-call(bf16[8,1024,1024]{2,1,0:T(8,128)(2,1)} %get-tuple-element.124.soft_ref, bf16[1024,1536]{1,0:T(8,128)(2,1)} %copy-done.2, bf16[1024,512]{1,0:T(8,128)(2,1)S(1)} %copy-done.5, bf16[1024,512]{1,0:T(8,128)(2,1)} %get-tuple-element.127.out_ref, ...), custom_call_target="tpu_custom_call" | custom-call | flops 10737418240 | bytes 8388608 | tf_op jit(solution)/shard_map/attend_backward/pallas_call | solution.py:207
  503.8 2.8 collective-permute-done.19
  506.5 4.6 fusion.38
  511.2 9.1 %convolution_convert_fusion.1 = bf16[2048,1536]{1,0:T(8,128)(2,1)} fusion(bf16[1024,1536]{1,0:T(8,128)(2,1)S(1)} %get-tuple-element.179, bf16[1024,2048]{1,0:T(8,128)(2,1)S(1)} %copy-done.8, f32[2048]{0:T(1024)S(1)} %bitcast.82, f32[1024]{0:T(1024)S(1)} %copy-done.45), kind=kOutput, calls=%fused_computation.8 | convolution fusion | flops 6453985280 | bytes 13643776 | tf_op jit(solution)/shard_map/dot_general | solution.py:29
  520.3 4.6 fusion.34
  524.9 7.8 %collective-permute-done.20 = bf16[1024,512]{1,0:T(8,128)(2,1)} collective-permute-done((bf16[1024,512]{1,0:T(8,128)(2,1)}, bf16[1024,512]{1,0:T(8,128)(2,1)}, u32[]{:S(2)}, u32[]{:S(2)}) %collective-permute-start.20) | collective-permute-done | bytes 1048608 | tf_op jit(solution)/shard_map/ppermute | solution.py:242
  534.1 3.6 add_convert_fusion.3
  540.2 4.8 fusion.32
  545.0 17.1 %collective-permute-done.21 = bf16[1024,512]{1,0:T(8,128)(2,1)} collective-permute-done((bf16[1024,512]{1,0:T(8,128)(2,1)}, bf16[1024,512]{1,0:T(8,128)(2,1)}, u32[]{:S(2)}, u32[]{:S(2)}) %collective-permute-start.21) | collective-permute-done | bytes 1048608 | tf_op jit(solution)/shard_map/ppermute | solution.py:242
  562.1 3.2 add_convert_fusion.2
  565.3 4.7 fusion.30
  571.5 4.2 collective-permute-start.25
  575.7 8.7 %collective-permute-done.24 = f32[8,128]{1,0:T(8,128)S(1)} collective-permute-done((f32[8,128]{1,0:T(8,128)S(1)}, f32[8,128]{1,0:T(8,128)S(1)}, u32[]{:S(2)}, u32[]{:S(2)}) %collective-permute-start.24) | collective-permute-done | bytes 4128 | tf_op jit(solution)/shard_map/ppermute | solution.py:274
  589.1 3.5 fusion.29
  595.6 4.2 collective-permute-done.25
  599.9 7.8 %all_gather.20 = f32[8,41,128]{2,1,0:T(8,128)S(1)} all-gather(f32[1,41,128]{2,1,0:T(8,128)S(1)} %bitcast.76), channel_id=1, replica_groups=mesh['dp'=8,'mp'=4] {'dp'}, dimensions={0}, use_global_device_ids=true | all-gather | bytes 188928 | tf_op jit(solution)/shard_map/all_gather | solution.py:567
  607.8 3.6 all-to-all-start.1
  611.6 3.2 fusion.83
  619.9 2.5 multiply_add_fusion
  (303 shorter events, 92.9 us)
Async XLA Ops:
  7.2 30.7 %collective-permute-start = (bf16[1024,512]{1,0:T(8,128)(2,1)}, bf16[1024,512]{1,0:T(8,128)(2,1)}, u32[]{:S(2)}, u32[]{:S(2)}) collective-permute-start(bf16[1024,512]{1,0:T(8,128)(2,1)} %bitcast.70), channel_id=1, source_target_pairs={{0,1},{1,2},{2,3},{3,0},{4,5},{5,6},{6,7},{7,4},{8,9},{9,10},{10,1... | collective-permute-start | bytes 3145736 | tf_op jit(solution)/shard_map/ppermute | solution.py:242
  12.3 23.4 %copy-start.41 = (f32[256,512]{1,0:T(8,128)S(1)}, f32[256,512]{1,0:T(8,128)}, u32[]{:S(2)}) copy-start(f32[256,512]{1,0:T(8,128)} %param.32) | copy-start | bytes 1572868
  12.3 23.5 %copy-start.42 = (f32[256,512]{1,0:T(8,128)S(1)}, f32[256,512]{1,0:T(8,128)}, u32[]{:S(2)}) copy-start(f32[256,512]{1,0:T(8,128)} %param.33) | copy-start | bytes 1572868
  13.4 24.5 %all-to-all-start = ((bf16[8,128,512]{2,1,0:T(8,128)(2,1)}), bf16[8,128,512]{2,1,0:T(8,128)(2,1)S(1)}, u32[]{:S(2)}, u32[]{:S(2)}) async-start(bf16[8,128,512]{2,1,0:T(8,128)(2,1)} %broadcast_select_fusion.1), calls=%async_computation | async-start | bytes 2097152 | tf_op jit(solution)/shard_map/all_to_all | solution.py:321
  17.1 104.2 %all-gather.5.cloned.1.call-start = ((), (), s32[]{:S(2)}) async-start(), calls=%async_computation.5 | async-start | bytes 7077888 | tf_op jit(solution)/shard_map/all_gather | solution.py:362
  37.9 59.9 %copy-start.9 = (bf16[8,128,512]{2,1,0:T(8,128)(2,1)}, bf16[8,128,512]{2,1,0:T(8,128)(2,1)S(1)}, u32[]{:S(2)}) copy-start(bf16[8,128,512]{2,1,0:T(8,128)(2,1)S(1)} %all-to-all-done) | copy-start | bytes 3145732
  38.0 129.8 %all-gather.7.cloned.1.call-start = ((), (), s32[]{:S(2)}) async-start(), calls=%async_computation.6 | async-start | bytes 8257536 | tf_op jit(solution)/shard_map/all_gather | solution.py:369
  38.0 27.2 %collective-permute-start.1 = (bf16[1024,512]{1,0:T(8,128)(2,1)S(1)}, bf16[1024,512]{1,0:T(8,128)(2,1)S(1)}, u32[]{:S(2)}, u32[]{:S(2)}) collective-permute-start(bf16[1024,512]{1,0:T(8,128)(2,1)S(1)} %bitcast.62), channel_id=1, source_target_pairs={{0,1},{1,2},{2,3},{3,0},{4,5},{5,6},{6,7},{7,4},{8,9},{9,10},{10,1... | collective-permute-start | bytes 3145736 | tf_op jit(solution)/shard_map/ppermute | solution.py:242
  40.8 24.6 %copy-start.24 = (f32[256,1280]{1,0:T(8,128)S(1)}, f32[256,1280]{1,0:T(8,128)}, u32[]{:S(2)}) copy-start(f32[256,1280]{1,0:T(8,128)} %param.36) | copy-start | bytes 3932164
  65.3 177.2 %all-gather.9.cloned.1.call-start = ((), (), s32[]{:S(2)}) async-start(), calls=%async_computation.7 | async-start | bytes 11796480 | tf_op jit(solution)/shard_map/all_gather | solution.py:371
  65.3 26.5 %collective-permute-start.2 = (bf16[1024,512]{1,0:T(8,128)(2,1)S(1)}, bf16[1024,512]{1,0:T(8,128)(2,1)}, u32[]{:S(2)}, u32[]{:S(2)}) collective-permute-start(bf16[1024,512]{1,0:T(8,128)(2,1)S(1)} %collective-permute-done.1), channel_id=1, source_target_pairs={{0,1},{1,2},{2,3},{3,0},{4,5},{5,6},{6,7},{7,4},{8,9},{9,10},{10,1... | collective-permute-start | bytes 3145736 | tf_op jit(solution)/shard_map/ppermute | solution.py:242
  67.1 25.0 %copy-start.58 = (s32[8]{0:T(128)S(1)}, s32[8]{0:T(128)}, u32[]{:S(2)}) copy-start(s32[8]{0:T(128)} %param.30) | copy-start | bytes 100
  67.1 27.6 %copy-start.57 = (s32[8]{0:T(128)S(1)}, s32[8]{0:T(128)}, u32[]{:S(2)}) copy-start(s32[8]{0:T(128)} %param.29) | copy-start | bytes 100
  67.1 28.1 %copy-start.48 = (s32[2047]{0:T(1024)S(1)}, s32[2047]{0:T(1024)}, u32[]{:S(2)}) copy-start(s32[2047]{0:T(1024)} %param.31) | copy-start | bytes 24568
  91.9 392.0 %reduce-scatter.4.cloned.1.call-start = ((), (), s32[]{:S(2)}) async-start(), calls=%async_computation.8 | async-start | bytes 11796480 | tf_op jit(solution)/shard_map/reduce_scatter | solution.py:459
  92.0 25.7 %collective-permute-start.3 = (bf16[1024,512]{1,0:T(8,128)(2,1)}, bf16[1024,512]{1,0:T(8,128)(2,1)S(1)}, u32[]{:S(2)}, u32[]{:S(2)}) collective-permute-start(bf16[1024,512]{1,0:T(8,128)(2,1)} %collective-permute-done.2), channel_id=1, source_target_pairs={{0,1},{1,2},{2,3},{3,0},{4,5},{5,6},{6,7},{7,4},{8,9},{9,10},{10,1... | collective-permute-start | bytes 3145736 | tf_op jit(solution)/shard_map/ppermute | solution.py:242
  95.9 25.4 %copy-start.46 = (f32[1,2,8,128]{3,1,2,0:T(2,128)}, f32[1,2,8,128]{3,1,2,0:T(2,128)S(1)}, u32[]{:S(2)}) copy-start(f32[1,2,8,128]{3,1,2,0:T(2,128)S(1)} %copy.44) | copy-start | bytes 24580
  117.7 24.9 %collective-permute-start.4 = (bf16[1024,512]{1,0:T(8,128)(2,1)}, bf16[1024,512]{1,0:T(8,128)(2,1)}, u32[]{:S(2)}, u32[]{:S(2)}) collective-permute-start(bf16[1024,512]{1,0:T(8,128)(2,1)} %collective-permute-done), channel_id=1, source_target_pairs={{0,1},{1,2},{2,3},{3,0},{4,5},{5,6},{6,7},{7,4},{8,9},{9,10},{10,1... | collective-permute-start | bytes 3145736 | tf_op jit(solution)/shard_map/ppermute | solution.py:242
  121.3 10.7 %copy-start.44 = (f32[1024]{0:T(1024)}, f32[1024]{0:T(1024)S(1)}, u32[]{:S(2)}) copy-start(f32[1024]{0:T(1024)S(1)} %get-tuple-element.234) | copy-start | bytes 12292
  132.0 11.2 %copy-start.2 = (bf16[1024,1536]{1,0:T(8,128)(2,1)}, bf16[1024,1536]{1,0:T(8,128)(2,1)S(1)}, u32[]{:S(2)}) copy-start(bf16[1024,1536]{1,0:T(8,128)(2,1)S(1)} %convolution_convert_fusion.3.query_ref.key_ref.value_ref) | copy-start | bytes 9437188
  142.6 23.9 %collective-permute-start.5 = (bf16[1024,512]{1,0:T(8,128)(2,1)}, bf16[1024,512]{1,0:T(8,128)(2,1)}, u32[]{:S(2)}, u32[]{:S(2)}) collective-permute-start(bf16[1024,512]{1,0:T(8,128)(2,1)} %collective-permute-done.4), channel_id=1, source_target_pairs={{0,1},{1,2},{2,3},{3,0},{4,5},{5,6},{6,7},{7,4},{8,9},{9,10},{10,1... | collective-permute-start | bytes 3145736 | tf_op jit(solution)/shard_map/ppermute | solution.py:242
  170.1 23.5 %collective-permute-start.6 = (bf16[256,2048]{1,0:T(8,128)(2,1)S(1)}, bf16[256,2048]{1,0:T(8,128)(2,1)S(1)}, u32[]{:S(2)}, u32[]{:S(2)}) collective-permute-start(bf16[256,2048]{1,0:T(8,128)(2,1)S(1)} %convolution_convert_fusion.6), channel_id=1, source_target_pairs={{0,1},{1,2},{2,3},{3,0},{4,5},{5,6},{6,7},{7,4},{8,9},{9,10},{10,1... | collective-permute-start | bytes 3145736 | tf_op jit(solution)/shard_map/ppermute | solution.py:242
  193.9 23.0 %collective-permute-start.7 = (bf16[256,2048]{1,0:T(8,128)(2,1)S(1)}, bf16[256,2048]{1,0:T(8,128)(2,1)S(1)}, u32[]{:S(2)}, u32[]{:S(2)}) collective-permute-start(bf16[256,2048]{1,0:T(8,128)(2,1)S(1)} %add_convert_fusion.8), channel_id=1, source_target_pairs={{0,1},{1,2},{2,3},{3,0},{4,5},{5,6},{6,7},{7,4},{8,9},{9,10},{10,1... | collective-permute-start | bytes 3145736 | tf_op jit(solution)/shard_map/ppermute | solution.py:242
  217.2 21.1 %collective-permute-start.8 = (bf16[256,2048]{1,0:T(8,128)(2,1)S(1)}, bf16[256,2048]{1,0:T(8,128)(2,1)S(1)}, u32[]{:S(2)}, u32[]{:S(2)}) collective-permute-start(bf16[256,2048]{1,0:T(8,128)(2,1)S(1)} %add_convert_fusion.7), channel_id=1, source_target_pairs={{0,1},{1,2},{2,3},{3,0},{4,5},{5,6},{6,7},{7,4},{8,9},{9,10},{10,1... | collective-permute-start | bytes 3145736 | tf_op jit(solution)/shard_map/ppermute | solution.py:242
  242.5 21.7 %collective-permute-start.9 = (bf16[256,2048]{1,0:T(8,128)(2,1)}, bf16[256,2048]{1,0:T(8,128)(2,1)}, u32[]{:S(2)}, u32[]{:S(2)}) collective-permute-start(bf16[256,2048]{1,0:T(8,128)(2,1)} %multiply_convert_fusion), channel_id=1, source_target_pairs={{0,1},{1,2},{2,3},{3,0},{4,5},{5,6},{6,7},{7,4},{8,9},{9,10},{10,1... | collective-permute-start | bytes 3145736 | tf_op jit(solution)/shard_map/ppermute | solution.py:242
  255.0 15.7 %slice-start = ((s8[7340032]{0:T(1024)(128)(4,1)}), s8[4194304]{0:T(1024)(128)(4,1)S(1)}, s32[]{:S(2)}) async-start(s8[7340032]{0:T(1024)(128)(4,1)} %bitcast.66), calls=%async_computation.11 | async-start | bytes 8388608
  263.4 7.3 %slice-start.1 = ((s8[7340032]{0:T(1024)(128)(4,1)}), s8[3145728]{0:T(1024)(128)(4,1)S(1)}, s32[]{:S(2)}) async-start(s8[7340032]{0:T(1024)(128)(4,1)} %bitcast.66), calls=%async_computation.12 | async-start | bytes 6291456
  264.1 23.5 %collective-permute-start.10 = (bf16[256,2048]{1,0:T(8,128)(2,1)}, bf16[256,2048]{1,0:T(8,128)(2,1)}, u32[]{:S(2)}, u32[]{:S(2)}) collective-permute-start(bf16[256,2048]{1,0:T(8,128)(2,1)} %collective-permute-done.9), channel_id=1, source_target_pairs={{0,1},{1,2},{2,3},{3,0},{4,5},{5,6},{6,7},{7,4},{8,9},{9,10},{10,1... | collective-permute-start | bytes 3145736 | tf_op jit(solution)/shard_map/ppermute | solution.py:242
  287.6 23.1 %collective-permute-start.11 = (bf16[256,2048]{1,0:T(8,128)(2,1)}, bf16[256,2048]{1,0:T(8,128)(2,1)}, u32[]{:S(2)}, u32[]{:S(2)}) collective-permute-start(bf16[256,2048]{1,0:T(8,128)(2,1)} %collective-permute-done.10), channel_id=1, source_target_pairs={{0,1},{1,2},{2,3},{3,0},{4,5},{5,6},{6,7},{7,4},{8,9},{9,10},{10,1... | collective-permute-start | bytes 3145736 | tf_op jit(solution)/shard_map/ppermute | solution.py:242
  310.7 22.4 %collective-permute-start.12 = (bf16[256,2048]{1,0:T(8,128)(2,1)}, bf16[256,2048]{1,0:T(8,128)(2,1)S(1)}, u32[]{:S(2)}, u32[]{:S(2)}) collective-permute-start(bf16[256,2048]{1,0:T(8,128)(2,1)} %convolution_convert_fusion.5), channel_id=1, source_target_pairs={{0,1},{1,2},{2,3},{3,0},{4,5},{5,6},{6,7},{7,4},{8,9},{9,10},{10,1... | collective-permute-start | bytes 3145736 | tf_op jit(solution)/shard_map/ppermute | solution.py:242
  334.4 20.7 %collective-permute-start.13 = (bf16[256,2048]{1,0:T(8,128)(2,1)}, bf16[256,2048]{1,0:T(8,128)(2,1)}, u32[]{:S(2)}, u32[]{:S(2)}) collective-permute-start(bf16[256,2048]{1,0:T(8,128)(2,1)} %add_convert_fusion.6), channel_id=1, source_target_pairs={{0,1},{1,2},{2,3},{3,0},{4,5},{5,6},{6,7},{7,4},{8,9},{9,10},{10,1... | collective-permute-start | bytes 3145736 | tf_op jit(solution)/shard_map/ppermute | solution.py:242
  355.1 189.9 %reduce-scatter.6.cloned.1.call-start = ((), (), s32[]{:S(2)}) async-start(), calls=%async_computation.9 | async-start | bytes 8257536 | tf_op jit(solution)/shard_map/reduce_scatter | solution.py:507
  355.2 26.3 %slice-start.2 = ((s8[7340032]{0:T(1024)(128)(4,1)}), s8[4194304]{0:T(1024)(128)(4,1)S(1)}, s32[]{:S(2)}) async-start(s8[7340032]{0:T(1024)(128)(4,1)} %bitcast.68), calls=%async_computation.13 | async-start | bytes 8388608
  357.5 20.8 %copy-start.11 = (f32[256,2048]{1,0:T(8,128)S(1)}, f32[256,2048]{1,0:T(8,128)}, u32[]{:S(2)}) copy-start(f32[256,2048]{1,0:T(8,128)} %fusion.136) | copy-start | bytes 6291460
  357.5 24.0 %slice-start.3 = ((s8[7340032]{0:T(1024)(128)(4,1)}), s8[3145728]{0:T(1024)(128)(4,1)S(1)}, s32[]{:S(2)}) async-start(s8[7340032]{0:T(1024)(128)(4,1)} %bitcast.68), calls=%async_computation.14 | async-start | bytes 6291456
  357.5 20.8 %collective-permute-start.14 = (bf16[256,2048]{1,0:T(8,128)(2,1)S(1)}, bf16[256,2048]{1,0:T(8,128)(2,1)S(1)}, u32[]{:S(2)}, u32[]{:S(2)}) collective-permute-start(bf16[256,2048]{1,0:T(8,128)(2,1)S(1)} %add_convert_fusion.5), channel_id=1, source_target_pairs={{0,1},{1,2},{2,3},{3,0},{4,5},{5,6},{6,7},{7,4},{8,9},{9,10},{10,1... | collective-permute-start | bytes 3145736 | tf_op jit(solution)/shard_map/ppermute | solution.py:242
  381.4 24.1 %collective-permute-start.15 = (bf16[256,2048]{1,0:T(8,128)(2,1)S(1)}, bf16[256,2048]{1,0:T(8,128)(2,1)S(1)}, u32[]{:S(2)}, u32[]{:S(2)}) collective-permute-start(bf16[256,2048]{1,0:T(8,128)(2,1)S(1)} %subtract_convert_fusion), channel_id=1, source_target_pairs={{0,1},{1,2},{2,3},{3,0},{4,5},{5,6},{6,7},{7,4},{8,9},{9,10},{10,1... | collective-permute-start | bytes 3145736 | tf_op jit(solution)/shard_map/ppermute | solution.py:242
  388.5 18.8 %copy-start.15 = (f32[1024,512]{1,0:T(8,128)}, f32[1024,512]{1,0:T(8,128)S(1)}, u32[]{:S(2)}) copy-start(f32[1024,512]{1,0:T(8,128)S(1)} %get-tuple-element.200) | copy-start | bytes 6291460
  388.6 18.8 %copy-start.16 = (f32[1024,512]{1,0:T(8,128)}, f32[1024,512]{1,0:T(8,128)S(1)}, u32[]{:S(2)}) copy-start(f32[1024,512]{1,0:T(8,128)S(1)} %get-tuple-element.187) | copy-start | bytes 6291460
  388.6 18.8 %copy-start.18 = (f32[1024,512]{1,0:T(8,128)}, f32[1024,512]{1,0:T(8,128)S(1)}, u32[]{:S(2)}) copy-start(f32[1024,512]{1,0:T(8,128)S(1)} %get-tuple-element.176) | copy-start | bytes 6291460
  405.4 24.9 %collective-permute-start.16 = (bf16[256,2048]{1,0:T(8,128)(2,1)S(1)}, bf16[256,2048]{1,0:T(8,128)(2,1)S(1)}, u32[]{:S(2)}, u32[]{:S(2)}) collective-permute-start(bf16[256,2048]{1,0:T(8,128)(2,1)S(1)} %collective-permute-done.15), channel_id=1, source_target_pairs={{0,1},{1,2},{2,3},{3,0},{4,5},{5,6},{6,7},{7,4},{8,9},{9,10},{10,1... | collective-permute-start | bytes 3145736 | tf_op jit(solution)/shard_map/ppermute | solution.py:242
  430.3 16.7 %collective-permute-start.17 = (bf16[256,2048]{1,0:T(8,128)(2,1)S(1)}, bf16[256,2048]{1,0:T(8,128)(2,1)S(1)}, u32[]{:S(2)}, u32[]{:S(2)}) collective-permute-start(bf16[256,2048]{1,0:T(8,128)(2,1)S(1)} %collective-permute-done.16), channel_id=1, source_target_pairs={{0,1},{1,2},{2,3},{3,0},{4,5},{5,6},{6,7},{7,4},{8,9},{9,10},{10,1... | collective-permute-start | bytes 3145736 | tf_op jit(solution)/shard_map/ppermute | solution.py:242
  448.9 12.2 %copy-start.4 = (bf16[1024,512]{1,0:T(8,128)(2,1)}, bf16[1024,512]{1,0:T(8,128)(2,1)S(1)}, u32[]{:S(2)}) copy-start(bf16[1024,512]{1,0:T(8,128)(2,1)S(1)} %fusion.82.grad_ref) | copy-start | bytes 3145732
  461.0 131.8 %reduce-scatter.8.cloned.1.call-start = ((), (), s32[]{:S(2)}) async-start(), calls=%async_computation.10 | async-start | bytes 7077888 | tf_op jit(solution)/shard_map/reduce_scatter | solution.py:527
  461.1 22.8 %collective-permute-start.18 = (bf16[1024,512]{1,0:T(8,128)(2,1)}, bf16[1024,512]{1,0:T(8,128)(2,1)}, u32[]{:S(2)}, u32[]{:S(2)}) collective-permute-start(bf16[1024,512]{1,0:T(8,128)(2,1)} %convert_element_type.243), channel_id=1, source_target_pairs={{0,1},{1,2},{2,3},{3,0},{4,5},{5,6},{6,7},{7,4},{8,9},{9,10},{10,1... | collective-permute-start | bytes 3145736 | tf_op jit(solution)/shard_map/ppermute | solution.py:242
  461.2 22.8 %copy-start.19 = (f32[1024,512]{1,0:T(8,128)S(1)}, f32[1024,512]{1,0:T(8,128)}, u32[]{:S(2)}) copy-start(f32[1024,512]{1,0:T(8,128)} %copy-done.18) | copy-start | bytes 6291460
  485.6 20.9 %collective-permute-start.19 = (bf16[1024,512]{1,0:T(8,128)(2,1)S(1)}, bf16[1024,512]{1,0:T(8,128)(2,1)S(1)}, u32[]{:S(2)}, u32[]{:S(2)}) collective-permute-start(bf16[1024,512]{1,0:T(8,128)(2,1)S(1)} %add_convert_fusion.4), channel_id=1, source_target_pairs={{0,1},{1,2},{2,3},{3,0},{4,5},{5,6},{6,7},{7,4},{8,9},{9,10},{10,1... | collective-permute-start | bytes 3145736 | tf_op jit(solution)/shard_map/ppermute | solution.py:242
  511.2 21.5 %collective-permute-start.20 = (bf16[1024,512]{1,0:T(8,128)(2,1)}, bf16[1024,512]{1,0:T(8,128)(2,1)}, u32[]{:S(2)}, u32[]{:S(2)}) collective-permute-start(bf16[1024,512]{1,0:T(8,128)(2,1)} %fusion.38), channel_id=1, source_target_pairs={{0,1},{1,2},{2,3},{3,0},{4,5},{5,6},{6,7},{7,4},{8,9},{9,10},{10,1... | collective-permute-start | bytes 3145736 | tf_op jit(solution)/shard_map/ppermute | solution.py:242
  524.9 7.8 %copy-start.59 = (s32[8]{0:T(128)S(1)}, s32[8]{0:T(128)}, u32[]{:S(2)}) copy-start(s32[8]{0:T(128)} %param.30) | copy-start | bytes 100
  524.9 8.6 %copy-start.50 = (s32[2048]{0:T(1024)S(1)}, s32[2048]{0:T(1024)}, u32[]{:S(2)}) copy-start(s32[2048]{0:T(1024)} %copy-done.49) | copy-start | bytes 24580
  537.7 24.4 %collective-permute-start.21 = (bf16[1024,512]{1,0:T(8,128)(2,1)}, bf16[1024,512]{1,0:T(8,128)(2,1)}, u32[]{:S(2)}, u32[]{:S(2)}) collective-permute-start(bf16[1024,512]{1,0:T(8,128)(2,1)} %add_convert_fusion.3), channel_id=1, source_target_pairs={{0,1},{1,2},{2,3},{3,0},{4,5},{5,6},{6,7},{7,4},{8,9},{9,10},{10,1... | collective-permute-start | bytes 3145736 | tf_op jit(solution)/shard_map/ppermute | solution.py:242
  540.1 29.9 %collective-permute-start.23 = (f32[8,128]{1,0:T(8,128)S(1)}, f32[8,128]{1,0:T(8,128)S(1)}, u32[]{:S(2)}, u32[]{:S(2)}) collective-permute-start(f32[8,128]{1,0:T(8,128)S(1)} %bitcast.79), channel_id=1, source_target_pairs={{0,1},{1,0},{2,3},{3,2},{4,5},{5,4},{6,7},{7,6},{8,9},{9,8},{10,11... | collective-permute-start | bytes 12296 | tf_op jit(solution)/shard_map/ppermute | solution.py:274
  565.3 23.4 %collective-permute-start.22 = (bf16[1024,512]{1,0:T(8,128)(2,1)}, bf16[1024,512]{1,0:T(8,128)(2,1)}, u32[]{:S(2)}, u32[]{:S(2)}) collective-permute-start(bf16[1024,512]{1,0:T(8,128)(2,1)} %add_convert_fusion.2), channel_id=1, source_target_pairs={{0,1},{1,2},{2,3},{3,0},{4,5},{5,6},{6,7},{7,4},{8,9},{9,10},{10,1... | collective-permute-start | bytes 3145736 | tf_op jit(solution)/shard_map/ppermute | solution.py:242
  570.0 14.4 %copy-start.14 = (bf16[1792,256]{1,0:T(8,128)(2,1)S(1)}, bf16[1792,256]{1,0:T(8,128)(2,1)}, u32[]{:S(2)}) copy-start(bf16[1792,256]{1,0:T(8,128)(2,1)} %reduce-scatter.6.cloned.1.call-done) | copy-start | bytes 2752516
  570.0 19.0 %copy-start.10 = (bf16[8,128,512]{2,1,0:T(8,128)(2,1)S(1)}, bf16[8,128,512]{2,1,0:T(8,128)(2,1)}, u32[]{:S(2)}) copy-start(bf16[8,128,512]{2,1,0:T(8,128)(2,1)} %copy-done.9) | copy-start | bytes 3145732
  570.0 19.0 %copy-start.43 = (f32[1024]{0:T(1024)S(1)}, f32[1024]{0:T(1024)}, u32[]{:S(2)}) copy-start(f32[1024]{0:T(1024)} %get-tuple-element.233) | copy-start | bytes 12292
  570.0 14.3 %collective-permute-start.24 = (f32[8,128]{1,0:T(8,128)S(1)}, f32[8,128]{1,0:T(8,128)S(1)}, u32[]{:S(2)}, u32[]{:S(2)}) collective-permute-start(f32[8,128]{1,0:T(8,128)S(1)} %bitcast_add_fusion), channel_id=1, source_target_pairs={{0,2},{1,3},{2,0},{3,1},{4,6},{5,7},{6,4},{7,5},{8,10},{9,11},{10,... | collective-permute-start | bytes 12296 | tf_op jit(solution)/shard_map/ppermute | solution.py:274
  571.5 28.4 %collective-permute-start.25 = (bf16[1024,512]{1,0:T(8,128)(2,1)}, bf16[1024,512]{1,0:T(8,128)(2,1)S(1)}, u32[]{:S(2)}, u32[]{:S(2)}) collective-permute-start(bf16[1024,512]{1,0:T(8,128)(2,1)} %add_convert_fusion.1), channel_id=1, source_target_pairs={{0,1},{1,2},{2,3},{3,0},{4,5},{5,6},{6,7},{7,4},{8,9},{9,10},{10,1... | collective-permute-start | bytes 3145736 | tf_op jit(solution)/shard_map/ppermute | solution.py:242
  599.9 7.9 %copy-start.31 = (bf16[1024,512]{1,0:T(8,128)(2,1)}, bf16[1024,512]{1,0:T(8,128)(2,1)S(1)}, u32[]{:S(2)}) copy-start(bf16[1024,512]{1,0:T(8,128)(2,1)S(1)} %collective-permute-done.25) | copy-start | bytes 3145732
  607.7 3.9 collective-permute-start.26
  607.8 19.2 %all-to-all-start.1 = ((bf16[8,128,512]{2,1,0:T(8,128)(2,1)}), bf16[8,128,512]{2,1,0:T(8,128)(2,1)S(1)}, u32[]{:S(2)}, u32[]{:S(2)}) async-start(bf16[8,128,512]{2,1,0:T(8,128)(2,1)} %bitcast.13), calls=%async_computation.4 | async-start | bytes 2097152 | tf_op jit(solution)/shard_map/all_to_all | solution.py:569
  611.6 7.4 %copy-start.37 = (f32[512,256]{1,0:T(8,128)S(1)}, f32[512,256]{1,0:T(8,128)}, u32[]{:S(2)}) copy-start(f32[512,256]{1,0:T(8,128)} %param.45) | copy-start | bytes 1572868
  611.6 4.8 collective-permute-start.27
  611.6 12.1 %copy-start.52 = (f32[4,8]{1,0:T(4,128)S(1)}, f32[4,8]{1,0:T(4,128)}, u32[]{:S(2)}) copy-start(f32[4,8]{1,0:T(4,128)} %param.51) | copy-start | bytes 388
  (36 other events, 115.7 us)
Sparse Core Ops, SparseCore 0:
  38.1 43.8 all-gather.4
  84.5 51.2 all-gather.6
  138.3 63.2 all-gather.8
  355.2 79.4 reduce-scatter.3
  461.2 62.7 reduce-scatter.5
  532.9 58.1 reduce-scatter.7

commit v6 on v5

--- a/solution.py
+++ b/solution.py
@@ -325,10 +325,7 @@
     features = quarter * tensor_count
     part_rows = seq_len // tensor_count
 
-    small = jnp.concatenate([attn_gain, ffn_gain, bias_table.reshape(-1)]).astype(low)
-    x_own, grad_next, small = together(
-        x_own, around(output_grad[0]), lax.all_gather(small, "dp", axis=0)
-    )
+    x_own, grad_next = together(x_own, around(output_grad[0]))
     grad_parts = [output_grad[0], grad_next]
     row_valid = lax.broadcasted_iota(jnp.int32, (seq_len, 1), 0) < length
 
@@ -353,10 +350,6 @@
             whole = set_columns(whole, part, step)
         return whole
 
-    gain_size = attn_gain.shape[0]
-    first_gain = small[:, :gain_size].reshape(-1).astype(f32)
-    second_gain = small[:, gain_size : 2 * gain_size].reshape(-1).astype(f32)
-    full_table = small[:, 2 * gain_size :].reshape(NB, bias_table.shape[1])
     qkv_weight = jnp.concatenate([query_weight, key_weight, value_weight], axis=1).astype(low)
     qkv_weight, x_own = together(qkv_weight, x_own)
     qkv_weight = lax.all_gather(qkv_weight, "dp", axis=0, tiled=True)
@@ -364,11 +357,20 @@
     out_down = jnp.concatenate([out_weight, down_weight], axis=0).astype(low)
     heads_columns = out_weight.shape[0]
     units = down_weight.shape[0]
-    x_parts = ring_gather(x_own)
+    x_parts = [x_own, around(x_own)]
+    small = jnp.concatenate([attn_gain, ffn_gain, bias_table.reshape(-1)]).astype(low)
+    small, x_parts[1] = together(lax.all_gather(small, "dp", axis=0), x_parts[1])
+    for step in range(1, tensor_count - 1):
+        x_parts.append(around(x_parts[step]))
     out_down, x_parts[1] = together(out_down, x_parts[1])
     out_down = lax.all_gather(out_down, "dp", axis=1, tiled=True)
     gate_up, x_parts[2] = together(gate_up, x_parts[2])
     gate_up = lax.all_gather(gate_up, "dp", axis=0, tiled=True)
+
+    gain_size = attn_gain.shape[0]
+    first_gain = small[:, :gain_size].reshape(-1).astype(f32)
+    second_gain = small[:, gain_size : 2 * gain_size].reshape(-1).astype(f32)
+    full_table = small[:, 2 * gain_size :].reshape(NB, bias_table.shape[1])
 
     def down_columns(step):
         return lax.dynamic_slice(
@@ -563,9 +565,8 @@
     sums = jnp.concatenate([first_wide, grad_ffn_gain, table_wide.reshape(-1)])
     small_count = sums.shape[0]
     sums = jnp.concatenate([sums, jnp.broadcast_to(local_sq, (LANES,))])
-    sums, output_sum = together(sums, output_sum)
     sums = jnp.sum(lax.all_gather(sums.reshape(-1, LANES), "dp", axis=0), axis=0)
-    sums, grad_input = together(sums, grad_input)
+    sums, grad_input, output_sum = together(sums, grad_input, output_sum)
     came_back = lax.all_to_all(
         grad_input.reshape(group_count, -1, quarter), "dp", split_axis=0, concat_axis=0, tiled=True
     )

time: 646 us -> 639 us (0.989)
  waiting for transfers between devices: 237 us -> 227 us
  blocking collectives: 26.1 us -> 18.2 us
    ppermute x24, waiting for transfers between devices: 227 us -> 204 us  [around(): lax.ppermute(block, 'mp', [(i, (i + 1) % count) for i in range(count)])]
    all_to_all x1, waiting for transfers between devices: 0.01 us -> 13.1 us  [shards(): lax.all_to_all(picked, 'dp', split_axis=0, concat_axis=0, tiled=True)]
    all_gather x1, blocking collectives: 18.3 us -> 9.02 us  [shards(): lax.all_gather(small, 'dp', axis=0)]
  transfers between devices with their start and end apart: 36 -> 36, of which waited for: 25 -> 26; matrix products, arithmetic and copies ran while one was open for 40% -> 42% of each run, Pallas kernels for 10% -> 10%
where the time goes in v6:
time: 639 us; the launch traced here: 630 us
  waiting for transfers between devices  227 us (36%)
  matrix products  166 us (26%)
  other arithmetic  78 us (12%)
  Pallas kernels  64.1 us (10%)
  local copies, waits for them, and re-layouts  29.7 us (5%)
  starting transfers between devices  24.6 us (4%)
  between operations  22.3 us (3%)
  blocking collectives  18.2 us (3%)
    ppermute x24, waiting for transfers between devices, around(): lax.ppermute(block, 'mp', [(i, (i + 1) % count) for i in range(count)])  204 us
    dot_general x34, matrix products, dot(): lax.dot_general(left, right, dims, preferred_element_type=jnp.float32)  165 us
    pallas_call x2, Pallas kernels, attend_backward(): pl.pallas_call(functools.partial(backward_kernel, first), grid=(last - fi...  34.6 us
    pallas_call x2, Pallas kernels, attend_forward(): pl.pallas_call(kernel, grid_spec=pltpu.PrefetchScalarGridSpec(num_scalar_...  29.5 us
    convert_element_type x8, other arithmetic, add_low(): return (received.astype(jnp.float32) + term).astype(jnp.bfloat16)  14.1 us
    all_to_all x1, waiting for transfers between devices, shards(): lax.all_to_all(picked, 'dp', split_axis=0, concat_axis=0, tiled=True)  13.1 us
    ppermute x24, starting transfers between devices, around(): lax.ppermute(block, 'mp', [(i, (i + 1) % count) for i in range(count)])  12.9 us
  transfers between devices with their start and end apart: 36, of which 26 were waited for; matrix products, arithmetic and copies ran while one was open for 42% of the time, Pallas kernels for 10%

profile of v6, /device:TPU:0, one launch (start us, length us, event | category | flops | bytes accessed | tf_op | source)
XLA Modules:
  0.0 630.0 jit_solution(2905808001754364889)
XLA Ops:
  7.2 3.1 collective-permute-start
  13.4 3.7 all-to-all-start
  19.4 13.1 %all-to-all-done = bf16[8,128,512]{2,1,0:T(8,128)(2,1)S(1)} async-done(((bf16[8,128,512]{2,1,0:T(8,128)(2,1)}), bf16[8,128,512]{2,1,0:T(8,128)(2,1)S(1)}, u32[]{:S(2)}, u32[]{:S(2)}) %all-to-all-start) | async-done | bytes 1048608 | tf_op jit(solution)/shard_map/all_to_all | solution.py:321
  32.5 3.3 collective-permute-done
  36.1 9.0 %all-gather = bf16[8,1,544]{2,1,0:T(2,128)(2,1)S(1)} all-gather(bf16[1,1,544]{2,1,0:T(2,128)(2,1)S(1)} %maximum_bitcast_fusion.1), channel_id=1, replica_groups=mesh['dp'=8,'mp'=4] {'dp'}, dimensions={0}, use_global_device_ids=true | all-gather | bytes 9792 | tf_op jit(solution)/shard_map/all_gather | solution.py:362
  47.3 14.8 %collective-permute-done.1 = bf16[1024,512]{1,0:T(8,128)(2,1)S(1)} collective-permute-done((bf16[1024,512]{1,0:T(8,128)(2,1)S(1)}, bf16[1024,512]{1,0:T(8,128)(2,1)S(1)}, u32[]{:S(2)}, u32[]{:S(2)}) %collective-permute-start.1) | collective-permute-done | bytes 1048608 | tf_op jit(solution)/shard_map/ppermute | solution.py:242
  65.0 22.5 %collective-permute-done.2 = bf16[1024,512]{1,0:T(8,128)(2,1)} collective-permute-done((bf16[1024,512]{1,0:T(8,128)(2,1)S(1)}, bf16[1024,512]{1,0:T(8,128)(2,1)}, u32[]{:S(2)}, u32[]{:S(2)}) %collective-permute-start.2) | collective-permute-done | bytes 1048608 | tf_op jit(solution)/shard_map/ppermute | solution.py:242
  91.4 3.1 broadcast_in_dim.78
  100.0 12.1 %collective-permute-done.3 = bf16[1024,512]{1,0:T(8,128)(2,1)S(1)} collective-permute-done((bf16[1024,512]{1,0:T(8,128)(2,1)}, bf16[1024,512]{1,0:T(8,128)(2,1)S(1)}, u32[]{:S(2)}, u32[]{:S(2)}) %collective-permute-start.3) | collective-permute-done | bytes 1048608 | tf_op jit(solution)/shard_map/ppermute | solution.py:242
  113.2 3.1 fusion
  117.0 10.5 %convolution_convert_fusion.3.query_ref.key_ref.value_ref = bf16[1024,1536]{1,0:T(8,128)(2,1)S(1)} fusion(bf16[2048,1536]{1,0:T(8,128)(2,1)} %all-gather.5.cloned.1.call-done, bf16[1024,2048]{1,0:T(8,128)(2,1)} %constant_dynamic-update-slice_fusion.4, f32[2048]{0:T(1024)S(1)} %bitcast.81, f32[1024]{0:T(1024)S(1)} %get-tuple-element.234), kind=kOutput, calls=%fused_computation.26 | convolution fusion | flops 6452412416 | bytes 13643776 | tf_op jit(solution)/shard_map/dot_general | solution.py:29
  127.5 8.2 %attend_forward.2 = (bf16[1024,512]{1,0:T(8,128)(2,1)}, bf16[8,1024,1024]{2,1,0:T(8,128)(2,1)}) custom-call(s32[1]{0:T(128)} %dynamic_slice.98.length, f32[4,2,2048]{2,1,0:T(2,128)S(1)} %reshape.185.rel_ref, bf16[1024,1536]{1,0:T(8,128)(2,1)S(1)} %convolution_convert_fusion.3.query_ref.key_ref.value_ref, ...), custom_call_target="tpu_custom_call" | custom-call | flops 2147483648 | bytes 4194304 | tf_op jit(solution)/shard_map/attend_forward/pallas_call | solution.py:91
  136.6 21.4 %attend_forward.3 = (bf16[1024,512]{1,0:T(8,128)(2,1)}, bf16[8,1024,1024]{2,1,0:T(8,128)(2,1)}) custom-call(s32[1]{0:T(128)} %dynamic_slice.98.length, f32[4,2,2048]{2,1,0:T(2,128)S(1)} %reshape.186.rel_ref, bf16[1024,1536]{1,0:T(8,128)(2,1)S(1)} %convolution_convert_fusion.3.query_ref.key_ref.value_ref, ...), custom_call_target="tpu_custom_call", output_to_operand_aliasing={{0}: (5, {}), {1}: (6, {})} | custom-call | flops 6442450944 | bytes 12582912 | tf_op jit(solution)/shard_map/attend_forward/pallas_call | solution.py:91
  163.8 3.3 broadcast_in_dim.80
  168.4 2.9 select_dynamic-update-slice_fusion.2
  171.4 2.6 select_dynamic-update-slice_fusion.1
  176.4 10.3 %collective-permute-done.6 = bf16[256,2048]{1,0:T(8,128)(2,1)S(1)} collective-permute-done((bf16[256,2048]{1,0:T(8,128)(2,1)S(1)}, bf16[256,2048]{1,0:T(8,128)(2,1)S(1)}, u32[]{:S(2)}, u32[]{:S(2)}) %collective-permute-start.6) | collective-permute-done | bytes 1048608 | tf_op jit(solution)/shard_map/ppermute | solution.py:242
  192.5 2.5 select_dynamic-update-slice_fusion
  195.0 15.0 %collective-permute-done.7 = bf16[256,2048]{1,0:T(8,128)(2,1)S(1)} collective-permute-done((bf16[256,2048]{1,0:T(8,128)(2,1)S(1)}, bf16[256,2048]{1,0:T(8,128)(2,1)S(1)}, u32[]{:S(2)}, u32[]{:S(2)}) %collective-permute-start.7) | collective-permute-done | bytes 1048608 | tf_op jit(solution)/shard_map/ppermute | solution.py:242
  211.0 20.2 %collective-permute-done.8 = bf16[256,2048]{1,0:T(8,128)(2,1)S(1)} collective-permute-done((bf16[256,2048]{1,0:T(8,128)(2,1)S(1)}, bf16[256,2048]{1,0:T(8,128)(2,1)S(1)}, u32[]{:S(2)}, u32[]{:S(2)}) %collective-permute-start.8) | collective-permute-done | bytes 1048608 | tf_op jit(solution)/shard_map/ppermute | solution.py:242
  235.4 6.0 fusion.137
  242.7 5.2 fusion.47
  248.0 8.4 %fusion.136 = f32[256,2048]{1,0:T(8,128)} fusion(bf16[2048,2560]{1,0:T(8,128)(2,1)} %all-gather.9.cloned.1.call-done, bf16[256,1280]{1,0:T(8,128)(2,1)S(1)} %get-tuple-element.219, bf16[256,1280]{1,0:T(8,128)(2,1)S(1)} %get-tuple-element.218), kind=kOutput, calls=%fused_computation.249 | convolution fusion | flops 2686976000 | bytes 13893632 | tf_op jit(solution)/shard_map/dot_general | solution.py:29
  258.4 5.9 fusion.138
  264.8 4.0 fusion.54
  270.0 7.8 %convolution_convert_fusion.5 = bf16[256,2048]{1,0:T(8,128)(2,1)} fusion(bf16[2048,2560]{1,0:T(8,128)(2,1)} %all-gather.9.cloned.1.call-done, bf16[256,1280]{1,0:T(8,128)(2,1)S(1)} %get-tuple-element.217, bf16[256,1280]{1,0:T(8,128)(2,1)S(1)} %get-tuple-element.216), kind=kOutput, calls=%fused_computation.39 | convolution fusion | flops 2687500288 | bytes 12845056 | tf_op jit(solution)/shard_map/dot_general | solution.py:29
  277.8 2.5 collective-permute-done.10
  280.3 6.0 fusion.139
  286.8 4.0 fusion.61
  292.8 5.8 fusion.135
  298.6 4.8 collective-permute-done.11
  303.6 6.0 fusion.140
  310.1 4.8 fusion.68
  317.2 8.7 %fusion.134 = f32[256,2048]{1,0:T(8,128)} fusion(bf16[2048,2560]{1,0:T(8,128)(2,1)} %all-gather.9.cloned.1.call-done, bf16[256,1280]{1,0:T(8,128)(2,1)} %copy-done.33, bf16[256,1280]{1,0:T(8,128)(2,1)} %copy-done.32), kind=kOutput, calls=%fused_computation.247 | convolution fusion | flops 2686976000 | bytes 13893632 | tf_op jit(solution)/shard_map/dot_general | solution.py:29
  327.8 16.7 %convolution_convert_fusion = bf16[2048,2560]{1,0:T(8,128)(2,1)} fusion(bf16[256,2560]{1,0:T(8,128)(2,1)} %pad_maximum_fusion.5, bf16[256,2560]{1,0:T(8,128)(2,1)} %pad_maximum_fusion.4, bf16[256,2560]{1,0:T(8,128)(2,1)} %pad_maximum_fusion.3, bf16[256,2560]{1,0:T(8,128)(2,1)S(1)} %pad_maximum_fusion.2, bf16[256,2048]{1,0:T(8,128)(2,1)} %collective-permute-done.11, ...), kind=kOutput, calls=%fused_computation.2 | convolution fusion | flops 10780409856 | bytes 19922944 | tf_op jit(solution)/shard_map/dot_general | solution.py:29
  344.5 3.3 collective-permute-done.13
  350.7 10.2 %convolution_convert_fusion.2 = bf16[1280,2048]{1,0:T(8,128)(2,1)} fusion(bf16[1024,1280]{1,0:T(8,128)(2,1)} %copy-done.19, bf16[1024,2048]{1,0:T(8,128)(2,1)} %select_dynamic-update-slice_fusion), kind=kOutput, calls=%fused_computation.9 | convolution fusion | flops 5371330560 | bytes 12058624 | tf_op jit(solution)/shard_map/dot_general | solution.py:29
  360.9 10.0 %collective-permute-done.14 = bf16[256,2048]{1,0:T(8,128)(2,1)S(1)} collective-permute-done((bf16[256,2048]{1,0:T(8,128)(2,1)S(1)}, bf16[256,2048]{1,0:T(8,128)(2,1)S(1)}, u32[]{:S(2)}, u32[]{:S(2)}) %collective-permute-start.14) | collective-permute-done | bytes 1048608 | tf_op jit(solution)/shard_map/ppermute | solution.py:242
  380.6 16.8 %collective-permute-done.15 = bf16[256,2048]{1,0:T(8,128)(2,1)S(1)} collective-permute-done((bf16[256,2048]{1,0:T(8,128)(2,1)S(1)}, bf16[256,2048]{1,0:T(8,128)(2,1)S(1)}, u32[]{:S(2)}, u32[]{:S(2)}) %collective-permute-start.15) | collective-permute-done | bytes 1048608 | tf_op jit(solution)/shard_map/ppermute | solution.py:242
  400.5 21.6 %collective-permute-done.16 = bf16[256,2048]{1,0:T(8,128)(2,1)S(1)} collective-permute-done((bf16[256,2048]{1,0:T(8,128)(2,1)S(1)}, bf16[256,2048]{1,0:T(8,128)(2,1)S(1)}, u32[]{:S(2)}, u32[]{:S(2)}) %collective-permute-start.16) | collective-permute-done | bytes 1048608 | tf_op jit(solution)/shard_map/ppermute | solution.py:242
  425.9 12.8 %collective-permute-done.17 = bf16[256,2048]{1,0:T(8,128)(2,1)S(1)} collective-permute-done((bf16[256,2048]{1,0:T(8,128)(2,1)S(1)}, bf16[256,2048]{1,0:T(8,128)(2,1)S(1)}, u32[]{:S(2)}, u32[]{:S(2)}) %collective-permute-start.17) | collective-permute-done | bytes 1048608 | tf_op jit(solution)/shard_map/ppermute | solution.py:242
  440.6 5.3 convolution_convert_fusion.4
  445.9 6.8 %pad_maximum_fusion = bf16[1792,2048]{1,0:T(8,128)(2,1)} fusion(bf16[1280,2048]{1,0:T(8,128)(2,1)} %convolution_convert_fusion.2, bf16[512,2048]{1,0:T(8,128)(2,1)S(1)} %convolution_convert_fusion.4), kind=kLoop, calls=%fused_computation.10 | loop fusion | flops 14680064 | bytes 14680064 | tf_op jit(solution)/shard_map/concatenate | solution.py:508
  452.8 16.7 %attend_backward.2 = (bf16[1024,1536]{1,0:T(8,128)(2,1)S(1)}, f32[2,2,2048]{2,1,0:T(2,128)S(1)}) custom-call(bf16[8,1024,1024]{2,1,0:T(8,128)(2,1)} %get-tuple-element.125.soft_ref, bf16[1024,1536]{1,0:T(8,128)(2,1)} %copy-done.2, bf16[1024,512]{1,0:T(8,128)(2,1)S(1)} %fusion.82.grad_ref, bf16[1024,512]{1,0:T(8,128)(2,1)} %get-tuple-element.128.out_ref, ...), custom_call_target="tpu_custom_call" | custom-call | flops 10737418240 | bytes 8388608 | tf_op jit(solution)/shard_map/attend_backward/pallas_call | solution.py:207
  471.2 4.1 collective-permute-done.18
  477.6 17.9 %attend_backward.3 = (bf16[1024,1536]{1,0:T(8,128)(2,1)S(1)}, f32[2,2,2048]{2,1,0:T(2,128)S(1)}) custom-call(bf16[8,1024,1024]{2,1,0:T(8,128)(2,1)} %get-tuple-element.125.soft_ref, bf16[1024,1536]{1,0:T(8,128)(2,1)} %copy-done.2, bf16[1024,512]{1,0:T(8,128)(2,1)S(1)} %copy-done.5, bf16[1024,512]{1,0:T(8,128)(2,1)} %get-tuple-element.128.out_ref, ...), custom_call_target="tpu_custom_call" | custom-call | flops 10737418240 | bytes 8388608 | tf_op jit(solution)/shard_map/attend_backward/pallas_call | solution.py:207
  495.5 3.0 collective-permute-done.19
  498.5 4.7 fusion.38
  503.2 11.9 %convolution_convert_fusion.1 = bf16[2048,1536]{1,0:T(8,128)(2,1)} fusion(bf16[1024,1536]{1,0:T(8,128)(2,1)S(1)} %get-tuple-element.180, bf16[1024,2048]{1,0:T(8,128)(2,1)} %constant_dynamic-update-slice_fusion.4, f32[2048]{0:T(1024)S(1)} %bitcast.82, f32[1024]{0:T(1024)S(1)} %copy-done.43), kind=kOutput, calls=%fused_computation.8 | convolution fusion | flops 6453985280 | bytes 13643776 | tf_op jit(solution)/shard_map/dot_general | solution.py:29
  515.0 4.6 fusion.34
  519.7 5.4 collective-permute-done.20
  526.5 3.3 add_convert_fusion.3
  532.3 4.8 fusion.32
  537.1 17.2 %collective-permute-done.21 = bf16[1024,512]{1,0:T(8,128)(2,1)} collective-permute-done((bf16[1024,512]{1,0:T(8,128)(2,1)}, bf16[1024,512]{1,0:T(8,128)(2,1)}, u32[]{:S(2)}, u32[]{:S(2)}) %collective-permute-start.21) | collective-permute-done | bytes 1048608 | tf_op jit(solution)/shard_map/ppermute | solution.py:242
  554.3 3.2 add_convert_fusion.2
  557.6 4.7 fusion.30
  563.7 4.2 collective-permute-start.25
  567.9 8.6 %collective-permute-done.24 = f32[8,128]{1,0:T(8,128)S(1)} collective-permute-done((f32[8,128]{1,0:T(8,128)S(1)}, f32[8,128]{1,0:T(8,128)S(1)}, u32[]{:S(2)}, u32[]{:S(2)}) %collective-permute-start.24) | collective-permute-done | bytes 4128 | tf_op jit(solution)/shard_map/ppermute | solution.py:274
  581.2 3.5 fusion.29
  588.6 9.2 %all_gather.20 = f32[8,41,128]{2,1,0:T(8,128)S(1)} all-gather(f32[1,41,128]{2,1,0:T(8,128)S(1)} %maximum_bitcast_fusion), channel_id=1, replica_groups=mesh['dp'=8,'mp'=4] {'dp'}, dimensions={0}, use_global_device_ids=true | all-gather | bytes 188928 | tf_op jit(solution)/shard_map/all_gather | solution.py:568
  597.8 2.9 collective-permute-start.26
  600.7 3.6 all-to-all-start.1
  605.5 3.2 fusion.83
  612.7 2.5 multiply_add_fusion
  (299 shorter events, 100.2 us)
Async XLA Ops:
  7.2 28.6 %collective-permute-start = (bf16[1024,512]{1,0:T(8,128)(2,1)}, bf16[1024,512]{1,0:T(8,128)(2,1)}, u32[]{:S(2)}, u32[]{:S(2)}) collective-permute-start(bf16[1024,512]{1,0:T(8,128)(2,1)} %bitcast.71), channel_id=1, source_target_pairs={{0,1},{1,2},{2,3},{3,0},{4,5},{5,6},{6,7},{7,4},{8,9},{9,10},{10,1... | collective-permute-start | bytes 3145736 | tf_op jit(solution)/shard_map/ppermute | solution.py:242
  13.4 19.1 %all-to-all-start = ((bf16[8,128,512]{2,1,0:T(8,128)(2,1)}), bf16[8,128,512]{2,1,0:T(8,128)(2,1)S(1)}, u32[]{:S(2)}, u32[]{:S(2)}) async-start(bf16[8,128,512]{2,1,0:T(8,128)(2,1)} %broadcast_select_fusion.1), calls=%async_computation | async-start | bytes 2097152 | tf_op jit(solution)/shard_map/all_to_all | solution.py:321
  17.1 99.9 %all-gather.5.cloned.1.call-start = ((), (), s32[]{:S(2)}) async-start(), calls=%async_computation.5 | async-start | bytes 7077888 | tf_op jit(solution)/shard_map/all_gather | solution.py:355
  17.2 18.7 %copy-start.53 = (f32[256]{0:T(256)S(1)}, f32[256]{0:T(256)}, u32[]{:S(2)}) copy-start(f32[256]{0:T(256)} %param.39) | copy-start | bytes 3076
  17.2 18.7 %copy-start.54 = (f32[256]{0:T(256)S(1)}, f32[256]{0:T(256)}, u32[]{:S(2)}) copy-start(f32[256]{0:T(256)} %param.40) | copy-start | bytes 3076
  17.2 18.7 %copy-start.49 = (f32[4,8]{1,0:T(4,128)S(1)}, f32[4,8]{1,0:T(4,128)}, u32[]{:S(2)}) copy-start(f32[4,8]{1,0:T(4,128)} %param.41) | copy-start | bytes 388
  17.3 28.9 %copy-start.21 = (f32[1280,256]{1,0:T(8,128)S(1)}, f32[1280,256]{1,0:T(8,128)}, u32[]{:S(2)}) copy-start(f32[1280,256]{1,0:T(8,128)} %param.38) | copy-start | bytes 3932164
  32.5 62.0 %copy-start.7 = (bf16[8,128,512]{2,1,0:T(8,128)(2,1)}, bf16[8,128,512]{2,1,0:T(8,128)(2,1)S(1)}, u32[]{:S(2)}) copy-start(bf16[8,128,512]{2,1,0:T(8,128)(2,1)S(1)} %all-to-all-done) | copy-start | bytes 3145732
  35.8 125.0 %all-gather.7.cloned.1.call-start = ((), (), s32[]{:S(2)}) async-start(), calls=%async_computation.6 | async-start | bytes 8257536 | tf_op jit(solution)/shard_map/all_gather | solution.py:366
  35.8 26.2 %collective-permute-start.1 = (bf16[1024,512]{1,0:T(8,128)(2,1)S(1)}, bf16[1024,512]{1,0:T(8,128)(2,1)S(1)}, u32[]{:S(2)}, u32[]{:S(2)}) collective-permute-start(bf16[1024,512]{1,0:T(8,128)(2,1)S(1)} %bitcast.63), channel_id=1, source_target_pairs={{0,1},{1,2},{2,3},{3,0},{4,5},{5,6},{6,7},{7,4},{8,9},{9,10},{10,1... | collective-permute-start | bytes 3145736 | tf_op jit(solution)/shard_map/ppermute | solution.py:242
  46.3 15.9 %copy-start.22 = (f32[256,1280]{1,0:T(8,128)S(1)}, f32[256,1280]{1,0:T(8,128)}, u32[]{:S(2)}) copy-start(f32[256,1280]{1,0:T(8,128)} %param.36) | copy-start | bytes 3932164
  62.1 173.3 %all-gather.9.cloned.1.call-start = ((), (), s32[]{:S(2)}) async-start(), calls=%async_computation.7 | async-start | bytes 11796480 | tf_op jit(solution)/shard_map/all_gather | solution.py:368
  62.1 25.4 %collective-permute-start.2 = (bf16[1024,512]{1,0:T(8,128)(2,1)S(1)}, bf16[1024,512]{1,0:T(8,128)(2,1)}, u32[]{:S(2)}, u32[]{:S(2)}) collective-permute-start(bf16[1024,512]{1,0:T(8,128)(2,1)S(1)} %collective-permute-done.1), channel_id=1, source_target_pairs={{0,1},{1,2},{2,3},{3,0},{4,5},{5,6},{6,7},{7,4},{8,9},{9,10},{10,1... | collective-permute-start | bytes 3145736 | tf_op jit(solution)/shard_map/ppermute | solution.py:242
  63.8 23.8 %copy-start.56 = (s32[8]{0:T(128)S(1)}, s32[8]{0:T(128)}, u32[]{:S(2)}) copy-start(s32[8]{0:T(128)} %param.30) | copy-start | bytes 100
  63.8 26.4 %copy-start.55 = (s32[8]{0:T(128)S(1)}, s32[8]{0:T(128)}, u32[]{:S(2)}) copy-start(s32[8]{0:T(128)} %param.29) | copy-start | bytes 100
  63.9 27.0 %copy-start.46 = (s32[2047]{0:T(1024)S(1)}, s32[2047]{0:T(1024)}, u32[]{:S(2)}) copy-start(s32[2047]{0:T(1024)} %param.31) | copy-start | bytes 24568
  87.5 387.8 %reduce-scatter.4.cloned.1.call-start = ((), (), s32[]{:S(2)}) async-start(), calls=%async_computation.8 | async-start | bytes 11796480 | tf_op jit(solution)/shard_map/reduce_scatter | solution.py:461
  87.6 24.6 %collective-permute-start.3 = (bf16[1024,512]{1,0:T(8,128)(2,1)}, bf16[1024,512]{1,0:T(8,128)(2,1)S(1)}, u32[]{:S(2)}, u32[]{:S(2)}) collective-permute-start(bf16[1024,512]{1,0:T(8,128)(2,1)} %collective-permute-done.2), channel_id=1, source_target_pairs={{0,1},{1,2},{2,3},{3,0},{4,5},{5,6},{6,7},{7,4},{8,9},{9,10},{10,1... | collective-permute-start | bytes 3145736 | tf_op jit(solution)/shard_map/ppermute | solution.py:242
  95.8 21.2 %copy-start.44 = (f32[1,2,8,128]{3,1,2,0:T(2,128)}, f32[1,2,8,128]{3,1,2,0:T(2,128)S(1)}, u32[]{:S(2)}) copy-start(f32[1,2,8,128]{3,1,2,0:T(2,128)S(1)} %copy.44) | copy-start | bytes 24580
  112.2 23.7 %collective-permute-start.4 = (bf16[1024,512]{1,0:T(8,128)(2,1)}, bf16[1024,512]{1,0:T(8,128)(2,1)}, u32[]{:S(2)}, u32[]{:S(2)}) collective-permute-start(bf16[1024,512]{1,0:T(8,128)(2,1)} %collective-permute-done), channel_id=1, source_target_pairs={{0,1},{1,2},{2,3},{3,0},{4,5},{5,6},{6,7},{7,4},{8,9},{9,10},{10,1... | collective-permute-start | bytes 3145736 | tf_op jit(solution)/shard_map/ppermute | solution.py:242
  117.0 10.5 %copy-start.42 = (f32[1024]{0:T(1024)}, f32[1024]{0:T(1024)S(1)}, u32[]{:S(2)}) copy-start(f32[1024]{0:T(1024)S(1)} %get-tuple-element.234) | copy-start | bytes 12292
  127.5 9.0 %copy-start.2 = (bf16[1024,1536]{1,0:T(8,128)(2,1)}, bf16[1024,1536]{1,0:T(8,128)(2,1)S(1)}, u32[]{:S(2)}) copy-start(bf16[1024,1536]{1,0:T(8,128)(2,1)S(1)} %convolution_convert_fusion.3.query_ref.key_ref.value_ref) | copy-start | bytes 9437188
  135.8 23.8 %collective-permute-start.5 = (bf16[1024,512]{1,0:T(8,128)(2,1)}, bf16[1024,512]{1,0:T(8,128)(2,1)}, u32[]{:S(2)}, u32[]{:S(2)}) collective-permute-start(bf16[1024,512]{1,0:T(8,128)(2,1)} %collective-permute-done.4), channel_id=1, source_target_pairs={{0,1},{1,2},{2,3},{3,0},{4,5},{5,6},{6,7},{7,4},{8,9},{9,10},{10,1... | collective-permute-start | bytes 3145736 | tf_op jit(solution)/shard_map/ppermute | solution.py:242
  163.2 23.5 %collective-permute-start.6 = (bf16[256,2048]{1,0:T(8,128)(2,1)S(1)}, bf16[256,2048]{1,0:T(8,128)(2,1)S(1)}, u32[]{:S(2)}, u32[]{:S(2)}) collective-permute-start(bf16[256,2048]{1,0:T(8,128)(2,1)S(1)} %convolution_convert_fusion.6), channel_id=1, source_target_pairs={{0,1},{1,2},{2,3},{3,0},{4,5},{5,6},{6,7},{7,4},{8,9},{9,10},{10,1... | collective-permute-start | bytes 3145736 | tf_op jit(solution)/shard_map/ppermute | solution.py:242
  187.0 23.0 %collective-permute-start.7 = (bf16[256,2048]{1,0:T(8,128)(2,1)S(1)}, bf16[256,2048]{1,0:T(8,128)(2,1)S(1)}, u32[]{:S(2)}, u32[]{:S(2)}) collective-permute-start(bf16[256,2048]{1,0:T(8,128)(2,1)S(1)} %add_convert_fusion.8), channel_id=1, source_target_pairs={{0,1},{1,2},{2,3},{3,0},{4,5},{5,6},{6,7},{7,4},{8,9},{9,10},{10,1... | collective-permute-start | bytes 3145736 | tf_op jit(solution)/shard_map/ppermute | solution.py:242
  210.3 20.9 %collective-permute-start.8 = (bf16[256,2048]{1,0:T(8,128)(2,1)S(1)}, bf16[256,2048]{1,0:T(8,128)(2,1)S(1)}, u32[]{:S(2)}, u32[]{:S(2)}) collective-permute-start(bf16[256,2048]{1,0:T(8,128)(2,1)S(1)} %add_convert_fusion.7), channel_id=1, source_target_pairs={{0,1},{1,2},{2,3},{3,0},{4,5},{5,6},{6,7},{7,4},{8,9},{9,10},{10,1... | collective-permute-start | bytes 3145736 | tf_op jit(solution)/shard_map/ppermute | solution.py:242
  235.4 21.5 %collective-permute-start.9 = (bf16[256,2048]{1,0:T(8,128)(2,1)}, bf16[256,2048]{1,0:T(8,128)(2,1)}, u32[]{:S(2)}, u32[]{:S(2)}) collective-permute-start(bf16[256,2048]{1,0:T(8,128)(2,1)} %multiply_convert_fusion), channel_id=1, source_target_pairs={{0,1},{1,2},{2,3},{3,0},{4,5},{5,6},{6,7},{7,4},{8,9},{9,10},{10,1... | collective-permute-start | bytes 3145736 | tf_op jit(solution)/shard_map/ppermute | solution.py:242
  248.0 16.8 %slice-start = ((s8[7340032]{0:T(1024)(128)(4,1)}), s8[4194304]{0:T(1024)(128)(4,1)S(1)}, s32[]{:S(2)}) async-start(s8[7340032]{0:T(1024)(128)(4,1)} %bitcast.67), calls=%async_computation.11 | async-start | bytes 8388608
  256.4 8.4 %slice-start.1 = ((s8[7340032]{0:T(1024)(128)(4,1)}), s8[3145728]{0:T(1024)(128)(4,1)S(1)}, s32[]{:S(2)}) async-start(s8[7340032]{0:T(1024)(128)(4,1)} %bitcast.67), calls=%async_computation.12 | async-start | bytes 6291456
  256.8 23.5 %collective-permute-start.10 = (bf16[256,2048]{1,0:T(8,128)(2,1)}, bf16[256,2048]{1,0:T(8,128)(2,1)}, u32[]{:S(2)}, u32[]{:S(2)}) collective-permute-start(bf16[256,2048]{1,0:T(8,128)(2,1)} %collective-permute-done.9), channel_id=1, source_target_pairs={{0,1},{1,2},{2,3},{3,0},{4,5},{5,6},{6,7},{7,4},{8,9},{9,10},{10,1... | collective-permute-start | bytes 3145736 | tf_op jit(solution)/shard_map/ppermute | solution.py:242
  280.3 23.1 %collective-permute-start.11 = (bf16[256,2048]{1,0:T(8,128)(2,1)}, bf16[256,2048]{1,0:T(8,128)(2,1)}, u32[]{:S(2)}, u32[]{:S(2)}) collective-permute-start(bf16[256,2048]{1,0:T(8,128)(2,1)} %collective-permute-done.10), channel_id=1, source_target_pairs={{0,1},{1,2},{2,3},{3,0},{4,5},{5,6},{6,7},{7,4},{8,9},{9,10},{10,1... | collective-permute-start | bytes 3145736 | tf_op jit(solution)/shard_map/ppermute | solution.py:242
  303.4 22.4 %collective-permute-start.12 = (bf16[256,2048]{1,0:T(8,128)(2,1)}, bf16[256,2048]{1,0:T(8,128)(2,1)S(1)}, u32[]{:S(2)}, u32[]{:S(2)}) collective-permute-start(bf16[256,2048]{1,0:T(8,128)(2,1)} %convolution_convert_fusion.5), channel_id=1, source_target_pairs={{0,1},{1,2},{2,3},{3,0},{4,5},{5,6},{6,7},{7,4},{8,9},{9,10},{10,1... | collective-permute-start | bytes 3145736 | tf_op jit(solution)/shard_map/ppermute | solution.py:242
  327.1 20.7 %collective-permute-start.13 = (bf16[256,2048]{1,0:T(8,128)(2,1)}, bf16[256,2048]{1,0:T(8,128)(2,1)}, u32[]{:S(2)}, u32[]{:S(2)}) collective-permute-start(bf16[256,2048]{1,0:T(8,128)(2,1)} %add_convert_fusion.6), channel_id=1, source_target_pairs={{0,1},{1,2},{2,3},{3,0},{4,5},{5,6},{6,7},{7,4},{8,9},{9,10},{10,1... | collective-permute-start | bytes 3145736 | tf_op jit(solution)/shard_map/ppermute | solution.py:242
  347.9 189.2 %reduce-scatter.6.cloned.1.call-start = ((), (), s32[]{:S(2)}) async-start(), calls=%async_computation.9 | async-start | bytes 8257536 | tf_op jit(solution)/shard_map/reduce_scatter | solution.py:509
  347.9 25.9 %slice-start.2 = ((s8[7340032]{0:T(1024)(128)(4,1)}), s8[4194304]{0:T(1024)(128)(4,1)S(1)}, s32[]{:S(2)}) async-start(s8[7340032]{0:T(1024)(128)(4,1)} %bitcast.69), calls=%async_computation.13 | async-start | bytes 8388608
  350.2 20.7 %copy-start.9 = (f32[256,2048]{1,0:T(8,128)S(1)}, f32[256,2048]{1,0:T(8,128)}, u32[]{:S(2)}) copy-start(f32[256,2048]{1,0:T(8,128)} %fusion.136) | copy-start | bytes 6291460
  350.2 23.6 %slice-start.3 = ((s8[7340032]{0:T(1024)(128)(4,1)}), s8[3145728]{0:T(1024)(128)(4,1)S(1)}, s32[]{:S(2)}) async-start(s8[7340032]{0:T(1024)(128)(4,1)} %bitcast.69), calls=%async_computation.14 | async-start | bytes 6291456
  350.2 20.7 %collective-permute-start.14 = (bf16[256,2048]{1,0:T(8,128)(2,1)S(1)}, bf16[256,2048]{1,0:T(8,128)(2,1)S(1)}, u32[]{:S(2)}, u32[]{:S(2)}) collective-permute-start(bf16[256,2048]{1,0:T(8,128)(2,1)S(1)} %add_convert_fusion.5), channel_id=1, source_target_pairs={{0,1},{1,2},{2,3},{3,0},{4,5},{5,6},{6,7},{7,4},{8,9},{9,10},{10,1... | collective-permute-start | bytes 3145736 | tf_op jit(solution)/shard_map/ppermute | solution.py:242
  373.7 23.7 %collective-permute-start.15 = (bf16[256,2048]{1,0:T(8,128)(2,1)S(1)}, bf16[256,2048]{1,0:T(8,128)(2,1)S(1)}, u32[]{:S(2)}, u32[]{:S(2)}) collective-permute-start(bf16[256,2048]{1,0:T(8,128)(2,1)S(1)} %subtract_convert_fusion), channel_id=1, source_target_pairs={{0,1},{1,2},{2,3},{3,0},{4,5},{5,6},{6,7},{7,4},{8,9},{9,10},{10,1... | collective-permute-start | bytes 3145736 | tf_op jit(solution)/shard_map/ppermute | solution.py:242
  380.6 18.8 %copy-start.14 = (f32[1024,512]{1,0:T(8,128)}, f32[1024,512]{1,0:T(8,128)S(1)}, u32[]{:S(2)}) copy-start(f32[1024,512]{1,0:T(8,128)S(1)} %get-tuple-element.188) | copy-start | bytes 6291460
  380.6 18.8 %copy-start.16 = (f32[1024,512]{1,0:T(8,128)}, f32[1024,512]{1,0:T(8,128)S(1)}, u32[]{:S(2)}) copy-start(f32[1024,512]{1,0:T(8,128)S(1)} %get-tuple-element.177) | copy-start | bytes 6291460
  380.6 42.7 %copy-start.13 = (f32[1024,512]{1,0:T(8,128)}, f32[1024,512]{1,0:T(8,128)S(1)}, u32[]{:S(2)}) copy-start(f32[1024,512]{1,0:T(8,128)S(1)} %get-tuple-element.202) | copy-start | bytes 6291460
  397.4 24.6 %collective-permute-start.16 = (bf16[256,2048]{1,0:T(8,128)(2,1)S(1)}, bf16[256,2048]{1,0:T(8,128)(2,1)S(1)}, u32[]{:S(2)}, u32[]{:S(2)}) collective-permute-start(bf16[256,2048]{1,0:T(8,128)(2,1)S(1)} %collective-permute-done.15), channel_id=1, source_target_pairs={{0,1},{1,2},{2,3},{3,0},{4,5},{5,6},{6,7},{7,4},{8,9},{9,10},{10,1... | collective-permute-start | bytes 3145736 | tf_op jit(solution)/shard_map/ppermute | solution.py:242
  422.0 16.7 %collective-permute-start.17 = (bf16[256,2048]{1,0:T(8,128)(2,1)S(1)}, bf16[256,2048]{1,0:T(8,128)(2,1)S(1)}, u32[]{:S(2)}, u32[]{:S(2)}) collective-permute-start(bf16[256,2048]{1,0:T(8,128)(2,1)S(1)} %collective-permute-done.16), channel_id=1, source_target_pairs={{0,1},{1,2},{2,3},{3,0},{4,5},{5,6},{6,7},{7,4},{8,9},{9,10},{10,1... | collective-permute-start | bytes 3145736 | tf_op jit(solution)/shard_map/ppermute | solution.py:242
  440.6 12.2 %copy-start.4 = (bf16[1024,512]{1,0:T(8,128)(2,1)}, bf16[1024,512]{1,0:T(8,128)(2,1)S(1)}, u32[]{:S(2)}) copy-start(bf16[1024,512]{1,0:T(8,128)(2,1)S(1)} %fusion.82.grad_ref) | copy-start | bytes 3145732
  452.7 133.1 %reduce-scatter.8.cloned.1.call-start = ((), (), s32[]{:S(2)}) async-start(), calls=%async_computation.10 | async-start | bytes 7077888 | tf_op jit(solution)/shard_map/reduce_scatter | solution.py:529
  452.7 22.6 %collective-permute-start.18 = (bf16[1024,512]{1,0:T(8,128)(2,1)}, bf16[1024,512]{1,0:T(8,128)(2,1)}, u32[]{:S(2)}, u32[]{:S(2)}) collective-permute-start(bf16[1024,512]{1,0:T(8,128)(2,1)} %convert_element_type.243), channel_id=1, source_target_pairs={{0,1},{1,2},{2,3},{3,0},{4,5},{5,6},{6,7},{7,4},{8,9},{9,10},{10,1... | collective-permute-start | bytes 3145736 | tf_op jit(solution)/shard_map/ppermute | solution.py:242
  452.8 22.5 %copy-start.17 = (f32[1024,512]{1,0:T(8,128)S(1)}, f32[1024,512]{1,0:T(8,128)}, u32[]{:S(2)}) copy-start(f32[1024,512]{1,0:T(8,128)} %copy-done.16) | copy-start | bytes 6291460
  477.3 21.1 %collective-permute-start.19 = (bf16[1024,512]{1,0:T(8,128)(2,1)S(1)}, bf16[1024,512]{1,0:T(8,128)(2,1)S(1)}, u32[]{:S(2)}, u32[]{:S(2)}) collective-permute-start(bf16[1024,512]{1,0:T(8,128)(2,1)S(1)} %add_convert_fusion.4), channel_id=1, source_target_pairs={{0,1},{1,2},{2,3},{3,0},{4,5},{5,6},{6,7},{7,4},{8,9},{9,10},{10,1... | collective-permute-start | bytes 3145736 | tf_op jit(solution)/shard_map/ppermute | solution.py:242
  503.2 21.9 %collective-permute-start.20 = (bf16[1024,512]{1,0:T(8,128)(2,1)}, bf16[1024,512]{1,0:T(8,128)(2,1)}, u32[]{:S(2)}, u32[]{:S(2)}) collective-permute-start(bf16[1024,512]{1,0:T(8,128)(2,1)} %fusion.38), channel_id=1, source_target_pairs={{0,1},{1,2},{2,3},{3,0},{4,5},{5,6},{6,7},{7,4},{8,9},{9,10},{10,1... | collective-permute-start | bytes 3145736 | tf_op jit(solution)/shard_map/ppermute | solution.py:242
  519.7 6.2 copy-start.48
  529.8 24.5 %collective-permute-start.21 = (bf16[1024,512]{1,0:T(8,128)(2,1)}, bf16[1024,512]{1,0:T(8,128)(2,1)}, u32[]{:S(2)}, u32[]{:S(2)}) collective-permute-start(bf16[1024,512]{1,0:T(8,128)(2,1)} %add_convert_fusion.3), channel_id=1, source_target_pairs={{0,1},{1,2},{2,3},{3,0},{4,5},{5,6},{6,7},{7,4},{8,9},{9,10},{10,1... | collective-permute-start | bytes 3145736 | tf_op jit(solution)/shard_map/ppermute | solution.py:242
  532.2 30.0 %collective-permute-start.23 = (f32[8,128]{1,0:T(8,128)S(1)}, f32[8,128]{1,0:T(8,128)S(1)}, u32[]{:S(2)}, u32[]{:S(2)}) collective-permute-start(f32[8,128]{1,0:T(8,128)S(1)} %bitcast.79), channel_id=1, source_target_pairs={{0,1},{1,0},{2,3},{3,2},{4,5},{5,4},{6,7},{7,6},{8,9},{9,8},{10,11... | collective-permute-start | bytes 12296 | tf_op jit(solution)/shard_map/ppermute | solution.py:274
  557.6 23.2 %collective-permute-start.22 = (bf16[1024,512]{1,0:T(8,128)(2,1)}, bf16[1024,512]{1,0:T(8,128)(2,1)}, u32[]{:S(2)}, u32[]{:S(2)}) collective-permute-start(bf16[1024,512]{1,0:T(8,128)(2,1)} %add_convert_fusion.2), channel_id=1, source_target_pairs={{0,1},{1,2},{2,3},{3,0},{4,5},{5,6},{6,7},{7,4},{8,9},{9,10},{10,1... | collective-permute-start | bytes 3145736 | tf_op jit(solution)/shard_map/ppermute | solution.py:242
  562.3 14.2 %copy-start.12 = (bf16[1792,256]{1,0:T(8,128)(2,1)S(1)}, bf16[1792,256]{1,0:T(8,128)(2,1)}, u32[]{:S(2)}) copy-start(bf16[1792,256]{1,0:T(8,128)(2,1)} %reduce-scatter.6.cloned.1.call-done) | copy-start | bytes 2752516
  562.3 18.9 %copy-start.8 = (bf16[8,128,512]{2,1,0:T(8,128)(2,1)S(1)}, bf16[8,128,512]{2,1,0:T(8,128)(2,1)}, u32[]{:S(2)}) copy-start(bf16[8,128,512]{2,1,0:T(8,128)(2,1)} %copy-done.7) | copy-start | bytes 3145732
  562.3 18.9 %copy-start.41 = (f32[1024]{0:T(1024)S(1)}, f32[1024]{0:T(1024)}, u32[]{:S(2)}) copy-start(f32[1024]{0:T(1024)} %get-tuple-element.233) | copy-start | bytes 12292
  562.3 14.2 %collective-permute-start.24 = (f32[8,128]{1,0:T(8,128)S(1)}, f32[8,128]{1,0:T(8,128)S(1)}, u32[]{:S(2)}, u32[]{:S(2)}) collective-permute-start(f32[8,128]{1,0:T(8,128)S(1)} %bitcast_add_fusion), channel_id=1, source_target_pairs={{0,2},{1,3},{2,0},{3,1},{4,6},{5,7},{6,4},{7,5},{8,10},{9,11},{10,... | collective-permute-start | bytes 12296 | tf_op jit(solution)/shard_map/ppermute | solution.py:274
  563.7 34.0 %collective-permute-start.25 = (bf16[1024,512]{1,0:T(8,128)(2,1)}, bf16[1024,512]{1,0:T(8,128)(2,1)S(1)}, u32[]{:S(2)}, u32[]{:S(2)}) collective-permute-start(bf16[1024,512]{1,0:T(8,128)(2,1)} %add_convert_fusion.1), channel_id=1, source_target_pairs={{0,1},{1,2},{2,3},{3,0},{4,5},{5,6},{6,7},{7,4},{8,9},{9,10},{10,1... | collective-permute-start | bytes 3145736 | tf_op jit(solution)/shard_map/ppermute | solution.py:242
  597.8 6.5 %collective-permute-start.26 = (f32[41,128]{1,0:T(8,128)S(1)}, f32[41,128]{1,0:T(8,128)S(1)}, u32[]{:S(2)}, u32[]{:S(2)}) collective-permute-start(f32[41,128]{1,0:T(8,128)S(1)} %reduce_sum.108), channel_id=1, source_target_pairs={{0,1},{1,0},{2,3},{3,2},{4,5},{5,4},{6,7},{7,6},{8,9},{9,8},{10,11... | collective-permute-start | bytes 62984 | tf_op jit(solution)/shard_map/ppermute | solution.py:274
  600.7 19.1 %all-to-all-start.1 = ((bf16[8,128,512]{2,1,0:T(8,128)(2,1)}), bf16[8,128,512]{2,1,0:T(8,128)(2,1)S(1)}, u32[]{:S(2)}, u32[]{:S(2)}) async-start(bf16[8,128,512]{2,1,0:T(8,128)(2,1)} %bitcast.13), calls=%async_computation.4 | async-start | bytes 2097152 | tf_op jit(solution)/shard_map/all_to_all | solution.py:570
  604.3 7.4 %copy-start.35 = (f32[512,256]{1,0:T(8,128)S(1)}, f32[512,256]{1,0:T(8,128)}, u32[]{:S(2)}) copy-start(f32[512,256]{1,0:T(8,128)} %param.45) | copy-start | bytes 1572868
  604.3 4.8 collective-permute-start.27
  605.5 11.1 %copy-start.50 = (f32[4,8]{1,0:T(4,128)S(1)}, f32[4,8]{1,0:T(4,128)}, u32[]{:S(2)}) copy-start(f32[4,8]{1,0:T(4,128)} %param.51) | copy-start | bytes 388
  (34 other events, 111.9 us)
Sparse Core Ops, SparseCore 0:
  35.9 44.8 all-gather.4
  83.3 51.2 all-gather.6
  137.1 63.2 all-gather.8
  348.0 81.8 reduce-scatter.3
  452.8 65.7 reduce-scatter.5
  525.2 60.5 reduce-scatter.7

commit v7 on v6

--- a/solution.py
+++ b/solution.py
@@ -433,7 +433,7 @@
                 h_parts[step],
                 gate_up_grads[last],
                 hidden,
-                term.astype(low) if last == 1 else term,
+                term.astype(low) if last > 0 else term,
             )
         if step < tensor_count - 1:
             h_parts.append(around(h_parts[step]))
@@ -451,7 +451,7 @@
         gate_up_grads.append(jnp.concatenate(mix_back(grad_hidden), axis=1).astype(low))
 
     received, terms[2], terms[3], gate_up_grads[3], hidden = together(
-        running, terms[2], normed_part(3), gate_up_grads[3], hidden
+        running, terms[2], normed_part(3).astype(low), gate_up_grads[3], hidden
     )
     running = around(add_low(received, terms[2]))
     h_rotated = jnp.concatenate(h_parts, axis=0)
@@ -520,9 +520,9 @@
 
     def first_part(step):
         weight = lax.dynamic_slice_in_dim(qkv_weight, back(step) * quarter, quarter, 0)
-        return dot(grad_qkv, weight, NT)
-
-    running, grad_qkv = together(first_part(1).astype(low), grad_qkv)
+        return dot(grad_qkv, weight, NT).astype(low)
+
+    running, grad_qkv = together(first_part(1), grad_qkv)
     running = around(running)
     grad_qkv_weight = dot(h_first, grad_qkv, TN).astype(low)
     received, term, grad_qkv_weight = together(running, first_part(2), grad_qkv_weight)

time: 639 us -> 634 us (level)
  waiting for transfers between devices: 227 us -> 218 us
  starting transfers between devices: 24.6 us -> 31.2 us
    ppermute x24, waiting for transfers between devices: 204 us -> 194 us  [around(): lax.ppermute(block, 'mp', [(i, (i + 1) % count) for i in range(count)])]
    ppermute x24, starting transfers between devices: 12.9 us -> 19.6 us  [around(): lax.ppermute(block, 'mp', [(i, (i + 1) % count) for i in range(count)])]
  transfers between devices with their start and end apart: 36 -> 36, of which waited for: 26 -> 24; matrix products, arithmetic and copies ran while one was open for 42% -> 42% of each run, Pallas kernels for 10% -> 10%
where the time goes in v7:
time: 634 us; the launch traced here: 625 us
  waiting for transfers between devices  218 us (34%)
  matrix products  167 us (26%)
  other arithmetic  75.6 us (12%)
  Pallas kernels  64.1 us (10%)
  starting transfers between devices  31.2 us (5%)
  local copies, waits for them, and re-layouts  30.3 us (5%)
  between operations  22.3 us (4%)
  blocking collectives  16.8 us (3%)
    ppermute x24, waiting for transfers between devices, around(): lax.ppermute(block, 'mp', [(i, (i + 1) % count) for i in range(count)])  194 us
    dot_general x34, matrix products, dot(): lax.dot_general(left, right, dims, preferred_element_type=jnp.float32)  166 us
    pallas_call x2, Pallas kernels, attend_backward(): pl.pallas_call(functools.partial(backward_kernel, first), grid=(last - fi...  34.5 us
    pallas_call x2, Pallas kernels, attend_forward(): pl.pallas_call(kernel, grid_spec=pltpu.PrefetchScalarGridSpec(num_scalar_...  29.5 us
    ppermute x24, starting transfers between devices, around(): lax.ppermute(block, 'mp', [(i, (i + 1) % count) for i in range(count)])  19.6 us
    convert_element_type x8, other arithmetic, add_low(): return (received.astype(jnp.float32) + term).astype(jnp.bfloat16)  13.8 us
    all_to_all x1, waiting for transfers between devices, shards(): lax.all_to_all(picked, 'dp', split_axis=0, concat_axis=0, tiled=True)  13.1 us
  transfers between devices with their start and end apart: 36, of which 24 were waited for; matrix products, arithmetic and copies ran while one was open for 42% of the time, Pallas kernels for 10%

profile of v7, /device:TPU:0, one launch (start us, length us, event | category | flops | bytes accessed | tf_op | source)
XLA Modules:
  0.0 624.9 jit_solution(15071906343976431322)
XLA Ops:
  7.2 3.1 collective-permute-start
  13.4 3.7 all-to-all-start
  19.4 13.1 %all-to-all-done = bf16[8,128,512]{2,1,0:T(8,128)(2,1)S(1)} async-done(((bf16[8,128,512]{2,1,0:T(8,128)(2,1)}), bf16[8,128,512]{2,1,0:T(8,128)(2,1)S(1)}, u32[]{:S(2)}, u32[]{:S(2)}) %all-to-all-start) | async-done | bytes 1048608 | tf_op jit(solution)/shard_map/all_to_all | solution.py:321
  32.5 3.3 collective-permute-done
  36.1 9.0 %all-gather = bf16[8,1,544]{2,1,0:T(2,128)(2,1)S(1)} all-gather(bf16[1,1,544]{2,1,0:T(2,128)(2,1)S(1)} %maximum_bitcast_fusion.1), channel_id=1, replica_groups=mesh['dp'=8,'mp'=4] {'dp'}, dimensions={0}, use_global_device_ids=true | all-gather | bytes 9792 | tf_op jit(solution)/shard_map/all_gather | solution.py:362
  47.3 14.8 %collective-permute-done.1 = bf16[1024,512]{1,0:T(8,128)(2,1)S(1)} collective-permute-done((bf16[1024,512]{1,0:T(8,128)(2,1)S(1)}, bf16[1024,512]{1,0:T(8,128)(2,1)S(1)}, u32[]{:S(2)}, u32[]{:S(2)}) %collective-permute-start.1) | collective-permute-done | bytes 1048608 | tf_op jit(solution)/shard_map/ppermute | solution.py:242
  65.0 22.5 %collective-permute-done.2 = bf16[1024,512]{1,0:T(8,128)(2,1)} collective-permute-done((bf16[1024,512]{1,0:T(8,128)(2,1)S(1)}, bf16[1024,512]{1,0:T(8,128)(2,1)}, u32[]{:S(2)}, u32[]{:S(2)}) %collective-permute-start.2) | collective-permute-done | bytes 1048608 | tf_op jit(solution)/shard_map/ppermute | solution.py:242
  91.4 3.1 broadcast_in_dim.78
  100.0 12.2 %collective-permute-done.3 = bf16[1024,512]{1,0:T(8,128)(2,1)S(1)} collective-permute-done((bf16[1024,512]{1,0:T(8,128)(2,1)}, bf16[1024,512]{1,0:T(8,128)(2,1)S(1)}, u32[]{:S(2)}, u32[]{:S(2)}) %collective-permute-start.3) | collective-permute-done | bytes 1048608 | tf_op jit(solution)/shard_map/ppermute | solution.py:242
  113.3 3.1 fusion
  117.0 10.5 %convolution_convert_fusion.3.query_ref.key_ref.value_ref = bf16[1024,1536]{1,0:T(8,128)(2,1)S(1)} fusion(bf16[2048,1536]{1,0:T(8,128)(2,1)} %all-gather.5.cloned.1.call-done, bf16[1024,2048]{1,0:T(8,128)(2,1)} %constant_dynamic-update-slice_fusion.4, f32[2048]{0:T(1024)S(1)} %bitcast.81, f32[1024]{0:T(1024)S(1)} %get-tuple-element.234), kind=kOutput, calls=%fused_computation.26 | convolution fusion | flops 6452412416 | bytes 13643776 | tf_op jit(solution)/shard_map/dot_general | solution.py:29
  127.6 8.2 %attend_forward.2 = (bf16[1024,512]{1,0:T(8,128)(2,1)}, bf16[8,1024,1024]{2,1,0:T(8,128)(2,1)}) custom-call(s32[1]{0:T(128)} %dynamic_slice.98.length, f32[4,2,2048]{2,1,0:T(2,128)S(1)} %reshape.185.rel_ref, bf16[1024,1536]{1,0:T(8,128)(2,1)S(1)} %convolution_convert_fusion.3.query_ref.key_ref.value_ref, ...), custom_call_target="tpu_custom_call" | custom-call | flops 2147483648 | bytes 4194304 | tf_op jit(solution)/shard_map/attend_forward/pallas_call | solution.py:91
  136.6 21.4 %attend_forward.3 = (bf16[1024,512]{1,0:T(8,128)(2,1)}, bf16[8,1024,1024]{2,1,0:T(8,128)(2,1)}) custom-call(s32[1]{0:T(128)} %dynamic_slice.98.length, f32[4,2,2048]{2,1,0:T(2,128)S(1)} %reshape.186.rel_ref, bf16[1024,1536]{1,0:T(8,128)(2,1)S(1)} %convolution_convert_fusion.3.query_ref.key_ref.value_ref, ...), custom_call_target="tpu_custom_call", output_to_operand_aliasing={{0}: (5, {}), {1}: (6, {})} | custom-call | flops 6442450944 | bytes 12582912 | tf_op jit(solution)/shard_map/attend_forward/pallas_call | solution.py:91
  163.8 3.3 broadcast_in_dim.80
  168.4 2.8 select_dynamic-update-slice_fusion.2
  171.3 2.6 select_dynamic-update-slice_fusion.1
  176.3 10.4 %collective-permute-done.6 = bf16[256,2048]{1,0:T(8,128)(2,1)S(1)} collective-permute-done((bf16[256,2048]{1,0:T(8,128)(2,1)S(1)}, bf16[256,2048]{1,0:T(8,128)(2,1)S(1)}, u32[]{:S(2)}, u32[]{:S(2)}) %collective-permute-start.6) | collective-permute-done | bytes 1048608 | tf_op jit(solution)/shard_map/ppermute | solution.py:242
  192.4 2.6 select_dynamic-update-slice_fusion
  195.0 15.0 %collective-permute-done.7 = bf16[256,2048]{1,0:T(8,128)(2,1)S(1)} collective-permute-done((bf16[256,2048]{1,0:T(8,128)(2,1)S(1)}, bf16[256,2048]{1,0:T(8,128)(2,1)S(1)}, u32[]{:S(2)}, u32[]{:S(2)}) %collective-permute-start.7) | collective-permute-done | bytes 1048608 | tf_op jit(solution)/shard_map/ppermute | solution.py:242
  210.9 20.3 %collective-permute-done.8 = bf16[256,2048]{1,0:T(8,128)(2,1)S(1)} collective-permute-done((bf16[256,2048]{1,0:T(8,128)(2,1)S(1)}, bf16[256,2048]{1,0:T(8,128)(2,1)S(1)}, u32[]{:S(2)}, u32[]{:S(2)}) %collective-permute-start.8) | collective-permute-done | bytes 1048608 | tf_op jit(solution)/shard_map/ppermute | solution.py:242
  234.2 5.6 fusion.144
  241.2 5.2 fusion.56
  246.5 8.4 %fusion.143 = f32[256,2048]{1,0:T(8,128)} fusion(bf16[2048,2560]{1,0:T(8,128)(2,1)} %all-gather.9.cloned.1.call-done, bf16[256,1280]{1,0:T(8,128)(2,1)S(1)} %get-tuple-element.217, bf16[256,1280]{1,0:T(8,128)(2,1)S(1)} %get-tuple-element.216), kind=kOutput, calls=%fused_computation.252 | convolution fusion | flops 2686976000 | bytes 13893632 | tf_op jit(solution)/shard_map/dot_general | solution.py:29
  257.5 5.9 fusion.145
  264.0 4.0 fusion.63
  268.1 7.9 %convolution_convert_fusion.7 = bf16[256,2048]{1,0:T(8,128)(2,1)} fusion(bf16[2048,2560]{1,0:T(8,128)(2,1)} %all-gather.9.cloned.1.call-done, bf16[256,1280]{1,0:T(8,128)(2,1)S(1)} %get-tuple-element.215, bf16[256,1280]{1,0:T(8,128)(2,1)S(1)} %get-tuple-element.214), kind=kOutput, calls=%fused_computation.41 | convolution fusion | flops 2687500288 | bytes 12845056 | tf_op jit(solution)/shard_map/dot_general | solution.py:29
  276.0 2.7 collective-permute-done.10
  279.0 5.9 fusion.146
  285.4 4.0 fusion.70
  291.6 7.3 %convolution_convert_fusion.6 = bf16[256,2048]{1,0:T(8,128)(2,1)S(1)} fusion(bf16[2048,2560]{1,0:T(8,128)(2,1)} %all-gather.9.cloned.1.call-done, bf16[256,1280]{1,0:T(8,128)(2,1)} %copy-done.37, bf16[256,1280]{1,0:T(8,128)(2,1)} %copy-done.36), kind=kOutput, calls=%fused_computation.40 | convolution fusion | flops 2687500288 | bytes 12845056 | tf_op jit(solution)/shard_map/dot_general | solution.py:29
  298.9 2.9 collective-permute-done.11
  302.3 5.9 fusion.147
  308.7 4.8 fusion.77
  315.8 8.3 %convolution_convert_fusion.5 = bf16[256,2048]{1,0:T(8,128)(2,1)} fusion(bf16[2048,2560]{1,0:T(8,128)(2,1)} %all-gather.9.cloned.1.call-done, bf16[256,1280]{1,0:T(8,128)(2,1)} %copy-done.35, bf16[256,1280]{1,0:T(8,128)(2,1)} %copy-done.34), kind=kOutput, calls=%fused_computation.39 | convolution fusion | flops 2687500288 | bytes 12845056 | tf_op jit(solution)/shard_map/dot_general | solution.py:29
  324.1 2.6 add_convert_fusion.6
  329.1 16.5 %convolution_convert_fusion = bf16[2048,2560]{1,0:T(8,128)(2,1)} fusion(bf16[256,2560]{1,0:T(8,128)(2,1)} %pad_maximum_fusion.5, bf16[256,2560]{1,0:T(8,128)(2,1)} %pad_maximum_fusion.4, bf16[256,2560]{1,0:T(8,128)(2,1)S(1)} %pad_maximum_fusion.3, bf16[256,2560]{1,0:T(8,128)(2,1)S(1)} %pad_maximum_fusion.2, bf16[256,2048]{1,0:T(8,128)(2,1)} %collective-permute-done.11, ...), kind=kOutput, calls=%fused_computation.2 | convolution fusion | flops 10780409856 | bytes 19922944 | tf_op jit(solution)/shard_map/dot_general | solution.py:29
  350.3 9.7 %convolution_convert_fusion.2 = bf16[1280,2048]{1,0:T(8,128)(2,1)} fusion(bf16[1024,1280]{1,0:T(8,128)(2,1)S(1)} %copy-done.20, bf16[1024,2048]{1,0:T(8,128)(2,1)} %select_dynamic-update-slice_fusion), kind=kOutput, calls=%fused_computation.9 | convolution fusion | flops 5371330560 | bytes 12058624 | tf_op jit(solution)/shard_map/dot_general | solution.py:29
  360.0 9.3 %collective-permute-done.14 = bf16[256,2048]{1,0:T(8,128)(2,1)S(1)} collective-permute-done((bf16[256,2048]{1,0:T(8,128)(2,1)S(1)}, bf16[256,2048]{1,0:T(8,128)(2,1)S(1)}, u32[]{:S(2)}, u32[]{:S(2)}) %collective-permute-start.14) | collective-permute-done | bytes 1048608 | tf_op jit(solution)/shard_map/ppermute | solution.py:242
  373.4 3.3 fusion.78
  381.9 13.8 %collective-permute-done.15 = bf16[256,2048]{1,0:T(8,128)(2,1)S(1)} collective-permute-done((bf16[256,2048]{1,0:T(8,128)(2,1)S(1)}, bf16[256,2048]{1,0:T(8,128)(2,1)S(1)}, u32[]{:S(2)}, u32[]{:S(2)}) %collective-permute-start.15) | collective-permute-done | bytes 1048608 | tf_op jit(solution)/shard_map/ppermute | solution.py:242
  399.6 20.7 %collective-permute-done.16 = bf16[256,2048]{1,0:T(8,128)(2,1)S(1)} collective-permute-done((bf16[256,2048]{1,0:T(8,128)(2,1)S(1)}, bf16[256,2048]{1,0:T(8,128)(2,1)S(1)}, u32[]{:S(2)}, u32[]{:S(2)}) %collective-permute-start.16) | collective-permute-done | bytes 1048608 | tf_op jit(solution)/shard_map/ppermute | solution.py:242
  424.3 12.9 %collective-permute-done.17 = bf16[256,2048]{1,0:T(8,128)(2,1)S(1)} collective-permute-done((bf16[256,2048]{1,0:T(8,128)(2,1)S(1)}, bf16[256,2048]{1,0:T(8,128)(2,1)S(1)}, u32[]{:S(2)}, u32[]{:S(2)}) %collective-permute-start.17) | collective-permute-done | bytes 1048608 | tf_op jit(solution)/shard_map/ppermute | solution.py:242
  439.0 5.3 convolution_convert_fusion.4
  444.2 6.8 %pad_maximum_fusion = bf16[1792,2048]{1,0:T(8,128)(2,1)} fusion(bf16[1280,2048]{1,0:T(8,128)(2,1)} %convolution_convert_fusion.2, bf16[512,2048]{1,0:T(8,128)(2,1)S(1)} %convolution_convert_fusion.4), kind=kLoop, calls=%fused_computation.10 | loop fusion | flops 14680064 | bytes 14680064 | tf_op jit(solution)/shard_map/concatenate | solution.py:508
  451.2 16.7 %attend_backward.2 = (bf16[1024,1536]{1,0:T(8,128)(2,1)S(1)}, f32[2,2,2048]{2,1,0:T(2,128)S(1)}) custom-call(bf16[8,1024,1024]{2,1,0:T(8,128)(2,1)} %get-tuple-element.125.soft_ref, bf16[1024,1536]{1,0:T(8,128)(2,1)} %copy-done.2, bf16[1024,512]{1,0:T(8,128)(2,1)S(1)} %fusion.91.grad_ref, bf16[1024,512]{1,0:T(8,128)(2,1)} %get-tuple-element.128.out_ref, ...), custom_call_target="tpu_custom_call" | custom-call | flops 10737418240 | bytes 8388608 | tf_op jit(solution)/shard_map/attend_backward/pallas_call | solution.py:207
  469.5 4.1 collective-permute-done.18
  475.6 17.9 %attend_backward.3 = (bf16[1024,1536]{1,0:T(8,128)(2,1)S(1)}, f32[2,2,2048]{2,1,0:T(2,128)S(1)}) custom-call(bf16[8,1024,1024]{2,1,0:T(8,128)(2,1)} %get-tuple-element.125.soft_ref, bf16[1024,1536]{1,0:T(8,128)(2,1)} %copy-done.2, bf16[1024,512]{1,0:T(8,128)(2,1)S(1)} %copy-done.5, bf16[1024,512]{1,0:T(8,128)(2,1)} %get-tuple-element.128.out_ref, ...), custom_call_target="tpu_custom_call" | custom-call | flops 10737418240 | bytes 8388608 | tf_op jit(solution)/shard_map/attend_backward/pallas_call | solution.py:207
  493.5 2.6 collective-permute-done.19
  496.1 4.6 fusion.38
  500.7 12.3 %convolution_convert_fusion.1 = bf16[2048,1536]{1,0:T(8,128)(2,1)} fusion(bf16[1024,1536]{1,0:T(8,128)(2,1)S(1)} %get-tuple-element.180, bf16[1024,2048]{1,0:T(8,128)(2,1)} %constant_dynamic-update-slice_fusion.4, f32[2048]{0:T(1024)S(1)} %bitcast.82, f32[1024]{0:T(1024)S(1)} %copy-done.46), kind=kOutput, calls=%fused_computation.8 | convolution fusion | flops 6453985280 | bytes 13643776 | tf_op jit(solution)/shard_map/dot_general | solution.py:29
  513.0 4.2 fusion.41
  517.2 5.2 collective-permute-done.20
  523.9 3.0 add_convert_fusion.3
  529.4 4.4 fusion.44
  533.8 17.7 %collective-permute-done.21 = bf16[1024,512]{1,0:T(8,128)(2,1)} collective-permute-done((bf16[1024,512]{1,0:T(8,128)(2,1)}, bf16[1024,512]{1,0:T(8,128)(2,1)}, u32[]{:S(2)}, u32[]{:S(2)}) %collective-permute-start.21) | collective-permute-done | bytes 1048608 | tf_op jit(solution)/shard_map/ppermute | solution.py:242
  551.6 2.8 add_convert_fusion.2
  554.4 4.4 fusion.47
  560.2 4.2 collective-permute-start.25
  564.4 9.2 %collective-permute-done.24 = f32[8,128]{1,0:T(8,128)S(1)} collective-permute-done((f32[8,128]{1,0:T(8,128)S(1)}, f32[8,128]{1,0:T(8,128)S(1)}, u32[]{:S(2)}, u32[]{:S(2)}) %collective-permute-start.24) | collective-permute-done | bytes 4128 | tf_op jit(solution)/shard_map/ppermute | solution.py:274
  578.2 3.4 fusion.29
  584.6 7.8 %all_gather.20 = f32[8,41,128]{2,1,0:T(8,128)S(1)} all-gather(f32[1,41,128]{2,1,0:T(8,128)S(1)} %maximum_bitcast_fusion), channel_id=1, replica_groups=mesh['dp'=8,'mp'=4] {'dp'}, dimensions={0}, use_global_device_ids=true | all-gather | bytes 188928 | tf_op jit(solution)/shard_map/all_gather | solution.py:568
  592.5 3.1 collective-permute-start.26
  595.6 3.6 all-to-all-start.1
  600.1 3.2 fusion.92
  (305 shorter events, 103.6 us)
Async XLA Ops:
  7.2 28.6 %collective-permute-start = (bf16[1024,512]{1,0:T(8,128)(2,1)}, bf16[1024,512]{1,0:T(8,128)(2,1)}, u32[]{:S(2)}, u32[]{:S(2)}) collective-permute-start(bf16[1024,512]{1,0:T(8,128)(2,1)} %bitcast.71), channel_id=1, source_target_pairs={{0,1},{1,2},{2,3},{3,0},{4,5},{5,6},{6,7},{7,4},{8,9},{9,10},{10,1... | collective-permute-start | bytes 3145736 | tf_op jit(solution)/shard_map/ppermute | solution.py:242
  13.4 19.1 %all-to-all-start = ((bf16[8,128,512]{2,1,0:T(8,128)(2,1)}), bf16[8,128,512]{2,1,0:T(8,128)(2,1)S(1)}, u32[]{:S(2)}, u32[]{:S(2)}) async-start(bf16[8,128,512]{2,1,0:T(8,128)(2,1)} %broadcast_select_fusion.1), calls=%async_computation | async-start | bytes 2097152 | tf_op jit(solution)/shard_map/all_to_all | solution.py:321
  17.1 99.9 %all-gather.5.cloned.1.call-start = ((), (), s32[]{:S(2)}) async-start(), calls=%async_computation.5 | async-start | bytes 7077888 | tf_op jit(solution)/shard_map/all_gather | solution.py:355
  17.2 18.7 %copy-start.56 = (f32[256]{0:T(256)S(1)}, f32[256]{0:T(256)}, u32[]{:S(2)}) copy-start(f32[256]{0:T(256)} %param.39) | copy-start | bytes 3076
  17.2 18.7 %copy-start.57 = (f32[256]{0:T(256)S(1)}, f32[256]{0:T(256)}, u32[]{:S(2)}) copy-start(f32[256]{0:T(256)} %param.40) | copy-start | bytes 3076
  17.2 18.7 %copy-start.52 = (f32[4,8]{1,0:T(4,128)S(1)}, f32[4,8]{1,0:T(4,128)}, u32[]{:S(2)}) copy-start(f32[4,8]{1,0:T(4,128)} %param.41) | copy-start | bytes 388
  17.3 28.9 %copy-start.21 = (f32[1280,256]{1,0:T(8,128)S(1)}, f32[1280,256]{1,0:T(8,128)}, u32[]{:S(2)}) copy-start(f32[1280,256]{1,0:T(8,128)} %param.38) | copy-start | bytes 3932164
  32.5 62.0 %copy-start.7 = (bf16[8,128,512]{2,1,0:T(8,128)(2,1)}, bf16[8,128,512]{2,1,0:T(8,128)(2,1)S(1)}, u32[]{:S(2)}) copy-start(bf16[8,128,512]{2,1,0:T(8,128)(2,1)S(1)} %all-to-all-done) | copy-start | bytes 3145732
  35.8 125.0 %all-gather.7.cloned.1.call-start = ((), (), s32[]{:S(2)}) async-start(), calls=%async_computation.6 | async-start | bytes 8257536 | tf_op jit(solution)/shard_map/all_gather | solution.py:366
  35.8 26.2 %collective-permute-start.1 = (bf16[1024,512]{1,0:T(8,128)(2,1)S(1)}, bf16[1024,512]{1,0:T(8,128)(2,1)S(1)}, u32[]{:S(2)}, u32[]{:S(2)}) collective-permute-start(bf16[1024,512]{1,0:T(8,128)(2,1)S(1)} %bitcast.63), channel_id=1, source_target_pairs={{0,1},{1,2},{2,3},{3,0},{4,5},{5,6},{6,7},{7,4},{8,9},{9,10},{10,1... | collective-permute-start | bytes 3145736 | tf_op jit(solution)/shard_map/ppermute | solution.py:242
  46.3 15.9 %copy-start.22 = (f32[256,1280]{1,0:T(8,128)S(1)}, f32[256,1280]{1,0:T(8,128)}, u32[]{:S(2)}) copy-start(f32[256,1280]{1,0:T(8,128)} %param.36) | copy-start | bytes 3932164
  62.1 172.2 %all-gather.9.cloned.1.call-start = ((), (), s32[]{:S(2)}) async-start(), calls=%async_computation.7 | async-start | bytes 11796480 | tf_op jit(solution)/shard_map/all_gather | solution.py:368
  62.1 25.4 %collective-permute-start.2 = (bf16[1024,512]{1,0:T(8,128)(2,1)S(1)}, bf16[1024,512]{1,0:T(8,128)(2,1)}, u32[]{:S(2)}, u32[]{:S(2)}) collective-permute-start(bf16[1024,512]{1,0:T(8,128)(2,1)S(1)} %collective-permute-done.1), channel_id=1, source_target_pairs={{0,1},{1,2},{2,3},{3,0},{4,5},{5,6},{6,7},{7,4},{8,9},{9,10},{10,1... | collective-permute-start | bytes 3145736 | tf_op jit(solution)/shard_map/ppermute | solution.py:242
  63.8 23.8 %copy-start.59 = (s32[8]{0:T(128)S(1)}, s32[8]{0:T(128)}, u32[]{:S(2)}) copy-start(s32[8]{0:T(128)} %param.30) | copy-start | bytes 100
  63.8 26.4 %copy-start.58 = (s32[8]{0:T(128)S(1)}, s32[8]{0:T(128)}, u32[]{:S(2)}) copy-start(s32[8]{0:T(128)} %param.29) | copy-start | bytes 100
  63.9 27.0 %copy-start.49 = (s32[2047]{0:T(1024)S(1)}, s32[2047]{0:T(1024)}, u32[]{:S(2)}) copy-start(s32[2047]{0:T(1024)} %param.31) | copy-start | bytes 24568
  87.5 386.1 %reduce-scatter.4.cloned.1.call-start = ((), (), s32[]{:S(2)}) async-start(), calls=%async_computation.8 | async-start | bytes 11796480 | tf_op jit(solution)/shard_map/reduce_scatter | solution.py:461
  87.6 24.6 %collective-permute-start.3 = (bf16[1024,512]{1,0:T(8,128)(2,1)}, bf16[1024,512]{1,0:T(8,128)(2,1)S(1)}, u32[]{:S(2)}, u32[]{:S(2)}) collective-permute-start(bf16[1024,512]{1,0:T(8,128)(2,1)} %collective-permute-done.2), channel_id=1, source_target_pairs={{0,1},{1,2},{2,3},{3,0},{4,5},{5,6},{6,7},{7,4},{8,9},{9,10},{10,1... | collective-permute-start | bytes 3145736 | tf_op jit(solution)/shard_map/ppermute | solution.py:242
  95.8 21.3 %copy-start.47 = (f32[1,2,8,128]{3,1,2,0:T(2,128)}, f32[1,2,8,128]{3,1,2,0:T(2,128)S(1)}, u32[]{:S(2)}) copy-start(f32[1,2,8,128]{3,1,2,0:T(2,128)S(1)} %copy.44) | copy-start | bytes 24580
  112.2 23.7 %collective-permute-start.4 = (bf16[1024,512]{1,0:T(8,128)(2,1)}, bf16[1024,512]{1,0:T(8,128)(2,1)}, u32[]{:S(2)}, u32[]{:S(2)}) collective-permute-start(bf16[1024,512]{1,0:T(8,128)(2,1)} %collective-permute-done), channel_id=1, source_target_pairs={{0,1},{1,2},{2,3},{3,0},{4,5},{5,6},{6,7},{7,4},{8,9},{9,10},{10,1... | collective-permute-start | bytes 3145736 | tf_op jit(solution)/shard_map/ppermute | solution.py:242
  117.0 10.5 %copy-start.45 = (f32[1024]{0:T(1024)}, f32[1024]{0:T(1024)S(1)}, u32[]{:S(2)}) copy-start(f32[1024]{0:T(1024)S(1)} %get-tuple-element.234) | copy-start | bytes 12292
  127.6 9.0 %copy-start.2 = (bf16[1024,1536]{1,0:T(8,128)(2,1)}, bf16[1024,1536]{1,0:T(8,128)(2,1)S(1)}, u32[]{:S(2)}) copy-start(bf16[1024,1536]{1,0:T(8,128)(2,1)S(1)} %convolution_convert_fusion.3.query_ref.key_ref.value_ref) | copy-start | bytes 9437188
  135.8 23.8 %collective-permute-start.5 = (bf16[1024,512]{1,0:T(8,128)(2,1)}, bf16[1024,512]{1,0:T(8,128)(2,1)}, u32[]{:S(2)}, u32[]{:S(2)}) collective-permute-start(bf16[1024,512]{1,0:T(8,128)(2,1)} %collective-permute-done.4), channel_id=1, source_target_pairs={{0,1},{1,2},{2,3},{3,0},{4,5},{5,6},{6,7},{7,4},{8,9},{9,10},{10,1... | collective-permute-start | bytes 3145736 | tf_op jit(solution)/shard_map/ppermute | solution.py:242
  163.2 23.5 %collective-permute-start.6 = (bf16[256,2048]{1,0:T(8,128)(2,1)S(1)}, bf16[256,2048]{1,0:T(8,128)(2,1)S(1)}, u32[]{:S(2)}, u32[]{:S(2)}) collective-permute-start(bf16[256,2048]{1,0:T(8,128)(2,1)S(1)} %convolution_convert_fusion.8), channel_id=1, source_target_pairs={{0,1},{1,2},{2,3},{3,0},{4,5},{5,6},{6,7},{7,4},{8,9},{9,10},{10,1... | collective-permute-start | bytes 3145736 | tf_op jit(solution)/shard_map/ppermute | solution.py:242
  187.0 23.0 %collective-permute-start.7 = (bf16[256,2048]{1,0:T(8,128)(2,1)S(1)}, bf16[256,2048]{1,0:T(8,128)(2,1)S(1)}, u32[]{:S(2)}, u32[]{:S(2)}) collective-permute-start(bf16[256,2048]{1,0:T(8,128)(2,1)S(1)} %add_convert_fusion.8), channel_id=1, source_target_pairs={{0,1},{1,2},{2,3},{3,0},{4,5},{5,6},{6,7},{7,4},{8,9},{9,10},{10,1... | collective-permute-start | bytes 3145736 | tf_op jit(solution)/shard_map/ppermute | solution.py:242
  210.4 20.9 %collective-permute-start.8 = (bf16[256,2048]{1,0:T(8,128)(2,1)S(1)}, bf16[256,2048]{1,0:T(8,128)(2,1)S(1)}, u32[]{:S(2)}, u32[]{:S(2)}) collective-permute-start(bf16[256,2048]{1,0:T(8,128)(2,1)S(1)} %add_convert_fusion.7), channel_id=1, source_target_pairs={{0,1},{1,2},{2,3},{3,0},{4,5},{5,6},{6,7},{7,4},{8,9},{9,10},{10,1... | collective-permute-start | bytes 3145736 | tf_op jit(solution)/shard_map/ppermute | solution.py:242
  233.3 6.6 %copy-start.30 = (bf16[256,2048]{1,0:T(8,128)(2,1)}, bf16[256,2048]{1,0:T(8,128)(2,1)S(1)}, u32[]{:S(2)}) copy-start(bf16[256,2048]{1,0:T(8,128)(2,1)S(1)} %multiply_convert_fusion) | copy-start | bytes 3145732
  233.8 21.4 %collective-permute-start.9 = (bf16[256,2048]{1,0:T(8,128)(2,1)S(1)}, bf16[256,2048]{1,0:T(8,128)(2,1)}, u32[]{:S(2)}, u32[]{:S(2)}) collective-permute-start(bf16[256,2048]{1,0:T(8,128)(2,1)S(1)} %multiply_convert_fusion), channel_id=1, source_target_pairs={{0,1},{1,2},{2,3},{3,0},{4,5},{5,6},{6,7},{7,4},{8,9},{9,10},{10,1... | collective-permute-start | bytes 3145736 | tf_op jit(solution)/shard_map/ppermute | solution.py:242
  246.5 17.4 %slice-start = ((s8[7340032]{0:T(1024)(128)(4,1)}), s8[4194304]{0:T(1024)(128)(4,1)S(1)}, s32[]{:S(2)}) async-start(s8[7340032]{0:T(1024)(128)(4,1)} %bitcast.67), calls=%async_computation.11 | async-start | bytes 8388608
  254.9 9.0 %slice-start.1 = ((s8[7340032]{0:T(1024)(128)(4,1)}), s8[3145728]{0:T(1024)(128)(4,1)S(1)}, s32[]{:S(2)}) async-start(s8[7340032]{0:T(1024)(128)(4,1)} %bitcast.67), calls=%async_computation.12 | async-start | bytes 6291456
  255.2 23.5 %collective-permute-start.10 = (bf16[256,2048]{1,0:T(8,128)(2,1)}, bf16[256,2048]{1,0:T(8,128)(2,1)}, u32[]{:S(2)}, u32[]{:S(2)}) collective-permute-start(bf16[256,2048]{1,0:T(8,128)(2,1)} %collective-permute-done.9), channel_id=1, source_target_pairs={{0,1},{1,2},{2,3},{3,0},{4,5},{5,6},{6,7},{7,4},{8,9},{9,10},{10,1... | collective-permute-start | bytes 3145736 | tf_op jit(solution)/shard_map/ppermute | solution.py:242
  278.7 23.1 %collective-permute-start.11 = (bf16[256,2048]{1,0:T(8,128)(2,1)}, bf16[256,2048]{1,0:T(8,128)(2,1)}, u32[]{:S(2)}, u32[]{:S(2)}) collective-permute-start(bf16[256,2048]{1,0:T(8,128)(2,1)} %collective-permute-done.10), channel_id=1, source_target_pairs={{0,1},{1,2},{2,3},{3,0},{4,5},{5,6},{6,7},{7,4},{8,9},{9,10},{10,1... | collective-permute-start | bytes 3145736 | tf_op jit(solution)/shard_map/ppermute | solution.py:242
  301.8 22.2 %collective-permute-start.12 = (bf16[256,2048]{1,0:T(8,128)(2,1)}, bf16[256,2048]{1,0:T(8,128)(2,1)}, u32[]{:S(2)}, u32[]{:S(2)}) collective-permute-start(bf16[256,2048]{1,0:T(8,128)(2,1)} %convolution_convert_fusion.7), channel_id=1, source_target_pairs={{0,1},{1,2},{2,3},{3,0},{4,5},{5,6},{6,7},{7,4},{8,9},{9,10},{10,1... | collective-permute-start | bytes 3145736 | tf_op jit(solution)/shard_map/ppermute | solution.py:242
  326.7 19.0 %collective-permute-start.13 = (bf16[256,2048]{1,0:T(8,128)(2,1)}, bf16[256,2048]{1,0:T(8,128)(2,1)}, u32[]{:S(2)}, u32[]{:S(2)}) collective-permute-start(bf16[256,2048]{1,0:T(8,128)(2,1)} %add_convert_fusion.6), channel_id=1, source_target_pairs={{0,1},{1,2},{2,3},{3,0},{4,5},{5,6},{6,7},{7,4},{8,9},{9,10},{10,1... | collective-permute-start | bytes 3145736 | tf_op jit(solution)/shard_map/ppermute | solution.py:242
  345.7 188.1 %reduce-scatter.6.cloned.1.call-start = ((), (), s32[]{:S(2)}) async-start(), calls=%async_computation.9 | async-start | bytes 8257536 | tf_op jit(solution)/shard_map/reduce_scatter | solution.py:509
  348.6 20.6 %copy-start.9 = (f32[256,2048]{1,0:T(8,128)S(1)}, f32[256,2048]{1,0:T(8,128)}, u32[]{:S(2)}) copy-start(f32[256,2048]{1,0:T(8,128)} %fusion.143) | copy-start | bytes 6291460
  348.6 20.6 %collective-permute-start.14 = (bf16[256,2048]{1,0:T(8,128)(2,1)S(1)}, bf16[256,2048]{1,0:T(8,128)(2,1)S(1)}, u32[]{:S(2)}, u32[]{:S(2)}) collective-permute-start(bf16[256,2048]{1,0:T(8,128)(2,1)S(1)} %add_convert_fusion.5), channel_id=1, source_target_pairs={{0,1},{1,2},{2,3},{3,0},{4,5},{5,6},{6,7},{7,4},{8,9},{9,10},{10,1... | collective-permute-start | bytes 3145736 | tf_op jit(solution)/shard_map/ppermute | solution.py:242
  369.9 6.7 %slice-start.2 = ((s8[7340032]{0:T(1024)(128)(4,1)}), s8[3145728]{0:T(1024)(128)(4,1)S(1)}, s32[]{:S(2)}) async-start(s8[7340032]{0:T(1024)(128)(4,1)} %bitcast.69), calls=%async_computation.13 | async-start | bytes 6291456
  372.1 23.7 %collective-permute-start.15 = (bf16[256,2048]{1,0:T(8,128)(2,1)S(1)}, bf16[256,2048]{1,0:T(8,128)(2,1)S(1)}, u32[]{:S(2)}, u32[]{:S(2)}) collective-permute-start(bf16[256,2048]{1,0:T(8,128)(2,1)S(1)} %subtract_convert_fusion), channel_id=1, source_target_pairs={{0,1},{1,2},{2,3},{3,0},{4,5},{5,6},{6,7},{7,4},{8,9},{9,10},{10,1... | collective-permute-start | bytes 3145736 | tf_op jit(solution)/shard_map/ppermute | solution.py:242
  381.9 16.6 %copy-start.14 = (f32[1024,512]{1,0:T(8,128)}, f32[1024,512]{1,0:T(8,128)S(1)}, u32[]{:S(2)}) copy-start(f32[1024,512]{1,0:T(8,128)S(1)} %get-tuple-element.188) | copy-start | bytes 6291460
  381.9 16.6 %copy-start.16 = (f32[1024,512]{1,0:T(8,128)}, f32[1024,512]{1,0:T(8,128)S(1)}, u32[]{:S(2)}) copy-start(f32[1024,512]{1,0:T(8,128)S(1)} %get-tuple-element.177) | copy-start | bytes 6291460
  381.9 39.7 %copy-start.13 = (f32[1024,512]{1,0:T(8,128)}, f32[1024,512]{1,0:T(8,128)S(1)}, u32[]{:S(2)}) copy-start(f32[1024,512]{1,0:T(8,128)S(1)} %get-tuple-element.202) | copy-start | bytes 6291460
  395.8 24.6 %collective-permute-start.16 = (bf16[256,2048]{1,0:T(8,128)(2,1)S(1)}, bf16[256,2048]{1,0:T(8,128)(2,1)S(1)}, u32[]{:S(2)}, u32[]{:S(2)}) collective-permute-start(bf16[256,2048]{1,0:T(8,128)(2,1)S(1)} %collective-permute-done.15), channel_id=1, source_target_pairs={{0,1},{1,2},{2,3},{3,0},{4,5},{5,6},{6,7},{7,4},{8,9},{9,10},{10,1... | collective-permute-start | bytes 3145736 | tf_op jit(solution)/shard_map/ppermute | solution.py:242
  420.4 16.7 %collective-permute-start.17 = (bf16[256,2048]{1,0:T(8,128)(2,1)S(1)}, bf16[256,2048]{1,0:T(8,128)(2,1)S(1)}, u32[]{:S(2)}, u32[]{:S(2)}) collective-permute-start(bf16[256,2048]{1,0:T(8,128)(2,1)S(1)} %collective-permute-done.16), channel_id=1, source_target_pairs={{0,1},{1,2},{2,3},{3,0},{4,5},{5,6},{6,7},{7,4},{8,9},{9,10},{10,1... | collective-permute-start | bytes 3145736 | tf_op jit(solution)/shard_map/ppermute | solution.py:242
  439.0 12.2 %copy-start.4 = (bf16[1024,512]{1,0:T(8,128)(2,1)}, bf16[1024,512]{1,0:T(8,128)(2,1)S(1)}, u32[]{:S(2)}) copy-start(bf16[1024,512]{1,0:T(8,128)(2,1)S(1)} %fusion.91.grad_ref) | copy-start | bytes 3145732
  451.1 130.8 %reduce-scatter.8.cloned.1.call-start = ((), (), s32[]{:S(2)}) async-start(), calls=%async_computation.10 | async-start | bytes 7077888 | tf_op jit(solution)/shard_map/reduce_scatter | solution.py:529
  451.1 22.5 %collective-permute-start.18 = (bf16[1024,512]{1,0:T(8,128)(2,1)}, bf16[1024,512]{1,0:T(8,128)(2,1)}, u32[]{:S(2)}, u32[]{:S(2)}) collective-permute-start(bf16[1024,512]{1,0:T(8,128)(2,1)} %convert_element_type.277), channel_id=1, source_target_pairs={{0,1},{1,2},{2,3},{3,0},{4,5},{5,6},{6,7},{7,4},{8,9},{9,10},{10,1... | collective-permute-start | bytes 3145736 | tf_op jit(solution)/shard_map/ppermute | solution.py:242
  451.2 22.4 %copy-start.17 = (f32[1024,512]{1,0:T(8,128)S(1)}, f32[1024,512]{1,0:T(8,128)}, u32[]{:S(2)}) copy-start(f32[1024,512]{1,0:T(8,128)} %copy-done.16) | copy-start | bytes 6291460
  475.3 20.7 %collective-permute-start.19 = (bf16[1024,512]{1,0:T(8,128)(2,1)S(1)}, bf16[1024,512]{1,0:T(8,128)(2,1)S(1)}, u32[]{:S(2)}, u32[]{:S(2)}) collective-permute-start(bf16[1024,512]{1,0:T(8,128)(2,1)S(1)} %add_convert_fusion.4), channel_id=1, source_target_pairs={{0,1},{1,2},{2,3},{3,0},{4,5},{5,6},{6,7},{7,4},{8,9},{9,10},{10,1... | collective-permute-start | bytes 3145736 | tf_op jit(solution)/shard_map/ppermute | solution.py:242
  500.7 21.8 %collective-permute-start.20 = (bf16[1024,512]{1,0:T(8,128)(2,1)}, bf16[1024,512]{1,0:T(8,128)(2,1)}, u32[]{:S(2)}, u32[]{:S(2)}) collective-permute-start(bf16[1024,512]{1,0:T(8,128)(2,1)} %fusion.38), channel_id=1, source_target_pairs={{0,1},{1,2},{2,3},{3,0},{4,5},{5,6},{6,7},{7,4},{8,9},{9,10},{10,1... | collective-permute-start | bytes 3145736 | tf_op jit(solution)/shard_map/ppermute | solution.py:242
  517.2 6.1 copy-start.51
  526.9 24.7 %collective-permute-start.21 = (bf16[1024,512]{1,0:T(8,128)(2,1)}, bf16[1024,512]{1,0:T(8,128)(2,1)}, u32[]{:S(2)}, u32[]{:S(2)}) collective-permute-start(bf16[1024,512]{1,0:T(8,128)(2,1)} %add_convert_fusion.3), channel_id=1, source_target_pairs={{0,1},{1,2},{2,3},{3,0},{4,5},{5,6},{6,7},{7,4},{8,9},{9,10},{10,1... | collective-permute-start | bytes 3145736 | tf_op jit(solution)/shard_map/ppermute | solution.py:242
  529.3 29.5 %collective-permute-start.23 = (f32[8,128]{1,0:T(8,128)S(1)}, f32[8,128]{1,0:T(8,128)S(1)}, u32[]{:S(2)}, u32[]{:S(2)}) collective-permute-start(f32[8,128]{1,0:T(8,128)S(1)} %bitcast.79), channel_id=1, source_target_pairs={{0,1},{1,0},{2,3},{3,2},{4,5},{5,4},{6,7},{7,6},{8,9},{9,8},{10,11... | collective-permute-start | bytes 12296 | tf_op jit(solution)/shard_map/ppermute | solution.py:274
  554.3 23.5 %collective-permute-start.22 = (bf16[1024,512]{1,0:T(8,128)(2,1)}, bf16[1024,512]{1,0:T(8,128)(2,1)}, u32[]{:S(2)}, u32[]{:S(2)}) collective-permute-start(bf16[1024,512]{1,0:T(8,128)(2,1)} %add_convert_fusion.2), channel_id=1, source_target_pairs={{0,1},{1,2},{2,3},{3,0},{4,5},{5,6},{6,7},{7,4},{8,9},{9,10},{10,1... | collective-permute-start | bytes 3145736 | tf_op jit(solution)/shard_map/ppermute | solution.py:242
  558.8 14.8 %copy-start.12 = (bf16[1792,256]{1,0:T(8,128)(2,1)S(1)}, bf16[1792,256]{1,0:T(8,128)(2,1)}, u32[]{:S(2)}) copy-start(bf16[1792,256]{1,0:T(8,128)(2,1)} %reduce-scatter.6.cloned.1.call-done) | copy-start | bytes 2752516
  558.8 19.5 %copy-start.8 = (bf16[8,128,512]{2,1,0:T(8,128)(2,1)S(1)}, bf16[8,128,512]{2,1,0:T(8,128)(2,1)}, u32[]{:S(2)}) copy-start(bf16[8,128,512]{2,1,0:T(8,128)(2,1)} %copy-done.7) | copy-start | bytes 3145732
  558.8 19.5 %copy-start.44 = (f32[1024]{0:T(1024)S(1)}, f32[1024]{0:T(1024)}, u32[]{:S(2)}) copy-start(f32[1024]{0:T(1024)} %get-tuple-element.233) | copy-start | bytes 12292
  558.8 14.8 %collective-permute-start.24 = (f32[8,128]{1,0:T(8,128)S(1)}, f32[8,128]{1,0:T(8,128)S(1)}, u32[]{:S(2)}, u32[]{:S(2)}) collective-permute-start(f32[8,128]{1,0:T(8,128)S(1)} %bitcast_add_fusion), channel_id=1, source_target_pairs={{0,2},{1,3},{2,0},{3,1},{4,6},{5,7},{6,4},{7,5},{8,10},{9,11},{10,... | collective-permute-start | bytes 12296 | tf_op jit(solution)/shard_map/ppermute | solution.py:274
  560.2 32.2 %collective-permute-start.25 = (bf16[1024,512]{1,0:T(8,128)(2,1)}, bf16[1024,512]{1,0:T(8,128)(2,1)S(1)}, u32[]{:S(2)}, u32[]{:S(2)}) collective-permute-start(bf16[1024,512]{1,0:T(8,128)(2,1)} %add_convert_fusion.1), channel_id=1, source_target_pairs={{0,1},{1,2},{2,3},{3,0},{4,5},{5,6},{6,7},{7,4},{8,9},{9,10},{10,1... | collective-permute-start | bytes 3145736 | tf_op jit(solution)/shard_map/ppermute | solution.py:242
  592.5 6.7 %collective-permute-start.26 = (f32[41,128]{1,0:T(8,128)S(1)}, f32[41,128]{1,0:T(8,128)S(1)}, u32[]{:S(2)}, u32[]{:S(2)}) collective-permute-start(f32[41,128]{1,0:T(8,128)S(1)} %reduce_sum.108), channel_id=1, source_target_pairs={{0,1},{1,0},{2,3},{3,2},{4,5},{5,4},{6,7},{7,6},{8,9},{9,8},{10,11... | collective-permute-start | bytes 62984 | tf_op jit(solution)/shard_map/ppermute | solution.py:274
  595.6 19.1 %all-to-all-start.1 = ((bf16[8,128,512]{2,1,0:T(8,128)(2,1)}), bf16[8,128,512]{2,1,0:T(8,128)(2,1)S(1)}, u32[]{:S(2)}, u32[]{:S(2)}) async-start(bf16[8,128,512]{2,1,0:T(8,128)(2,1)} %bitcast.13), calls=%async_computation.4 | async-start | bytes 2097152 | tf_op jit(solution)/shard_map/all_to_all | solution.py:570
  599.2 7.4 %copy-start.38 = (f32[512,256]{1,0:T(8,128)S(1)}, f32[512,256]{1,0:T(8,128)}, u32[]{:S(2)}) copy-start(f32[512,256]{1,0:T(8,128)} %param.45) | copy-start | bytes 1572868
  599.2 4.8 collective-permute-start.27
  600.1 11.3 %copy-start.53 = (f32[4,8]{1,0:T(4,128)S(1)}, f32[4,8]{1,0:T(4,128)}, u32[]{:S(2)}) copy-start(f32[4,8]{1,0:T(4,128)} %param.51) | copy-start | bytes 388
  (37 other events, 118.1 us)
Sparse Core Ops, SparseCore 0:
  35.9 44.8 all-gather.4
  83.3 51.3 all-gather.6
  137.1 63.2 all-gather.8
  345.8 83.0 reduce-scatter.3
  451.2 63.7 reduce-scatter.5
  522.6 57.7 reduce-scatter.7

commit v8 on v7

--- a/solution.py
+++ b/solution.py
@@ -485,8 +485,9 @@
         after_parts[1], output_terms[1], output_terms[2]
     )
     after_parts.append(around(after_parts[1]))
-    after_parts[2], output_terms[3], output_terms[0] = together(
-        after_parts[2], output_terms[3], output_terms[0]
+    grad_out_down = jnp.pad(grad_down, ((heads_columns, 0), (0, 0)))
+    after_parts[2], output_terms[3], output_terms[0], grad_out_down = together(
+        after_parts[2], output_terms[3], output_terms[0], grad_out_down
     )
     after_parts.append(around(after_parts[2]))
     grad_after = grad_y
@@ -504,8 +505,8 @@
     output_sum = around(output_first)
 
     grad_out = dot(attended, grad_after, TN).astype(low)
-    grad_heads, grad_out = together(grad_heads, grad_out)
-    grad_out_down = jnp.concatenate([grad_out, grad_down], axis=0)
+    grad_out_down = lax.dynamic_update_slice(grad_out_down, grad_out, (0, 0))
+    grad_heads, grad_out_down = together(grad_heads, grad_out_down)
     owned_out_down = lax.psum_scatter(grad_out_down, "dp", scatter_dimension=1, tiled=True)
     half = pairs // 2
     first_grads, first_rel = attend_backward(soft_low, qkv, grad_heads, attended, 0, half)

time: 634 us -> 631 us (level)
  local copies, waits for them, and re-layouts: 30.3 us -> 37.9 us
  waiting for transfers between devices: 218 us -> 211 us
    concatenate x1 -> x0, other arithmetic: 6.82 us -> none  [shards(): grad_out_down = jnp.concatenate([grad_out, grad_down], axis=0)]
    pad x0 -> x1, local copies, waits for them, and re-layouts: none -> 6.63 us  [shards(): grad_out_down = jnp.pad(grad_down, ((heads_columns, 0), (0, 0)))]
  transfers between devices with their start and end apart: 36 -> 36, of which waited for: 24 -> 24; matrix products, arithmetic and copies ran while one was open for 42% -> 43% of each run, Pallas kernels for 10% -> 10%
where the time goes in v8:
time: 631 us; the launch traced here: 624 us
  waiting for transfers between devices  211 us (33%)
  matrix products  169 us (27%)
  other arithmetic  70.4 us (11%)
  Pallas kernels  64.5 us (10%)
  local copies, waits for them, and re-layouts  37.9 us (6%)
  starting transfers between devices  31.3 us (5%)
  between operations  22.3 us (4%)
  blocking collectives  16.8 us (3%)
    ppermute x24, waiting for transfers between devices, around(): lax.ppermute(block, 'mp', [(i, (i + 1) % count) for i in range(count)])  189 us
    dot_general x34, matrix products, dot(): lax.dot_general(left, right, dims, preferred_element_type=jnp.float32)  169 us
    pallas_call x2, Pallas kernels, attend_backward(): pl.pallas_call(functools.partial(backward_kernel, first), grid=(last - fi...  34.9 us
    pallas_call x2, Pallas kernels, attend_forward(): pl.pallas_call(kernel, grid_spec=pltpu.PrefetchScalarGridSpec(num_scalar_...  29.5 us
    ppermute x24, starting transfers between devices, around(): lax.ppermute(block, 'mp', [(i, (i + 1) % count) for i in range(count)])  19.8 us
    convert_element_type x8, other arithmetic, add_low(): return (received.astype(jnp.float32) + term).astype(jnp.bfloat16)  13.8 us
    all_to_all x1, waiting for transfers between devices, shards(): lax.all_to_all(picked, 'dp', split_axis=0, concat_axis=0, tiled=True)  13.1 us
  transfers between devices with their start and end apart: 36, of which 24 were waited for; matrix products, arithmetic and copies ran while one was open for 43% of the time, Pallas kernels for 10%

profile of v8, /device:TPU:0, one launch (start us, length us, event | category | flops | bytes accessed | tf_op | source)
XLA Modules:
  0.0 623.5 jit_solution(793004432292077448)
XLA Ops:
  7.2 3.1 collective-permute-start
  13.4 3.7 all-to-all-start
  19.4 13.1 %all-to-all-done = bf16[8,128,512]{2,1,0:T(8,128)(2,1)S(1)} async-done(((bf16[8,128,512]{2,1,0:T(8,128)(2,1)}), bf16[8,128,512]{2,1,0:T(8,128)(2,1)S(1)}, u32[]{:S(2)}, u32[]{:S(2)}) %all-to-all-start) | async-done | bytes 1048608 | tf_op jit(solution)/shard_map/all_to_all | solution.py:321
  32.5 3.3 collective-permute-done
  36.1 9.0 %all-gather = bf16[8,1,544]{2,1,0:T(2,128)(2,1)S(1)} all-gather(bf16[1,1,544]{2,1,0:T(2,128)(2,1)S(1)} %maximum_bitcast_fusion.1), channel_id=1, replica_groups=mesh['dp'=8,'mp'=4] {'dp'}, dimensions={0}, use_global_device_ids=true | all-gather | bytes 9792 | tf_op jit(solution)/shard_map/all_gather | solution.py:362
  47.3 14.8 %collective-permute-done.1 = bf16[1024,512]{1,0:T(8,128)(2,1)S(1)} collective-permute-done((bf16[1024,512]{1,0:T(8,128)(2,1)S(1)}, bf16[1024,512]{1,0:T(8,128)(2,1)S(1)}, u32[]{:S(2)}, u32[]{:S(2)}) %collective-permute-start.1) | collective-permute-done | bytes 1048608 | tf_op jit(solution)/shard_map/ppermute | solution.py:242
  65.0 22.5 %collective-permute-done.2 = bf16[1024,512]{1,0:T(8,128)(2,1)} collective-permute-done((bf16[1024,512]{1,0:T(8,128)(2,1)S(1)}, bf16[1024,512]{1,0:T(8,128)(2,1)}, u32[]{:S(2)}, u32[]{:S(2)}) %collective-permute-start.2) | collective-permute-done | bytes 1048608 | tf_op jit(solution)/shard_map/ppermute | solution.py:242
  91.4 3.1 broadcast_in_dim.78
  100.0 12.1 %collective-permute-done.3 = bf16[1024,512]{1,0:T(8,128)(2,1)S(1)} collective-permute-done((bf16[1024,512]{1,0:T(8,128)(2,1)}, bf16[1024,512]{1,0:T(8,128)(2,1)S(1)}, u32[]{:S(2)}, u32[]{:S(2)}) %collective-permute-start.3) | collective-permute-done | bytes 1048608 | tf_op jit(solution)/shard_map/ppermute | solution.py:242
  113.3 3.1 fusion
  117.0 10.5 %convolution_convert_fusion.3.query_ref.key_ref.value_ref = bf16[1024,1536]{1,0:T(8,128)(2,1)S(1)} fusion(bf16[2048,1536]{1,0:T(8,128)(2,1)} %all-gather.5.cloned.1.call-done, bf16[1024,2048]{1,0:T(8,128)(2,1)} %constant_dynamic-update-slice_fusion.4, f32[2048]{0:T(1024)S(1)} %bitcast.81, f32[1024]{0:T(1024)S(1)} %get-tuple-element.236), kind=kOutput, calls=%fused_computation.25 | convolution fusion | flops 6452412416 | bytes 13643776 | tf_op jit(solution)/shard_map/dot_general | solution.py:29
  127.5 8.2 %attend_forward.2 = (bf16[1024,512]{1,0:T(8,128)(2,1)}, bf16[8,1024,1024]{2,1,0:T(8,128)(2,1)}) custom-call(s32[1]{0:T(128)} %dynamic_slice.98.length, f32[4,2,2048]{2,1,0:T(2,128)S(1)} %reshape.185.rel_ref, bf16[1024,1536]{1,0:T(8,128)(2,1)S(1)} %convolution_convert_fusion.3.query_ref.key_ref.value_ref, ...), custom_call_target="tpu_custom_call" | custom-call | flops 2147483648 | bytes 4194304 | tf_op jit(solution)/shard_map/attend_forward/pallas_call | solution.py:91
  136.6 21.3 %attend_forward.3 = (bf16[1024,512]{1,0:T(8,128)(2,1)}, bf16[8,1024,1024]{2,1,0:T(8,128)(2,1)}) custom-call(s32[1]{0:T(128)} %dynamic_slice.98.length, f32[4,2,2048]{2,1,0:T(2,128)S(1)} %reshape.186.rel_ref, bf16[1024,1536]{1,0:T(8,128)(2,1)S(1)} %convolution_convert_fusion.3.query_ref.key_ref.value_ref, ...), custom_call_target="tpu_custom_call", output_to_operand_aliasing={{0}: (5, {}), {1}: (6, {})} | custom-call | flops 6442450944 | bytes 12582912 | tf_op jit(solution)/shard_map/attend_forward/pallas_call | solution.py:91
  163.7 3.3 broadcast_in_dim.80
  168.4 2.9 select_dynamic-update-slice_fusion.2
  171.3 2.6 select_dynamic-update-slice_fusion.1
  176.3 10.3 %collective-permute-done.6 = bf16[256,2048]{1,0:T(8,128)(2,1)S(1)} collective-permute-done((bf16[256,2048]{1,0:T(8,128)(2,1)S(1)}, bf16[256,2048]{1,0:T(8,128)(2,1)S(1)}, u32[]{:S(2)}, u32[]{:S(2)}) %collective-permute-start.6) | collective-permute-done | bytes 1048608 | tf_op jit(solution)/shard_map/ppermute | solution.py:242
  195.0 15.0 %collective-permute-done.7 = bf16[256,2048]{1,0:T(8,128)(2,1)S(1)} collective-permute-done((bf16[256,2048]{1,0:T(8,128)(2,1)S(1)}, bf16[256,2048]{1,0:T(8,128)(2,1)S(1)}, u32[]{:S(2)}, u32[]{:S(2)}) %collective-permute-start.7) | collective-permute-done | bytes 1048608 | tf_op jit(solution)/shard_map/ppermute | solution.py:242
  210.9 20.2 %collective-permute-done.8 = bf16[256,2048]{1,0:T(8,128)(2,1)S(1)} collective-permute-done((bf16[256,2048]{1,0:T(8,128)(2,1)S(1)}, bf16[256,2048]{1,0:T(8,128)(2,1)S(1)}, u32[]{:S(2)}, u32[]{:S(2)}) %collective-permute-start.8) | collective-permute-done | bytes 1048608 | tf_op jit(solution)/shard_map/ppermute | solution.py:242
  234.3 5.6 fusion.145
  241.2 5.2 fusion.57
  246.5 8.4 %fusion.144 = f32[256,2048]{1,0:T(8,128)} fusion(bf16[2048,2560]{1,0:T(8,128)(2,1)} %all-gather.9.cloned.1.call-done, bf16[256,1280]{1,0:T(8,128)(2,1)S(1)} %get-tuple-element.219, bf16[256,1280]{1,0:T(8,128)(2,1)S(1)} %get-tuple-element.218), kind=kOutput, calls=%fused_computation.252 | convolution fusion | flops 2686976000 | bytes 13893632 | tf_op jit(solution)/shard_map/dot_general | solution.py:29
  257.5 5.9 fusion.146
  264.0 4.0 fusion.64
  268.1 7.9 %convolution_convert_fusion.7 = bf16[256,2048]{1,0:T(8,128)(2,1)} fusion(bf16[2048,2560]{1,0:T(8,128)(2,1)} %all-gather.9.cloned.1.call-done, bf16[256,1280]{1,0:T(8,128)(2,1)S(1)} %get-tuple-element.217, bf16[256,1280]{1,0:T(8,128)(2,1)S(1)} %get-tuple-element.216), kind=kOutput, calls=%fused_computation.41 | convolution fusion | flops 2687500288 | bytes 12845056 | tf_op jit(solution)/shard_map/dot_general | solution.py:29
  276.0 2.6 collective-permute-done.10
  279.0 5.9 fusion.147
  285.4 4.0 fusion.71
  291.7 7.3 %convolution_convert_fusion.6 = bf16[256,2048]{1,0:T(8,128)(2,1)S(1)} fusion(bf16[2048,2560]{1,0:T(8,128)(2,1)} %all-gather.9.cloned.1.call-done, bf16[256,1280]{1,0:T(8,128)(2,1)} %copy-done.38, bf16[256,1280]{1,0:T(8,128)(2,1)} %copy-done.37), kind=kOutput, calls=%fused_computation.40 | convolution fusion | flops 2687500288 | bytes 12845056 | tf_op jit(solution)/shard_map/dot_general | solution.py:29
  299.0 2.8 collective-permute-done.11
  302.3 5.9 fusion.148
  308.8 4.8 fusion.78
  315.9 8.3 %convolution_convert_fusion.5 = bf16[256,2048]{1,0:T(8,128)(2,1)} fusion(bf16[2048,2560]{1,0:T(8,128)(2,1)} %all-gather.9.cloned.1.call-done, bf16[256,1280]{1,0:T(8,128)(2,1)} %copy-done.36, bf16[256,1280]{1,0:T(8,128)(2,1)} %copy-done.35), kind=kOutput, calls=%fused_computation.39 | convolution fusion | flops 2687500288 | bytes 12845056 | tf_op jit(solution)/shard_map/dot_general | solution.py:29
  324.1 2.6 add_convert_fusion.6
  329.2 16.5 %convolution_convert_fusion = bf16[2048,2560]{1,0:T(8,128)(2,1)} fusion(bf16[256,2560]{1,0:T(8,128)(2,1)} %pad_maximum_fusion.4, bf16[256,2560]{1,0:T(8,128)(2,1)} %pad_maximum_fusion.3, bf16[256,2560]{1,0:T(8,128)(2,1)S(1)} %pad_maximum_fusion.2, bf16[256,2560]{1,0:T(8,128)(2,1)S(1)} %pad_maximum_fusion.1, bf16[256,2048]{1,0:T(8,128)(2,1)} %collective-permute-done.11, ...), kind=kOutput, calls=%fused_computation.2 | convolution fusion | flops 10780409856 | bytes 19922944 | tf_op jit(solution)/shard_map/dot_general | solution.py:29
  350.5 9.7 %convolution_convert_fusion.2 = bf16[1280,2048]{1,0:T(8,128)(2,1)} fusion(bf16[1024,1280]{1,0:T(8,128)(2,1)S(1)} %copy-done.21, bf16[1024,2048]{1,0:T(8,128)(2,1)} %select_dynamic-update-slice_fusion), kind=kOutput, calls=%fused_computation.9 | convolution fusion | flops 5371330560 | bytes 12058624 | tf_op jit(solution)/shard_map/dot_general | solution.py:29
  360.2 9.3 %collective-permute-done.14 = bf16[256,2048]{1,0:T(8,128)(2,1)S(1)} collective-permute-done((bf16[256,2048]{1,0:T(8,128)(2,1)S(1)}, bf16[256,2048]{1,0:T(8,128)(2,1)S(1)}, u32[]{:S(2)}, u32[]{:S(2)}) %collective-permute-start.14) | collective-permute-done | bytes 1048608 | tf_op jit(solution)/shard_map/ppermute | solution.py:242
  373.6 4.5 fusion.79
  385.1 11.2 %collective-permute-done.15 = bf16[256,2048]{1,0:T(8,128)(2,1)S(1)} collective-permute-done((bf16[256,2048]{1,0:T(8,128)(2,1)S(1)}, bf16[256,2048]{1,0:T(8,128)(2,1)S(1)}, u32[]{:S(2)}, u32[]{:S(2)}) %collective-permute-start.15) | collective-permute-done | bytes 1048608 | tf_op jit(solution)/shard_map/ppermute | solution.py:242
  396.8 6.6 %pad.4 = bf16[1792,2048]{1,0:T(8,128)(2,1)} pad(bf16[1280,2048]{1,0:T(8,128)(2,1)} %convolution_convert_fusion.2, bf16[]{:T(256)} %constant.96.clone.1), padding=512_0x0_0 | pad | bytes 12582914 | tf_op jit(solution)/shard_map/jit(_pad)/pad | solution.py:488
  407.3 13.9 %collective-permute-done.16 = bf16[256,2048]{1,0:T(8,128)(2,1)S(1)} collective-permute-done((bf16[256,2048]{1,0:T(8,128)(2,1)S(1)}, bf16[256,2048]{1,0:T(8,128)(2,1)S(1)}, u32[]{:S(2)}, u32[]{:S(2)}) %collective-permute-start.16) | collective-permute-done | bytes 1048608 | tf_op jit(solution)/shard_map/ppermute | solution.py:242
  425.1 13.5 %collective-permute-done.17 = bf16[256,2048]{1,0:T(8,128)(2,1)S(1)} collective-permute-done((bf16[256,2048]{1,0:T(8,128)(2,1)S(1)}, bf16[256,2048]{1,0:T(8,128)(2,1)S(1)}, u32[]{:S(2)}, u32[]{:S(2)}) %collective-permute-start.17) | collective-permute-done | bytes 1048608 | tf_op jit(solution)/shard_map/ppermute | solution.py:242
  440.5 6.7 %fusion.25 = bf16[1792,2048]{1,0:T(8,128)(2,1)} fusion(bf16[1792,2048]{1,0:T(8,128)(2,1)} %pad.4, bf16[1024,512]{1,0:T(8,128)(2,1)} %get-tuple-element.129.out_ref, bf16[1024,2048]{1,0:T(8,128)(2,1)} %constant_dynamic-update-slice_fusion), kind=kOutput, calls=%fused_computation.35 | convolution fusion | flops 2148532224 | bytes 7340032 | tf_op jit(solution)/shard_map/dot_general | solution.py:29
  447.3 17.1 %attend_backward.2 = (bf16[1024,1536]{1,0:T(8,128)(2,1)S(1)}, f32[2,2,2048]{2,1,0:T(2,128)S(1)}) custom-call(bf16[8,1024,1024]{2,1,0:T(8,128)(2,1)} %get-tuple-element.126.soft_ref, bf16[1024,1536]{1,0:T(8,128)(2,1)} %copy-done.2, bf16[1024,512]{1,0:T(8,128)(2,1)S(1)} %fusion.92.grad_ref, bf16[1024,512]{1,0:T(8,128)(2,1)} %get-tuple-element.129.out_ref, ...), custom_call_target="tpu_custom_call" | custom-call | flops 10737418240 | bytes 8388608 | tf_op jit(solution)/shard_map/attend_backward/pallas_call | solution.py:207
  466.1 4.6 collective-permute-done.18
  472.7 17.9 %attend_backward.3 = (bf16[1024,1536]{1,0:T(8,128)(2,1)S(1)}, f32[2,2,2048]{2,1,0:T(2,128)S(1)}) custom-call(bf16[8,1024,1024]{2,1,0:T(8,128)(2,1)} %get-tuple-element.126.soft_ref, bf16[1024,1536]{1,0:T(8,128)(2,1)} %copy-done.2, bf16[1024,512]{1,0:T(8,128)(2,1)S(1)} %copy-done.5, bf16[1024,512]{1,0:T(8,128)(2,1)} %get-tuple-element.129.out_ref, ...), custom_call_target="tpu_custom_call" | custom-call | flops 10737418240 | bytes 8388608 | tf_op jit(solution)/shard_map/attend_backward/pallas_call | solution.py:207
  490.5 3.4 collective-permute-done.19
  494.0 4.6 fusion.39
  498.6 11.8 %convolution_convert_fusion.1 = bf16[2048,1536]{1,0:T(8,128)(2,1)} fusion(bf16[1024,1536]{1,0:T(8,128)(2,1)S(1)} %get-tuple-element.183, bf16[1024,2048]{1,0:T(8,128)(2,1)} %constant_dynamic-update-slice_fusion.4, f32[2048]{0:T(1024)S(1)} %bitcast.82, f32[1024]{0:T(1024)S(1)} %copy-done.47), kind=kOutput, calls=%fused_computation.8 | convolution fusion | flops 6453985280 | bytes 13643776 | tf_op jit(solution)/shard_map/dot_general | solution.py:29
  510.4 4.2 fusion.42
  514.6 6.5 %collective-permute-done.20 = bf16[1024,512]{1,0:T(8,128)(2,1)} collective-permute-done((bf16[1024,512]{1,0:T(8,128)(2,1)}, bf16[1024,512]{1,0:T(8,128)(2,1)}, u32[]{:S(2)}, u32[]{:S(2)}) %collective-permute-start.20) | collective-permute-done | bytes 1048608 | tf_op jit(solution)/shard_map/ppermute | solution.py:242
  522.6 3.0 add_convert_fusion.3
  528.1 4.4 fusion.45
  532.5 18.5 %collective-permute-done.21 = bf16[1024,512]{1,0:T(8,128)(2,1)} collective-permute-done((bf16[1024,512]{1,0:T(8,128)(2,1)}, bf16[1024,512]{1,0:T(8,128)(2,1)}, u32[]{:S(2)}, u32[]{:S(2)}) %collective-permute-start.21) | collective-permute-done | bytes 1048608 | tf_op jit(solution)/shard_map/ppermute | solution.py:242
  551.0 2.8 add_convert_fusion.2
  553.8 4.4 fusion.48
  559.6 4.2 collective-permute-start.25
  563.8 8.4 %collective-permute-done.24 = f32[8,128]{1,0:T(8,128)S(1)} collective-permute-done((f32[8,128]{1,0:T(8,128)S(1)}, f32[8,128]{1,0:T(8,128)S(1)}, u32[]{:S(2)}, u32[]{:S(2)}) %collective-permute-start.24) | collective-permute-done | bytes 4128 | tf_op jit(solution)/shard_map/ppermute | solution.py:274
  576.9 3.4 fusion.30
  583.3 7.8 %all_gather.20 = f32[8,41,128]{2,1,0:T(8,128)S(1)} all-gather(f32[1,41,128]{2,1,0:T(8,128)S(1)} %maximum_bitcast_fusion), channel_id=1, replica_groups=mesh['dp'=8,'mp'=4] {'dp'}, dimensions={0}, use_global_device_ids=true | all-gather | bytes 188928 | tf_op jit(solution)/shard_map/all_gather | solution.py:569
  591.1 3.1 collective-permute-start.26
  594.3 3.6 all-to-all-start.1
  598.7 3.2 fusion.93
  606.2 2.5 multiply_add_fusion
  (307 shorter events, 106.3 us)
Async XLA Ops:
  7.2 28.6 %collective-permute-start = (bf16[1024,512]{1,0:T(8,128)(2,1)}, bf16[1024,512]{1,0:T(8,128)(2,1)}, u32[]{:S(2)}, u32[]{:S(2)}) collective-permute-start(bf16[1024,512]{1,0:T(8,128)(2,1)} %bitcast.71), channel_id=1, source_target_pairs={{0,1},{1,2},{2,3},{3,0},{4,5},{5,6},{6,7},{7,4},{8,9},{9,10},{10,1... | collective-permute-start | bytes 3145736 | tf_op jit(solution)/shard_map/ppermute | solution.py:242
  13.4 19.1 %all-to-all-start = ((bf16[8,128,512]{2,1,0:T(8,128)(2,1)}), bf16[8,128,512]{2,1,0:T(8,128)(2,1)S(1)}, u32[]{:S(2)}, u32[]{:S(2)}) async-start(bf16[8,128,512]{2,1,0:T(8,128)(2,1)} %broadcast_select_fusion.1), calls=%async_computation | async-start | bytes 2097152 | tf_op jit(solution)/shard_map/all_to_all | solution.py:321
  17.1 99.9 %all-gather.5.cloned.1.call-start = ((), (), s32[]{:S(2)}) async-start(), calls=%async_computation.5 | async-start | bytes 7077888 | tf_op jit(solution)/shard_map/all_gather | solution.py:355
  17.2 18.7 %copy-start.57 = (f32[256]{0:T(256)S(1)}, f32[256]{0:T(256)}, u32[]{:S(2)}) copy-start(f32[256]{0:T(256)} %param.39) | copy-start | bytes 3076
  17.2 18.7 %copy-start.58 = (f32[256]{0:T(256)S(1)}, f32[256]{0:T(256)}, u32[]{:S(2)}) copy-start(f32[256]{0:T(256)} %param.40) | copy-start | bytes 3076
  17.2 18.7 %copy-start.53 = (f32[4,8]{1,0:T(4,128)S(1)}, f32[4,8]{1,0:T(4,128)}, u32[]{:S(2)}) copy-start(f32[4,8]{1,0:T(4,128)} %param.41) | copy-start | bytes 388
  17.3 28.9 %copy-start.22 = (f32[1280,256]{1,0:T(8,128)S(1)}, f32[1280,256]{1,0:T(8,128)}, u32[]{:S(2)}) copy-start(f32[1280,256]{1,0:T(8,128)} %param.38) | copy-start | bytes 3932164
  32.5 62.0 %copy-start.7 = (bf16[8,128,512]{2,1,0:T(8,128)(2,1)}, bf16[8,128,512]{2,1,0:T(8,128)(2,1)S(1)}, u32[]{:S(2)}) copy-start(bf16[8,128,512]{2,1,0:T(8,128)(2,1)S(1)} %all-to-all-done) | copy-start | bytes 3145732
  35.8 125.0 %all-gather.7.cloned.1.call-start = ((), (), s32[]{:S(2)}) async-start(), calls=%async_computation.6 | async-start | bytes 8257536 | tf_op jit(solution)/shard_map/all_gather | solution.py:366
  35.8 26.2 %collective-permute-start.1 = (bf16[1024,512]{1,0:T(8,128)(2,1)S(1)}, bf16[1024,512]{1,0:T(8,128)(2,1)S(1)}, u32[]{:S(2)}, u32[]{:S(2)}) collective-permute-start(bf16[1024,512]{1,0:T(8,128)(2,1)S(1)} %bitcast.63), channel_id=1, source_target_pairs={{0,1},{1,2},{2,3},{3,0},{4,5},{5,6},{6,7},{7,4},{8,9},{9,10},{10,1... | collective-permute-start | bytes 3145736 | tf_op jit(solution)/shard_map/ppermute | solution.py:242
  46.3 15.9 %copy-start.23 = (f32[256,1280]{1,0:T(8,128)S(1)}, f32[256,1280]{1,0:T(8,128)}, u32[]{:S(2)}) copy-start(f32[256,1280]{1,0:T(8,128)} %param.36) | copy-start | bytes 3932164
  62.1 172.2 %all-gather.9.cloned.1.call-start = ((), (), s32[]{:S(2)}) async-start(), calls=%async_computation.7 | async-start | bytes 11796480 | tf_op jit(solution)/shard_map/all_gather | solution.py:368
  62.1 25.4 %collective-permute-start.2 = (bf16[1024,512]{1,0:T(8,128)(2,1)S(1)}, bf16[1024,512]{1,0:T(8,128)(2,1)}, u32[]{:S(2)}, u32[]{:S(2)}) collective-permute-start(bf16[1024,512]{1,0:T(8,128)(2,1)S(1)} %collective-permute-done.1), channel_id=1, source_target_pairs={{0,1},{1,2},{2,3},{3,0},{4,5},{5,6},{6,7},{7,4},{8,9},{9,10},{10,1... | collective-permute-start | bytes 3145736 | tf_op jit(solution)/shard_map/ppermute | solution.py:242
  63.8 23.8 %copy-start.60 = (s32[8]{0:T(128)S(1)}, s32[8]{0:T(128)}, u32[]{:S(2)}) copy-start(s32[8]{0:T(128)} %param.30) | copy-start | bytes 100
  63.8 26.4 %copy-start.59 = (s32[8]{0:T(128)S(1)}, s32[8]{0:T(128)}, u32[]{:S(2)}) copy-start(s32[8]{0:T(128)} %param.29) | copy-start | bytes 100
  63.9 27.0 %copy-start.50 = (s32[2047]{0:T(1024)S(1)}, s32[2047]{0:T(1024)}, u32[]{:S(2)}) copy-start(s32[2047]{0:T(1024)} %param.31) | copy-start | bytes 24568
  87.5 383.2 %reduce-scatter.4.cloned.1.call-start = ((), (), s32[]{:S(2)}) async-start(), calls=%async_computation.8 | async-start | bytes 11796480 | tf_op jit(solution)/shard_map/reduce_scatter | solution.py:461
  87.6 24.6 %collective-permute-start.3 = (bf16[1024,512]{1,0:T(8,128)(2,1)}, bf16[1024,512]{1,0:T(8,128)(2,1)S(1)}, u32[]{:S(2)}, u32[]{:S(2)}) collective-permute-start(bf16[1024,512]{1,0:T(8,128)(2,1)} %collective-permute-done.2), channel_id=1, source_target_pairs={{0,1},{1,2},{2,3},{3,0},{4,5},{5,6},{6,7},{7,4},{8,9},{9,10},{10,1... | collective-permute-start | bytes 3145736 | tf_op jit(solution)/shard_map/ppermute | solution.py:242
  95.8 21.2 %copy-start.48 = (f32[1,2,8,128]{3,1,2,0:T(2,128)}, f32[1,2,8,128]{3,1,2,0:T(2,128)S(1)}, u32[]{:S(2)}) copy-start(f32[1,2,8,128]{3,1,2,0:T(2,128)S(1)} %copy.44) | copy-start | bytes 24580
  112.2 23.7 %collective-permute-start.4 = (bf16[1024,512]{1,0:T(8,128)(2,1)}, bf16[1024,512]{1,0:T(8,128)(2,1)}, u32[]{:S(2)}, u32[]{:S(2)}) collective-permute-start(bf16[1024,512]{1,0:T(8,128)(2,1)} %collective-permute-done), channel_id=1, source_target_pairs={{0,1},{1,2},{2,3},{3,0},{4,5},{5,6},{6,7},{7,4},{8,9},{9,10},{10,1... | collective-permute-start | bytes 3145736 | tf_op jit(solution)/shard_map/ppermute | solution.py:242
  117.0 10.5 %copy-start.46 = (f32[1024]{0:T(1024)}, f32[1024]{0:T(1024)S(1)}, u32[]{:S(2)}) copy-start(f32[1024]{0:T(1024)S(1)} %get-tuple-element.236) | copy-start | bytes 12292
  127.5 9.0 %copy-start.2 = (bf16[1024,1536]{1,0:T(8,128)(2,1)}, bf16[1024,1536]{1,0:T(8,128)(2,1)S(1)}, u32[]{:S(2)}) copy-start(bf16[1024,1536]{1,0:T(8,128)(2,1)S(1)} %convolution_convert_fusion.3.query_ref.key_ref.value_ref) | copy-start | bytes 9437188
  135.8 23.8 %collective-permute-start.5 = (bf16[1024,512]{1,0:T(8,128)(2,1)}, bf16[1024,512]{1,0:T(8,128)(2,1)}, u32[]{:S(2)}, u32[]{:S(2)}) collective-permute-start(bf16[1024,512]{1,0:T(8,128)(2,1)} %collective-permute-done.4), channel_id=1, source_target_pairs={{0,1},{1,2},{2,3},{3,0},{4,5},{5,6},{6,7},{7,4},{8,9},{9,10},{10,1... | collective-permute-start | bytes 3145736 | tf_op jit(solution)/shard_map/ppermute | solution.py:242
  163.2 23.5 %collective-permute-start.6 = (bf16[256,2048]{1,0:T(8,128)(2,1)S(1)}, bf16[256,2048]{1,0:T(8,128)(2,1)S(1)}, u32[]{:S(2)}, u32[]{:S(2)}) collective-permute-start(bf16[256,2048]{1,0:T(8,128)(2,1)S(1)} %convolution_convert_fusion.8), channel_id=1, source_target_pairs={{0,1},{1,2},{2,3},{3,0},{4,5},{5,6},{6,7},{7,4},{8,9},{9,10},{10,1... | collective-permute-start | bytes 3145736 | tf_op jit(solution)/shard_map/ppermute | solution.py:242
  187.0 23.0 %collective-permute-start.7 = (bf16[256,2048]{1,0:T(8,128)(2,1)S(1)}, bf16[256,2048]{1,0:T(8,128)(2,1)S(1)}, u32[]{:S(2)}, u32[]{:S(2)}) collective-permute-start(bf16[256,2048]{1,0:T(8,128)(2,1)S(1)} %add_convert_fusion.8), channel_id=1, source_target_pairs={{0,1},{1,2},{2,3},{3,0},{4,5},{5,6},{6,7},{7,4},{8,9},{9,10},{10,1... | collective-permute-start | bytes 3145736 | tf_op jit(solution)/shard_map/ppermute | solution.py:242
  210.3 20.9 %collective-permute-start.8 = (bf16[256,2048]{1,0:T(8,128)(2,1)S(1)}, bf16[256,2048]{1,0:T(8,128)(2,1)S(1)}, u32[]{:S(2)}, u32[]{:S(2)}) collective-permute-start(bf16[256,2048]{1,0:T(8,128)(2,1)S(1)} %add_convert_fusion.7), channel_id=1, source_target_pairs={{0,1},{1,2},{2,3},{3,0},{4,5},{5,6},{6,7},{7,4},{8,9},{9,10},{10,1... | collective-permute-start | bytes 3145736 | tf_op jit(solution)/shard_map/ppermute | solution.py:242
  233.2 6.7 %copy-start.31 = (bf16[256,2048]{1,0:T(8,128)(2,1)}, bf16[256,2048]{1,0:T(8,128)(2,1)S(1)}, u32[]{:S(2)}) copy-start(bf16[256,2048]{1,0:T(8,128)(2,1)S(1)} %multiply_convert_fusion) | copy-start | bytes 3145732
  233.8 21.4 %collective-permute-start.9 = (bf16[256,2048]{1,0:T(8,128)(2,1)S(1)}, bf16[256,2048]{1,0:T(8,128)(2,1)}, u32[]{:S(2)}, u32[]{:S(2)}) collective-permute-start(bf16[256,2048]{1,0:T(8,128)(2,1)S(1)} %multiply_convert_fusion), channel_id=1, source_target_pairs={{0,1},{1,2},{2,3},{3,0},{4,5},{5,6},{6,7},{7,4},{8,9},{9,10},{10,1... | collective-permute-start | bytes 3145736 | tf_op jit(solution)/shard_map/ppermute | solution.py:242
  246.5 17.5 %slice-start = ((s8[7340032]{0:T(1024)(128)(4,1)}), s8[4194304]{0:T(1024)(128)(4,1)S(1)}, s32[]{:S(2)}) async-start(s8[7340032]{0:T(1024)(128)(4,1)} %bitcast.67), calls=%async_computation.11 | async-start | bytes 8388608
  254.9 9.1 %slice-start.1 = ((s8[7340032]{0:T(1024)(128)(4,1)}), s8[3145728]{0:T(1024)(128)(4,1)S(1)}, s32[]{:S(2)}) async-start(s8[7340032]{0:T(1024)(128)(4,1)} %bitcast.67), calls=%async_computation.12 | async-start | bytes 6291456
  255.2 23.5 %collective-permute-start.10 = (bf16[256,2048]{1,0:T(8,128)(2,1)}, bf16[256,2048]{1,0:T(8,128)(2,1)}, u32[]{:S(2)}, u32[]{:S(2)}) collective-permute-start(bf16[256,2048]{1,0:T(8,128)(2,1)} %collective-permute-done.9), channel_id=1, source_target_pairs={{0,1},{1,2},{2,3},{3,0},{4,5},{5,6},{6,7},{7,4},{8,9},{9,10},{10,1... | collective-permute-start | bytes 3145736 | tf_op jit(solution)/shard_map/ppermute | solution.py:242
  278.6 23.1 %collective-permute-start.11 = (bf16[256,2048]{1,0:T(8,128)(2,1)}, bf16[256,2048]{1,0:T(8,128)(2,1)}, u32[]{:S(2)}, u32[]{:S(2)}) collective-permute-start(bf16[256,2048]{1,0:T(8,128)(2,1)} %collective-permute-done.10), channel_id=1, source_target_pairs={{0,1},{1,2},{2,3},{3,0},{4,5},{5,6},{6,7},{7,4},{8,9},{9,10},{10,1... | collective-permute-start | bytes 3145736 | tf_op jit(solution)/shard_map/ppermute | solution.py:242
  301.8 22.4 %collective-permute-start.12 = (bf16[256,2048]{1,0:T(8,128)(2,1)}, bf16[256,2048]{1,0:T(8,128)(2,1)}, u32[]{:S(2)}, u32[]{:S(2)}) collective-permute-start(bf16[256,2048]{1,0:T(8,128)(2,1)} %convolution_convert_fusion.7), channel_id=1, source_target_pairs={{0,1},{1,2},{2,3},{3,0},{4,5},{5,6},{6,7},{7,4},{8,9},{9,10},{10,1... | collective-permute-start | bytes 3145736 | tf_op jit(solution)/shard_map/ppermute | solution.py:242
  326.8 19.0 %collective-permute-start.13 = (bf16[256,2048]{1,0:T(8,128)(2,1)}, bf16[256,2048]{1,0:T(8,128)(2,1)}, u32[]{:S(2)}, u32[]{:S(2)}) collective-permute-start(bf16[256,2048]{1,0:T(8,128)(2,1)} %add_convert_fusion.6), channel_id=1, source_target_pairs={{0,1},{1,2},{2,3},{3,0},{4,5},{5,6},{6,7},{7,4},{8,9},{9,10},{10,1... | collective-permute-start | bytes 3145736 | tf_op jit(solution)/shard_map/ppermute | solution.py:242
  345.8 186.7 %reduce-scatter.6.cloned.1.call-start = ((), (), s32[]{:S(2)}) async-start(), calls=%async_computation.9 | async-start | bytes 8257536 | tf_op jit(solution)/shard_map/reduce_scatter | solution.py:510
  348.8 20.7 %copy-start.9 = (f32[256,2048]{1,0:T(8,128)S(1)}, f32[256,2048]{1,0:T(8,128)}, u32[]{:S(2)}) copy-start(f32[256,2048]{1,0:T(8,128)} %fusion.144) | copy-start | bytes 6291460
  348.8 20.7 %collective-permute-start.14 = (bf16[256,2048]{1,0:T(8,128)(2,1)S(1)}, bf16[256,2048]{1,0:T(8,128)(2,1)S(1)}, u32[]{:S(2)}, u32[]{:S(2)}) collective-permute-start(bf16[256,2048]{1,0:T(8,128)(2,1)S(1)} %add_convert_fusion.5), channel_id=1, source_target_pairs={{0,1},{1,2},{2,3},{3,0},{4,5},{5,6},{6,7},{7,4},{8,9},{9,10},{10,1... | collective-permute-start | bytes 3145736 | tf_op jit(solution)/shard_map/ppermute | solution.py:242
  370.2 7.9 %slice-start.2 = ((s8[7340032]{0:T(1024)(128)(4,1)}), s8[4194304]{0:T(1024)(128)(4,1)S(1)}, s32[]{:S(2)}) async-start(s8[7340032]{0:T(1024)(128)(4,1)} %bitcast.69), calls=%async_computation.13 | async-start | bytes 8388608
  372.3 24.0 %collective-permute-start.15 = (bf16[256,2048]{1,0:T(8,128)(2,1)S(1)}, bf16[256,2048]{1,0:T(8,128)(2,1)S(1)}, u32[]{:S(2)}, u32[]{:S(2)}) collective-permute-start(bf16[256,2048]{1,0:T(8,128)(2,1)S(1)} %subtract_convert_fusion), channel_id=1, source_target_pairs={{0,1},{1,2},{2,3},{3,0},{4,5},{5,6},{6,7},{7,4},{8,9},{9,10},{10,1... | collective-permute-start | bytes 3145736 | tf_op jit(solution)/shard_map/ppermute | solution.py:242
  385.1 11.2 %copy-start.13 = (f32[1024,512]{1,0:T(8,128)}, f32[1024,512]{1,0:T(8,128)S(1)}, u32[]{:S(2)}) copy-start(f32[1024,512]{1,0:T(8,128)S(1)} %get-tuple-element.190) | copy-start | bytes 6291460
  385.1 11.2 %copy-start.15 = (f32[1024,512]{1,0:T(8,128)}, f32[1024,512]{1,0:T(8,128)S(1)}, u32[]{:S(2)}) copy-start(f32[1024,512]{1,0:T(8,128)S(1)} %get-tuple-element.180) | copy-start | bytes 6291460
  385.1 11.2 %copy-start.17 = (f32[1024,512]{1,0:T(8,128)}, f32[1024,512]{1,0:T(8,128)S(1)}, u32[]{:S(2)}) copy-start(f32[1024,512]{1,0:T(8,128)S(1)} %get-tuple-element.163) | copy-start | bytes 6291460
  396.3 25.0 %collective-permute-start.16 = (bf16[256,2048]{1,0:T(8,128)(2,1)S(1)}, bf16[256,2048]{1,0:T(8,128)(2,1)S(1)}, u32[]{:S(2)}, u32[]{:S(2)}) collective-permute-start(bf16[256,2048]{1,0:T(8,128)(2,1)S(1)} %collective-permute-done.15), channel_id=1, source_target_pairs={{0,1},{1,2},{2,3},{3,0},{4,5},{5,6},{6,7},{7,4},{8,9},{9,10},{10,1... | collective-permute-start | bytes 3145736 | tf_op jit(solution)/shard_map/ppermute | solution.py:242
  421.2 17.4 %collective-permute-start.17 = (bf16[256,2048]{1,0:T(8,128)(2,1)S(1)}, bf16[256,2048]{1,0:T(8,128)(2,1)S(1)}, u32[]{:S(2)}, u32[]{:S(2)}) collective-permute-start(bf16[256,2048]{1,0:T(8,128)(2,1)S(1)} %collective-permute-done.16), channel_id=1, source_target_pairs={{0,1},{1,2},{2,3},{3,0},{4,5},{5,6},{6,7},{7,4},{8,9},{9,10},{10,1... | collective-permute-start | bytes 3145736 | tf_op jit(solution)/shard_map/ppermute | solution.py:242
  440.5 6.9 %copy-start.4 = (bf16[1024,512]{1,0:T(8,128)(2,1)}, bf16[1024,512]{1,0:T(8,128)(2,1)S(1)}, u32[]{:S(2)}) copy-start(bf16[1024,512]{1,0:T(8,128)(2,1)S(1)} %fusion.92.grad_ref) | copy-start | bytes 3145732
  447.2 133.3 %reduce-scatter.8.cloned.1.call-start = ((), (), s32[]{:S(2)}) async-start(), calls=%async_computation.10 | async-start | bytes 7077888 | tf_op jit(solution)/shard_map/reduce_scatter | solution.py:530
  447.3 23.5 %collective-permute-start.18 = (bf16[1024,512]{1,0:T(8,128)(2,1)}, bf16[1024,512]{1,0:T(8,128)(2,1)}, u32[]{:S(2)}, u32[]{:S(2)}) collective-permute-start(bf16[1024,512]{1,0:T(8,128)(2,1)} %convert_element_type.279), channel_id=1, source_target_pairs={{0,1},{1,2},{2,3},{3,0},{4,5},{5,6},{6,7},{7,4},{8,9},{9,10},{10,1... | collective-permute-start | bytes 3145736 | tf_op jit(solution)/shard_map/ppermute | solution.py:242
  447.3 23.4 %copy-start.16 = (f32[1024,512]{1,0:T(8,128)S(1)}, f32[1024,512]{1,0:T(8,128)}, u32[]{:S(2)}) copy-start(f32[1024,512]{1,0:T(8,128)} %copy-done.15) | copy-start | bytes 6291460
  472.4 21.6 %collective-permute-start.19 = (bf16[1024,512]{1,0:T(8,128)(2,1)S(1)}, bf16[1024,512]{1,0:T(8,128)(2,1)S(1)}, u32[]{:S(2)}, u32[]{:S(2)}) collective-permute-start(bf16[1024,512]{1,0:T(8,128)(2,1)S(1)} %add_convert_fusion.4), channel_id=1, source_target_pairs={{0,1},{1,2},{2,3},{3,0},{4,5},{5,6},{6,7},{7,4},{8,9},{9,10},{10,1... | collective-permute-start | bytes 3145736 | tf_op jit(solution)/shard_map/ppermute | solution.py:242
  498.6 22.6 %collective-permute-start.20 = (bf16[1024,512]{1,0:T(8,128)(2,1)}, bf16[1024,512]{1,0:T(8,128)(2,1)}, u32[]{:S(2)}, u32[]{:S(2)}) collective-permute-start(bf16[1024,512]{1,0:T(8,128)(2,1)} %fusion.39), channel_id=1, source_target_pairs={{0,1},{1,2},{2,3},{3,0},{4,5},{5,6},{6,7},{7,4},{8,9},{9,10},{10,1... | collective-permute-start | bytes 3145736 | tf_op jit(solution)/shard_map/ppermute | solution.py:242
  514.6 7.4 %copy-start.52 = (s32[2048]{0:T(1024)S(1)}, s32[2048]{0:T(1024)}, u32[]{:S(2)}) copy-start(s32[2048]{0:T(1024)} %copy-done.51) | copy-start | bytes 24580
  525.6 25.5 %collective-permute-start.21 = (bf16[1024,512]{1,0:T(8,128)(2,1)}, bf16[1024,512]{1,0:T(8,128)(2,1)}, u32[]{:S(2)}, u32[]{:S(2)}) collective-permute-start(bf16[1024,512]{1,0:T(8,128)(2,1)} %add_convert_fusion.3), channel_id=1, source_target_pairs={{0,1},{1,2},{2,3},{3,0},{4,5},{5,6},{6,7},{7,4},{8,9},{9,10},{10,1... | collective-permute-start | bytes 3145736 | tf_op jit(solution)/shard_map/ppermute | solution.py:242
  528.0 30.2 %collective-permute-start.23 = (f32[8,128]{1,0:T(8,128)S(1)}, f32[8,128]{1,0:T(8,128)S(1)}, u32[]{:S(2)}, u32[]{:S(2)}) collective-permute-start(f32[8,128]{1,0:T(8,128)S(1)} %bitcast.79), channel_id=1, source_target_pairs={{0,1},{1,0},{2,3},{3,2},{4,5},{5,4},{6,7},{7,6},{8,9},{9,8},{10,11... | collective-permute-start | bytes 12296 | tf_op jit(solution)/shard_map/ppermute | solution.py:274
  553.8 22.7 %collective-permute-start.22 = (bf16[1024,512]{1,0:T(8,128)(2,1)}, bf16[1024,512]{1,0:T(8,128)(2,1)}, u32[]{:S(2)}, u32[]{:S(2)}) collective-permute-start(bf16[1024,512]{1,0:T(8,128)(2,1)} %add_convert_fusion.2), channel_id=1, source_target_pairs={{0,1},{1,2},{2,3},{3,0},{4,5},{5,6},{6,7},{7,4},{8,9},{9,10},{10,1... | collective-permute-start | bytes 3145736 | tf_op jit(solution)/shard_map/ppermute | solution.py:242
  558.2 14.1 %copy-start.12 = (bf16[1792,256]{1,0:T(8,128)(2,1)S(1)}, bf16[1792,256]{1,0:T(8,128)(2,1)}, u32[]{:S(2)}) copy-start(bf16[1792,256]{1,0:T(8,128)(2,1)} %reduce-scatter.6.cloned.1.call-done) | copy-start | bytes 2752516
  558.2 18.7 %copy-start.8 = (bf16[8,128,512]{2,1,0:T(8,128)(2,1)S(1)}, bf16[8,128,512]{2,1,0:T(8,128)(2,1)}, u32[]{:S(2)}) copy-start(bf16[8,128,512]{2,1,0:T(8,128)(2,1)} %copy-done.7) | copy-start | bytes 3145732
  558.2 18.7 %copy-start.45 = (f32[1024]{0:T(1024)S(1)}, f32[1024]{0:T(1024)}, u32[]{:S(2)}) copy-start(f32[1024]{0:T(1024)} %get-tuple-element.235) | copy-start | bytes 12292
  558.2 14.0 %collective-permute-start.24 = (f32[8,128]{1,0:T(8,128)S(1)}, f32[8,128]{1,0:T(8,128)S(1)}, u32[]{:S(2)}, u32[]{:S(2)}) collective-permute-start(f32[8,128]{1,0:T(8,128)S(1)} %bitcast_add_fusion), channel_id=1, source_target_pairs={{0,2},{1,3},{2,0},{3,1},{4,6},{5,7},{6,4},{7,5},{8,10},{9,11},{10,... | collective-permute-start | bytes 12296 | tf_op jit(solution)/shard_map/ppermute | solution.py:274
  559.6 31.5 %collective-permute-start.25 = (bf16[1024,512]{1,0:T(8,128)(2,1)}, bf16[1024,512]{1,0:T(8,128)(2,1)S(1)}, u32[]{:S(2)}, u32[]{:S(2)}) collective-permute-start(bf16[1024,512]{1,0:T(8,128)(2,1)} %add_convert_fusion.1), channel_id=1, source_target_pairs={{0,1},{1,2},{2,3},{3,0},{4,5},{5,6},{6,7},{7,4},{8,9},{9,10},{10,1... | collective-permute-start | bytes 3145736 | tf_op jit(solution)/shard_map/ppermute | solution.py:242
  591.1 6.7 %collective-permute-start.26 = (f32[41,128]{1,0:T(8,128)S(1)}, f32[41,128]{1,0:T(8,128)S(1)}, u32[]{:S(2)}, u32[]{:S(2)}) collective-permute-start(f32[41,128]{1,0:T(8,128)S(1)} %reduce_sum.108), channel_id=1, source_target_pairs={{0,1},{1,0},{2,3},{3,2},{4,5},{5,4},{6,7},{7,6},{8,9},{9,8},{10,11... | collective-permute-start | bytes 62984 | tf_op jit(solution)/shard_map/ppermute | solution.py:274
  594.3 19.1 %all-to-all-start.1 = ((bf16[8,128,512]{2,1,0:T(8,128)(2,1)}), bf16[8,128,512]{2,1,0:T(8,128)(2,1)S(1)}, u32[]{:S(2)}, u32[]{:S(2)}) async-start(bf16[8,128,512]{2,1,0:T(8,128)(2,1)} %bitcast.13), calls=%async_computation.4 | async-start | bytes 2097152 | tf_op jit(solution)/shard_map/all_to_all | solution.py:571
  597.9 7.4 %copy-start.39 = (f32[512,256]{1,0:T(8,128)S(1)}, f32[512,256]{1,0:T(8,128)}, u32[]{:S(2)}) copy-start(f32[512,256]{1,0:T(8,128)} %param.45) | copy-start | bytes 1572868
  597.9 4.8 collective-permute-start.27
  598.6 11.4 %copy-start.54 = (f32[4,8]{1,0:T(4,128)S(1)}, f32[4,8]{1,0:T(4,128)}, u32[]{:S(2)}) copy-start(f32[4,8]{1,0:T(4,128)} %param.51) | copy-start | bytes 388
  (38 other events, 122.3 us)
Sparse Core Ops, SparseCore 0:
  35.9 44.8 all-gather.4
  83.3 51.3 all-gather.6
  137.1 63.2 all-gather.8
  345.9 82.9 reduce-scatter.3
  447.3 62.7 reduce-scatter.5
  521.3 57.6 reduce-scatter.7

commit v9 on v8

--- a/solution.py
+++ b/solution.py
@@ -325,7 +325,7 @@
     features = quarter * tensor_count
     part_rows = seq_len // tensor_count
 
-    x_own, grad_next = together(x_own, around(output_grad[0]))
+    grad_next = around(output_grad[0])
     grad_parts = [output_grad[0], grad_next]
     row_valid = lax.broadcasted_iota(jnp.int32, (seq_len, 1), 0) < length
 
@@ -359,7 +359,9 @@
     units = down_weight.shape[0]
     x_parts = [x_own, around(x_own)]
     small = jnp.concatenate([attn_gain, ffn_gain, bias_table.reshape(-1)]).astype(low)
-    small, x_parts[1] = together(lax.all_gather(small, "dp", axis=0), x_parts[1])
+    small, grad_parts[1], x_parts[1] = together(
+        lax.all_gather(small, "dp", axis=0), grad_parts[1], x_parts[1]
+    )
     for step in range(1, tensor_count - 1):
         x_parts.append(around(x_parts[step]))
     out_down, x_parts[1] = together(out_down, x_parts[1])

time: 631 us -> 683 us (1.082)
  waiting for transfers between devices: 211 us -> 264 us
    ppermute x24, waiting for transfers between devices: 189 us -> 247 us  [around(): lax.ppermute(block, 'mp', [(i, (i + 1) % count) for i in range(count)])]
  transfers between devices with their start and end apart: 36 -> 36, of which waited for: 24 -> 24; matrix products, arithmetic and copies ran while one was open for 43% -> 39% of each run, Pallas kernels for 10% -> 10%
where the time goes in v9:
time: 683 us; the launch traced here: 673 us
  waiting for transfers between devices  264 us (39%)
  matrix products  169 us (25%)
  other arithmetic  71.5 us (10%)
  Pallas kernels  64.6 us (9%)
  local copies, waits for them, and re-layouts  36.4 us (5%)
  starting transfers between devices  27.6 us (4%)
  between operations  22.2 us (3%)
  blocking collectives  17.2 us (3%)
    ppermute x24, waiting for transfers between devices, around(): lax.ppermute(block, 'mp', [(i, (i + 1) % count) for i in range(count)])  247 us
    dot_general x34, matrix products, dot(): lax.dot_general(left, right, dims, preferred_element_type=jnp.float32)  169 us
    pallas_call x2, Pallas kernels, attend_backward(): pl.pallas_call(functools.partial(backward_kernel, first), grid=(last - fi...  35 us
    pallas_call x2, Pallas kernels, attend_forward(): pl.pallas_call(kernel, grid_spec=pltpu.PrefetchScalarGridSpec(num_scalar_...  29.6 us
    ppermute x24, starting transfers between devices, around(): lax.ppermute(block, 'mp', [(i, (i + 1) % count) for i in range(count)])  14.5 us
    convert_element_type x8, other arithmetic, add_low(): return (received.astype(jnp.float32) + term).astype(jnp.bfloat16)  13.8 us
  transfers between devices with their start and end apart: 36, of which 24 were waited for; matrix products, arithmetic and copies ran while one was open for 39% of the time, Pallas kernels for 10%

profile of v9, /device:TPU:0, one launch (start us, length us, event | category | flops | bytes accessed | tf_op | source)
XLA Modules:
  0.0 673.3 jit_solution(5396779794842941836)
XLA Ops:
  10.4 5.2 all-to-all-start
  17.9 13.1 %all-to-all-done = bf16[8,128,512]{2,1,0:T(8,128)(2,1)S(1)} async-done(((bf16[8,128,512]{2,1,0:T(8,128)(2,1)}), bf16[8,128,512]{2,1,0:T(8,128)(2,1)S(1)}, u32[]{:S(2)}, u32[]{:S(2)}) %all-to-all-start) | async-done | bytes 1048608 | tf_op jit(solution)/shard_map/all_to_all | solution.py:321
  34.4 8.1 %all-gather = bf16[8,1,544]{2,1,0:T(2,128)(2,1)S(1)} all-gather(bf16[1,1,544]{2,1,0:T(2,128)(2,1)S(1)} %maximum_bitcast_fusion.1), channel_id=1, replica_groups=mesh['dp'=8,'mp'=4] {'dp'}, dimensions={0}, use_global_device_ids=true | all-gather | bytes 9792 | tf_op jit(solution)/shard_map/all_gather | solution.py:363
  44.6 14.7 %collective-permute-done = bf16[1024,512]{1,0:T(8,128)(2,1)} collective-permute-done((bf16[1024,512]{1,0:T(8,128)(2,1)}, bf16[1024,512]{1,0:T(8,128)(2,1)}, u32[]{:S(2)}, u32[]{:S(2)}) %collective-permute-start) | collective-permute-done | bytes 1048608 | tf_op jit(solution)/shard_map/ppermute | solution.py:242
  59.3 18.5 %collective-permute-done.1 = bf16[1024,512]{1,0:T(8,128)(2,1)S(1)} collective-permute-done((bf16[1024,512]{1,0:T(8,128)(2,1)S(1)}, bf16[1024,512]{1,0:T(8,128)(2,1)S(1)}, u32[]{:S(2)}, u32[]{:S(2)}) %collective-permute-start.1) | collective-permute-done | bytes 1048608 | tf_op jit(solution)/shard_map/ppermute | solution.py:242
  80.7 20.3 %collective-permute-done.2 = bf16[1024,512]{1,0:T(8,128)(2,1)} collective-permute-done((bf16[1024,512]{1,0:T(8,128)(2,1)S(1)}, bf16[1024,512]{1,0:T(8,128)(2,1)}, u32[]{:S(2)}, u32[]{:S(2)}) %collective-permute-start.2) | collective-permute-done | bytes 1048608 | tf_op jit(solution)/shard_map/ppermute | solution.py:242
  105.0 3.1 broadcast_in_dim.78
  113.5 11.0 %collective-permute-done.3 = bf16[1024,512]{1,0:T(8,128)(2,1)S(1)} collective-permute-done((bf16[1024,512]{1,0:T(8,128)(2,1)}, bf16[1024,512]{1,0:T(8,128)(2,1)S(1)}, u32[]{:S(2)}, u32[]{:S(2)}) %collective-permute-start.3) | collective-permute-done | bytes 1048608 | tf_op jit(solution)/shard_map/ppermute | solution.py:242
  125.7 3.1 fusion
  129.4 10.5 %convolution_convert_fusion.3.query_ref.key_ref.value_ref = bf16[1024,1536]{1,0:T(8,128)(2,1)S(1)} fusion(bf16[2048,1536]{1,0:T(8,128)(2,1)} %all-gather.5.cloned.1.call-done, bf16[1024,2048]{1,0:T(8,128)(2,1)} %constant_dynamic-update-slice_fusion.4, f32[2048]{0:T(1024)S(1)} %bitcast.80, f32[1024]{0:T(1024)S(1)} %get-tuple-element.234), kind=kOutput, calls=%fused_computation.25 | convolution fusion | flops 6452412416 | bytes 13643776 | tf_op jit(solution)/shard_map/dot_general | solution.py:29
  139.9 8.2 %attend_forward.2 = (bf16[1024,512]{1,0:T(8,128)(2,1)}, bf16[8,1024,1024]{2,1,0:T(8,128)(2,1)}) custom-call(s32[1]{0:T(128)} %dynamic_slice.98.length, f32[4,2,2048]{2,1,0:T(2,128)S(1)} %reshape.185.rel_ref, bf16[1024,1536]{1,0:T(8,128)(2,1)S(1)} %convolution_convert_fusion.3.query_ref.key_ref.value_ref, ...), custom_call_target="tpu_custom_call" | custom-call | flops 2147483648 | bytes 4194304 | tf_op jit(solution)/shard_map/attend_forward/pallas_call | solution.py:91
  151.2 21.4 %attend_forward.3 = (bf16[1024,512]{1,0:T(8,128)(2,1)}, bf16[8,1024,1024]{2,1,0:T(8,128)(2,1)}) custom-call(s32[1]{0:T(128)} %dynamic_slice.98.length, f32[4,2,2048]{2,1,0:T(2,128)S(1)} %reshape.186.rel_ref, bf16[1024,1536]{1,0:T(8,128)(2,1)S(1)} %convolution_convert_fusion.3.query_ref.key_ref.value_ref, ...), custom_call_target="tpu_custom_call", output_to_operand_aliasing={{0}: (5, {}), {1}: (6, {})} | custom-call | flops 6442450944 | bytes 12582912 | tf_op jit(solution)/shard_map/attend_forward/pallas_call | solution.py:91
  178.3 3.2 broadcast_in_dim.80
  186.6 2.6 select_dynamic-update-slice_fusion.1
  191.6 8.1 %collective-permute-done.6 = bf16[256,2048]{1,0:T(8,128)(2,1)S(1)} collective-permute-done((bf16[256,2048]{1,0:T(8,128)(2,1)S(1)}, bf16[256,2048]{1,0:T(8,128)(2,1)S(1)}, u32[]{:S(2)}, u32[]{:S(2)}) %collective-permute-start.6) | collective-permute-done | bytes 1048608 | tf_op jit(solution)/shard_map/ppermute | solution.py:242
  205.2 2.6 select_dynamic-update-slice_fusion
  207.8 15.2 %collective-permute-done.7 = bf16[256,2048]{1,0:T(8,128)(2,1)S(1)} collective-permute-done((bf16[256,2048]{1,0:T(8,128)(2,1)S(1)}, bf16[256,2048]{1,0:T(8,128)(2,1)S(1)}, u32[]{:S(2)}, u32[]{:S(2)}) %collective-permute-start.7) | collective-permute-done | bytes 1048608 | tf_op jit(solution)/shard_map/ppermute | solution.py:242
  223.7 21.0 %collective-permute-done.8 = bf16[256,2048]{1,0:T(8,128)(2,1)S(1)} collective-permute-done((bf16[256,2048]{1,0:T(8,128)(2,1)S(1)}, bf16[256,2048]{1,0:T(8,128)(2,1)S(1)}, u32[]{:S(2)}, u32[]{:S(2)}) %collective-permute-start.8) | collective-permute-done | bytes 1048608 | tf_op jit(solution)/shard_map/ppermute | solution.py:242
  247.2 5.6 fusion.145
  254.2 5.2 fusion.57
  259.5 8.4 %fusion.144 = f32[256,2048]{1,0:T(8,128)} fusion(bf16[2048,2560]{1,0:T(8,128)(2,1)} %all-gather.9.cloned.1.call-done, bf16[256,1280]{1,0:T(8,128)(2,1)S(1)} %get-tuple-element.217, bf16[256,1280]{1,0:T(8,128)(2,1)S(1)} %get-tuple-element.216), kind=kOutput, calls=%fused_computation.252 | convolution fusion | flops 2686976000 | bytes 13893632 | tf_op jit(solution)/shard_map/dot_general | solution.py:29
  267.9 2.7 collective-permute-done.9
  270.8 5.9 fusion.146
  277.2 4.0 fusion.64
  281.3 7.9 %convolution_convert_fusion.7 = bf16[256,2048]{1,0:T(8,128)(2,1)} fusion(bf16[2048,2560]{1,0:T(8,128)(2,1)} %all-gather.9.cloned.1.call-done, bf16[256,1280]{1,0:T(8,128)(2,1)S(1)} %get-tuple-element.215, bf16[256,1280]{1,0:T(8,128)(2,1)S(1)} %get-tuple-element.214), kind=kOutput, calls=%fused_computation.41 | convolution fusion | flops 2687500288 | bytes 12845056 | tf_op jit(solution)/shard_map/dot_general | solution.py:29
  289.2 6.3 collective-permute-done.10
  295.6 5.9 fusion.147
  301.9 4.0 fusion.71
  308.2 7.3 %convolution_convert_fusion.6 = bf16[256,2048]{1,0:T(8,128)(2,1)S(1)} fusion(bf16[2048,2560]{1,0:T(8,128)(2,1)} %all-gather.9.cloned.1.call-done, bf16[256,1280]{1,0:T(8,128)(2,1)} %copy-done.37, bf16[256,1280]{1,0:T(8,128)(2,1)} %copy-done.36), kind=kOutput, calls=%fused_computation.40 | convolution fusion | flops 2687500288 | bytes 12845056 | tf_op jit(solution)/shard_map/dot_general | solution.py:29
  315.5 5.8 collective-permute-done.11
  321.5 5.9 fusion.148
  327.9 4.8 fusion.78
  334.9 8.3 %convolution_convert_fusion.5 = bf16[256,2048]{1,0:T(8,128)(2,1)} fusion(bf16[2048,2560]{1,0:T(8,128)(2,1)} %all-gather.9.cloned.1.call-done, bf16[256,1280]{1,0:T(8,128)(2,1)} %copy-done.35, bf16[256,1280]{1,0:T(8,128)(2,1)} %copy-done.34), kind=kOutput, calls=%fused_computation.39 | convolution fusion | flops 2687500288 | bytes 12845056 | tf_op jit(solution)/shard_map/dot_general | solution.py:29
  343.2 2.6 collective-permute-done.12
  345.8 2.6 add_convert_fusion.6
  348.4 16.5 %convolution_convert_fusion = bf16[2048,2560]{1,0:T(8,128)(2,1)} fusion(bf16[256,2560]{1,0:T(8,128)(2,1)} %pad_maximum_fusion.4, bf16[256,2560]{1,0:T(8,128)(2,1)} %pad_maximum_fusion.3, bf16[256,2560]{1,0:T(8,128)(2,1)S(1)} %pad_maximum_fusion.2, bf16[256,2560]{1,0:T(8,128)(2,1)S(1)} %pad_maximum_fusion.1, bf16[256,2048]{1,0:T(8,128)(2,1)} %collective-permute-done.11, ...), kind=kOutput, calls=%fused_computation.2 | convolution fusion | flops 10780409856 | bytes 19922944 | tf_op jit(solution)/shard_map/dot_general | solution.py:29
  364.9 9.4 %collective-permute-done.13 = bf16[256,2048]{1,0:T(8,128)(2,1)} collective-permute-done((bf16[256,2048]{1,0:T(8,128)(2,1)}, bf16[256,2048]{1,0:T(8,128)(2,1)}, u32[]{:S(2)}, u32[]{:S(2)}) %collective-permute-start.13) | collective-permute-done | bytes 1048608 | tf_op jit(solution)/shard_map/ppermute | solution.py:242
  376.7 10.2 %convolution_convert_fusion.2 = bf16[1280,2048]{1,0:T(8,128)(2,1)} fusion(bf16[1024,1280]{1,0:T(8,128)(2,1)S(1)} %copy-done.21, bf16[1024,2048]{1,0:T(8,128)(2,1)} %select_dynamic-update-slice_fusion), kind=kOutput, calls=%fused_computation.9 | convolution fusion | flops 5371330560 | bytes 12058624 | tf_op jit(solution)/shard_map/dot_general | solution.py:29
  386.9 16.0 %collective-permute-done.14 = bf16[256,2048]{1,0:T(8,128)(2,1)S(1)} collective-permute-done((bf16[256,2048]{1,0:T(8,128)(2,1)S(1)}, bf16[256,2048]{1,0:T(8,128)(2,1)S(1)}, u32[]{:S(2)}, u32[]{:S(2)}) %collective-permute-start.14) | collective-permute-done | bytes 1048608 | tf_op jit(solution)/shard_map/ppermute | solution.py:242
  405.8 4.3 fusion.79
  417.0 14.2 %collective-permute-done.15 = bf16[256,2048]{1,0:T(8,128)(2,1)S(1)} collective-permute-done((bf16[256,2048]{1,0:T(8,128)(2,1)S(1)}, bf16[256,2048]{1,0:T(8,128)(2,1)S(1)}, u32[]{:S(2)}, u32[]{:S(2)}) %collective-permute-start.15) | collective-permute-done | bytes 1048608 | tf_op jit(solution)/shard_map/ppermute | solution.py:242
  431.3 6.6 pad.4
  441.8 14.2 %collective-permute-done.16 = bf16[256,2048]{1,0:T(8,128)(2,1)S(1)} collective-permute-done((bf16[256,2048]{1,0:T(8,128)(2,1)S(1)}, bf16[256,2048]{1,0:T(8,128)(2,1)S(1)}, u32[]{:S(2)}, u32[]{:S(2)}) %collective-permute-start.16) | collective-permute-done | bytes 1048608 | tf_op jit(solution)/shard_map/ppermute | solution.py:242
  459.8 19.4 %collective-permute-done.17 = bf16[256,2048]{1,0:T(8,128)(2,1)S(1)} collective-permute-done((bf16[256,2048]{1,0:T(8,128)(2,1)S(1)}, bf16[256,2048]{1,0:T(8,128)(2,1)S(1)}, u32[]{:S(2)}, u32[]{:S(2)}) %collective-permute-start.17) | collective-permute-done | bytes 1048608 | tf_op jit(solution)/shard_map/ppermute | solution.py:242
  481.1 6.7 fusion.25
  488.0 17.1 %attend_backward.2 = (bf16[1024,1536]{1,0:T(8,128)(2,1)S(1)}, f32[2,2,2048]{2,1,0:T(2,128)S(1)}) custom-call(bf16[8,1024,1024]{2,1,0:T(8,128)(2,1)} %get-tuple-element.124.soft_ref, bf16[1024,1536]{1,0:T(8,128)(2,1)} %copy-done.2, bf16[1024,512]{1,0:T(8,128)(2,1)S(1)} %fusion.92.grad_ref, bf16[1024,512]{1,0:T(8,128)(2,1)} %get-tuple-element.127.out_ref, ...), custom_call_target="tpu_custom_call" | custom-call | flops 10737418240 | bytes 8388608 | tf_op jit(solution)/shard_map/attend_backward/pallas_call | solution.py:207
  506.7 6.0 collective-permute-done.18
  514.7 17.9 %attend_backward.3 = (bf16[1024,1536]{1,0:T(8,128)(2,1)S(1)}, f32[2,2,2048]{2,1,0:T(2,128)S(1)}) custom-call(bf16[8,1024,1024]{2,1,0:T(8,128)(2,1)} %get-tuple-element.124.soft_ref, bf16[1024,1536]{1,0:T(8,128)(2,1)} %copy-done.2, bf16[1024,512]{1,0:T(8,128)(2,1)S(1)} %copy-done.5, bf16[1024,512]{1,0:T(8,128)(2,1)} %get-tuple-element.127.out_ref, ...), custom_call_target="tpu_custom_call" | custom-call | flops 10737418240 | bytes 8388608 | tf_op jit(solution)/shard_map/attend_backward/pallas_call | solution.py:207
  532.6 8.6 %collective-permute-done.19 = bf16[1024,512]{1,0:T(8,128)(2,1)S(1)} collective-permute-done((bf16[1024,512]{1,0:T(8,128)(2,1)S(1)}, bf16[1024,512]{1,0:T(8,128)(2,1)S(1)}, u32[]{:S(2)}, u32[]{:S(2)}) %collective-permute-start.19) | collective-permute-done | bytes 1048608 | tf_op jit(solution)/shard_map/ppermute | solution.py:242
  541.2 4.6 fusion.39
  545.9 11.8 %convolution_convert_fusion.1 = bf16[2048,1536]{1,0:T(8,128)(2,1)} fusion(bf16[1024,1536]{1,0:T(8,128)(2,1)S(1)} %get-tuple-element.181, bf16[1024,2048]{1,0:T(8,128)(2,1)} %constant_dynamic-update-slice_fusion.4, f32[2048]{0:T(1024)S(1)} %bitcast.81, f32[1024]{0:T(1024)S(1)} %copy-done.46), kind=kOutput, calls=%fused_computation.8 | convolution fusion | flops 6453985280 | bytes 13643776 | tf_op jit(solution)/shard_map/dot_general | solution.py:29
  557.6 4.2 fusion.42
  561.8 10.0 %collective-permute-done.20 = bf16[1024,512]{1,0:T(8,128)(2,1)} collective-permute-done((bf16[1024,512]{1,0:T(8,128)(2,1)}, bf16[1024,512]{1,0:T(8,128)(2,1)}, u32[]{:S(2)}, u32[]{:S(2)}) %collective-permute-start.20) | collective-permute-done | bytes 1048608 | tf_op jit(solution)/shard_map/ppermute | solution.py:242
  573.3 3.0 add_convert_fusion.3
  578.7 4.4 fusion.45
  583.2 21.6 %collective-permute-done.21 = bf16[1024,512]{1,0:T(8,128)(2,1)} collective-permute-done((bf16[1024,512]{1,0:T(8,128)(2,1)}, bf16[1024,512]{1,0:T(8,128)(2,1)}, u32[]{:S(2)}, u32[]{:S(2)}) %collective-permute-start.21) | collective-permute-done | bytes 1048608 | tf_op jit(solution)/shard_map/ppermute | solution.py:242
  604.7 2.8 add_convert_fusion.2
  607.5 4.4 fusion.48
  613.4 4.2 collective-permute-start.25
  617.6 2.6 collective-permute-done.24
  624.9 3.4 fusion.30
  632.4 9.2 %all_gather.20 = f32[8,41,128]{2,1,0:T(8,128)S(1)} all-gather(f32[1,41,128]{2,1,0:T(8,128)S(1)} %maximum_bitcast_fusion), channel_id=1, replica_groups=mesh['dp'=8,'mp'=4] {'dp'}, dimensions={0}, use_global_device_ids=true | all-gather | bytes 188928 | tf_op jit(solution)/shard_map/all_gather | solution.py:571
  643.2 3.6 all-to-all-start.1
  649.3 3.2 fusion.93
  (305 shorter events, 108.1 us)
Async XLA Ops:
  10.4 20.6 %all-to-all-start = ((bf16[8,128,512]{2,1,0:T(8,128)(2,1)}), bf16[8,128,512]{2,1,0:T(8,128)(2,1)S(1)}, u32[]{:S(2)}, u32[]{:S(2)}) async-start(bf16[8,128,512]{2,1,0:T(8,128)(2,1)} %broadcast_select_fusion.1), calls=%async_computation | async-start | bytes 2097152 | tf_op jit(solution)/shard_map/all_to_all | solution.py:321
  15.6 113.8 %all-gather.5.cloned.1.call-start = ((), (), s32[]{:S(2)}) async-start(), calls=%async_computation.5 | async-start | bytes 7077888 | tf_op jit(solution)/shard_map/all_gather | solution.py:355
  15.7 18.6 %copy-start.56 = (f32[256]{0:T(256)S(1)}, f32[256]{0:T(256)}, u32[]{:S(2)}) copy-start(f32[256]{0:T(256)} %param.39) | copy-start | bytes 3076
  15.7 18.6 %copy-start.57 = (f32[256]{0:T(256)S(1)}, f32[256]{0:T(256)}, u32[]{:S(2)}) copy-start(f32[256]{0:T(256)} %param.40) | copy-start | bytes 3076
  15.7 18.6 %copy-start.52 = (f32[4,8]{1,0:T(4,128)S(1)}, f32[4,8]{1,0:T(4,128)}, u32[]{:S(2)}) copy-start(f32[4,8]{1,0:T(4,128)} %param.41) | copy-start | bytes 388
  15.8 27.8 %copy-start.22 = (f32[1280,256]{1,0:T(8,128)S(1)}, f32[1280,256]{1,0:T(8,128)}, u32[]{:S(2)}) copy-start(f32[1280,256]{1,0:T(8,128)} %param.38) | copy-start | bytes 3932164
  31.0 77.1 %copy-start.7 = (bf16[8,128,512]{2,1,0:T(8,128)(2,1)}, bf16[8,128,512]{2,1,0:T(8,128)(2,1)S(1)}, u32[]{:S(2)}) copy-start(bf16[8,128,512]{2,1,0:T(8,128)(2,1)S(1)} %all-to-all-done) | copy-start | bytes 3145732
  31.0 142.8 %all-gather.7.cloned.1.call-start = ((), (), s32[]{:S(2)}) async-start(), calls=%async_computation.6 | async-start | bytes 8257536 | tf_op jit(solution)/shard_map/all_gather | solution.py:368
  31.1 28.3 %collective-permute-start = (bf16[1024,512]{1,0:T(8,128)(2,1)}, bf16[1024,512]{1,0:T(8,128)(2,1)}, u32[]{:S(2)}, u32[]{:S(2)}) collective-permute-start(bf16[1024,512]{1,0:T(8,128)(2,1)} %bitcast.2), channel_id=1, source_target_pairs={{0,1},{1,2},{2,3},{3,0},{4,5},{5,6},{6,7},{7,4},{8,9},{9,10},{10,1... | collective-permute-start | bytes 3145736 | tf_op jit(solution)/shard_map/ppermute | solution.py:242
  32.7 45.1 %collective-permute-start.1 = (bf16[1024,512]{1,0:T(8,128)(2,1)S(1)}, bf16[1024,512]{1,0:T(8,128)(2,1)S(1)}, u32[]{:S(2)}, u32[]{:S(2)}) collective-permute-start(bf16[1024,512]{1,0:T(8,128)(2,1)S(1)} %bitcast.63), channel_id=1, source_target_pairs={{0,1},{1,2},{2,3},{3,0},{4,5},{5,6},{6,7},{7,4},{8,9},{9,10},{10,1... | collective-permute-start | bytes 3145736 | tf_op jit(solution)/shard_map/ppermute | solution.py:242
  43.6 34.4 %copy-start.23 = (f32[256,1280]{1,0:T(8,128)S(1)}, f32[256,1280]{1,0:T(8,128)}, u32[]{:S(2)}) copy-start(f32[256,1280]{1,0:T(8,128)} %param.36) | copy-start | bytes 3932164
  77.8 169.4 %all-gather.9.cloned.1.call-start = ((), (), s32[]{:S(2)}) async-start(), calls=%async_computation.7 | async-start | bytes 11796480 | tf_op jit(solution)/shard_map/all_gather | solution.py:370
  77.9 23.2 %collective-permute-start.2 = (bf16[1024,512]{1,0:T(8,128)(2,1)S(1)}, bf16[1024,512]{1,0:T(8,128)(2,1)}, u32[]{:S(2)}, u32[]{:S(2)}) collective-permute-start(bf16[1024,512]{1,0:T(8,128)(2,1)S(1)} %collective-permute-done.1), channel_id=1, source_target_pairs={{0,1},{1,2},{2,3},{3,0},{4,5},{5,6},{6,7},{7,4},{8,9},{9,10},{10,1... | collective-permute-start | bytes 3145736 | tf_op jit(solution)/shard_map/ppermute | solution.py:242
  79.6 21.7 %copy-start.59 = (s32[8]{0:T(128)S(1)}, s32[8]{0:T(128)}, u32[]{:S(2)}) copy-start(s32[8]{0:T(128)} %param.30) | copy-start | bytes 100
  79.6 24.2 %copy-start.58 = (s32[8]{0:T(128)S(1)}, s32[8]{0:T(128)}, u32[]{:S(2)}) copy-start(s32[8]{0:T(128)} %param.29) | copy-start | bytes 100
  79.6 24.8 %copy-start.49 = (s32[2047]{0:T(1024)S(1)}, s32[2047]{0:T(1024)}, u32[]{:S(2)}) copy-start(s32[2047]{0:T(1024)} %param.31) | copy-start | bytes 24568
  101.1 411.7 %reduce-scatter.4.cloned.1.call-start = ((), (), s32[]{:S(2)}) async-start(), calls=%async_computation.8 | async-start | bytes 11796480 | tf_op jit(solution)/shard_map/reduce_scatter | solution.py:463
  101.1 23.4 %collective-permute-start.3 = (bf16[1024,512]{1,0:T(8,128)(2,1)}, bf16[1024,512]{1,0:T(8,128)(2,1)S(1)}, u32[]{:S(2)}, u32[]{:S(2)}) collective-permute-start(bf16[1024,512]{1,0:T(8,128)(2,1)} %collective-permute-done.2), channel_id=1, source_target_pairs={{0,1},{1,2},{2,3},{3,0},{4,5},{5,6},{6,7},{7,4},{8,9},{9,10},{10,1... | collective-permute-start | bytes 3145736 | tf_op jit(solution)/shard_map/ppermute | solution.py:242
  109.3 20.1 %copy-start.47 = (f32[1,2,8,128]{3,1,2,0:T(2,128)}, f32[1,2,8,128]{3,1,2,0:T(2,128)S(1)}, u32[]{:S(2)}) copy-start(f32[1,2,8,128]{3,1,2,0:T(2,128)S(1)} %copy.44) | copy-start | bytes 24580
  124.5 23.6 %collective-permute-start.4 = (bf16[1024,512]{1,0:T(8,128)(2,1)}, bf16[1024,512]{1,0:T(8,128)(2,1)}, u32[]{:S(2)}, u32[]{:S(2)}) collective-permute-start(bf16[1024,512]{1,0:T(8,128)(2,1)} %collective-permute-done), channel_id=1, source_target_pairs={{0,1},{1,2},{2,3},{3,0},{4,5},{5,6},{6,7},{7,4},{8,9},{9,10},{10,1... | collective-permute-start | bytes 3145736 | tf_op jit(solution)/shard_map/ppermute | solution.py:242
  129.4 10.5 %copy-start.45 = (f32[1024]{0:T(1024)}, f32[1024]{0:T(1024)S(1)}, u32[]{:S(2)}) copy-start(f32[1024]{0:T(1024)S(1)} %get-tuple-element.234) | copy-start | bytes 12292
  139.9 11.3 %copy-start.2 = (bf16[1024,1536]{1,0:T(8,128)(2,1)}, bf16[1024,1536]{1,0:T(8,128)(2,1)S(1)}, u32[]{:S(2)}) copy-start(bf16[1024,1536]{1,0:T(8,128)(2,1)S(1)} %convolution_convert_fusion.3.query_ref.key_ref.value_ref) | copy-start | bytes 9437188
  148.2 24.4 %collective-permute-start.5 = (bf16[1024,512]{1,0:T(8,128)(2,1)}, bf16[1024,512]{1,0:T(8,128)(2,1)}, u32[]{:S(2)}, u32[]{:S(2)}) collective-permute-start(bf16[1024,512]{1,0:T(8,128)(2,1)} %collective-permute-done.4), channel_id=1, source_target_pairs={{0,1},{1,2},{2,3},{3,0},{4,5},{5,6},{6,7},{7,4},{8,9},{9,10},{10,1... | collective-permute-start | bytes 3145736 | tf_op jit(solution)/shard_map/ppermute | solution.py:242
  176.2 23.5 %collective-permute-start.6 = (bf16[256,2048]{1,0:T(8,128)(2,1)S(1)}, bf16[256,2048]{1,0:T(8,128)(2,1)S(1)}, u32[]{:S(2)}, u32[]{:S(2)}) collective-permute-start(bf16[256,2048]{1,0:T(8,128)(2,1)S(1)} %convolution_convert_fusion.8), channel_id=1, source_target_pairs={{0,1},{1,2},{2,3},{3,0},{4,5},{5,6},{6,7},{7,4},{8,9},{9,10},{10,1... | collective-permute-start | bytes 3145736 | tf_op jit(solution)/shard_map/ppermute | solution.py:242
  200.0 23.0 %collective-permute-start.7 = (bf16[256,2048]{1,0:T(8,128)(2,1)S(1)}, bf16[256,2048]{1,0:T(8,128)(2,1)S(1)}, u32[]{:S(2)}, u32[]{:S(2)}) collective-permute-start(bf16[256,2048]{1,0:T(8,128)(2,1)S(1)} %add_convert_fusion.8), channel_id=1, source_target_pairs={{0,1},{1,2},{2,3},{3,0},{4,5},{5,6},{6,7},{7,4},{8,9},{9,10},{10,1... | collective-permute-start | bytes 3145736 | tf_op jit(solution)/shard_map/ppermute | solution.py:242
  223.3 21.3 %collective-permute-start.8 = (bf16[256,2048]{1,0:T(8,128)(2,1)S(1)}, bf16[256,2048]{1,0:T(8,128)(2,1)S(1)}, u32[]{:S(2)}, u32[]{:S(2)}) collective-permute-start(bf16[256,2048]{1,0:T(8,128)(2,1)S(1)} %add_convert_fusion.7), channel_id=1, source_target_pairs={{0,1},{1,2},{2,3},{3,0},{4,5},{5,6},{6,7},{7,4},{8,9},{9,10},{10,1... | collective-permute-start | bytes 3145736 | tf_op jit(solution)/shard_map/ppermute | solution.py:242
  247.2 23.4 %collective-permute-start.9 = (bf16[256,2048]{1,0:T(8,128)(2,1)S(1)}, bf16[256,2048]{1,0:T(8,128)(2,1)}, u32[]{:S(2)}, u32[]{:S(2)}) collective-permute-start(bf16[256,2048]{1,0:T(8,128)(2,1)S(1)} %multiply_convert_fusion), channel_id=1, source_target_pairs={{0,1},{1,2},{2,3},{3,0},{4,5},{5,6},{6,7},{7,4},{8,9},{9,10},{10,1... | collective-permute-start | bytes 3145736 | tf_op jit(solution)/shard_map/ppermute | solution.py:242
  259.5 17.7 %slice-start = ((s8[7340032]{0:T(1024)(128)(4,1)}), s8[4194304]{0:T(1024)(128)(4,1)S(1)}, s32[]{:S(2)}) async-start(s8[7340032]{0:T(1024)(128)(4,1)} %bitcast.67), calls=%async_computation.11 | async-start | bytes 8388608
  267.9 9.3 %slice-start.1 = ((s8[7340032]{0:T(1024)(128)(4,1)}), s8[3145728]{0:T(1024)(128)(4,1)S(1)}, s32[]{:S(2)}) async-start(s8[7340032]{0:T(1024)(128)(4,1)} %bitcast.67), calls=%async_computation.12 | async-start | bytes 6291456
  270.6 25.0 %collective-permute-start.10 = (bf16[256,2048]{1,0:T(8,128)(2,1)}, bf16[256,2048]{1,0:T(8,128)(2,1)}, u32[]{:S(2)}, u32[]{:S(2)}) collective-permute-start(bf16[256,2048]{1,0:T(8,128)(2,1)} %collective-permute-done.9), channel_id=1, source_target_pairs={{0,1},{1,2},{2,3},{3,0},{4,5},{5,6},{6,7},{7,4},{8,9},{9,10},{10,1... | collective-permute-start | bytes 3145736 | tf_op jit(solution)/shard_map/ppermute | solution.py:242
  295.6 25.7 %collective-permute-start.11 = (bf16[256,2048]{1,0:T(8,128)(2,1)}, bf16[256,2048]{1,0:T(8,128)(2,1)}, u32[]{:S(2)}, u32[]{:S(2)}) collective-permute-start(bf16[256,2048]{1,0:T(8,128)(2,1)} %collective-permute-done.10), channel_id=1, source_target_pairs={{0,1},{1,2},{2,3},{3,0},{4,5},{5,6},{6,7},{7,4},{8,9},{9,10},{10,1... | collective-permute-start | bytes 3145736 | tf_op jit(solution)/shard_map/ppermute | solution.py:242
  321.2 24.6 %collective-permute-start.12 = (bf16[256,2048]{1,0:T(8,128)(2,1)}, bf16[256,2048]{1,0:T(8,128)(2,1)}, u32[]{:S(2)}, u32[]{:S(2)}) collective-permute-start(bf16[256,2048]{1,0:T(8,128)(2,1)} %convolution_convert_fusion.7), channel_id=1, source_target_pairs={{0,1},{1,2},{2,3},{3,0},{4,5},{5,6},{6,7},{7,4},{8,9},{9,10},{10,1... | collective-permute-start | bytes 3145736 | tf_op jit(solution)/shard_map/ppermute | solution.py:242
  348.4 25.9 %collective-permute-start.13 = (bf16[256,2048]{1,0:T(8,128)(2,1)}, bf16[256,2048]{1,0:T(8,128)(2,1)}, u32[]{:S(2)}, u32[]{:S(2)}) collective-permute-start(bf16[256,2048]{1,0:T(8,128)(2,1)} %add_convert_fusion.6), channel_id=1, source_target_pairs={{0,1},{1,2},{2,3},{3,0},{4,5},{5,6},{6,7},{7,4},{8,9},{9,10},{10,1... | collective-permute-start | bytes 3145736 | tf_op jit(solution)/shard_map/ppermute | solution.py:242
  364.9 9.5 %copy-start.27 = (bf16[256,2048]{1,0:T(8,128)(2,1)S(1)}, bf16[256,2048]{1,0:T(8,128)(2,1)}, u32[]{:S(2)}) copy-start(bf16[256,2048]{1,0:T(8,128)(2,1)} %convolution_convert_fusion.5) | copy-start | bytes 3145732
  374.4 208.8 %reduce-scatter.6.cloned.1.call-start = ((), (), s32[]{:S(2)}) async-start(), calls=%async_computation.9 | async-start | bytes 8257536 | tf_op jit(solution)/shard_map/reduce_scatter | solution.py:512
  376.2 26.7 %copy-start.9 = (f32[256,2048]{1,0:T(8,128)S(1)}, f32[256,2048]{1,0:T(8,128)}, u32[]{:S(2)}) copy-start(f32[256,2048]{1,0:T(8,128)} %fusion.144) | copy-start | bytes 6291460
  376.2 26.7 %collective-permute-start.14 = (bf16[256,2048]{1,0:T(8,128)(2,1)S(1)}, bf16[256,2048]{1,0:T(8,128)(2,1)S(1)}, u32[]{:S(2)}, u32[]{:S(2)}) collective-permute-start(bf16[256,2048]{1,0:T(8,128)(2,1)S(1)} %add_convert_fusion.5), channel_id=1, source_target_pairs={{0,1},{1,2},{2,3},{3,0},{4,5},{5,6},{6,7},{7,4},{8,9},{9,10},{10,1... | collective-permute-start | bytes 3145736 | tf_op jit(solution)/shard_map/ppermute | solution.py:242
  405.7 25.5 %collective-permute-start.15 = (bf16[256,2048]{1,0:T(8,128)(2,1)S(1)}, bf16[256,2048]{1,0:T(8,128)(2,1)S(1)}, u32[]{:S(2)}, u32[]{:S(2)}) collective-permute-start(bf16[256,2048]{1,0:T(8,128)(2,1)S(1)} %subtract_convert_fusion), channel_id=1, source_target_pairs={{0,1},{1,2},{2,3},{3,0},{4,5},{5,6},{6,7},{7,4},{8,9},{9,10},{10,1... | collective-permute-start | bytes 3145736 | tf_op jit(solution)/shard_map/ppermute | solution.py:242
  417.0 14.2 %copy-start.13 = (f32[1024,512]{1,0:T(8,128)}, f32[1024,512]{1,0:T(8,128)S(1)}, u32[]{:S(2)}) copy-start(f32[1024,512]{1,0:T(8,128)S(1)} %get-tuple-element.188) | copy-start | bytes 6291460
  417.0 14.2 %copy-start.15 = (f32[1024,512]{1,0:T(8,128)}, f32[1024,512]{1,0:T(8,128)S(1)}, u32[]{:S(2)}) copy-start(f32[1024,512]{1,0:T(8,128)S(1)} %get-tuple-element.178) | copy-start | bytes 6291460
  417.0 14.2 %copy-start.17 = (f32[1024,512]{1,0:T(8,128)}, f32[1024,512]{1,0:T(8,128)S(1)}, u32[]{:S(2)}) copy-start(f32[1024,512]{1,0:T(8,128)S(1)} %get-tuple-element.161) | copy-start | bytes 6291460
  431.3 24.7 %collective-permute-start.16 = (bf16[256,2048]{1,0:T(8,128)(2,1)S(1)}, bf16[256,2048]{1,0:T(8,128)(2,1)S(1)}, u32[]{:S(2)}, u32[]{:S(2)}) collective-permute-start(bf16[256,2048]{1,0:T(8,128)(2,1)S(1)} %collective-permute-done.15), channel_id=1, source_target_pairs={{0,1},{1,2},{2,3},{3,0},{4,5},{5,6},{6,7},{7,4},{8,9},{9,10},{10,1... | collective-permute-start | bytes 3145736 | tf_op jit(solution)/shard_map/ppermute | solution.py:242
  456.0 23.3 %collective-permute-start.17 = (bf16[256,2048]{1,0:T(8,128)(2,1)S(1)}, bf16[256,2048]{1,0:T(8,128)(2,1)S(1)}, u32[]{:S(2)}, u32[]{:S(2)}) collective-permute-start(bf16[256,2048]{1,0:T(8,128)(2,1)S(1)} %collective-permute-done.16), channel_id=1, source_target_pairs={{0,1},{1,2},{2,3},{3,0},{4,5},{5,6},{6,7},{7,4},{8,9},{9,10},{10,1... | collective-permute-start | bytes 3145736 | tf_op jit(solution)/shard_map/ppermute | solution.py:242
  481.1 6.9 %copy-start.4 = (bf16[1024,512]{1,0:T(8,128)(2,1)}, bf16[1024,512]{1,0:T(8,128)(2,1)S(1)}, u32[]{:S(2)}) copy-start(bf16[1024,512]{1,0:T(8,128)(2,1)S(1)} %fusion.92.grad_ref) | copy-start | bytes 3145732
  487.8 141.8 %reduce-scatter.8.cloned.1.call-start = ((), (), s32[]{:S(2)}) async-start(), calls=%async_computation.10 | async-start | bytes 7077888 | tf_op jit(solution)/shard_map/reduce_scatter | solution.py:532
  487.9 24.9 %collective-permute-start.18 = (bf16[1024,512]{1,0:T(8,128)(2,1)}, bf16[1024,512]{1,0:T(8,128)(2,1)}, u32[]{:S(2)}, u32[]{:S(2)}) collective-permute-start(bf16[1024,512]{1,0:T(8,128)(2,1)} %convert_element_type.279), channel_id=1, source_target_pairs={{0,1},{1,2},{2,3},{3,0},{4,5},{5,6},{6,7},{7,4},{8,9},{9,10},{10,1... | collective-permute-start | bytes 3145736 | tf_op jit(solution)/shard_map/ppermute | solution.py:242
  488.0 24.8 %copy-start.16 = (f32[1024,512]{1,0:T(8,128)S(1)}, f32[1024,512]{1,0:T(8,128)}, u32[]{:S(2)}) copy-start(f32[1024,512]{1,0:T(8,128)} %copy-done.15) | copy-start | bytes 6291460
  514.5 26.8 %collective-permute-start.19 = (bf16[1024,512]{1,0:T(8,128)(2,1)S(1)}, bf16[1024,512]{1,0:T(8,128)(2,1)S(1)}, u32[]{:S(2)}, u32[]{:S(2)}) collective-permute-start(bf16[1024,512]{1,0:T(8,128)(2,1)S(1)} %add_convert_fusion.4), channel_id=1, source_target_pairs={{0,1},{1,2},{2,3},{3,0},{4,5},{5,6},{6,7},{7,4},{8,9},{9,10},{10,1... | collective-permute-start | bytes 3145736 | tf_op jit(solution)/shard_map/ppermute | solution.py:242
  545.8 26.0 %collective-permute-start.20 = (bf16[1024,512]{1,0:T(8,128)(2,1)}, bf16[1024,512]{1,0:T(8,128)(2,1)}, u32[]{:S(2)}, u32[]{:S(2)}) collective-permute-start(bf16[1024,512]{1,0:T(8,128)(2,1)} %fusion.39), channel_id=1, source_target_pairs={{0,1},{1,2},{2,3},{3,0},{4,5},{5,6},{6,7},{7,4},{8,9},{9,10},{10,1... | collective-permute-start | bytes 3145736 | tf_op jit(solution)/shard_map/ppermute | solution.py:242
  561.8 10.1 %copy-start.60 = (s32[8]{0:T(128)S(1)}, s32[8]{0:T(128)}, u32[]{:S(2)}) copy-start(s32[8]{0:T(128)} %param.30) | copy-start | bytes 100
  561.8 10.9 %copy-start.51 = (s32[2048]{0:T(1024)S(1)}, s32[2048]{0:T(1024)}, u32[]{:S(2)}) copy-start(s32[2048]{0:T(1024)} %copy-done.50) | copy-start | bytes 24580
  576.2 28.5 %collective-permute-start.21 = (bf16[1024,512]{1,0:T(8,128)(2,1)}, bf16[1024,512]{1,0:T(8,128)(2,1)}, u32[]{:S(2)}, u32[]{:S(2)}) collective-permute-start(bf16[1024,512]{1,0:T(8,128)(2,1)} %add_convert_fusion.3), channel_id=1, source_target_pairs={{0,1},{1,2},{2,3},{3,0},{4,5},{5,6},{6,7},{7,4},{8,9},{9,10},{10,1... | collective-permute-start | bytes 3145736 | tf_op jit(solution)/shard_map/ppermute | solution.py:242
  578.7 33.3 %collective-permute-start.23 = (f32[8,128]{1,0:T(8,128)S(1)}, f32[8,128]{1,0:T(8,128)S(1)}, u32[]{:S(2)}, u32[]{:S(2)}) collective-permute-start(f32[8,128]{1,0:T(8,128)S(1)} %bitcast.78), channel_id=1, source_target_pairs={{0,1},{1,0},{2,3},{3,2},{4,5},{5,4},{6,7},{7,6},{8,9},{9,8},{10,11... | collective-permute-start | bytes 12296 | tf_op jit(solution)/shard_map/ppermute | solution.py:274
  607.5 17.0 %collective-permute-start.22 = (bf16[1024,512]{1,0:T(8,128)(2,1)}, bf16[1024,512]{1,0:T(8,128)(2,1)}, u32[]{:S(2)}, u32[]{:S(2)}) collective-permute-start(bf16[1024,512]{1,0:T(8,128)(2,1)} %add_convert_fusion.2), channel_id=1, source_target_pairs={{0,1},{1,2},{2,3},{3,0},{4,5},{5,6},{6,7},{7,4},{8,9},{9,10},{10,1... | collective-permute-start | bytes 3145736 | tf_op jit(solution)/shard_map/ppermute | solution.py:242
  612.0 8.2 %copy-start.12 = (bf16[1792,256]{1,0:T(8,128)(2,1)S(1)}, bf16[1792,256]{1,0:T(8,128)(2,1)}, u32[]{:S(2)}) copy-start(bf16[1792,256]{1,0:T(8,128)(2,1)} %reduce-scatter.6.cloned.1.call-done) | copy-start | bytes 2752516
  612.0 12.9 %copy-start.8 = (bf16[8,128,512]{2,1,0:T(8,128)(2,1)S(1)}, bf16[8,128,512]{2,1,0:T(8,128)(2,1)}, u32[]{:S(2)}) copy-start(bf16[8,128,512]{2,1,0:T(8,128)(2,1)} %copy-done.7) | copy-start | bytes 3145732
  612.0 12.9 %copy-start.44 = (f32[1024]{0:T(1024)S(1)}, f32[1024]{0:T(1024)}, u32[]{:S(2)}) copy-start(f32[1024]{0:T(1024)} %get-tuple-element.233) | copy-start | bytes 12292
  612.0 8.2 %collective-permute-start.24 = (f32[8,128]{1,0:T(8,128)S(1)}, f32[8,128]{1,0:T(8,128)S(1)}, u32[]{:S(2)}, u32[]{:S(2)}) collective-permute-start(f32[8,128]{1,0:T(8,128)S(1)} %bitcast_add_fusion), channel_id=1, source_target_pairs={{0,2},{1,3},{2,0},{3,1},{4,6},{5,7},{6,4},{7,5},{8,10},{9,11},{10,... | collective-permute-start | bytes 12296 | tf_op jit(solution)/shard_map/ppermute | solution.py:274
  613.4 28.2 %collective-permute-start.25 = (bf16[1024,512]{1,0:T(8,128)(2,1)}, bf16[1024,512]{1,0:T(8,128)(2,1)S(1)}, u32[]{:S(2)}, u32[]{:S(2)}) collective-permute-start(bf16[1024,512]{1,0:T(8,128)(2,1)} %add_convert_fusion.1), channel_id=1, source_target_pairs={{0,1},{1,2},{2,3},{3,0},{4,5},{5,6},{6,7},{7,4},{8,9},{9,10},{10,1... | collective-permute-start | bytes 3145736 | tf_op jit(solution)/shard_map/ppermute | solution.py:242
  641.7 5.1 collective-permute-start.26
  643.2 19.9 %all-to-all-start.1 = ((bf16[8,128,512]{2,1,0:T(8,128)(2,1)}), bf16[8,128,512]{2,1,0:T(8,128)(2,1)S(1)}, u32[]{:S(2)}, u32[]{:S(2)}) async-start(bf16[8,128,512]{2,1,0:T(8,128)(2,1)} %bitcast.13), calls=%async_computation.4 | async-start | bytes 2097152 | tf_op jit(solution)/shard_map/all_to_all | solution.py:573
  646.8 8.3 %copy-start.38 = (f32[512,256]{1,0:T(8,128)S(1)}, f32[512,256]{1,0:T(8,128)}, u32[]{:S(2)}) copy-start(f32[512,256]{1,0:T(8,128)} %param.45) | copy-start | bytes 1572868
  646.8 5.7 collective-permute-start.27
  649.3 10.5 %copy-start.53 = (f32[4,8]{1,0:T(4,128)S(1)}, f32[4,8]{1,0:T(4,128)}, u32[]{:S(2)}) copy-start(f32[4,8]{1,0:T(4,128)} %param.51) | copy-start | bytes 388
  (37 other events, 119.5 us)
Sparse Core Ops, SparseCore 0:
  31.1 44.9 all-gather.4
  78.5 51.2 all-gather.6
  132.3 63.2 all-gather.8
  374.5 78.1 reduce-scatter.3
  487.9 62.7 reduce-scatter.5
  572.0 57.6 reduce-scatter.7
